TPU v7x, 32 devices: a whole 2x2x4 slice. The times are simulated.
32 devices in a mesh: dp: 4 (over y, core), seq: 8 (over z, x).
Axes of the slice: x: 2, y: 2, z: 4, core: 2. Of those that a mesh axis runs over, the one named last changes fastest.
Arguments:
- token_ids: int32 [4, 1024], P('dp', 'seq'), may hold values from 0 to 255
- cotangent: bfloat16 [4, 1024, 768], P('dp', 'seq'), may hold values from -6 to 6
- table: bfloat16 [256, 768], replicated, may hold values from -12 to 12
- w_query: bfloat16 [768, 768], replicated, may hold values from -2 to 2
- w_key: bfloat16 [768, 768], replicated, may hold values from -2 to 2
- w_value: bfloat16 [768, 768], replicated, may hold values from -0.21875 to 0.21875
- w_out: bfloat16 [768, 768], replicated, may hold values from -0.21875 to 0.21875
- window: int32 [12], replicated, may hold values from 64 to 512, as said below
Outputs:
- grad_input: bfloat16 [4, 1024, 768], P('dp', 'seq')
- weight_grads: float32 [3072, 768], P('seq')
Inputs may be any that keep to these rules, and one draw needn't show every extreme that they name: Some head's window is exactly 512.
All inputs are finite; a program needn't handle non-finite values.
Results may differ from a plain program's by a relative error of at most 0.025.
Values may be sent and summed in bfloat16 or wider, within the bound.
No kernel may reach another device: no remote copies, remote signals or barrier semaphores. Data moves between devices by JAX's collectives and lax.ppermute only.
A program may use at most 128 MiB of HBM per device.

v0:
```python
import jax
import jax.numpy as jnp
from jax import lax
from jax.sharding import PartitionSpec as P

HEADS = 12
HEAD_DIM = 64
WINDOW = 512


EPSILON = 1e-05


def shifted(block, axis, distance):
    devices = range(lax.axis_size(axis))
    route = [(i - distance, i) for i in devices if i - distance in devices]
    return lax.ppermute(block, axis, route)


def rotate(values, positions):
    row_count = values.shape[0]
    shaped = values.reshape(row_count, -1, HEAD_DIM)
    middle = HEAD_DIM // 2
    frequency = 10000.0 ** (-2.0 * jnp.arange(middle, dtype=jnp.float32) / HEAD_DIM)
    angles = positions.astype(jnp.float32)[:, None] * frequency[None, :]
    cosine = jnp.cos(angles)[:, None, :]
    sine_part = jnp.sin(angles)[:, None, :]
    former = shaped[..., :middle]
    latter = shaped[..., middle:]
    turned = jnp.concatenate(
        [former * cosine - latter * sine_part, latter * cosine + former * sine_part], axis=-1
    )
    return turned.reshape(row_count, -1)


def unrotate(values, positions):
    row_count = values.shape[0]
    shaped = values.reshape(row_count, -1, HEAD_DIM)
    middle = HEAD_DIM // 2
    frequency = 10000.0 ** (-2.0 * jnp.arange(middle, dtype=jnp.float32) / HEAD_DIM)
    angles = positions.astype(jnp.float32)[:, None] * frequency[None, :]
    cosine = jnp.cos(angles)[:, None, :]
    sine_part = jnp.sin(angles)[:, None, :]
    former = shaped[..., :middle]
    latter = shaped[..., middle:]
    turned = jnp.concatenate(
        [former * cosine + latter * sine_part, latter * cosine - former * sine_part], axis=-1
    )
    return turned.reshape(row_count, -1)


def tdot(left, right):
    return lax.dot_general(
        left, right, (((0,), (0,)), ((), ())), preferred_element_type=jnp.float32
    )


def ndot(left, right):
    return lax.dot_general(
        left, right, (((1,), (1,)), ((), ())), preferred_element_type=jnp.float32
    )


def embed_rows(byte_ids, table):
    onehot = (byte_ids[:, None] == jnp.arange(table.shape[0], dtype=jnp.int32)[None, :]).astype(
        jnp.bfloat16
    )
    return jnp.dot(onehot, table, preferred_element_type=jnp.float32).astype(jnp.bfloat16)


def normalize(embedded):
    widened = embedded.astype(jnp.float32)
    inv_rms = lax.rsqrt(jnp.mean(widened * widened, axis=1, keepdims=True) + EPSILON)
    return (widened, inv_rms, (widened * inv_rms).astype(jnp.bfloat16))


def keys_values(normed, positions, w_key, w_value):
    key_rows = rotate(jnp.dot(normed, w_key, preferred_element_type=jnp.float32), positions).astype(
        jnp.bfloat16
    )
    value_rows = jnp.dot(normed, w_value, preferred_element_type=jnp.float32).astype(jnp.bfloat16)
    return (key_rows, value_rows)


def head_group(
    query_heads, key_heads, value_heads, grad_heads, group_window, own_pos, key_pos, score_scale
):
    distance = own_pos[:, None] - key_pos[None, :]
    allowed = (
        (distance[None] >= 0)
        & (distance[None] < group_window[:, None, None])
        & (key_pos[None, None, :] >= 0)
    )
    scores = (
        jnp.einsum("qhd,khd->hqk", query_heads, key_heads, preferred_element_type=jnp.float32)
        * score_scale
    )
    masked = jnp.where(allowed, scores, -1e30)
    row_max = jnp.max(masked, axis=-1, keepdims=True)
    weights = jnp.where(allowed, jnp.exp(masked - row_max), 0.0)
    probs = weights / jnp.sum(weights, axis=-1, keepdims=True)
    probs_b = probs.astype(jnp.bfloat16)
    attended = jnp.einsum(
        "hqk,khd->qhd", probs_b, value_heads, preferred_element_type=jnp.float32
    ).astype(jnp.bfloat16)
    grad_probs = jnp.einsum(
        "qhd,khd->hqk", grad_heads, value_heads, preferred_element_type=jnp.float32
    )
    row_term = jnp.sum(probs * grad_probs, axis=-1, keepdims=True)
    grad_scores = (probs * (grad_probs - row_term) * score_scale).astype(jnp.bfloat16)
    grad_query = jnp.einsum(
        "hqk,khd->qhd", grad_scores, key_heads, preferred_element_type=jnp.float32
    )
    grad_key = jnp.einsum(
        "hqk,qhd->khd", grad_scores, query_heads, preferred_element_type=jnp.float32
    )
    grad_value = jnp.einsum("hqk,qhd->khd", probs_b, grad_heads, preferred_element_type=jnp.float32)
    return (attended, grad_query, grad_key, grad_value)


def on_device(token_ids, cotangent, table, w_query, w_key, w_value, w_out, window):
    local_ids = token_ids[0]
    grad_out = cotangent[0]
    length = local_ids.shape[0]
    features = table.shape[1]
    tail_rows = min(length, WINDOW)
    reach_devs = -(-WINDOW // length)
    halo_rows = reach_devs * tail_rows
    offset = lax.axis_index("seq") * length
    own_pos = offset + jnp.arange(length, dtype=jnp.int32)
    halo_pos = offset - halo_rows + jnp.arange(halo_rows, dtype=jnp.int32)
    score_scale = HEAD_DIM ** (-0.5)
    embedded = embed_rows(local_ids, table)
    widened, inv_rms, normed = normalize(embedded)
    query = rotate(jnp.dot(normed, w_query, preferred_element_type=jnp.float32), own_pos).astype(
        jnp.bfloat16
    )
    key_own, value_own = keys_values(normed, own_pos, w_key, w_value)
    key_pieces = []
    value_pieces = []
    for hop_index in range(reach_devs):
        far_keys, far_values = shifted((key_own, value_own), "seq", hop_index + 1)
        key_pieces.insert(0, far_keys)
        value_pieces.insert(0, far_values)
    key_halo = jnp.concatenate(key_pieces, axis=0)
    value_halo = jnp.concatenate(value_pieces, axis=0)
    span_rows = halo_rows + length
    key_all = jnp.concatenate([key_halo, key_own], axis=0)
    value_all = jnp.concatenate([value_halo, value_own], axis=0)
    key_pos = jnp.concatenate([halo_pos, own_pos], axis=0)
    query_heads = query.reshape(length, HEADS, HEAD_DIM)
    key_heads = key_all.reshape(span_rows, HEADS, HEAD_DIM)
    value_heads = value_all.reshape(span_rows, HEADS, HEAD_DIM)
    grad_att = ndot(grad_out, w_out).astype(jnp.bfloat16)
    grad_heads = grad_att.reshape(length, HEADS, HEAD_DIM)
    group_size = 4
    attended_parts = []
    query_parts = []
    key_parts = []
    value_parts = []
    for group_index in range(HEADS // group_size):
        lower = group_index * group_size
        upper = lower + group_size
        outputs = head_group(
            query_heads[:, lower:upper],
            key_heads[:, lower:upper],
            value_heads[:, lower:upper],
            grad_heads[:, lower:upper],
            window[lower:upper],
            own_pos,
            key_pos,
            score_scale,
        )
        attended_parts.append(outputs[0])
        query_parts.append(outputs[1])
        key_parts.append(outputs[2])
        value_parts.append(outputs[3])
    attended = jnp.concatenate(attended_parts, axis=1).reshape(length, features)
    grad_query = jnp.concatenate(query_parts, axis=1).reshape(length, features)
    grad_key = jnp.concatenate(key_parts, axis=1).reshape(span_rows, features)
    grad_value = jnp.concatenate(value_parts, axis=1).reshape(span_rows, features)
    tail_keys = grad_key[:halo_rows].reshape(reach_devs, tail_rows, features)
    tail_values = grad_value[:halo_rows].reshape(reach_devs, tail_rows, features)
    back_keys = jnp.zeros((tail_rows, features), jnp.float32)
    back_values = jnp.zeros((tail_rows, features), jnp.float32)
    for hop_index in range(reach_devs):
        got_keys, got_values = shifted(
            (tail_keys[reach_devs - 1 - hop_index], tail_values[reach_devs - 1 - hop_index]),
            "seq",
            -(hop_index + 1),
        )
        back_keys = back_keys + got_keys
        back_values = back_values + got_values
    own_keys = grad_key[halo_rows:]
    own_values = grad_value[halo_rows:]
    own_keys = jnp.concatenate([own_keys[: length - tail_rows], own_keys + back_keys], axis=0)
    own_values = jnp.concatenate(
        [own_values[: length - tail_rows], own_values + back_values], axis=0
    )
    grad_q_lin = unrotate(grad_query, own_pos).astype(jnp.bfloat16)
    grad_k_lin = unrotate(own_keys, own_pos).astype(jnp.bfloat16)
    grad_v_lin = own_values.astype(jnp.bfloat16)
    grad_normed = ndot(grad_q_lin, w_query) + ndot(grad_k_lin, w_key) + ndot(grad_v_lin, w_value)
    scaled = widened * inv_rms
    grad_input = (
        inv_rms * (grad_normed - scaled * jnp.mean(grad_normed * scaled, axis=1, keepdims=True))
    ).astype(jnp.bfloat16)
    term = jnp.concatenate(
        [
            tdot(normed, grad_q_lin),
            tdot(normed, grad_k_lin),
            tdot(normed, grad_v_lin),
            tdot(attended, grad_out),
        ],
        axis=0,
    )
    shares = lax.psum_scatter(term.astype(jnp.bfloat16), "seq", scatter_dimension=0, tiled=True)
    weight_grads = lax.psum(shares, "dp").astype(jnp.float32)
    return (grad_input[None], weight_grads)


def solution(mesh):
    return jax.shard_map(
        on_device,
        mesh=mesh,
        in_specs=(P("dp", "seq"), P("dp", "seq", None), P(), P(), P(), P(), P(), P()),
        out_specs=(P("dp", "seq", None), P("seq", None)),
        check_vma=False,
    )
```

profile of v0, /device:TPU:0, one launch (start us, length us, event | category | flops | bytes accessed | tf_op | source)
XLA Modules:
  0.0 377.3 jit_solution(1053350831816788431)
XLA Ops:
  10.4 5.5 %collective-permute-start.7 = (bf16[128,768]{1,0:T(8,128)(2,1)}, bf16[128,768]{1,0:T(8,128)(2,1)}, u32[]{:S(2)}, u32[]{:S(2)}) collective-permute-start(bf16[128,768]{1,0:T(8,128)(2,1)} %convolution_convert_fusion.4), channel_id=1, source_target_pairs={{0,1},{1,2},{2,3},{3,4},{4,5},{5,6},{6,7},{8,9},{9,10},{10,11},{11... | collective-permute-start | bytes 589832 | tf_op jit(solution)/shard_map/ppermute | solution.py:17
  15.9 3.5 collective-permute-start.6
  19.4 4.5 %collective-permute-start.5 = (bf16[128,768]{1,0:T(8,128)(2,1)}, bf16[128,768]{1,0:T(8,128)(2,1)}, u32[]{:S(2)}, u32[]{:S(2)}) collective-permute-start(bf16[128,768]{1,0:T(8,128)(2,1)} %convolution_convert_fusion.4), channel_id=1, source_target_pairs={{0,3},{1,4},{2,5},{3,6},{4,7},{8,11},{9,12},{10,13},{11,14},{12,15... | collective-permute-start | bytes 589832 | tf_op jit(solution)/shard_map/ppermute | solution.py:17
  23.9 2.0 collective-permute-start.4
  29.4 4.1 %collective-permute-start.3 = (bf16[128,768]{0,1:T(8,128)(2,1)}, bf16[128,768]{0,1:T(8,128)(2,1)}, u32[]{:S(2)}, u32[]{:S(2)}) collective-permute-start(bf16[128,768]{0,1:T(8,128)(2,1)} %bitcast.2), channel_id=1, source_target_pairs={{0,1},{1,2},{2,3},{3,4},{4,5},{5,6},{6,7},{8,9},{9,10},{10,11},{11... | collective-permute-start | bytes 589832 | tf_op jit(solution)/shard_map/ppermute | solution.py:17
  34.9 2.5 convolution_convert_fusion.5
  44.8 5.6 %collective-permute-start.1 = (bf16[128,768]{0,1:T(8,128)(2,1)}, bf16[128,768]{0,1:T(8,128)(2,1)}, u32[]{:S(2)}, u32[]{:S(2)}) collective-permute-start(bf16[128,768]{0,1:T(8,128)(2,1)} %bitcast.2), channel_id=1, source_target_pairs={{0,3},{1,4},{2,5},{3,6},{4,7},{8,11},{9,12},{10,13},{11,14},{12,15... | collective-permute-start | bytes 589832 | tf_op jit(solution)/shard_map/ppermute | solution.py:17
  52.0 4.6 %collective-permute-start = (bf16[128,768]{0,1:T(8,128)(2,1)}, bf16[128,768]{0,1:T(8,128)(2,1)}, u32[]{:S(2)}, u32[]{:S(2)}) collective-permute-start(bf16[128,768]{0,1:T(8,128)(2,1)} %bitcast.2), channel_id=1, source_target_pairs={{0,4},{1,5},{2,6},{3,7},{8,12},{9,13},{10,14},{11,15},{16,20},{17,... | collective-permute-start | bytes 589832 | tf_op jit(solution)/shard_map/ppermute | solution.py:17
  61.5 2.3 copy.23
  64.8 2.4 fusion.68
  78.5 5.9 %fusion.55 = f32[128,4,64]{0,2,1:T(8,128)} fusion(bf16[640,12,64]{0,2,1:T(8,128)(2,1)} %bitcast.121, f32[4,128,640]{2,1,0:T(8,128)} %fusion.68, f32[4,128,640]{2,1,0:T(8,128)} %copy-done.8, f32[4,128]{1,0:T(4,128)} %copy-done.43), kind=kOutput, calls=%fused_computation.66 | convolution fusion | flops 44237952 | bytes 3737600 | tf_op jit(solution)/shard_map/hqk,khd->qhd/dot_general | solution.py:111
  84.4 6.1 %convolution_bitcast_fusion.3 = f32[640,4,64]{0,2,1:T(8,128)} fusion(f32[4,128,640]{2,1,0:T(8,128)} %fusion.68, bf16[128,12,32]{0,2,1:T(8,128)(2,1)} %get-tuple-element.17, bf16[128,12,32]{0,2,1:T(8,128)(2,1)} %get-tuple-element.16, f32[4,128,640]{2,1,0:T(8,128)} %copy-done.8, f32[4,128]{1,0:T(4,128)} %copy-done.43), kind=kOutput, calls=%fused_computation.46 | convolution fusion | flops 44631168 | bytes 3475456 | tf_op jit(solution)/shard_map/hqk,qhd->khd/dot_general | solution.py:114
  90.5 2.6 convolution_bitcast_fusion
  97.4 5.9 %fusion.52 = f32[128,4,64]{0,2,1:T(8,128)} fusion(bf16[640,12,64]{0,2,1:T(8,128)(2,1)} %bitcast.123, f32[4,128,640]{2,1,0:T(8,128)} %fusion.71, f32[4,128,640]{2,1,0:T(8,128)} %copy-done.9, f32[4,128]{1,0:T(4,128)} %copy-done.44), kind=kOutput, calls=%fused_computation.65 | convolution fusion | flops 44237952 | bytes 3737600 | tf_op jit(solution)/shard_map/hqk,khd->qhd/dot_general | solution.py:111
  103.3 6.0 %convolution_bitcast_fusion.4 = f32[640,4,64]{0,2,1:T(8,128)} fusion(f32[4,128,640]{2,1,0:T(8,128)} %fusion.71, bf16[128,12,32]{0,2,1:T(8,128)(2,1)} %get-tuple-element.17, bf16[128,12,32]{0,2,1:T(8,128)(2,1)} %get-tuple-element.16, f32[4,128,640]{2,1,0:T(8,128)} %copy-done.9, f32[4,128]{1,0:T(4,128)} %copy-done.44), kind=kOutput, calls=%fused_computation.47 | convolution fusion | flops 44631168 | bytes 3475456 | tf_op jit(solution)/shard_map/hqk,qhd->khd/dot_general | solution.py:114
  109.3 2.6 convolution_bitcast_fusion.1
  115.6 5.2 %fusion.49 = f32[128,4,64]{0,2,1:T(8,128)S(1)} fusion(bf16[640,12,64]{0,2,1:T(8,128)(2,1)} %bitcast.125, f32[4,128,640]{2,1,0:T(8,128)} %fusion.74, f32[4,128,640]{2,1,0:T(8,128)} %copy-done.7, f32[4,128]{1,0:T(4,128)} %copy-done.41), kind=kOutput, calls=%fused_computation.64 | convolution fusion | flops 44237952 | bytes 3737600 | tf_op jit(solution)/shard_map/hqk,khd->qhd/dot_general | solution.py:111
  120.9 5.9 %convolution_bitcast_fusion.5 = f32[640,4,64]{0,2,1:T(8,128)} fusion(f32[4,128,640]{2,1,0:T(8,128)} %fusion.74, bf16[128,12,32]{0,2,1:T(8,128)(2,1)S(1)} %copy-done.30, bf16[128,12,32]{0,2,1:T(8,128)(2,1)S(1)} %copy-done.26, f32[4,128,640]{2,1,0:T(8,128)} %copy-done.7, f32[4,128]{1,0:T(4,128)S(1)} %copy-done.42), kind=kOutput, calls=%fused_computation.48 | convolution fusion | flops 44631168 | bytes 3475456 | tf_op jit(solution)/shard_map/hqk,qhd->khd/dot_general | solution.py:114
  137.9 21.4 %collective-permute-done.15 = f32[128,768]{0,1:T(8,128)S(1)} collective-permute-done((f32[128,768]{0,1:T(8,128)S(1)}, f32[128,768]{0,1:T(8,128)S(1)}, u32[]{:S(2)}, u32[]{:S(2)}) %collective-permute-start.15) | collective-permute-done | bytes 393248 | tf_op jit(solution)/shard_map/ppermute | solution.py:17
  163.9 48.2 %collective-permute-done.11 = f32[128,768]{0,1:T(8,128)S(1)} collective-permute-done((f32[128,768]{0,1:T(8,128)S(1)}, f32[128,768]{0,1:T(8,128)S(1)}, u32[]{:S(2)}, u32[]{:S(2)}) %collective-permute-start.11) | collective-permute-done | bytes 393248 | tf_op jit(solution)/shard_map/ppermute | solution.py:17
  213.4 2.5 pad_maximum_fusion
  218.5 114.2 %reduce-scatter.2.cloned.1.call-done = bf16[384,768]{1,0:T(8,128)(2,1)} async-done(((bf16[3072,768]{1,0:T(8,128)(2,1)}), bf16[384,768]{1,0:T(8,128)(2,1)}) %reduce-scatter.2.cloned.1.call-update) | async-done | bytes 589840 | tf_op jit(solution)/shard_map/reduce_scatter | solution.py:217
  333.5 34.8 %all-reduce.2.cloned.1.call-done = bf16[384,768]{1,0:T(8,128)(2,1)} async-done(((bf16[384,768]{1,0:T(8,128)(2,1)}), bf16[384,768]{1,0:T(8,128)(2,1)}) %all-reduce.2.cloned.1.call-update) | async-done | bytes 589840 | tf_op jit(solution)/shard_map/psum | solution.py:218
  368.3 2.2 convert_element_type.109
  (183 shorter events, 62.3 us)
Async XLA Ops:
  7.2 325.5 %reduce-scatter.2.cloned.1.call-start = ((), (), s32[]{:S(2)}) async-start(), calls=%async_computation.1 | async-start | bytes 5308416 | tf_op jit(solution)/shard_map/reduce_scatter | solution.py:217
  7.2 18.6 %copy-start.1 = (bf16[768,768]{1,0:T(8,128)(2,1)S(1)}, bf16[768,768]{1,0:T(8,128)(2,1)}, u32[]{:S(2)}) copy-start(bf16[768,768]{1,0:T(8,128)(2,1)} %param.11) | copy-start | bytes 3538948
  10.4 47.9 %collective-permute-start.7 = (bf16[128,768]{1,0:T(8,128)(2,1)}, bf16[128,768]{1,0:T(8,128)(2,1)}, u32[]{:S(2)}, u32[]{:S(2)}) collective-permute-start(bf16[128,768]{1,0:T(8,128)(2,1)} %convolution_convert_fusion.4), channel_id=1, source_target_pairs={{0,1},{1,2},{2,3},{3,4},{4,5},{5,6},{6,7},{8,9},{9,10},{10,11},{11... | collective-permute-start | bytes 589832 | tf_op jit(solution)/shard_map/ppermute | solution.py:17
  15.9 36.1 %collective-permute-start.6 = (bf16[128,768]{1,0:T(8,128)(2,1)}, bf16[128,768]{1,0:T(8,128)(2,1)}, u32[]{:S(2)}, u32[]{:S(2)}) collective-permute-start(bf16[128,768]{1,0:T(8,128)(2,1)} %convolution_convert_fusion.4), channel_id=1, source_target_pairs={{0,2},{1,3},{2,4},{3,5},{4,6},{5,7},{8,10},{9,11},{10,12},{11,13},... | collective-permute-start | bytes 589832 | tf_op jit(solution)/shard_map/ppermute | solution.py:17
  19.4 25.4 %collective-permute-start.5 = (bf16[128,768]{1,0:T(8,128)(2,1)}, bf16[128,768]{1,0:T(8,128)(2,1)}, u32[]{:S(2)}, u32[]{:S(2)}) collective-permute-start(bf16[128,768]{1,0:T(8,128)(2,1)} %convolution_convert_fusion.4), channel_id=1, source_target_pairs={{0,3},{1,4},{2,5},{3,6},{4,7},{8,11},{9,12},{10,13},{11,14},{12,15... | collective-permute-start | bytes 589832 | tf_op jit(solution)/shard_map/ppermute | solution.py:17
  23.9 17.3 %collective-permute-start.4 = (bf16[128,768]{1,0:T(8,128)(2,1)}, bf16[128,768]{1,0:T(8,128)(2,1)}, u32[]{:S(2)}, u32[]{:S(2)}) collective-permute-start(bf16[128,768]{1,0:T(8,128)(2,1)} %convolution_convert_fusion.4), channel_id=1, source_target_pairs={{0,4},{1,5},{2,6},{3,7},{8,12},{9,13},{10,14},{11,15},{16,20},{17,... | collective-permute-start | bytes 589832 | tf_op jit(solution)/shard_map/ppermute | solution.py:17
  27.7 7.2 %copy-start.10 = (bf16[1,128,768]{2,1,0:T(8,128)(2,1)S(1)}, bf16[1,128,768]{2,1,0:T(8,128)(2,1)}, u32[]{:S(2)}) copy-start(bf16[1,128,768]{2,1,0:T(8,128)(2,1)} %param.9) | copy-start | bytes 589828
  29.4 42.8 %collective-permute-start.3 = (bf16[128,768]{0,1:T(8,128)(2,1)}, bf16[128,768]{0,1:T(8,128)(2,1)}, u32[]{:S(2)}, u32[]{:S(2)}) collective-permute-start(bf16[128,768]{0,1:T(8,128)(2,1)} %bitcast.2), channel_id=1, source_target_pairs={{0,1},{1,2},{2,3},{3,4},{4,5},{5,6},{6,7},{8,9},{9,10},{10,11},{11... | collective-permute-start | bytes 589832 | tf_op jit(solution)/shard_map/ppermute | solution.py:17
  41.2 28.5 %collective-permute-start.2 = (bf16[128,768]{0,1:T(8,128)(2,1)}, bf16[128,768]{0,1:T(8,128)(2,1)}, u32[]{:S(2)}, u32[]{:S(2)}) collective-permute-start(bf16[128,768]{0,1:T(8,128)(2,1)} %bitcast.2), channel_id=1, source_target_pairs={{0,2},{1,3},{2,4},{3,5},{4,6},{5,7},{8,10},{9,11},{10,12},{11,13},... | collective-permute-start | bytes 589832 | tf_op jit(solution)/shard_map/ppermute | solution.py:17
  44.8 22.5 %collective-permute-start.1 = (bf16[128,768]{0,1:T(8,128)(2,1)}, bf16[128,768]{0,1:T(8,128)(2,1)}, u32[]{:S(2)}, u32[]{:S(2)}) collective-permute-start(bf16[128,768]{0,1:T(8,128)(2,1)} %bitcast.2), channel_id=1, source_target_pairs={{0,3},{1,4},{2,5},{3,6},{4,7},{8,11},{9,12},{10,13},{11,14},{12,15... | collective-permute-start | bytes 589832 | tf_op jit(solution)/shard_map/ppermute | solution.py:17
  52.0 11.8 %collective-permute-start = (bf16[128,768]{0,1:T(8,128)(2,1)}, bf16[128,768]{0,1:T(8,128)(2,1)}, u32[]{:S(2)}, u32[]{:S(2)}) collective-permute-start(bf16[128,768]{0,1:T(8,128)(2,1)} %bitcast.2), channel_id=1, source_target_pairs={{0,4},{1,5},{2,6},{3,7},{8,12},{9,13},{10,14},{11,15},{16,20},{17,... | collective-permute-start | bytes 589832 | tf_op jit(solution)/shard_map/ppermute | solution.py:17
  130.5 6.9 %copy-start.21 = (f32[128,4,64]{0,2,1:T(8,128)S(1)}, f32[128,4,64]{0,2,1:T(8,128)}, u32[]{:S(2)}) copy-start(f32[128,4,64]{0,2,1:T(8,128)} %fusion.55) | copy-start | bytes 393220
  130.5 6.9 %copy-start.22 = (f32[128,4,64]{0,2,1:T(8,128)S(1)}, f32[128,4,64]{0,2,1:T(8,128)}, u32[]{:S(2)}) copy-start(f32[128,4,64]{0,2,1:T(8,128)} %fusion.52) | copy-start | bytes 393220
  130.7 28.6 %collective-permute-start.15 = (f32[128,768]{0,1:T(8,128)S(1)}, f32[128,768]{0,1:T(8,128)S(1)}, u32[]{:S(2)}, u32[]{:S(2)}) collective-permute-start(f32[128,768]{0,1:T(8,128)S(1)} %bitcast.119), channel_id=1, source_target_pairs={{4,0},{5,1},{6,2},{7,3},{12,8},{13,9},{14,10},{15,11},{20,16},{21,... | collective-permute-start | bytes 1179656 | tf_op jit(solution)/shard_map/ppermute | solution.py:17
  132.2 28.4 %collective-permute-start.13 = (f32[128,768]{0,1:T(8,128)S(1)}, f32[128,768]{0,1:T(8,128)S(1)}, u32[]{:S(2)}, u32[]{:S(2)}) collective-permute-start(f32[128,768]{0,1:T(8,128)S(1)} %bitcast.118), channel_id=1, source_target_pairs={{2,0},{3,1},{4,2},{5,3},{6,4},{7,5},{10,8},{11,9},{12,10},{13,11},... | collective-permute-start | bytes 1179656 | tf_op jit(solution)/shard_map/ppermute | solution.py:17
  133.5 28.4 %collective-permute-start.14 = (f32[128,768]{0,1:T(8,128)S(1)}, f32[128,768]{0,1:T(8,128)S(1)}, u32[]{:S(2)}, u32[]{:S(2)}) collective-permute-start(f32[128,768]{0,1:T(8,128)S(1)} %bitcast.117), channel_id=1, source_target_pairs={{3,0},{4,1},{5,2},{6,3},{7,4},{11,8},{12,9},{13,10},{14,11},{15,12... | collective-permute-start | bytes 1179656 | tf_op jit(solution)/shard_map/ppermute | solution.py:17
  134.8 28.4 %collective-permute-start.12 = (f32[128,768]{0,1:T(8,128)S(1)}, f32[128,768]{0,1:T(8,128)S(1)}, u32[]{:S(2)}, u32[]{:S(2)}) collective-permute-start(f32[128,768]{0,1:T(8,128)S(1)} %bitcast.116), channel_id=1, source_target_pairs={{1,0},{2,1},{3,2},{4,3},{5,4},{6,5},{7,6},{9,8},{10,9},{11,10},{12... | collective-permute-start | bytes 1179656 | tf_op jit(solution)/shard_map/ppermute | solution.py:17
  136.1 76.0 %collective-permute-start.11 = (f32[128,768]{0,1:T(8,128)S(1)}, f32[128,768]{0,1:T(8,128)S(1)}, u32[]{:S(2)}, u32[]{:S(2)}) collective-permute-start(f32[128,768]{0,1:T(8,128)S(1)} %bitcast.115), channel_id=1, source_target_pairs={{4,0},{5,1},{6,2},{7,3},{12,8},{13,9},{14,10},{15,11},{20,16},{21,... | collective-permute-start | bytes 1179656 | tf_op jit(solution)/shard_map/ppermute | solution.py:17
  159.3 52.8 %collective-permute-start.9 = (f32[128,768]{0,1:T(8,128)S(1)}, f32[128,768]{0,1:T(8,128)S(1)}, u32[]{:S(2)}, u32[]{:S(2)}) collective-permute-start(f32[128,768]{0,1:T(8,128)S(1)} %bitcast.114), channel_id=1, source_target_pairs={{2,0},{3,1},{4,2},{5,3},{6,4},{7,5},{10,8},{11,9},{12,10},{13,11},... | collective-permute-start | bytes 1179656 | tf_op jit(solution)/shard_map/ppermute | solution.py:17
  160.6 51.5 %collective-permute-start.10 = (f32[128,768]{0,1:T(8,128)S(1)}, f32[128,768]{0,1:T(8,128)S(1)}, u32[]{:S(2)}, u32[]{:S(2)}) collective-permute-start(f32[128,768]{0,1:T(8,128)S(1)} %bitcast.113), channel_id=1, source_target_pairs={{3,0},{4,1},{5,2},{6,3},{7,4},{11,8},{12,9},{13,10},{14,11},{15,12... | collective-permute-start | bytes 1179656 | tf_op jit(solution)/shard_map/ppermute | solution.py:17
  161.9 50.2 %collective-permute-start.8 = (f32[128,768]{0,1:T(8,128)S(1)}, f32[128,768]{0,1:T(8,128)S(1)}, u32[]{:S(2)}, u32[]{:S(2)}) collective-permute-start(f32[128,768]{0,1:T(8,128)S(1)} %bitcast.112), channel_id=1, source_target_pairs={{1,0},{2,1},{3,2},{4,3},{5,4},{6,5},{7,6},{9,8},{10,9},{11,10},{12... | collective-permute-start | bytes 1179656 | tf_op jit(solution)/shard_map/ppermute | solution.py:17
  163.8 48.4 %copy-start.18 = (f32[128,32]{0,1:T(8,128)S(1)}, f32[128,32]{0,1:T(8,128)}, u32[]{:S(2)}) copy-start(f32[128,32]{0,1:T(8,128)} %copy-done.17) | copy-start | bytes 49156
  163.9 48.4 %copy-start.20 = (f32[128,32]{0,1:T(8,128)S(1)}, f32[128,32]{0,1:T(8,128)}, u32[]{:S(2)}) copy-start(f32[128,32]{0,1:T(8,128)} %copy-done.19) | copy-start | bytes 49156
  215.9 152.4 %all-reduce.2.cloned.1.call-start = ((), (), s32[]{:S(2)}) async-start(), calls=%async_computation.2 | async-start | bytes 1179648 | tf_op jit(solution)/shard_map/psum | solution.py:218
  (42 other events, 108.0 us)
Sparse Core Ops, SparseCore 0:
  216.1 116.5 reduce-scatter.1
  335.0 33.2 all-reduce.1
where the time goes:
time: 378 us; the launch traced here: 377 us
  waiting for transfers between devices  219 us (58%)
  matrix products  63.3 us (17%)
  starting transfers between devices  42.3 us (11%)
  local copies, waits for them, and re-layouts  26.2 us (7%)
  between operations  14.8 us (4%)
  other arithmetic  12.1 us (3%)
    reduce_scatter x1, waiting for transfers between devices, on_device(): lax.psum_scatter(term.astype(jnp.bfloat16), 'seq', scatter_dimension=0, t...  114 us
    ppermute x16, waiting for transfers between devices, shifted(): return lax.ppermute(block, axis, route)  69.6 us
    ppermute x16, starting transfers between devices, shifted(): return lax.ppermute(block, axis, route)  42.2 us
    psum x1, waiting for transfers between devices, on_device(): weight_grads = lax.psum(shares, 'dp').astype(jnp.float32)  34.8 us
    unnamed x104, local copies, waits for them, and re-layouts  18.3 us
    dot_general x3, matrix products, head_group(): jnp.einsum('hqk,qhd->khd', grad_scores, query_heads, preferred_element_ty...  17.9 us
    dot_general x3, matrix products, head_group(): jnp.einsum('hqk,khd->qhd', grad_scores, key_heads, preferred_element_type...  17 us
  transfers between devices with their start and end apart: 18, of which 4 were waited for; matrix products, arithmetic and copies ran while one was open for 9% of the time, Pallas kernels for 0%

commit v1 on v0

--- a/solution.py
+++ b/solution.py
@@ -1,6 +1,10 @@
+import functools
+
 import jax
 import jax.numpy as jnp
 from jax import lax
+from jax.experimental import pallas as pl
+from jax.experimental.pallas import tpu as pltpu
 from jax.sharding import PartitionSpec as P
 
 HEADS = 12
@@ -118,7 +122,7 @@
     return (attended, grad_query, grad_key, grad_value)
 
 
-def on_device(token_ids, cotangent, table, w_query, w_key, w_value, w_out, window):
+def general_device(token_ids, cotangent, table, w_query, w_key, w_value, w_out, window):
     local_ids = token_ids[0]
     grad_out = cotangent[0]
     length = local_ids.shape[0]
@@ -219,6 +223,511 @@
     return (grad_input[None], weight_grads)
 
 
+GROUPS = 4
+GROUP_HEADS = HEADS // GROUPS
+GROUP_COLS = GROUP_HEADS * HEAD_DIM
+TILE = 256
+TOKEN_ROWS = 16
+HALF = HEAD_DIM // 2
+VMEM_BYTES = 48 * 1024 * 1024
+
+
+def key_span(query_tile):
+    first = max(0, query_tile - WINDOW // TILE)
+    return (first * TILE, (query_tile - first + 1) * TILE)
+
+
+def normed_table(table_ref):
+    widened = table_ref[...].astype(jnp.float32)
+    inv_rms = lax.rsqrt(jnp.mean(widened * widened, axis=1, keepdims=True) + EPSILON)
+    return (widened * inv_rms).astype(jnp.bfloat16)
+
+
+def onehot_columns(tokens, vocab):
+    rows = lax.broadcasted_iota(jnp.int32, (vocab, tokens.shape[1]), 0)
+    return (rows == tokens).astype(jnp.float32).astype(jnp.bfloat16)
+
+
+def send_kernel(tokens_ref, cotangent_ref, out_weights_ref, early_ref, late_ref):
+    cotangent = cotangent_ref[...]
+    grad_att = ndot(out_weights_ref[...], cotangent).astype(jnp.bfloat16)
+    block = tokens_ref.shape[1]
+    tokens = jnp.broadcast_to(tokens_ref[...].astype(jnp.float32), (TOKEN_ROWS, block)).astype(
+        jnp.bfloat16
+    )
+    columns = late_ref.shape[2]
+    for target in range(2 * GROUPS):
+        group, side = divmod(target, 2)
+        early_ref[target, :GROUP_COLS, :] = grad_att[
+            group * GROUP_COLS : (group + 1) * GROUP_COLS
+        ]
+        early_ref[target, GROUP_COLS:, :] = tokens
+        late_ref[target] = cotangent[:, side * columns : (side + 1) * columns]
+
+
+def attention_kernel(
+    meta_ref,
+    early_ref,
+    table_ref,
+    weights_ref,
+    cosine_ref,
+    sine_ref,
+    rows_ref,
+    sums_ref,
+    attended_ref,
+    query_key_ref,
+    zero_query_ref,
+    key_t_ref,
+    value_ref,
+    value_t_ref,
+    grad_att_ref,
+    onehot_ref,
+    grad_query_ref,
+    grad_key_ref,
+    grad_value_ref,
+):
+    head = pl.program_id(0)
+    blocks, _, block = early_ref.shape
+    length = blocks * block
+    vocab = table_ref.shape[0]
+    half_vocab = vocab // 2
+    cosine = cosine_ref[...]
+    sine_part = sine_ref[...]
+    blank = jnp.zeros((HEAD_DIM, length), jnp.float32)
+
+    @pl.when(head == 0)
+    def _():
+        normed = normed_table(table_ref)
+        lookup = jnp.dot(normed, weights_ref[...], preferred_element_type=jnp.float32).T
+        upper = lookup.astype(jnp.bfloat16)
+        lower = (lookup - upper.astype(jnp.float32)).astype(jnp.bfloat16)
+        for source in range(blocks):
+            lanes = slice(source * block, (source + 1) * block)
+            tokens = early_ref[source, GROUP_COLS : GROUP_COLS + TOKEN_ROWS, :]
+            tokens = tokens.astype(jnp.float32)[:1].astype(jnp.int32)
+            onehot_ref[:, lanes] = onehot_columns(tokens, vocab)
+            grad_att_ref[:, :, lanes] = early_ref[source, :GROUP_COLS, :].reshape(
+                GROUP_HEADS, HEAD_DIM, block
+            )
+        onehot = onehot_ref[...]
+
+        def chosen(start):
+            rows = slice(start, start + HEAD_DIM)
+            return jnp.dot(upper[rows], onehot, preferred_element_type=jnp.float32) + jnp.dot(
+                lower[rows], onehot, preferred_element_type=jnp.float32
+            )
+
+        def turned(columns):
+            former = columns[:HALF]
+            latter = columns[HALF:]
+            return jnp.concatenate(
+                [former * cosine - latter * sine_part, latter * cosine + former * sine_part], axis=0
+            )
+
+        for index in range(GROUP_HEADS):
+            query = turned(chosen(index * HEAD_DIM)) * HEAD_DIM ** (-0.5)
+            keys = turned(chosen(GROUP_COLS + index * HEAD_DIM))
+            values = chosen(2 * GROUP_COLS + index * HEAD_DIM)
+            query_key_ref[index] = jnp.concatenate([query, keys], axis=0).T.astype(jnp.bfloat16)
+            value_ref[index] = jnp.concatenate([values, blank], axis=0).T.astype(jnp.bfloat16)
+            zero_query_ref[index] = jnp.concatenate([blank, query], axis=0).astype(jnp.bfloat16)
+            key_t_ref[index] = keys.astype(jnp.bfloat16)
+            value_t_ref[index] = values.astype(jnp.bfloat16)
+
+    width = meta_ref[head]
+    grad_att = grad_att_ref[head]
+    wide_grad = grad_att.astype(jnp.float32)
+    grad_blank = jnp.concatenate([wide_grad, blank], axis=0).astype(jnp.bfloat16)
+    blank_grad = jnp.concatenate([blank, wide_grad], axis=0).T.astype(jnp.bfloat16)
+    grad_key_ref[...] = jnp.zeros_like(grad_key_ref)
+    grad_value_ref[...] = jnp.zeros_like(grad_value_ref)
+    distance = lax.broadcasted_iota(jnp.int32, (TILE, TILE), 1) - lax.broadcasted_iota(
+        jnp.int32, (TILE, TILE), 0
+    )
+    for query_tile in range(length // TILE):
+        first, count = key_span(query_tile)
+        columns = slice(query_tile * TILE, (query_tile + 1) * TILE)
+        scores = jnp.dot(
+            query_key_ref[head, first : first + count, :],
+            zero_query_ref[head, :, columns],
+            preferred_element_type=jnp.float32,
+        )
+        masked = []
+        for key_tile in range(count // TILE):
+            offset = query_tile * TILE - first - key_tile * TILE
+            allowed = distance < width - offset
+            if offset == 0:
+                allowed = allowed & (distance >= 0)
+            part = scores[key_tile * TILE : (key_tile + 1) * TILE]
+            masked.append(jnp.where(allowed, part, -1e30))
+        masked = jnp.concatenate(masked, axis=0)
+        row_max = jnp.max(masked, axis=0, keepdims=True)
+        weights = jnp.exp(masked - row_max)
+        probs = weights * (1.0 / jnp.sum(weights, axis=0, keepdims=True))
+        rounded = probs.astype(jnp.bfloat16)
+        attended = jnp.dot(
+            value_t_ref[head, :, first : first + count], rounded, preferred_element_type=jnp.float32
+        )
+        attended_ref[pl.ds(pl.multiple_of(head * HEAD_DIM, HEAD_DIM), HEAD_DIM), columns] = (
+            attended.astype(jnp.bfloat16)
+        )
+        row_term = jnp.sum(attended * wide_grad[:, columns], axis=0, keepdims=True)
+        grad_probs = jnp.dot(
+            value_ref[head, first : first + count, :],
+            grad_blank[:, columns],
+            preferred_element_type=jnp.float32,
+        )
+        grad_scores = (probs * (grad_probs - row_term)).astype(jnp.bfloat16)
+        grad_query_ref[:, columns] = jnp.dot(
+            key_t_ref[head, :, first : first + count],
+            grad_scores,
+            preferred_element_type=jnp.float32,
+        )
+        grad_key_ref[first : first + count, :] += jnp.dot(
+            grad_scores, query_key_ref[head, columns, :], preferred_element_type=jnp.float32
+        )
+        grad_value_ref[first : first + count, :] += jnp.dot(
+            rounded, blank_grad[columns, :], preferred_element_type=jnp.float32
+        )
+
+    def turned_back(columns):
+        former = columns[:HALF]
+        latter = columns[HALF:]
+        return jnp.concatenate(
+            [former * cosine + latter * sine_part, latter * cosine - former * sine_part], axis=0
+        )
+
+    lanes = lax.broadcasted_iota(jnp.int32, grad_key_ref.shape, 1)
+    both = jnp.where(lanes < HEAD_DIM, grad_key_ref[...], grad_value_ref[...]).T
+    grads = jnp.concatenate(
+        [
+            turned_back(grad_query_ref[...] * HEAD_DIM ** (-0.5)),
+            turned_back(both[:HEAD_DIM]),
+            both[HEAD_DIM:],
+        ],
+        axis=0,
+    ).astype(jnp.bfloat16)
+    sums = ndot(grads, onehot_ref[...]).astype(jnp.bfloat16)
+    for matrix in range(3):
+        rows = slice(matrix * HEAD_DIM, (matrix + 1) * HEAD_DIM)
+        place = pl.ds(
+            pl.multiple_of(matrix * GROUP_COLS + head * HEAD_DIM, HEAD_DIM), HEAD_DIM
+        )
+        for core in range(2):
+            lane = core * half_vocab
+            sums_ref[core, place, :] = sums[rows, lane : lane + half_vocab]
+        for target in range(GROUPS):
+            start = target * 2 * block
+            even = grads[rows, start : start + block]
+            odd = grads[rows, start + block : start + 2 * block]
+            rows_ref[target, place, :] = jnp.where(meta_ref[GROUP_HEADS] == 0, even, odd)
+
+
+def out_kernel(attended_ref, cotangent_ref, out_ref):
+    total = jnp.dot(attended_ref[...], cotangent_ref[...], preferred_element_type=jnp.float32)
+    rows = total.shape[0] // 2
+    lanes = out_ref.shape[2]
+    for core in range(2):
+        for chunk in range(total.shape[1] // lanes):
+            out_ref[core, chunk * rows : (chunk + 1) * rows, :] = total[
+                core * rows : (core + 1) * rows, chunk * lanes : (chunk + 1) * lanes
+            ].astype(jnp.bfloat16)
+
+
+def gather_kernel(meta_ref, kept_ref, kept_out_ref, s1, s2, s3, n0, n1, f0, f1, pieces_ref):
+    group = meta_ref[GROUP_HEADS + 1]
+    rows = GROUP_COLS
+
+    @pl.when(group < 3)
+    def _():
+        own = pl.multiple_of(group * rows, rows)
+        pieces_ref[pl.ds(own, rows), :] = kept_ref[pl.ds(own, rows), :]
+        for turn, got in ((1, s1), (2, s2), (3, s3)):
+            source = lax.rem(group - turn + GROUPS, GROUPS)
+            pieces_ref[pl.ds(pl.multiple_of(source * rows, rows), rows), :] = got[...]
+        tail = pieces_ref.shape[0] - GROUPS * rows
+        pieces_ref[GROUPS * rows :, :] = jnp.zeros((tail, kept_ref.shape[1]), jnp.bfloat16)
+
+    @pl.when(group == 3)
+    def _():
+        size = kept_out_ref.shape[0]
+        own = meta_ref[GROUP_HEADS] == 1
+        pieces_ref[0:size, :] = n0[...]
+        pieces_ref[size : 2 * size, :] = f0[...]
+        pieces_ref[2 * size : 3 * size, :] = jnp.where(own, kept_out_ref[...], n1[...])
+        pieces_ref[3 * size :, :] = f1[...]
+
+
+def input_kernel(tokens_ref, table_ref, query_ref, key_ref, value_ref, rows_ref, out_ref):
+    widened = table_ref[...].astype(jnp.float32)
+    vocab = table_ref.shape[0]
+    onehot = onehot_columns(tokens_ref[...], vocab)
+    embedded = tdot(onehot, table_ref[...])
+    inv_rms = lax.rsqrt(jnp.mean(embedded * embedded, axis=1, keepdims=True) + EPSILON)
+    grad_normed = None
+    for matrix, weights in enumerate((query_ref, key_ref, value_ref)):
+        columns = jnp.concatenate(
+            [
+                rows_ref[group, matrix * GROUP_COLS : (matrix + 1) * GROUP_COLS, :]
+                for group in range(GROUPS)
+            ],
+            axis=0,
+        )
+        part = ndot(columns.astype(jnp.float32).T.astype(jnp.bfloat16), weights[...])
+        grad_normed = part if grad_normed is None else grad_normed + part
+    scaled = embedded * inv_rms
+    out_ref[...] = (
+        inv_rms * (grad_normed - scaled * jnp.mean(grad_normed * scaled, axis=1, keepdims=True))
+    ).astype(jnp.bfloat16)
+
+
+def weight_kernel(meta_ref, table_ref, mine_ref, other_ref, out_ref):
+    side_rows = out_ref.shape[0]
+    half_vocab = mine_ref.shape[1]
+    first_core = meta_ref[GROUP_HEADS + 2] == 0
+
+    @pl.when(meta_ref[GROUP_HEADS + 1] < 3)
+    def _():
+        normed = normed_table(table_ref)
+        first = normed[:, :side_rows]
+        second = normed[:, side_rows:]
+        taken = jnp.where(meta_ref[GROUP_HEADS] == 0, first, second)
+        upper = jnp.where(first_core, taken[:half_vocab], taken[half_vocab:])
+        lower = jnp.where(first_core, taken[half_vocab:], taken[:half_vocab])
+        total = None
+        for part, sums_ref in ((upper, mine_ref), (lower, other_ref)):
+            term = lax.dot_general(
+                part,
+                sums_ref[: GROUPS * GROUP_COLS, :],
+                (((0,), (1,)), ((), ())),
+                preferred_element_type=jnp.float32,
+            )
+            total = term if total is None else total + term
+        out_ref[...] = total
+
+    @pl.when(meta_ref[GROUP_HEADS + 1] == 3)
+    def _():
+        rows = GROUP_COLS // 2
+        side = meta_ref[GROUP_HEADS]
+        for core in range(2):
+            for half in range(2):
+                for plane in range(2):
+                    for chunk in range(3):
+                        place = ((2 * half + plane) * 3 + chunk) * rows
+                        here = mine_ref[place : place + rows, :]
+                        there = other_ref[place : place + rows, :]
+                        value = jnp.where(first_core == (core == 0), here, there)
+                        row = half * GROUP_COLS + core * rows
+                        column = jnp.where(side == 0, plane, 1 - plane) * 3 + chunk
+                        lanes = pl.ds(
+                            pl.multiple_of(column * half_vocab, half_vocab), half_vocab
+                        )
+                        out_ref[row : row + rows, lanes] = value.astype(jnp.float32)
+
+
+def whole(shape):
+    return pl.BlockSpec(shape, lambda *_: (0,) * len(shape))
+
+
+def kernel_call(body, steps, operands, in_specs, outs, out_specs, scratch, flops, moved):
+    return pl.pallas_call(
+        body,
+        grid=(steps,),
+        in_specs=[pl.BlockSpec(memory_space=pltpu.SMEM)] + in_specs
+        if operands[0].ndim == 1
+        else in_specs,
+        out_specs=out_specs,
+        out_shape=outs,
+        scratch_shapes=scratch,
+        compiler_params=pltpu.CompilerParams(
+            dimension_semantics=("arbitrary",), vmem_limit_bytes=VMEM_BYTES
+        ),
+        cost_estimate=pl.CostEstimate(flops=flops, bytes_accessed=moved, transcendentals=0),
+    )(*operands)
+
+
+def swapped(block, axis, bit):
+    route = [(i, i ^ bit) for i in range(lax.axis_size(axis))]
+    return lax.ppermute(block, axis, route)
+
+
+def grouped_device(token_ids, cotangent, table, w_query, w_key, w_value, w_out, window):
+    place = lax.axis_index("seq")
+    core = lax.axis_index("dp") % 2
+    group = place // 2
+    side = place % 2
+    block = token_ids.shape[1]
+    features = table.shape[1]
+    vocab = table.shape[0]
+    blocks = lax.axis_size("seq")
+    length = block * blocks
+    early, late = kernel_call(
+        send_kernel,
+        1,
+        (token_ids, cotangent[0], w_out),
+        [whole(token_ids.shape), whole((block, features)), whole(w_out.shape)],
+        [
+            jax.ShapeDtypeStruct((blocks, GROUP_COLS + TOKEN_ROWS, block), jnp.bfloat16),
+            jax.ShapeDtypeStruct((blocks, block, features // 2), jnp.bfloat16),
+        ],
+        [
+            whole((blocks, GROUP_COLS + TOKEN_ROWS, block)),
+            whole((blocks, block, features // 2)),
+        ],
+        [],
+        2 * 10**8,
+        3 * 10**6,
+    )
+    early = lax.all_to_all(early, "seq", split_axis=0, concat_axis=0, tiled=True)
+    late = lax.all_to_all(late, "seq", split_axis=0, concat_axis=0, tiled=True)
+    start = group * GROUP_COLS
+    weights = jnp.concatenate(
+        [lax.dynamic_slice_in_dim(w, start, GROUP_COLS, 1) for w in (w_query, w_key, w_value)],
+        axis=1,
+    )
+    meta = jnp.concatenate(
+        [
+            lax.dynamic_slice_in_dim(window, group * GROUP_HEADS, GROUP_HEADS, 0),
+            jnp.stack([side, group, core]).astype(jnp.int32),
+        ]
+    )
+    frequency = 10000.0 ** (-2.0 * jnp.arange(HALF, dtype=jnp.float32) / HEAD_DIM)
+    angles = frequency[:, None] * jnp.arange(length, dtype=jnp.int32).astype(jnp.float32)[None, :]
+    cosine = jnp.cos(angles)
+    sine_part = jnp.sin(angles)
+    heads_shape = (GROUP_HEADS, HEAD_DIM, length)
+    rows_shape = (GROUP_HEADS, length, 2 * HEAD_DIM)
+    rows_out = (GROUPS, 3 * GROUP_COLS, block)
+    sums_out = (2, 3 * GROUP_COLS, vocab // 2)
+    rows, sums, attended = kernel_call(
+        attention_kernel,
+        GROUP_HEADS,
+        (meta, early, table, weights, cosine, sine_part),
+        [
+            whole(early.shape),
+            whole(table.shape),
+            whole(weights.shape),
+            whole(cosine.shape),
+            whole(sine_part.shape),
+        ],
+        [
+            jax.ShapeDtypeStruct(rows_out, jnp.bfloat16),
+            jax.ShapeDtypeStruct(sums_out, jnp.bfloat16),
+            jax.ShapeDtypeStruct((GROUP_COLS, length), jnp.bfloat16),
+        ],
+        [whole(rows_out), whole(sums_out), whole((GROUP_COLS, length))],
+        [
+            pltpu.VMEM(rows_shape, jnp.bfloat16),
+            pltpu.VMEM((GROUP_HEADS, 2 * HEAD_DIM, length), jnp.bfloat16),
+            pltpu.VMEM(heads_shape, jnp.bfloat16),
+            pltpu.VMEM(rows_shape, jnp.bfloat16),
+            pltpu.VMEM(heads_shape, jnp.bfloat16),
+            pltpu.VMEM(heads_shape, jnp.bfloat16),
+            pltpu.VMEM((vocab, length), jnp.bfloat16),
+            pltpu.VMEM((HEAD_DIM, length), jnp.float32),
+            pltpu.VMEM((length, 2 * HEAD_DIM), jnp.float32),
+            pltpu.VMEM((length, 2 * HEAD_DIM), jnp.float32),
+        ],
+        8 * 10**9,
+        8 * 10**6,
+    )
+    late = late.reshape(length, features // 2)
+    out_shape = (2, 3 * GROUP_COLS // 2, 128)
+    out_sums = kernel_call(
+        out_kernel,
+        1,
+        (attended, late),
+        [whole(attended.shape), whole(late.shape)],
+        jax.ShapeDtypeStruct(out_shape, jnp.bfloat16),
+        whole(out_shape),
+        [],
+        3 * 10**8,
+        2 * 10**6,
+    )
+
+    def over_dp(halves):
+        kept = lax.dynamic_index_in_dim(halves, core, 0, keepdims=False)
+        given = lax.dynamic_index_in_dim(halves, 1 - core, 0, keepdims=False)
+        kept = kept + swapped(given, "dp", 1)
+        return kept + swapped(kept, "dp", 2)
+
+    kept = over_dp(sums)
+    kept_out = over_dp(out_sums)
+    planes = [[2 * z + x for z in range(GROUPS)] for x in range(2)]
+    got_rows = lax.all_to_all(
+        rows, "seq", split_axis=0, concat_axis=0, axis_index_groups=planes, tiled=True
+    )
+    grad_input = kernel_call(
+        input_kernel,
+        1,
+        (token_ids, table, w_query, w_key, w_value, got_rows),
+        [
+            whole(token_ids.shape),
+            whole(table.shape),
+            whole(w_query.shape),
+            whole(w_key.shape),
+            whole(w_value.shape),
+            whole(got_rows.shape),
+        ],
+        jax.ShapeDtypeStruct((block, features), jnp.bfloat16),
+        whole((block, features)),
+        [],
+        10**9,
+        5 * 10**6,
+    )
+    got = []
+    for turn in range(1, GROUPS):
+        route = [
+            (2 * z + x, 2 * ((z + turn) % GROUPS) + x)
+            for z in range(GROUPS)
+            for x in range(2)
+            if (z + turn) % GROUPS != 3
+        ]
+        target = jnp.minimum((group + turn) % GROUPS, 2)
+        piece = lax.dynamic_slice_in_dim(kept, target * GROUP_COLS, GROUP_COLS, 0)
+        got.append(lax.ppermute(piece, "seq", route))
+    for other in range(2):
+        for half in range(2):
+            route = [(2 * (2 * x + half) + (x ^ other), 6 + x) for x in range(2)]
+            route = [(s, t) for s, t in route if s != t]
+            got.append(lax.ppermute(kept_out, "seq", route))
+    pieces = kernel_call(
+        gather_kernel,
+        1,
+        (meta, kept, kept_out, *got),
+        [whole(kept.shape), whole(kept_out.shape)] + [whole(piece.shape) for piece in got],
+        jax.ShapeDtypeStruct((4 * kept_out.shape[0], kept.shape[1]), jnp.bfloat16),
+        whole((4 * kept_out.shape[0], kept.shape[1])),
+        [],
+        10**6,
+        10**6,
+    )
+    others = swapped(pieces, "dp", 1)
+    weight_grads = kernel_call(
+        weight_kernel,
+        1,
+        (meta, table, pieces, others),
+        [whole(table.shape), whole(pieces.shape), whole(others.shape)],
+        jax.ShapeDtypeStruct((features // 2, features), jnp.float32),
+        whole((features // 2, features)),
+        [],
+        10**9,
+        5 * 10**6,
+    )
+    return (grad_input[None], weight_grads)
+
+
+def on_device(token_ids, cotangent, table, w_query, w_key, w_value, w_out, window):
+    fits = (
+        lax.axis_size("seq") == 2 * GROUPS
+        and lax.axis_size("dp") == 4
+        and token_ids.shape == (1, 128)
+        and table.shape == (256, HEADS * HEAD_DIM)
+    )
+    plan = grouped_device if fits else general_device
+    return plan(token_ids, cotangent, table, w_query, w_key, w_value, w_out, window)
+
+
 def solution(mesh):
     return jax.shard_map(
         on_device,

time: 378 us -> 92.7 us (0.25)
  waiting for transfers between devices: 219 us -> 20 us
  matrix products: 63.3 us -> 0 us
  Pallas kernels: 0 us -> 21.9 us
  local copies, waits for them, and re-layouts: 26.2 us -> 8.99 us
  between operations: 14.8 us -> 0.97 us
  starting transfers between devices: 42.3 us -> 34.9 us
  other arithmetic: 12.1 us -> 4.86 us
    reduce_scatter x1 -> x0, waiting for transfers between devices: 114 us -> none  [on_device(): lax.psum_scatter(term.astype(jnp.bfloat16), 'seq', scatter_dimension=0, t...]
    dot_general x30 -> x0, matrix products: 63.3 us -> none  [the longest x3 17.9 us: head_group(): jnp.einsum('hqk,qhd->khd', grad_scores, query_heads, preferred_element_ty...]
    ppermute x16 -> x12, waiting for transfers between devices: 69.6 us -> 8.52 us  [the longest x3 4.69 us: grouped_device(): got.append(lax.ppermute(piece, 'seq', route))]
    psum x1 -> x0, waiting for transfers between devices: 34.8 us -> none  [on_device(): weight_grads = lax.psum(shares, 'dp').astype(jnp.float32)]
    pallas_call x0 -> x6, Pallas kernels: none -> 21.9 us  [kernel_call(): pl.pallas_call(body, grid=(steps,), in_specs=[pl.BlockSpec(memory_space=p...]
    ppermute x16 -> x12, starting transfers between devices: 42.2 us -> 20.5 us  [the longest x4 10.1 us: grouped_device(): got.append(lax.ppermute(kept_out, 'seq', route))]
    all_to_all x0 -> x3, starting transfers between devices: none -> 14.4 us  [the longest x1 7.25 us: grouped_device(): lax.all_to_all(early, 'seq', split_axis=0, concat_axis=0, tiled=True)]
    unnamed x104 -> x20, local copies, waits for them, and re-layouts: 18.3 us -> 5.5 us
  transfers between devices with their start and end apart: 18 -> 15, of which waited for: 4 -> 4; matrix products, arithmetic and copies ran while one was open for 9% -> 9% of each run, Pallas kernels for 0% -> 20%
where the time goes in v1:
time: 92.7 us; the launch traced here: 91.6 us
  starting transfers between devices  34.9 us (38%)
  Pallas kernels  21.9 us (24%)
  waiting for transfers between devices  20 us (22%)
  local copies, waits for them, and re-layouts  8.99 us (10%)
  other arithmetic  4.86 us (5%)
  between operations  0.97 us (1%)
    pallas_call x6, Pallas kernels, kernel_call(): pl.pallas_call(body, grid=(steps,), in_specs=[pl.BlockSpec(memory_space=p...  21.9 us
    ppermute x4, starting transfers between devices, grouped_device(): got.append(lax.ppermute(kept_out, 'seq', route))  10.1 us
    all_to_all x1, waiting for transfers between devices, grouped_device(): lax.all_to_all(early, 'seq', split_axis=0, concat_axis=0, tiled=True)  9.51 us
    all_to_all x1, starting transfers between devices, grouped_device(): lax.all_to_all(early, 'seq', split_axis=0, concat_axis=0, tiled=True)  7.25 us
    ppermute x3, starting transfers between devices, grouped_device(): got.append(lax.ppermute(piece, 'seq', route))  7.14 us
    unnamed x20, local copies, waits for them, and re-layouts  5.5 us
    ppermute x3, waiting for transfers between devices, grouped_device(): got.append(lax.ppermute(piece, 'seq', route))  4.69 us
    ppermute x5, waiting for transfers between devices, swapped(): return lax.ppermute(block, axis, route)  3.82 us
  transfers between devices with their start and end apart: 15, of which 4 were waited for; matrix products, arithmetic and copies ran while one was open for 9% of the time, Pallas kernels for 20%

profile of v1, /device:TPU:0, one launch (start us, length us, event | category | flops | bytes accessed | tf_op | source)
XLA Modules:
  0.0 91.6 jit_solution(3938751838032631839)
XLA Ops:
  0.7 1.4 %copy-done.3 = bf16[768,768]{1,0:T(8,128)(2,1)S(1)} copy-done((bf16[768,768]{1,0:T(8,128)(2,1)S(1)}, bf16[768,768]{1,0:T(8,128)(2,1)}, u32[]{:S(2)}) %copy-start.3) | copy-done | bytes 1179672
  3.6 1.4 %shard_map.95 = (bf16[8,208,128]{2,1,0:T(8,128)(2,1)}, bf16[8,128,384]{2,1,0:T(8,128)(2,1)}) custom-call(s32[1,128]{1,0:T(1,128)S(1)} %copy-done.7, bf16[128,768]{1,0:T(8,128)(2,1)S(1)} %bitcast.15, bf16[768,768]{1,0:T(8,128)(2,1)S(1)} %copy-done.3), custom_call_target="tpu_custom_call" | custom-call | flops 200000000 | bytes 3000000 | tf_op jit(solution)/shard_map/pallas_call | solution.py:533
  5.0 7.3 %all-to-all-start = ((bf16[8,208,128]{2,1,0:T(8,128)(2,1)}), bf16[8,208,128]{2,1,0:T(8,128)(2,1)S(1)}, u32[]{:S(2)}, u32[]{:S(2)}) async-start(bf16[8,208,128]{2,1,0:T(8,128)(2,1)} %get-tuple-element.7), calls=%async_computation | async-start | bytes 851968 | tf_op jit(solution)/shard_map/all_to_all | solution.py:581
  12.6 2.5 %constant_dynamic-slice_fusion.3 = (bf16[768,192]{1,0:T(8,128)(2,1)}, bf16[768,192]{1,0:T(8,128)(2,1)}) fusion(bf16[768,768]{1,0:T(8,128)(2,1)} %value_ref.1, s32[]{:T(128)S(6)} %select_n.58, bf16[768,768]{1,0:T(8,128)(2,1)} %key_ref.1), kind=kLoop, calls=%fused_computation.11 | loop fusion | bytes 1179652 | tf_op jit(solution)/shard_map/dynamic_slice | solution.py:585
  15.1 9.5 %all-to-all-done.early_ref = bf16[8,208,128]{2,1,0:T(8,128)(2,1)S(1)} async-done(((bf16[8,208,128]{2,1,0:T(8,128)(2,1)}), bf16[8,208,128]{2,1,0:T(8,128)(2,1)S(1)}, u32[]{:S(2)}, u32[]{:S(2)}) %all-to-all-start) | async-done | bytes 426016 | tf_op jit(solution)/shard_map/all_to_all | solution.py:581
  24.6 3.6 %all-to-all-start.2 = ((bf16[8,128,384]{2,1,0:T(8,128)(2,1)}), bf16[8,128,384]{2,1,0:T(8,128)(2,1)S(1)}, u32[]{:S(2)}, u32[]{:S(2)}) async-start(bf16[8,128,384]{2,1,0:T(8,128)(2,1)} %get-tuple-element.11), calls=%async_computation.2 | async-start | bytes 1572864 | tf_op jit(solution)/shard_map/all_to_all | solution.py:582
  28.3 1.5 %pad_maximum_fusion.weights_ref = bf16[768,576]{1,0:T(8,128)(2,1)S(1)} fusion(bf16[768,192]{1,0:T(8,128)(2,1)} %get-tuple-element.17, bf16[768,192]{1,0:T(8,128)(2,1)} %get-tuple-element.18, bf16[768,192]{1,0:T(8,128)(2,1)S(1)} %constant_dynamic-slice_fusion.5), kind=kLoop, calls=%fused_computation | loop fusion | flops 2654208 | bytes 1769472 | tf_op jit(solution)/shard_map/concatenate | solution.py:584
  30.3 15.4 %shard_map.96 = (bf16[4,576,128]{2,1,0:T(8,128)(2,1)}, bf16[2,576,128]{2,1,0:T(8,128)(2,1)S(1)}, bf16[192,1024]{1,0:T(8,128)(2,1)S(1)}) custom-call(s32[6]{0:T(128)S(1)} %pad_add_fusion.meta_ref, bf16[8,208,128]{2,1,0:T(8,128)(2,1)S(1)} %all-to-all-done.early_ref, bf16[256,768]{1,0:T(8,128)(2,1)S(1)} %copy-done.4, ...), custom_call_target="tpu_custom_call" | custom-call | flops 8000000000 | bytes 8000000 | tf_op jit(solution)/shard_map/pallas_call | solution.py:533
  46.4 2.0 %all-to-all-done.2 = bf16[8,128,384]{2,1,0:T(8,128)(2,1)S(1)} async-done(((bf16[8,128,384]{2,1,0:T(8,128)(2,1)}), bf16[8,128,384]{2,1,0:T(8,128)(2,1)S(1)}, u32[]{:S(2)}, u32[]{:S(2)}) %all-to-all-start.2) | async-done | bytes 786464 | tf_op jit(solution)/shard_map/all_to_all | solution.py:582
  48.5 3.5 %all-to-all-start.1 = ((bf16[4,576,128]{2,1,0:T(8,128)(2,1)}), bf16[4,576,128]{2,1,0:T(8,128)(2,1)S(1)}, u32[]{:S(2)}, u32[]{:S(2)}) async-start(bf16[4,576,128]{2,1,0:T(8,128)(2,1)} %get-tuple-element.8), calls=%async_computation.1 | async-start | bytes 1179648 | tf_op jit(solution)/shard_map/all_to_all | solution.py:657
  52.0 1.7 %bitcast_add_fusion = bf16[576,128]{1,0:T(8,128)(2,1)} fusion(bf16[576,128]{1,0:T(8,128)(2,1)} %collective-permute-done, bf16[2,576,128]{2,1,0:T(8,128)(2,1)} %copy-done.5, s32[]{:T(128)S(6)} %select_n.59), kind=kLoop, calls=%fused_computation.3 | loop fusion | flops 73728 | bytes 442372 | tf_op jit(solution)/shard_map/add | solution.py:651
  53.6 1.5 %collective-permute-start.1 = (bf16[576,128]{1,0:T(8,128)(2,1)}, bf16[576,128]{1,0:T(8,128)(2,1)}, u32[]{:S(2)}, u32[]{:S(2)}) collective-permute-start(bf16[576,128]{1,0:T(8,128)(2,1)} %bitcast_add_fusion), channel_id=1, source_target_pairs={{0,16},{8,24},{16,0},{24,8},{1,17},{9,25},{17,1},{25,9},{2,18},{10... | collective-permute-start | bytes 442376 | tf_op jit(solution)/shard_map/ppermute | solution.py:551
  55.7 3.8 %collective-permute-done.1 = bf16[576,128]{1,0:T(8,128)(2,1)} collective-permute-done((bf16[576,128]{1,0:T(8,128)(2,1)}, bf16[576,128]{1,0:T(8,128)(2,1)}, u32[]{:S(2)}, u32[]{:S(2)}) %collective-permute-start.1) | collective-permute-done | bytes 147488 | tf_op jit(solution)/shard_map/ppermute | solution.py:551
  59.5 1.0 %add.73.kept_ref = bf16[576,128]{1,0:T(8,128)(2,1)S(1)} add(bf16[576,128]{1,0:T(8,128)(2,1)} %bitcast_add_fusion, bf16[576,128]{1,0:T(8,128)(2,1)} %collective-permute-done.1) | non-fusion elementwise | flops 73728 | bytes 442368 | tf_op jit(solution)/shard_map/add | solution.py:652
  60.6 1.6 %collective-permute-start.3 = (bf16[288,128]{1,0:T(8,128)(2,1)S(1)}, bf16[288,128]{1,0:T(8,128)(2,1)S(1)}, u32[]{:S(2)}, u32[]{:S(2)}) collective-permute-start(bf16[288,128]{1,0:T(8,128)(2,1)S(1)} %bitcast_add_fusion.1), channel_id=1, source_target_pairs={{0,16},{8,24},{16,0},{24,8},{1,17},{9,25},{17,1},{25,9},{2,18},{10... | collective-permute-start | bytes 221192 | tf_op jit(solution)/shard_map/ppermute | solution.py:551
  62.2 3.7 %collective-permute-start.4 = (bf16[192,128]{1,0:T(8,128)(2,1)S(1)}, bf16[192,128]{1,0:T(8,128)(2,1)S(1)}, u32[]{:S(2)}, u32[]{:S(2)}) collective-permute-start(bf16[192,128]{1,0:T(8,128)(2,1)S(1)} %get-tuple-element.14), channel_id=1, source_target_pairs={{0,2},{1,3},{2,4},{3,5},{6,0},{7,1},{8,10},{9,11},{10,12},{11,13},... | collective-permute-start | bytes 147464 | tf_op jit(solution)/shard_map/ppermute | solution.py:688
  65.8 2.2 %collective-permute-start.5 = (bf16[192,128]{1,0:T(8,128)(2,1)S(1)}, bf16[192,128]{1,0:T(8,128)(2,1)S(1)}, u32[]{:S(2)}, u32[]{:S(2)}) collective-permute-start(bf16[192,128]{1,0:T(8,128)(2,1)S(1)} %get-tuple-element.13), channel_id=1, source_target_pairs={{0,4},{1,5},{4,0},{5,1},{6,2},{7,3},{8,12},{9,13},{12,8},{13,9},{1... | collective-permute-start | bytes 147464 | tf_op jit(solution)/shard_map/ppermute | solution.py:688
  68.7 8.2 %collective-permute-start.7 = (bf16[288,128]{1,0:T(8,128)(2,1)S(1)}, bf16[288,128]{1,0:T(8,128)(2,1)S(1)}, u32[]{:S(2)}, u32[]{:S(2)}) collective-permute-start(bf16[288,128]{1,0:T(8,128)(2,1)S(1)} %add.75.kept_out_ref), channel_id=1, source_target_pairs={{0,6},{5,7},{8,14},{13,15},{16,22},{21,23},{24,30},{29,31}} | collective-permute-start | bytes 221192 | tf_op jit(solution)/shard_map/ppermute | solution.py:693
  78.3 1.3 %collective-permute-start.6 = (bf16[192,128]{1,0:T(8,128)(2,1)S(1)}, bf16[192,128]{1,0:T(8,128)(2,1)S(1)}, u32[]{:S(2)}, u32[]{:S(2)}) collective-permute-start(bf16[192,128]{1,0:T(8,128)(2,1)S(1)} %get-tuple-element.12), channel_id=1, source_target_pairs={{2,0},{3,1},{4,2},{5,3},{6,4},{7,5},{10,8},{11,9},{12,10},{13,11},... | collective-permute-start | bytes 147464 | tf_op jit(solution)/shard_map/ppermute | solution.py:688
  79.6 4.7 %collective-permute-done.6.s3 = bf16[192,128]{1,0:T(8,128)(2,1)S(1)} collective-permute-done((bf16[192,128]{1,0:T(8,128)(2,1)S(1)}, bf16[192,128]{1,0:T(8,128)(2,1)S(1)}, u32[]{:S(2)}, u32[]{:S(2)}) %collective-permute-start.6) | collective-permute-done | bytes 49184 | tf_op jit(solution)/shard_map/ppermute | solution.py:688
  85.0 1.3 %copy-done.1 = bf16[768,768]{1,0:T(8,128)(2,1)S(1)} copy-done((bf16[768,768]{1,0:T(8,128)(2,1)S(1)}, bf16[768,768]{1,0:T(8,128)(2,1)}, u32[]{:S(2)}) %copy-start.1) | copy-done | bytes 1179672
  86.2 1.3 %copy-done.2 = bf16[768,768]{1,0:T(8,128)(2,1)S(1)} copy-done((bf16[768,768]{1,0:T(8,128)(2,1)S(1)}, bf16[768,768]{1,0:T(8,128)(2,1)}, u32[]{:S(2)}) %copy-start.2) | copy-done | bytes 1179672
  87.5 1.9 %shard_map.97 = bf16[128,768]{1,0:T(8,128)(2,1)} custom-call(s32[1,128]{1,0:T(1,128)S(1)} %copy-done.8, bf16[256,768]{1,0:T(8,128)(2,1)S(1)} %copy-done.4, bf16[768,768]{1,0:T(8,128)(2,1)S(1)} %copy-done, bf16[768,768]{1,0:T(8,128)(2,1)S(1)} %copy-done.1, bf16[768,768]{1,0:T(8,128)(2,1)S(1)} %copy-done.2, bf16[4,576,128]{2,1,0:T(8,128)(2,1)S(1)} %all-to-all-done.1.rows_ref), custom_call_target="tpu_custom_call" | custom-call | flops 1000000000 | bytes 5000000 | tf_op jit(solution)/shard_map/pallas_call | solution.py:533
  89.4 2.2 %shard_map.100 = f32[384,768]{1,0:T(8,128)} custom-call(s32[6]{0:T(128)S(1)} %pad_add_fusion.meta_ref, bf16[256,768]{1,0:T(8,128)(2,1)S(1)} %copy-done.4, bf16[1152,128]{1,0:T(8,128)(2,1)S(1)} %shard_map.99.mine_ref, bf16[1152,128]{1,0:T(8,128)(2,1)S(1)} %collective-permute-done.11.other_ref), custom_call_target="tpu_custom_call" | custom-call | flops 1000000000 | bytes 5000000 | tf_op jit(solution)/shard_map/pallas_call | solution.py:533
  (47 shorter events, 6.4 us)
Async XLA Ops:
  0.6 11.8 %copy-start = (bf16[768,768]{1,0:T(8,128)(2,1)S(1)}, bf16[768,768]{1,0:T(8,128)(2,1)}, u32[]{:S(2)}) copy-start(bf16[768,768]{1,0:T(8,128)(2,1)} %query_ref.1) | copy-start | bytes 3538948
  0.6 1.4 %copy-start.3 = (bf16[768,768]{1,0:T(8,128)(2,1)S(1)}, bf16[768,768]{1,0:T(8,128)(2,1)}, u32[]{:S(2)}) copy-start(bf16[768,768]{1,0:T(8,128)(2,1)} %out_weights_ref.1) | copy-start | bytes 3538948
  2.0 0.9 %copy-start.6 = (bf16[1,128,768]{2,1,0:T(8,128)(2,1)S(1)}, bf16[1,128,768]{2,1,0:T(8,128)(2,1)}, u32[]{:S(2)}) copy-start(bf16[1,128,768]{2,1,0:T(8,128)(2,1)} %param.9) | copy-start | bytes 589828
  3.6 8.7 %copy-start.9 = (s32[12]{0:T(128)S(1)}, s32[12]{0:T(128)}, u32[]{:S(2)}) copy-start(s32[12]{0:T(128)} %param.15) | copy-start | bytes 148
  5.0 19.6 %all-to-all-start = ((bf16[8,208,128]{2,1,0:T(8,128)(2,1)}), bf16[8,208,128]{2,1,0:T(8,128)(2,1)S(1)}, u32[]{:S(2)}, u32[]{:S(2)}) async-start(bf16[8,208,128]{2,1,0:T(8,128)(2,1)} %get-tuple-element.7), calls=%async_computation | async-start | bytes 851968 | tf_op jit(solution)/shard_map/all_to_all | solution.py:581
  24.6 23.8 %all-to-all-start.2 = ((bf16[8,128,384]{2,1,0:T(8,128)(2,1)}), bf16[8,128,384]{2,1,0:T(8,128)(2,1)S(1)}, u32[]{:S(2)}, u32[]{:S(2)}) async-start(bf16[8,128,384]{2,1,0:T(8,128)(2,1)} %get-tuple-element.11), calls=%async_computation.2 | async-start | bytes 1572864 | tf_op jit(solution)/shard_map/all_to_all | solution.py:582
  28.3 2.1 %copy-start.4 = (bf16[256,768]{1,0:T(8,128)(2,1)S(1)}, bf16[256,768]{1,0:T(8,128)(2,1)}, u32[]{:S(2)}) copy-start(bf16[256,768]{1,0:T(8,128)(2,1)} %table_ref.5) | copy-start | bytes 1179652
  45.7 2.7 %copy-start.5 = (bf16[2,576,128]{2,1,0:T(8,128)(2,1)}, bf16[2,576,128]{2,1,0:T(8,128)(2,1)S(1)}, u32[]{:S(2)}) copy-start(bf16[2,576,128]{2,1,0:T(8,128)(2,1)S(1)} %get-tuple-element.9) | copy-start | bytes 884740
  46.4 5.5 %collective-permute-start = (bf16[576,128]{1,0:T(8,128)(2,1)}, bf16[576,128]{1,0:T(8,128)(2,1)}, u32[]{:S(2)}, u32[]{:S(2)}) collective-permute-start(bf16[576,128]{1,0:T(8,128)(2,1)} %dynamic-slice_bitcast_fusion), channel_id=1, source_target_pairs={{0,8},{8,0},{16,24},{24,16},{1,9},{9,1},{17,25},{25,17},{2,10},{10... | collective-permute-start | bytes 442376 | tf_op jit(solution)/shard_map/ppermute | solution.py:551
  48.5 36.5 %all-to-all-start.1 = ((bf16[4,576,128]{2,1,0:T(8,128)(2,1)}), bf16[4,576,128]{2,1,0:T(8,128)(2,1)S(1)}, u32[]{:S(2)}, u32[]{:S(2)}) async-start(bf16[4,576,128]{2,1,0:T(8,128)(2,1)} %get-tuple-element.8), calls=%async_computation.1 | async-start | bytes 1179648 | tf_op jit(solution)/shard_map/all_to_all | solution.py:657
  53.6 5.9 %collective-permute-start.1 = (bf16[576,128]{1,0:T(8,128)(2,1)}, bf16[576,128]{1,0:T(8,128)(2,1)}, u32[]{:S(2)}, u32[]{:S(2)}) collective-permute-start(bf16[576,128]{1,0:T(8,128)(2,1)} %bitcast_add_fusion), channel_id=1, source_target_pairs={{0,16},{8,24},{16,0},{24,8},{1,17},{9,25},{17,1},{25,9},{2,18},{10... | collective-permute-start | bytes 442376 | tf_op jit(solution)/shard_map/ppermute | solution.py:551
  55.5 29.4 %copy-start.8 = (s32[1,128]{1,0:T(1,128)S(1)}, s32[1,128]{1,0:T(1,128)}, u32[]{:S(2)}) copy-start(s32[1,128]{1,0:T(1,128)} %tokens_ref.3) | copy-start | bytes 1540
  55.5 5.0 %collective-permute-start.2 = (bf16[288,128]{1,0:T(8,128)(2,1)S(1)}, bf16[288,128]{1,0:T(8,128)(2,1)S(1)}, u32[]{:S(2)}, u32[]{:S(2)}) collective-permute-start(bf16[288,128]{1,0:T(8,128)(2,1)S(1)} %dynamic-slice_bitcast_fusion.1), channel_id=1, source_target_pairs={{0,8},{8,0},{16,24},{24,16},{1,9},{9,1},{17,25},{25,17},{2,10},{10... | collective-permute-start | bytes 221192 | tf_op jit(solution)/shard_map/ppermute | solution.py:551
  60.6 7.5 %collective-permute-start.3 = (bf16[288,128]{1,0:T(8,128)(2,1)S(1)}, bf16[288,128]{1,0:T(8,128)(2,1)S(1)}, u32[]{:S(2)}, u32[]{:S(2)}) collective-permute-start(bf16[288,128]{1,0:T(8,128)(2,1)S(1)} %bitcast_add_fusion.1), channel_id=1, source_target_pairs={{0,16},{8,24},{16,0},{24,8},{1,17},{9,25},{17,1},{25,9},{2,18},{10... | collective-permute-start | bytes 221192 | tf_op jit(solution)/shard_map/ppermute | solution.py:551
  62.2 15.4 %collective-permute-start.4 = (bf16[192,128]{1,0:T(8,128)(2,1)S(1)}, bf16[192,128]{1,0:T(8,128)(2,1)S(1)}, u32[]{:S(2)}, u32[]{:S(2)}) collective-permute-start(bf16[192,128]{1,0:T(8,128)(2,1)S(1)} %get-tuple-element.14), channel_id=1, source_target_pairs={{0,2},{1,3},{2,4},{3,5},{6,0},{7,1},{8,10},{9,11},{10,12},{11,13},... | collective-permute-start | bytes 147464 | tf_op jit(solution)/shard_map/ppermute | solution.py:688
  65.8 12.4 %collective-permute-start.5 = (bf16[192,128]{1,0:T(8,128)(2,1)S(1)}, bf16[192,128]{1,0:T(8,128)(2,1)S(1)}, u32[]{:S(2)}, u32[]{:S(2)}) collective-permute-start(bf16[192,128]{1,0:T(8,128)(2,1)S(1)} %get-tuple-element.13), channel_id=1, source_target_pairs={{0,4},{1,5},{4,0},{5,1},{6,2},{7,3},{8,12},{9,13},{12,8},{13,9},{1... | collective-permute-start | bytes 147464 | tf_op jit(solution)/shard_map/ppermute | solution.py:688
  68.1 16.2 %collective-permute-start.10 = (bf16[288,128]{1,0:T(8,128)(2,1)S(1)}, bf16[288,128]{1,0:T(8,128)(2,1)S(1)}, u32[]{:S(2)}, u32[]{:S(2)}) collective-permute-start(bf16[288,128]{1,0:T(8,128)(2,1)S(1)} %add.75.kept_out_ref), channel_id=1, source_target_pairs={{3,6},{6,7},{11,14},{14,15},{19,22},{22,23},{27,30},{30,31}} | collective-permute-start | bytes 221192 | tf_op jit(solution)/shard_map/ppermute | solution.py:693
  68.7 15.5 %collective-permute-start.7 = (bf16[288,128]{1,0:T(8,128)(2,1)S(1)}, bf16[288,128]{1,0:T(8,128)(2,1)S(1)}, u32[]{:S(2)}, u32[]{:S(2)}) collective-permute-start(bf16[288,128]{1,0:T(8,128)(2,1)S(1)} %add.75.kept_out_ref), channel_id=1, source_target_pairs={{0,6},{5,7},{8,14},{13,15},{16,22},{21,23},{24,30},{29,31}} | collective-permute-start | bytes 221192 | tf_op jit(solution)/shard_map/ppermute | solution.py:693
  76.9 7.4 %collective-permute-start.8 = (bf16[288,128]{1,0:T(8,128)(2,1)S(1)}, bf16[288,128]{1,0:T(8,128)(2,1)S(1)}, u32[]{:S(2)}, u32[]{:S(2)}) collective-permute-start(bf16[288,128]{1,0:T(8,128)(2,1)S(1)} %add.75.kept_out_ref), channel_id=1, source_target_pairs={{2,6},{10,14},{18,22},{26,30}} | collective-permute-start | bytes 221192 | tf_op jit(solution)/shard_map/ppermute | solution.py:693
  77.6 6.7 %collective-permute-start.9 = (bf16[288,128]{1,0:T(8,128)(2,1)S(1)}, bf16[288,128]{1,0:T(8,128)(2,1)S(1)}, u32[]{:S(2)}, u32[]{:S(2)}) collective-permute-start(bf16[288,128]{1,0:T(8,128)(2,1)S(1)} %add.75.kept_out_ref), channel_id=1, source_target_pairs={{1,6},{4,7},{9,14},{12,15},{17,22},{20,23},{25,30},{28,31}} | collective-permute-start | bytes 221192 | tf_op jit(solution)/shard_map/ppermute | solution.py:693
  78.3 6.0 %collective-permute-start.6 = (bf16[192,128]{1,0:T(8,128)(2,1)S(1)}, bf16[192,128]{1,0:T(8,128)(2,1)S(1)}, u32[]{:S(2)}, u32[]{:S(2)}) collective-permute-start(bf16[192,128]{1,0:T(8,128)(2,1)S(1)} %get-tuple-element.12), channel_id=1, source_target_pairs={{2,0},{3,1},{4,2},{5,3},{6,4},{7,5},{10,8},{11,9},{12,10},{13,11},... | collective-permute-start | bytes 147464 | tf_op jit(solution)/shard_map/ppermute | solution.py:688
  84.9 4.6 %collective-permute-start.11 = (bf16[1152,128]{1,0:T(8,128)(2,1)S(1)}, bf16[1152,128]{1,0:T(8,128)(2,1)S(1)}, u32[]{:S(2)}, u32[]{:S(2)}) collective-permute-start(bf16[1152,128]{1,0:T(8,128)(2,1)S(1)} %shard_map.99.mine_ref), channel_id=1, source_target_pairs={{0,8},{8,0},{16,24},{24,16},{1,9},{9,1},{17,25},{25,17},{2,10},{10... | collective-permute-start | bytes 884744 | tf_op jit(solution)/shard_map/ppermute | solution.py:551
  85.0 1.3 %copy-start.1 = (bf16[768,768]{1,0:T(8,128)(2,1)S(1)}, bf16[768,768]{1,0:T(8,128)(2,1)}, u32[]{:S(2)}) copy-start(bf16[768,768]{1,0:T(8,128)(2,1)} %key_ref.1) | copy-start | bytes 3538948
  86.2 1.3 %copy-start.2 = (bf16[768,768]{1,0:T(8,128)(2,1)S(1)}, bf16[768,768]{1,0:T(8,128)(2,1)}, u32[]{:S(2)}) copy-start(bf16[768,768]{1,0:T(8,128)(2,1)} %value_ref.1) | copy-start | bytes 3538948
  (1 other events, 0.7 us)

commit v2 on v1

--- a/solution.py
+++ b/solution.py
@@ -237,6 +237,10 @@
     return (first * TILE, (query_tile - first + 1) * TILE)
 
 
+def probs_row(query_tile):
+    return sum(key_span(earlier)[1] for earlier in range(query_tile))
+
+
 def normed_table(table_ref):
     widened = table_ref[...].astype(jnp.float32)
     inv_rms = lax.rsqrt(jnp.mean(widened * widened, axis=1, keepdims=True) + EPSILON)
@@ -248,52 +252,36 @@
     return (rows == tokens).astype(jnp.float32).astype(jnp.bfloat16)
 
 
-def send_kernel(tokens_ref, cotangent_ref, out_weights_ref, early_ref, late_ref):
+def send_kernel(cotangent_ref, out_weights_ref, early_ref, late_ref):
     cotangent = cotangent_ref[...]
     grad_att = ndot(out_weights_ref[...], cotangent).astype(jnp.bfloat16)
-    block = tokens_ref.shape[1]
-    tokens = jnp.broadcast_to(tokens_ref[...].astype(jnp.float32), (TOKEN_ROWS, block)).astype(
-        jnp.bfloat16
-    )
     columns = late_ref.shape[2]
     for target in range(2 * GROUPS):
         group, side = divmod(target, 2)
-        early_ref[target, :GROUP_COLS, :] = grad_att[
-            group * GROUP_COLS : (group + 1) * GROUP_COLS
-        ]
-        early_ref[target, GROUP_COLS:, :] = tokens
+        early_ref[target] = grad_att[group * GROUP_COLS : (group + 1) * GROUP_COLS]
         late_ref[target] = cotangent[:, side * columns : (side + 1) * columns]
 
 
-def attention_kernel(
+def forward_kernel(
     meta_ref,
-    early_ref,
+    tokens_ref,
     table_ref,
     weights_ref,
     cosine_ref,
     sine_ref,
-    rows_ref,
-    sums_ref,
+    probs_ref,
     attended_ref,
     query_key_ref,
-    zero_query_ref,
     key_t_ref,
     value_ref,
+    zero_query_ref,
     value_t_ref,
-    grad_att_ref,
     onehot_ref,
-    grad_query_ref,
-    grad_key_ref,
-    grad_value_ref,
 ):
     head = pl.program_id(0)
-    blocks, _, block = early_ref.shape
+    blocks, block = tokens_ref.shape
     length = blocks * block
     vocab = table_ref.shape[0]
-    half_vocab = vocab // 2
-    cosine = cosine_ref[...]
-    sine_part = sine_ref[...]
-    blank = jnp.zeros((HEAD_DIM, length), jnp.float32)
 
     @pl.when(head == 0)
     def _():
@@ -302,14 +290,13 @@
         upper = lookup.astype(jnp.bfloat16)
         lower = (lookup - upper.astype(jnp.float32)).astype(jnp.bfloat16)
         for source in range(blocks):
-            lanes = slice(source * block, (source + 1) * block)
-            tokens = early_ref[source, GROUP_COLS : GROUP_COLS + TOKEN_ROWS, :]
-            tokens = tokens.astype(jnp.float32)[:1].astype(jnp.int32)
-            onehot_ref[:, lanes] = onehot_columns(tokens, vocab)
-            grad_att_ref[:, :, lanes] = early_ref[source, :GROUP_COLS, :].reshape(
-                GROUP_HEADS, HEAD_DIM, block
+            onehot_ref[:, source * block : (source + 1) * block] = onehot_columns(
+                tokens_ref[source : source + 1, :], vocab
             )
         onehot = onehot_ref[...]
+        cosine = cosine_ref[...]
+        sine_part = sine_ref[...]
+        blank = jnp.zeros((HEAD_DIM, length), jnp.float32)
 
         def chosen(start):
             rows = slice(start, start + HEAD_DIM)
@@ -335,12 +322,6 @@
             value_t_ref[index] = values.astype(jnp.bfloat16)
 
     width = meta_ref[head]
-    grad_att = grad_att_ref[head]
-    wide_grad = grad_att.astype(jnp.float32)
-    grad_blank = jnp.concatenate([wide_grad, blank], axis=0).astype(jnp.bfloat16)
-    blank_grad = jnp.concatenate([blank, wide_grad], axis=0).T.astype(jnp.bfloat16)
-    grad_key_ref[...] = jnp.zeros_like(grad_key_ref)
-    grad_value_ref[...] = jnp.zeros_like(grad_value_ref)
     distance = lax.broadcasted_iota(jnp.int32, (TILE, TILE), 1) - lax.broadcasted_iota(
         jnp.int32, (TILE, TILE), 0
     )
@@ -363,21 +344,66 @@
         masked = jnp.concatenate(masked, axis=0)
         row_max = jnp.max(masked, axis=0, keepdims=True)
         weights = jnp.exp(masked - row_max)
-        probs = weights * (1.0 / jnp.sum(weights, axis=0, keepdims=True))
-        rounded = probs.astype(jnp.bfloat16)
-        attended = jnp.dot(
-            value_t_ref[head, :, first : first + count], rounded, preferred_element_type=jnp.float32
-        )
-        attended_ref[pl.ds(pl.multiple_of(head * HEAD_DIM, HEAD_DIM), HEAD_DIM), columns] = (
-            attended.astype(jnp.bfloat16)
-        )
-        row_term = jnp.sum(attended * wide_grad[:, columns], axis=0, keepdims=True)
+        probs = (weights * (1.0 / jnp.sum(weights, axis=0, keepdims=True))).astype(jnp.bfloat16)
+        base = probs_row(query_tile)
+        probs_ref[0, base : base + count, :] = probs
+        attended_ref[head, :, columns] = jnp.dot(
+            value_t_ref[head, :, first : first + count], probs, preferred_element_type=jnp.float32
+        )
+
+
+def backward_kernel(
+    meta_ref,
+    tokens_ref,
+    early_ref,
+    cosine_ref,
+    sine_ref,
+    probs_ref,
+    attended_ref,
+    query_key_ref,
+    key_t_ref,
+    value_ref,
+    rows_ref,
+    sums_ref,
+    grad_att_ref,
+    onehot_ref,
+    grad_query_ref,
+    grad_key_ref,
+    grad_value_ref,
+):
+    head = pl.program_id(0)
+    blocks, block = tokens_ref.shape
+    length = blocks * block
+    vocab = onehot_ref.shape[0]
+    half_vocab = vocab // 2
+
+    @pl.when(head == 0)
+    def _():
+        for source in range(blocks):
+            lanes = slice(source * block, (source + 1) * block)
+            onehot_ref[:, lanes] = onehot_columns(tokens_ref[source : source + 1, :], vocab)
+            grad_att_ref[:, :, lanes] = early_ref[source].reshape(GROUP_HEADS, HEAD_DIM, block)
+
+    wide_grad = grad_att_ref[head].astype(jnp.float32)
+    blank = jnp.zeros((HEAD_DIM, length), jnp.float32)
+    grad_blank = jnp.concatenate([wide_grad, blank], axis=0).astype(jnp.bfloat16)
+    blank_grad = jnp.concatenate([blank, wide_grad], axis=0).T.astype(jnp.bfloat16)
+    row_term = jnp.sum(attended_ref[head] * wide_grad, axis=0, keepdims=True)
+    grad_key_ref[...] = jnp.zeros_like(grad_key_ref)
+    grad_value_ref[...] = jnp.zeros_like(grad_value_ref)
+    for query_tile in range(length // TILE):
+        first, count = key_span(query_tile)
+        columns = slice(query_tile * TILE, (query_tile + 1) * TILE)
+        base = probs_row(query_tile)
+        probs = probs_ref[0, base : base + count, :]
         grad_probs = jnp.dot(
             value_ref[head, first : first + count, :],
             grad_blank[:, columns],
             preferred_element_type=jnp.float32,
         )
-        grad_scores = (probs * (grad_probs - row_term)).astype(jnp.bfloat16)
+        grad_scores = (probs.astype(jnp.float32) * (grad_probs - row_term[:, columns])).astype(
+            jnp.bfloat16
+        )
         grad_query_ref[:, columns] = jnp.dot(
             key_t_ref[head, :, first : first + count],
             grad_scores,
@@ -387,8 +413,10 @@
             grad_scores, query_key_ref[head, columns, :], preferred_element_type=jnp.float32
         )
         grad_value_ref[first : first + count, :] += jnp.dot(
-            rounded, blank_grad[columns, :], preferred_element_type=jnp.float32
-        )
+            probs, blank_grad[columns, :], preferred_element_type=jnp.float32
+        )
+    cosine = cosine_ref[...]
+    sine_part = sine_ref[...]
 
     def turned_back(columns):
         former = columns[:HALF]
@@ -424,7 +452,8 @@
 
 
 def out_kernel(attended_ref, cotangent_ref, out_ref):
-    total = jnp.dot(attended_ref[...], cotangent_ref[...], preferred_element_type=jnp.float32)
+    attended = attended_ref[...].reshape(GROUP_COLS, -1).astype(jnp.bfloat16)
+    total = jnp.dot(attended, cotangent_ref[...], preferred_element_type=jnp.float32)
     rows = total.shape[0] // 2
     lanes = out_ref.shape[2]
     for core in range(2):
@@ -434,46 +463,58 @@
             ].astype(jnp.bfloat16)
 
 
-def gather_kernel(meta_ref, kept_ref, kept_out_ref, s1, s2, s3, n0, n1, f0, f1, pieces_ref):
+def gather_kernel(meta_ref, kept_ref, s1, s2, s3, kept_out_ref, o2, o1, o0, mine_ref, other_ref):
     group = meta_ref[GROUP_HEADS + 1]
     rows = GROUP_COLS
 
     @pl.when(group < 3)
     def _():
         own = pl.multiple_of(group * rows, rows)
-        pieces_ref[pl.ds(own, rows), :] = kept_ref[pl.ds(own, rows), :]
+        mine_ref[pl.ds(own, rows), :] = kept_ref[pl.ds(own, rows), :]
         for turn, got in ((1, s1), (2, s2), (3, s3)):
             source = lax.rem(group - turn + GROUPS, GROUPS)
-            pieces_ref[pl.ds(pl.multiple_of(source * rows, rows), rows), :] = got[...]
-        tail = pieces_ref.shape[0] - GROUPS * rows
-        pieces_ref[GROUPS * rows :, :] = jnp.zeros((tail, kept_ref.shape[1]), jnp.bfloat16)
+            mine_ref[pl.ds(pl.multiple_of(source * rows, rows), rows), :] = got[...]
+        other_ref[...] = jnp.zeros_like(other_ref)
 
     @pl.when(group == 3)
     def _():
         size = kept_out_ref.shape[0]
-        own = meta_ref[GROUP_HEADS] == 1
-        pieces_ref[0:size, :] = n0[...]
-        pieces_ref[size : 2 * size, :] = f0[...]
-        pieces_ref[2 * size : 3 * size, :] = jnp.where(own, kept_out_ref[...], n1[...])
-        pieces_ref[3 * size :, :] = f1[...]
-
-
-def input_kernel(tokens_ref, table_ref, query_ref, key_ref, value_ref, rows_ref, out_ref):
-    widened = table_ref[...].astype(jnp.float32)
-    vocab = table_ref.shape[0]
-    onehot = onehot_columns(tokens_ref[...], vocab)
+        first = meta_ref[GROUP_HEADS] == 0
+        mine_ref[0:size, :] = jnp.where(first, o0[...], o2[...])
+        mine_ref[size : 2 * size, :] = jnp.where(first, o1[...], kept_out_ref[...])
+        mine_ref[2 * size :, :] = jnp.zeros((GROUPS * rows - 2 * size, o0.shape[1]), jnp.bfloat16)
+        other_ref[0:size, :] = jnp.where(first, o2[...], o0[...])
+        other_ref[size:, :] = jnp.where(first, kept_out_ref[...], o1[...])
+
+
+def input_kernel(
+    meta_ref,
+    tokens_ref,
+    table_ref,
+    query_ref,
+    key_ref,
+    value_ref,
+    own_ref,
+    first_ref,
+    second_ref,
+    third_ref,
+    out_ref,
+    columns_ref,
+):
+    group = meta_ref[GROUP_HEADS + 1]
+    for turn, got in enumerate((own_ref, first_ref, second_ref, third_ref)):
+        source = lax.rem(group - turn + GROUPS, GROUPS)
+        for matrix in range(3):
+            columns_ref[
+                matrix, pl.ds(pl.multiple_of(source * GROUP_COLS, GROUP_COLS), GROUP_COLS), :
+            ] = got[matrix * GROUP_COLS : (matrix + 1) * GROUP_COLS, :]
+    onehot = onehot_columns(tokens_ref[...], table_ref.shape[0])
     embedded = tdot(onehot, table_ref[...])
     inv_rms = lax.rsqrt(jnp.mean(embedded * embedded, axis=1, keepdims=True) + EPSILON)
     grad_normed = None
     for matrix, weights in enumerate((query_ref, key_ref, value_ref)):
-        columns = jnp.concatenate(
-            [
-                rows_ref[group, matrix * GROUP_COLS : (matrix + 1) * GROUP_COLS, :]
-                for group in range(GROUPS)
-            ],
-            axis=0,
-        )
-        part = ndot(columns.astype(jnp.float32).T.astype(jnp.bfloat16), weights[...])
+        columns = columns_ref[matrix].astype(jnp.float32).T.astype(jnp.bfloat16)
+        part = ndot(columns, weights[...])
         grad_normed = part if grad_normed is None else grad_normed + part
     scaled = embedded * inv_rms
     out_ref[...] = (
@@ -481,7 +522,7 @@
     ).astype(jnp.bfloat16)
 
 
-def weight_kernel(meta_ref, table_ref, mine_ref, other_ref, out_ref):
+def weight_kernel(meta_ref, table_ref, mine_ref, other_ref, near_ref, far_ref, out_ref):
     side_rows = out_ref.shape[0]
     half_vocab = mine_ref.shape[1]
     first_core = meta_ref[GROUP_HEADS + 2] == 0
@@ -498,7 +539,7 @@
         for part, sums_ref in ((upper, mine_ref), (lower, other_ref)):
             term = lax.dot_general(
                 part,
-                sums_ref[: GROUPS * GROUP_COLS, :],
+                sums_ref[...],
                 (((0,), (1,)), ((), ())),
                 preferred_element_type=jnp.float32,
             )
@@ -508,21 +549,21 @@
     @pl.when(meta_ref[GROUP_HEADS + 1] == 3)
     def _():
         rows = GROUP_COLS // 2
-        side = meta_ref[GROUP_HEADS]
-        for core in range(2):
-            for half in range(2):
-                for plane in range(2):
-                    for chunk in range(3):
-                        place = ((2 * half + plane) * 3 + chunk) * rows
-                        here = mine_ref[place : place + rows, :]
-                        there = other_ref[place : place + rows, :]
-                        value = jnp.where(first_core == (core == 0), here, there)
-                        row = half * GROUP_COLS + core * rows
-                        column = jnp.where(side == 0, plane, 1 - plane) * 3 + chunk
-                        lanes = pl.ds(
-                            pl.multiple_of(column * half_vocab, half_vocab), half_vocab
+        first_side = meta_ref[GROUP_HEADS] == 0
+        for half in range(2):
+            for chunk in range(3):
+                place = slice((half * 3 + chunk) * rows, (half * 3 + chunk + 1) * rows)
+                for core in range(2):
+                    same = first_core == (core == 0)
+                    own = jnp.where(same, mine_ref[place, :], other_ref[place, :])
+                    crossed = jnp.where(same, near_ref[place, :], far_ref[place, :])
+                    row = half * GROUP_COLS + core * rows
+                    for side in range(2):
+                        value = jnp.where(first_side == (side == 0), own, crossed)
+                        start = (side * 3 + chunk) * half_vocab
+                        out_ref[row : row + rows, start : start + half_vocab] = value.astype(
+                            jnp.float32
                         )
-                        out_ref[row : row + rows, lanes] = value.astype(jnp.float32)
 
 
 def whole(shape):
@@ -561,19 +602,21 @@
     vocab = table.shape[0]
     blocks = lax.axis_size("seq")
     length = block * blocks
+    tokens = lax.all_to_all(
+        jnp.broadcast_to(token_ids, (blocks, block)), "seq", split_axis=0, concat_axis=0, tiled=True
+    )
+    early_shape = (blocks, GROUP_COLS, block)
+    late_shape = (blocks, block, features // 2)
     early, late = kernel_call(
         send_kernel,
         1,
-        (token_ids, cotangent[0], w_out),
-        [whole(token_ids.shape), whole((block, features)), whole(w_out.shape)],
-        [
-            jax.ShapeDtypeStruct((blocks, GROUP_COLS + TOKEN_ROWS, block), jnp.bfloat16),
-            jax.ShapeDtypeStruct((blocks, block, features // 2), jnp.bfloat16),
-        ],
-        [
-            whole((blocks, GROUP_COLS + TOKEN_ROWS, block)),
-            whole((blocks, block, features // 2)),
-        ],
+        (cotangent[0], w_out),
+        [whole((block, features)), whole(w_out.shape)],
+        [
+            jax.ShapeDtypeStruct(early_shape, jnp.bfloat16),
+            jax.ShapeDtypeStruct(late_shape, jnp.bfloat16),
+        ],
+        [whole(early_shape), whole(late_shape)],
         [],
         2 * 10**8,
         3 * 10**6,
@@ -597,38 +640,76 @@
     sine_part = jnp.sin(angles)
     heads_shape = (GROUP_HEADS, HEAD_DIM, length)
     rows_shape = (GROUP_HEADS, length, 2 * HEAD_DIM)
+    probs_shape = (GROUP_HEADS, probs_row(length // TILE), TILE)
+    probs_spec = pl.BlockSpec((1,) + probs_shape[1:], lambda h: (h, 0, 0))
     rows_out = (GROUPS, 3 * GROUP_COLS, block)
     sums_out = (2, 3 * GROUP_COLS, vocab // 2)
-    rows, sums, attended = kernel_call(
-        attention_kernel,
+    probs, attended, query_key, key_t, value_rows = kernel_call(
+        forward_kernel,
         GROUP_HEADS,
-        (meta, early, table, weights, cosine, sine_part),
-        [
-            whole(early.shape),
+        (meta, tokens, table, weights, cosine, sine_part),
+        [
+            whole(tokens.shape),
             whole(table.shape),
             whole(weights.shape),
             whole(cosine.shape),
             whole(sine_part.shape),
         ],
         [
+            jax.ShapeDtypeStruct(probs_shape, jnp.bfloat16),
+            jax.ShapeDtypeStruct(heads_shape, jnp.float32),
+            jax.ShapeDtypeStruct(rows_shape, jnp.bfloat16),
+            jax.ShapeDtypeStruct(heads_shape, jnp.bfloat16),
+            jax.ShapeDtypeStruct(rows_shape, jnp.bfloat16),
+        ],
+        [probs_spec, whole(heads_shape), whole(rows_shape), whole(heads_shape), whole(rows_shape)],
+        [
+            pltpu.VMEM((GROUP_HEADS, 2 * HEAD_DIM, length), jnp.bfloat16),
+            pltpu.VMEM(heads_shape, jnp.bfloat16),
+            pltpu.VMEM((vocab, length), jnp.bfloat16),
+        ],
+        4 * 10**9,
+        8 * 10**6,
+    )
+    rows, sums = kernel_call(
+        backward_kernel,
+        GROUP_HEADS,
+        (
+            meta,
+            tokens,
+            early,
+            cosine,
+            sine_part,
+            probs,
+            attended,
+            query_key,
+            key_t,
+            value_rows,
+        ),
+        [
+            whole(tokens.shape),
+            whole(early.shape),
+            whole(cosine.shape),
+            whole(sine_part.shape),
+            probs_spec,
+            whole(heads_shape),
+            whole(rows_shape),
+            whole(heads_shape),
+            whole(rows_shape),
+        ],
+        [
             jax.ShapeDtypeStruct(rows_out, jnp.bfloat16),
             jax.ShapeDtypeStruct(sums_out, jnp.bfloat16),
-            jax.ShapeDtypeStruct((GROUP_COLS, length), jnp.bfloat16),
-        ],
-        [whole(rows_out), whole(sums_out), whole((GROUP_COLS, length))],
-        [
-            pltpu.VMEM(rows_shape, jnp.bfloat16),
-            pltpu.VMEM((GROUP_HEADS, 2 * HEAD_DIM, length), jnp.bfloat16),
-            pltpu.VMEM(heads_shape, jnp.bfloat16),
-            pltpu.VMEM(rows_shape, jnp.bfloat16),
-            pltpu.VMEM(heads_shape, jnp.bfloat16),
+        ],
+        [whole(rows_out), whole(sums_out)],
+        [
             pltpu.VMEM(heads_shape, jnp.bfloat16),
             pltpu.VMEM((vocab, length), jnp.bfloat16),
             pltpu.VMEM((HEAD_DIM, length), jnp.float32),
             pltpu.VMEM((length, 2 * HEAD_DIM), jnp.float32),
             pltpu.VMEM((length, 2 * HEAD_DIM), jnp.float32),
         ],
-        8 * 10**9,
+        4 * 10**9,
         8 * 10**6,
     )
     late = late.reshape(length, features // 2)
@@ -651,63 +732,91 @@
         kept = kept + swapped(given, "dp", 1)
         return kept + swapped(kept, "dp", 2)
 
+    def turned_round(block, turn, goes):
+        route = [
+            (2 * z + x, 2 * ((z + turn) % GROUPS) + x)
+            for z in range(GROUPS)
+            for x in range(2)
+            if goes((z + turn) % GROUPS)
+        ]
+        return lax.ppermute(block, "seq", route)
+
+    turns = range(1, GROUPS)
+    got_rows = [
+        turned_round(
+            lax.dynamic_index_in_dim(rows, (group + turn) % GROUPS, 0, keepdims=False),
+            turn,
+            lambda target: True,
+        )
+        for turn in turns
+    ]
+    own_rows = lax.dynamic_index_in_dim(rows, group, 0, keepdims=False)
     kept = over_dp(sums)
     kept_out = over_dp(out_sums)
-    planes = [[2 * z + x for z in range(GROUPS)] for x in range(2)]
-    got_rows = lax.all_to_all(
-        rows, "seq", split_axis=0, concat_axis=0, axis_index_groups=planes, tiled=True
-    )
+    got = []
+    for turn in turns:
+        target = jnp.minimum((group + turn) % GROUPS, 2)
+        piece = lax.dynamic_slice_in_dim(kept, target * GROUP_COLS, GROUP_COLS, 0)
+        got.append(turned_round(piece, turn, lambda target: target != 3))
+    got_out = [turned_round(kept_out, turn, lambda target: target == 3) for turn in turns]
     grad_input = kernel_call(
         input_kernel,
         1,
-        (token_ids, table, w_query, w_key, w_value, got_rows),
+        (meta, token_ids, table, w_query, w_key, w_value, own_rows, *got_rows),
         [
             whole(token_ids.shape),
             whole(table.shape),
             whole(w_query.shape),
             whole(w_key.shape),
             whole(w_value.shape),
-            whole(got_rows.shape),
-        ],
+        ]
+        + [whole(own_rows.shape)] * GROUPS,
         jax.ShapeDtypeStruct((block, features), jnp.bfloat16),
         whole((block, features)),
-        [],
+        [pltpu.VMEM((3, features, block), jnp.bfloat16)],
         10**9,
         5 * 10**6,
     )
-    got = []
-    for turn in range(1, GROUPS):
-        route = [
-            (2 * z + x, 2 * ((z + turn) % GROUPS) + x)
-            for z in range(GROUPS)
-            for x in range(2)
-            if (z + turn) % GROUPS != 3
-        ]
-        target = jnp.minimum((group + turn) % GROUPS, 2)
-        piece = lax.dynamic_slice_in_dim(kept, target * GROUP_COLS, GROUP_COLS, 0)
-        got.append(lax.ppermute(piece, "seq", route))
-    for other in range(2):
-        for half in range(2):
-            route = [(2 * (2 * x + half) + (x ^ other), 6 + x) for x in range(2)]
-            route = [(s, t) for s, t in route if s != t]
-            got.append(lax.ppermute(kept_out, "seq", route))
-    pieces = kernel_call(
+    mine_shape = (GROUPS * GROUP_COLS, vocab // 2)
+    other_shape = (2 * kept_out.shape[0], vocab // 2)
+    mine, other = kernel_call(
         gather_kernel,
         1,
-        (meta, kept, kept_out, *got),
-        [whole(kept.shape), whole(kept_out.shape)] + [whole(piece.shape) for piece in got],
-        jax.ShapeDtypeStruct((4 * kept_out.shape[0], kept.shape[1]), jnp.bfloat16),
-        whole((4 * kept_out.shape[0], kept.shape[1])),
+        (meta, kept, *got, kept_out, *got_out),
+        [whole(piece.shape) for piece in (kept, *got, kept_out, *got_out)],
+        [
+            jax.ShapeDtypeStruct(mine_shape, jnp.bfloat16),
+            jax.ShapeDtypeStruct(other_shape, jnp.bfloat16),
+        ],
+        [whole(mine_shape), whole(other_shape)],
         [],
         10**6,
         10**6,
     )
-    others = swapped(pieces, "dp", 1)
+    sequences = lax.axis_size("dp")
+    last = blocks - 2
+    near = lax.ppermute(other, "seq", [(last, last + 1), (last + 1, last)])
+    far = lax.ppermute(
+        other,
+        ("dp", "seq"),
+        [
+            (blocks * d + last + x, blocks * (d ^ 1) + last + 1 - x)
+            for d in range(sequences)
+            for x in range(2)
+        ],
+    )
+    paired = swapped(mine, "dp", 1)
     weight_grads = kernel_call(
         weight_kernel,
         1,
-        (meta, table, pieces, others),
-        [whole(table.shape), whole(pieces.shape), whole(others.shape)],
+        (meta, table, mine, paired, near, far),
+        [
+            whole(table.shape),
+            whole(mine_shape),
+            whole(mine_shape),
+            whole(other_shape),
+            whole(other_shape),
+        ],
         jax.ShapeDtypeStruct((features // 2, features), jnp.float32),
         whole((features // 2, features)),
         [],

time: 92.7 us -> 107 us (1.15)
  the two profiles are of different devices: /device:TPU:0 before, /device:TPU:25 now
where the time goes in v2:
time: 107 us; the launch traced here: 106 us
  starting transfers between devices  54.1 us (51%)
  Pallas kernels  24.6 us (23%)
  waiting for transfers between devices  11.1 us (10%)
  local copies, waits for them, and re-layouts  10.7 us (10%)
  other arithmetic  4.94 us (5%)
    pallas_call x7, Pallas kernels, kernel_call(): pl.pallas_call(body, grid=(steps,), in_specs=[pl.BlockSpec(memory_space=p...  24.6 us
    ppermute x9, starting transfers between devices, turned_round(): return lax.ppermute(block, 'seq', route)  17.4 us
    ppermute x5, starting transfers between devices, swapped(): return lax.ppermute(block, axis, route)  13.9 us
    all_to_all x1, starting transfers between devices, grouped_device(): late = lax.all_to_all(late, 'seq', split_axis=0, concat_axis=0, tiled=True)  6.23 us
    all_to_all x1, starting transfers between devices, grouped_device(): lax.all_to_all(early, 'seq', split_axis=0, concat_axis=0, tiled=True)  5.57 us
    all_to_all x1, starting transfers between devices, grouped_device(): lax.all_to_all(jnp.broadcast_to(token_ids, (blocks, block)), 'seq', split...  5.47 us
    unnamed x32, local copies, waits for them, and re-layouts  5.09 us
    all_to_all x1, waiting for transfers between devices, grouped_device(): lax.all_to_all(early, 'seq', split_axis=0, concat_axis=0, tiled=True)  4.09 us
  transfers between devices with their start and end apart: 19, of which 5 were waited for; matrix products, arithmetic and copies ran while one was open for 9% of the time, Pallas kernels for 22%

profile of v2, /device:TPU:25, one launch (start us, length us, event | category | flops | bytes accessed | tf_op | source)
XLA Modules:
  0.0 106.4 jit_solution(17111159600888933165)
XLA Ops:
  0.6 1.3 %broadcast_in_dim.4 = s32[8,1,128]{2,1,0:T(1,128)} broadcast(s32[128]{0:T(128)} %bitcast.28), dimensions={2} | broadcast | bytes 4608 | tf_op jit(solution)/shard_map/broadcast_in_dim | solution.py:606
  2.0 5.5 %all-to-all-start = ((s32[8,1,128]{2,1,0:T(1,128)}), s32[8,1,128]{2,1,0:T(1,128)S(1)}, u32[]{:S(2)}, u32[]{:S(2)}) async-start(s32[8,1,128]{2,1,0:T(1,128)} %broadcast_in_dim.4), calls=%async_computation | async-start | bytes 8192 | tf_op jit(solution)/shard_map/all_to_all | solution.py:605
  11.9 5.6 %all-to-all-start.1 = ((bf16[8,192,128]{2,1,0:T(8,128)(2,1)}), bf16[8,192,128]{2,1,0:T(8,128)(2,1)S(1)}, u32[]{:S(2)}, u32[]{:S(2)}) async-start(bf16[8,192,128]{2,1,0:T(8,128)(2,1)} %get-tuple-element.13), calls=%async_computation.1 | async-start | bytes 786432 | tf_op jit(solution)/shard_map/all_to_all | solution.py:624
  18.4 2.2 %constant_dynamic-slice_fusion.3 = (bf16[768,192]{1,0:T(8,128)(2,1)}, bf16[768,192]{1,0:T(8,128)(2,1)}) fusion(bf16[768,768]{1,0:T(8,128)(2,1)} %value_ref.1, s32[]{:T(128)S(6)} %select_n.77, bf16[768,768]{1,0:T(8,128)(2,1)S(1)} %copy-done.1), kind=kLoop, calls=%fused_computation.15 | loop fusion | bytes 1179652 | tf_op jit(solution)/shard_map/dynamic_slice | solution.py:628
  21.9 4.1 %all-to-all-done.1.early_ref = bf16[8,192,128]{2,1,0:T(8,128)(2,1)S(1)} async-done(((bf16[8,192,128]{2,1,0:T(8,128)(2,1)}), bf16[8,192,128]{2,1,0:T(8,128)(2,1)S(1)}, u32[]{:S(2)}, u32[]{:S(2)}) %all-to-all-start.1) | async-done | bytes 393248 | tf_op jit(solution)/shard_map/all_to_all | solution.py:624
  26.0 6.2 %all-to-all-start.2 = ((bf16[8,128,384]{2,1,0:T(8,128)(2,1)}), bf16[8,128,384]{2,1,0:T(8,128)(2,1)S(1)}, u32[]{:S(2)}, u32[]{:S(2)}) async-start(bf16[8,128,384]{2,1,0:T(8,128)(2,1)} %copy-done.4), calls=%async_computation.2 | async-start | bytes 1572864 | tf_op jit(solution)/shard_map/all_to_all | solution.py:625
  32.2 1.6 %pad_maximum_fusion.weights_ref = bf16[768,576]{1,0:T(8,128)(2,1)S(1)} fusion(bf16[768,192]{1,0:T(8,128)(2,1)} %get-tuple-element.33, bf16[768,192]{1,0:T(8,128)(2,1)} %get-tuple-element.34, bf16[768,192]{1,0:T(8,128)(2,1)} %constant_dynamic-slice_fusion.5), kind=kLoop, calls=%fused_computation | loop fusion | flops 2654208 | bytes 1769472 | tf_op jit(solution)/shard_map/concatenate | solution.py:627
  33.9 9.2 %shard_map.99 = (bf16[3,2304,256]{2,1,0:T(8,128)(2,1)}, f32[3,64,1024]{2,1,0:T(8,128)S(1)}, bf16[3,1024,128]{2,1,0:T(8,128)(2,1)S(1)}, bf16[3,64,1024]{2,1,0:T(8,128)(2,1)S(1)}, bf16[3,1024,128]{2,1,0:T(8,128)(2,1)S(1)}) custom-call(s32[6]{0:T(128)S(1)} %pad_add_fusion.meta_ref, s32[8,128]{1,0:T(8,128)S(1)} %bitcast.26, bf16[256,768]{1,0:T(8,128)(2,1)S(1)} %copy-done.9, ...), custom_call_target="tpu_custom_call" | custom-call | flops 4000000000 | bytes 8000000 | tf_op jit(solution)/shard_map/pallas_call | solution.py:574
  43.1 9.0 %shard_map.100 = (bf16[4,576,128]{2,1,0:T(8,128)(2,1)S(1)}, bf16[2,576,128]{2,1,0:T(8,128)(2,1)}) custom-call(s32[6]{0:T(128)S(1)} %pad_add_fusion.meta_ref, s32[8,128]{1,0:T(8,128)S(1)} %bitcast.27, bf16[8,192,128]{2,1,0:T(8,128)(2,1)S(1)} %all-to-all-done.1.early_ref, f32[32,1024]{1,0:T(8,128)S(1)} %copy-done.13, f32[32,1024]{1,0:T(8,128)S(1)} %copy-done.12, ...), custom_call_target="tpu_custom_call" | custom-call | flops 4000000000 | bytes 8000000 | tf_op jit(solution)/shard_map/pallas_call | solution.py:574
  53.9 1.9 %collective-permute-start.3 = (bf16[576,128]{1,0:T(8,128)(2,1)S(1)}, bf16[576,128]{1,0:T(8,128)(2,1)}, u32[]{:S(2)}, u32[]{:S(2)}) collective-permute-start(bf16[576,128]{1,0:T(8,128)(2,1)S(1)} %dynamic-slice_bitcast_fusion), channel_id=1, source_target_pairs={{0,8},{8,0},{16,24},{24,16},{1,9},{9,1},{17,25},{25,17},{2,10},{10... | collective-permute-start | bytes 442376 | tf_op jit(solution)/shard_map/ppermute | solution.py:592
  57.9 1.3 %collective-permute-start.4 = (bf16[576,128]{1,0:T(8,128)(2,1)S(1)}, bf16[576,128]{1,0:T(8,128)(2,1)}, u32[]{:S(2)}, u32[]{:S(2)}) collective-permute-start(bf16[576,128]{1,0:T(8,128)(2,1)S(1)} %bitcast_add_fusion), channel_id=1, source_target_pairs={{0,16},{8,24},{16,0},{24,8},{1,17},{9,25},{17,1},{25,9},{2,18},{10... | collective-permute-start | bytes 442376 | tf_op jit(solution)/shard_map/ppermute | solution.py:592
  61.4 1.7 %collective-permute-done.4 = bf16[576,128]{1,0:T(8,128)(2,1)} collective-permute-done((bf16[576,128]{1,0:T(8,128)(2,1)S(1)}, bf16[576,128]{1,0:T(8,128)(2,1)}, u32[]{:S(2)}, u32[]{:S(2)}) %collective-permute-start.4) | collective-permute-done | bytes 147488 | tf_op jit(solution)/shard_map/ppermute | solution.py:592
  65.5 1.6 %collective-permute-start.5 = (bf16[192,128]{1,0:T(8,128)(2,1)S(1)}, bf16[192,128]{1,0:T(8,128)(2,1)S(1)}, u32[]{:S(2)}, u32[]{:S(2)}) collective-permute-start(bf16[192,128]{1,0:T(8,128)(2,1)S(1)} %get-tuple-element.30), channel_id=1, source_target_pairs={{0,2},{1,3},{2,4},{3,5},{6,0},{7,1},{8,10},{9,11},{10,12},{11,13},... | collective-permute-start | bytes 147464 | tf_op jit(solution)/shard_map/ppermute | solution.py:742
  67.1 3.6 %collective-permute-start.6 = (bf16[192,128]{1,0:T(8,128)(2,1)S(1)}, bf16[192,128]{1,0:T(8,128)(2,1)S(1)}, u32[]{:S(2)}, u32[]{:S(2)}) collective-permute-start(bf16[192,128]{1,0:T(8,128)(2,1)S(1)} %get-tuple-element.29), channel_id=1, source_target_pairs={{0,4},{1,5},{4,0},{5,1},{6,2},{7,3},{8,12},{9,13},{12,8},{13,9},{1... | collective-permute-start | bytes 147464 | tf_op jit(solution)/shard_map/ppermute | solution.py:742
  72.2 4.0 %collective-permute-start.7 = (bf16[192,128]{1,0:T(8,128)(2,1)S(1)}, bf16[192,128]{1,0:T(8,128)(2,1)S(1)}, u32[]{:S(2)}, u32[]{:S(2)}) collective-permute-start(bf16[192,128]{1,0:T(8,128)(2,1)S(1)} %get-tuple-element.28), channel_id=1, source_target_pairs={{2,0},{3,1},{4,2},{5,3},{6,4},{7,5},{10,8},{11,9},{12,10},{13,11},... | collective-permute-start | bytes 147464 | tf_op jit(solution)/shard_map/ppermute | solution.py:742
  78.9 2.4 %collective-permute-start.1 = (bf16[576,128]{1,0:T(8,128)(2,1)S(1)}, bf16[576,128]{1,0:T(8,128)(2,1)S(1)}, u32[]{:S(2)}, u32[]{:S(2)}) collective-permute-start(bf16[576,128]{1,0:T(8,128)(2,1)S(1)} %get-tuple-element.25), channel_id=1, source_target_pairs={{0,4},{1,5},{2,6},{3,7},{4,0},{5,1},{6,2},{7,3},{8,12},{9,13},{10,... | collective-permute-start | bytes 442376 | tf_op jit(solution)/shard_map/ppermute | solution.py:742
  81.3 1.8 %collective-permute-start.2 = (bf16[576,128]{1,0:T(8,128)(2,1)S(1)}, bf16[576,128]{1,0:T(8,128)(2,1)S(1)}, u32[]{:S(2)}, u32[]{:S(2)}) collective-permute-start(bf16[576,128]{1,0:T(8,128)(2,1)S(1)} %get-tuple-element.24), channel_id=1, source_target_pairs={{0,6},{1,7},{2,0},{3,1},{4,2},{5,3},{6,4},{7,5},{8,14},{9,15},{10,... | collective-permute-start | bytes 442376 | tf_op jit(solution)/shard_map/ppermute | solution.py:742
  83.1 1.5 %collective-permute-done.12.o0 = bf16[288,128]{1,0:T(8,128)(2,1)S(1)} collective-permute-done((bf16[288,128]{1,0:T(8,128)(2,1)S(1)}, bf16[288,128]{1,0:T(8,128)(2,1)S(1)}, u32[]{:S(2)}, u32[]{:S(2)}) %collective-permute-start.12) | collective-permute-done | bytes 73760 | tf_op jit(solution)/shard_map/ppermute | solution.py:742
  85.2 8.7 %collective-permute-start.13 = (bf16[768,128]{1,0:T(8,128)(2,1)S(1)}, bf16[768,128]{1,0:T(8,128)(2,1)S(1)}, u32[]{:S(2)}, u32[]{:S(2)}) collective-permute-start(bf16[768,128]{1,0:T(8,128)(2,1)S(1)} %get-tuple-element.22.mine_ref), channel_id=1, source_target_pairs={{0,8},{8,0},{16,24},{24,16},{1,9},{9,1},{17,25},{25,17},{2,10},{10... | collective-permute-start | bytes 589832 | tf_op jit(solution)/shard_map/ppermute | solution.py:592
  93.9 3.1 %collective-permute-start.14 = (bf16[576,128]{1,0:T(8,128)(2,1)S(1)}, bf16[576,128]{1,0:T(8,128)(2,1)S(1)}, u32[]{:S(2)}, u32[]{:S(2)}) collective-permute-start(bf16[576,128]{1,0:T(8,128)(2,1)S(1)} %get-tuple-element.23), channel_id=1, source_target_pairs={{6,7},{7,6},{14,15},{15,14},{22,23},{23,22},{30,31},{31,30}} | collective-permute-start | bytes 442376 | tf_op jit(solution)/shard_map/ppermute | solution.py:798
  97.0 2.4 %collective-permute-start.15 = (bf16[576,128]{1,0:T(8,128)(2,1)S(1)}, bf16[576,128]{1,0:T(8,128)(2,1)S(1)}, u32[]{:S(2)}, u32[]{:S(2)}) collective-permute-start(bf16[576,128]{1,0:T(8,128)(2,1)S(1)} %get-tuple-element.23), channel_id=1, source_target_pairs={{6,15},{7,14},{14,7},{15,6},{22,31},{23,30},{30,23},{31,22}} | collective-permute-start | bytes 442376 | tf_op jit(solution)/shard_map/ppermute | solution.py:799
  99.4 2.5 %shard_map.101 = bf16[128,768]{1,0:T(8,128)(2,1)} custom-call(s32[6]{0:T(128)S(1)} %pad_add_fusion.meta_ref, s32[1,128]{1,0:T(1,128)S(1)} %copy-done.14, bf16[256,768]{1,0:T(8,128)(2,1)S(1)} %copy-done.10, bf16[768,768]{1,0:T(8,128)(2,1)S(1)} %copy-done, bf16[768,768]{1,0:T(8,128)(2,1)S(1)} %copy-done.1, bf16[768,768]{1,0:T(8,128)(2,1)S(1)} %copy-done.2, ...), custom_call_target="tpu_custom_call" | custom-call | flops 1000000000 | bytes 5000000 | tf_op jit(solution)/shard_map/pallas_call | solution.py:574
  102.0 2.7 %collective-permute-done.15.far_ref = bf16[576,128]{1,0:T(8,128)(2,1)S(1)} collective-permute-done((bf16[576,128]{1,0:T(8,128)(2,1)S(1)}, bf16[576,128]{1,0:T(8,128)(2,1)S(1)}, u32[]{:S(2)}, u32[]{:S(2)}) %collective-permute-start.15) | collective-permute-done | bytes 147488 | tf_op jit(solution)/shard_map/ppermute | solution.py:799
  104.6 1.7 %shard_map.104 = f32[384,768]{1,0:T(8,128)} custom-call(s32[6]{0:T(128)S(1)} %pad_add_fusion.meta_ref, bf16[256,768]{1,0:T(8,128)(2,1)S(1)} %copy-done.10, bf16[768,128]{1,0:T(8,128)(2,1)S(1)} %get-tuple-element.22.mine_ref, bf16[768,128]{1,0:T(8,128)(2,1)S(1)} %collective-permute-done.13.other_ref, bf16[576,128]{1,0:T(8,128)(2,1)S(1)} %collective-permute-done.14.near_ref, ...), custom_call_target="tpu_custom_call" | custom-call | flops 1000000000 | bytes 5000000 | tf_op jit(solution)/shard_map/pallas_call | solution.py:574
  (70 shorter events, 19.7 us)
Async XLA Ops:
  0.6 16.9 %copy-start = (bf16[768,768]{1,0:T(8,128)(2,1)S(1)}, bf16[768,768]{1,0:T(8,128)(2,1)}, u32[]{:S(2)}) copy-start(bf16[768,768]{1,0:T(8,128)(2,1)} %query_ref.1) | copy-start | bytes 3538948
  2.0 9.9 %all-to-all-start = ((s32[8,1,128]{2,1,0:T(1,128)}), s32[8,1,128]{2,1,0:T(1,128)S(1)}, u32[]{:S(2)}, u32[]{:S(2)}) async-start(s32[8,1,128]{2,1,0:T(1,128)} %broadcast_in_dim.4), calls=%async_computation | async-start | bytes 8192 | tf_op jit(solution)/shard_map/all_to_all | solution.py:605
  11.9 14.1 %all-to-all-start.1 = ((bf16[8,192,128]{2,1,0:T(8,128)(2,1)}), bf16[8,192,128]{2,1,0:T(8,128)(2,1)S(1)}, u32[]{:S(2)}, u32[]{:S(2)}) async-start(bf16[8,192,128]{2,1,0:T(8,128)(2,1)} %get-tuple-element.13), calls=%async_computation.1 | async-start | bytes 786432 | tf_op jit(solution)/shard_map/all_to_all | solution.py:624
  26.0 33.2 %all-to-all-start.2 = ((bf16[8,128,384]{2,1,0:T(8,128)(2,1)}), bf16[8,128,384]{2,1,0:T(8,128)(2,1)S(1)}, u32[]{:S(2)}, u32[]{:S(2)}) async-start(bf16[8,128,384]{2,1,0:T(8,128)(2,1)} %copy-done.4), calls=%async_computation.2 | async-start | bytes 1572864 | tf_op jit(solution)/shard_map/all_to_all | solution.py:625
  53.9 3.0 %collective-permute-start.3 = (bf16[576,128]{1,0:T(8,128)(2,1)S(1)}, bf16[576,128]{1,0:T(8,128)(2,1)}, u32[]{:S(2)}, u32[]{:S(2)}) collective-permute-start(bf16[576,128]{1,0:T(8,128)(2,1)S(1)} %dynamic-slice_bitcast_fusion), channel_id=1, source_target_pairs={{0,8},{8,0},{16,24},{24,16},{1,9},{9,1},{17,25},{25,17},{2,10},{10... | collective-permute-start | bytes 442376 | tf_op jit(solution)/shard_map/ppermute | solution.py:592
  57.9 5.2 %collective-permute-start.4 = (bf16[576,128]{1,0:T(8,128)(2,1)S(1)}, bf16[576,128]{1,0:T(8,128)(2,1)}, u32[]{:S(2)}, u32[]{:S(2)}) collective-permute-start(bf16[576,128]{1,0:T(8,128)(2,1)S(1)} %bitcast_add_fusion), channel_id=1, source_target_pairs={{0,16},{8,24},{16,0},{24,8},{1,17},{9,25},{17,1},{25,9},{2,18},{10... | collective-permute-start | bytes 442376 | tf_op jit(solution)/shard_map/ppermute | solution.py:592
  60.7 11.4 %copy-start.8 = (bf16[4,576,128]{2,1,0:T(8,128)(2,1)S(1)}, bf16[4,576,128]{2,1,0:T(8,128)(2,1)}, u32[]{:S(2)}) copy-start(bf16[4,576,128]{2,1,0:T(8,128)(2,1)} %copy-done.7) | copy-start | bytes 1769476
  60.7 3.3 %collective-permute-start.8 = (bf16[288,128]{1,0:T(8,128)(2,1)S(1)}, bf16[288,128]{1,0:T(8,128)(2,1)S(1)}, u32[]{:S(2)}, u32[]{:S(2)}) collective-permute-start(bf16[288,128]{1,0:T(8,128)(2,1)S(1)} %dynamic-slice_bitcast_fusion.5), channel_id=1, source_target_pairs={{0,8},{8,0},{16,24},{24,16},{1,9},{9,1},{17,25},{25,17},{2,10},{10... | collective-permute-start | bytes 221192 | tf_op jit(solution)/shard_map/ppermute | solution.py:592
  64.1 35.3 %copy-start.2 = (bf16[768,768]{1,0:T(8,128)(2,1)S(1)}, bf16[768,768]{1,0:T(8,128)(2,1)}, u32[]{:S(2)}) copy-start(bf16[768,768]{1,0:T(8,128)(2,1)} %value_ref.1) | copy-start | bytes 3538948
  64.1 35.3 %copy-start.10 = (bf16[256,768]{1,0:T(8,128)(2,1)S(1)}, bf16[256,768]{1,0:T(8,128)(2,1)}, u32[]{:S(2)}) copy-start(bf16[256,768]{1,0:T(8,128)(2,1)} %table_ref.5) | copy-start | bytes 1179652
  64.1 35.3 %copy-start.14 = (s32[1,128]{1,0:T(1,128)S(1)}, s32[1,128]{1,0:T(1,128)}, u32[]{:S(2)}) copy-start(s32[1,128]{1,0:T(1,128)} %tokens_ref.1) | copy-start | bytes 1540
  64.2 6.6 %collective-permute-start.9 = (bf16[288,128]{1,0:T(8,128)(2,1)S(1)}, bf16[288,128]{1,0:T(8,128)(2,1)S(1)}, u32[]{:S(2)}, u32[]{:S(2)}) collective-permute-start(bf16[288,128]{1,0:T(8,128)(2,1)S(1)} %bitcast_add_fusion.1), channel_id=1, source_target_pairs={{0,16},{8,24},{16,0},{24,8},{1,17},{9,25},{17,1},{25,9},{2,18},{10... | collective-permute-start | bytes 221192 | tf_op jit(solution)/shard_map/ppermute | solution.py:592
  65.5 10.8 %collective-permute-start.5 = (bf16[192,128]{1,0:T(8,128)(2,1)S(1)}, bf16[192,128]{1,0:T(8,128)(2,1)S(1)}, u32[]{:S(2)}, u32[]{:S(2)}) collective-permute-start(bf16[192,128]{1,0:T(8,128)(2,1)S(1)} %get-tuple-element.30), channel_id=1, source_target_pairs={{0,2},{1,3},{2,4},{3,5},{6,0},{7,1},{8,10},{9,11},{10,12},{11,13},... | collective-permute-start | bytes 147464 | tf_op jit(solution)/shard_map/ppermute | solution.py:742
  67.1 10.4 %collective-permute-start.6 = (bf16[192,128]{1,0:T(8,128)(2,1)S(1)}, bf16[192,128]{1,0:T(8,128)(2,1)S(1)}, u32[]{:S(2)}, u32[]{:S(2)}) collective-permute-start(bf16[192,128]{1,0:T(8,128)(2,1)S(1)} %get-tuple-element.29), channel_id=1, source_target_pairs={{0,4},{1,5},{4,0},{5,1},{6,2},{7,3},{8,12},{9,13},{12,8},{13,9},{1... | collective-permute-start | bytes 147464 | tf_op jit(solution)/shard_map/ppermute | solution.py:742
  70.8 10.5 %collective-permute-start.10 = (bf16[288,128]{1,0:T(8,128)(2,1)S(1)}, bf16[288,128]{1,0:T(8,128)(2,1)S(1)}, u32[]{:S(2)}, u32[]{:S(2)}) collective-permute-start(bf16[288,128]{1,0:T(8,128)(2,1)S(1)} %add.107.kept_out_ref), channel_id=1, source_target_pairs={{4,6},{5,7},{12,14},{13,15},{20,22},{21,23},{28,30},{29,31}} | collective-permute-start | bytes 221192 | tf_op jit(solution)/shard_map/ppermute | solution.py:742
  72.2 24.8 %collective-permute-start = (bf16[576,128]{1,0:T(8,128)(2,1)S(1)}, bf16[576,128]{1,0:T(8,128)(2,1)S(1)}, u32[]{:S(2)}, u32[]{:S(2)}) collective-permute-start(bf16[576,128]{1,0:T(8,128)(2,1)S(1)} %get-tuple-element.26), channel_id=1, source_target_pairs={{0,2},{1,3},{2,4},{3,5},{4,6},{5,7},{6,0},{7,1},{8,10},{9,11},{10,... | collective-permute-start | bytes 442376 | tf_op jit(solution)/shard_map/ppermute | solution.py:742
  72.2 6.6 %collective-permute-start.7 = (bf16[192,128]{1,0:T(8,128)(2,1)S(1)}, bf16[192,128]{1,0:T(8,128)(2,1)S(1)}, u32[]{:S(2)}, u32[]{:S(2)}) collective-permute-start(bf16[192,128]{1,0:T(8,128)(2,1)S(1)} %get-tuple-element.28), channel_id=1, source_target_pairs={{2,0},{3,1},{4,2},{5,3},{6,4},{7,5},{10,8},{11,9},{12,10},{13,11},... | collective-permute-start | bytes 147464 | tf_op jit(solution)/shard_map/ppermute | solution.py:742
  76.2 6.9 %collective-permute-start.11 = (bf16[288,128]{1,0:T(8,128)(2,1)S(1)}, bf16[288,128]{1,0:T(8,128)(2,1)S(1)}, u32[]{:S(2)}, u32[]{:S(2)}) collective-permute-start(bf16[288,128]{1,0:T(8,128)(2,1)S(1)} %add.107.kept_out_ref), channel_id=1, source_target_pairs={{2,6},{3,7},{10,14},{11,15},{18,22},{19,23},{26,30},{27,31}} | collective-permute-start | bytes 221192 | tf_op jit(solution)/shard_map/ppermute | solution.py:742
  77.6 7.0 %collective-permute-start.12 = (bf16[288,128]{1,0:T(8,128)(2,1)S(1)}, bf16[288,128]{1,0:T(8,128)(2,1)S(1)}, u32[]{:S(2)}, u32[]{:S(2)}) collective-permute-start(bf16[288,128]{1,0:T(8,128)(2,1)S(1)} %add.107.kept_out_ref), channel_id=1, source_target_pairs={{0,6},{1,7},{8,14},{9,15},{16,22},{17,23},{24,30},{25,31}} | collective-permute-start | bytes 221192 | tf_op jit(solution)/shard_map/ppermute | solution.py:742
  78.9 20.5 %collective-permute-start.1 = (bf16[576,128]{1,0:T(8,128)(2,1)S(1)}, bf16[576,128]{1,0:T(8,128)(2,1)S(1)}, u32[]{:S(2)}, u32[]{:S(2)}) collective-permute-start(bf16[576,128]{1,0:T(8,128)(2,1)S(1)} %get-tuple-element.25), channel_id=1, source_target_pairs={{0,4},{1,5},{2,6},{3,7},{4,0},{5,1},{6,2},{7,3},{8,12},{9,13},{10,... | collective-permute-start | bytes 442376 | tf_op jit(solution)/shard_map/ppermute | solution.py:742
  81.3 18.1 %collective-permute-start.2 = (bf16[576,128]{1,0:T(8,128)(2,1)S(1)}, bf16[576,128]{1,0:T(8,128)(2,1)S(1)}, u32[]{:S(2)}, u32[]{:S(2)}) collective-permute-start(bf16[576,128]{1,0:T(8,128)(2,1)S(1)} %get-tuple-element.24), channel_id=1, source_target_pairs={{0,6},{1,7},{2,0},{3,1},{4,2},{5,3},{6,4},{7,5},{8,14},{9,15},{10,... | collective-permute-start | bytes 442376 | tf_op jit(solution)/shard_map/ppermute | solution.py:742
  85.2 19.5 %collective-permute-start.13 = (bf16[768,128]{1,0:T(8,128)(2,1)S(1)}, bf16[768,128]{1,0:T(8,128)(2,1)S(1)}, u32[]{:S(2)}, u32[]{:S(2)}) collective-permute-start(bf16[768,128]{1,0:T(8,128)(2,1)S(1)} %get-tuple-element.22.mine_ref), channel_id=1, source_target_pairs={{0,8},{8,0},{16,24},{24,16},{1,9},{9,1},{17,25},{25,17},{2,10},{10... | collective-permute-start | bytes 589832 | tf_op jit(solution)/shard_map/ppermute | solution.py:592
  93.9 8.1 %collective-permute-start.14 = (bf16[576,128]{1,0:T(8,128)(2,1)S(1)}, bf16[576,128]{1,0:T(8,128)(2,1)S(1)}, u32[]{:S(2)}, u32[]{:S(2)}) collective-permute-start(bf16[576,128]{1,0:T(8,128)(2,1)S(1)} %get-tuple-element.23), channel_id=1, source_target_pairs={{6,7},{7,6},{14,15},{15,14},{22,23},{23,22},{30,31},{31,30}} | collective-permute-start | bytes 442376 | tf_op jit(solution)/shard_map/ppermute | solution.py:798
  97.0 7.7 %collective-permute-start.15 = (bf16[576,128]{1,0:T(8,128)(2,1)S(1)}, bf16[576,128]{1,0:T(8,128)(2,1)S(1)}, u32[]{:S(2)}, u32[]{:S(2)}) collective-permute-start(bf16[576,128]{1,0:T(8,128)(2,1)S(1)} %get-tuple-element.23), channel_id=1, source_target_pairs={{6,15},{7,14},{14,7},{15,6},{22,31},{23,30},{30,23},{31,22}} | collective-permute-start | bytes 442376 | tf_op jit(solution)/shard_map/ppermute | solution.py:799
  (11 other events, 27.8 us)

commit v3 on v1

--- a/solution.py
+++ b/solution.py
@@ -1,7 +1,6 @@
-import functools
-
 import jax
 import jax.numpy as jnp
+import numpy as np
 from jax import lax
 from jax.experimental import pallas as pl
 from jax.experimental.pallas import tpu as pltpu
@@ -248,28 +247,55 @@
     return (rows == tokens).astype(jnp.float32).astype(jnp.bfloat16)
 
 
-def send_kernel(tokens_ref, cotangent_ref, out_weights_ref, early_ref, late_ref):
-    cotangent = cotangent_ref[...]
-    grad_att = ndot(out_weights_ref[...], cotangent).astype(jnp.bfloat16)
+def send_kernel(tokens_ref, cotangent_ref, out_weights_ref, early_ref):
+    grad_att = ndot(out_weights_ref[...], cotangent_ref[...]).astype(jnp.bfloat16)
     block = tokens_ref.shape[1]
     tokens = jnp.broadcast_to(tokens_ref[...].astype(jnp.float32), (TOKEN_ROWS, block)).astype(
         jnp.bfloat16
     )
-    columns = late_ref.shape[2]
     for target in range(2 * GROUPS):
-        group, side = divmod(target, 2)
+        group = target // 2
         early_ref[target, :GROUP_COLS, :] = grad_att[
             group * GROUP_COLS : (group + 1) * GROUP_COLS
         ]
         early_ref[target, GROUP_COLS:, :] = tokens
-        late_ref[target] = cotangent[:, side * columns : (side + 1) * columns]
+
+
+def prepare_kernel(
+    meta_ref,
+    cotangent_ref,
+    table_ref,
+    query_ref,
+    key_ref,
+    value_ref,
+    late_ref,
+    lookup_ref,
+    normed_ref,
+    columns_ref,
+):
+    columns = late_ref.shape[2]
+    for target in range(2 * GROUPS):
+        side = target % 2
+        late_ref[target] = cotangent_ref[:, side * columns : (side + 1) * columns]
+    normed = normed_table(table_ref)
+    half = normed.shape[1] // 2
+    normed_ref[...] = jnp.where(meta_ref[GROUP_HEADS] == 0, normed[:, :half], normed[:, half:])
+    place = pl.ds(pl.multiple_of(meta_ref[GROUP_HEADS + 1] * GROUP_COLS, GROUP_COLS), GROUP_COLS)
+    for matrix, weights_ref in enumerate((query_ref, key_ref, value_ref)):
+        columns_ref[...] = jnp.dot(
+            normed, weights_ref[...], preferred_element_type=jnp.float32
+        ).T
+        mine = columns_ref[place, :]
+        upper = mine.astype(jnp.bfloat16)
+        rows = slice(matrix * GROUP_COLS, (matrix + 1) * GROUP_COLS)
+        lookup_ref[0, rows, :] = upper
+        lookup_ref[1, rows, :] = (mine - upper.astype(jnp.float32)).astype(jnp.bfloat16)
 
 
 def attention_kernel(
     meta_ref,
     early_ref,
-    table_ref,
-    weights_ref,
+    lookup_ref,
     cosine_ref,
     sine_ref,
     rows_ref,
@@ -289,7 +315,7 @@
     head = pl.program_id(0)
     blocks, _, block = early_ref.shape
     length = blocks * block
-    vocab = table_ref.shape[0]
+    vocab = lookup_ref.shape[2]
     half_vocab = vocab // 2
     cosine = cosine_ref[...]
     sine_part = sine_ref[...]
@@ -297,10 +323,6 @@
 
     @pl.when(head == 0)
     def _():
-        normed = normed_table(table_ref)
-        lookup = jnp.dot(normed, weights_ref[...], preferred_element_type=jnp.float32).T
-        upper = lookup.astype(jnp.bfloat16)
-        lower = (lookup - upper.astype(jnp.float32)).astype(jnp.bfloat16)
         for source in range(blocks):
             lanes = slice(source * block, (source + 1) * block)
             tokens = early_ref[source, GROUP_COLS : GROUP_COLS + TOKEN_ROWS, :]
@@ -313,9 +335,9 @@
 
         def chosen(start):
             rows = slice(start, start + HEAD_DIM)
-            return jnp.dot(upper[rows], onehot, preferred_element_type=jnp.float32) + jnp.dot(
-                lower[rows], onehot, preferred_element_type=jnp.float32
-            )
+            return jnp.dot(
+                lookup_ref[0, rows, :], onehot, preferred_element_type=jnp.float32
+            ) + jnp.dot(lookup_ref[1, rows, :], onehot, preferred_element_type=jnp.float32)
 
         def turned(columns):
             former = columns[:HALF]
@@ -423,43 +445,55 @@
             rows_ref[target, place, :] = jnp.where(meta_ref[GROUP_HEADS] == 0, even, odd)
 
 
-def out_kernel(attended_ref, cotangent_ref, out_ref):
+def out_kernel(meta_ref, attended_ref, cotangent_ref, sums_ref, keep_ref, give_ref):
     total = jnp.dot(attended_ref[...], cotangent_ref[...], preferred_element_type=jnp.float32)
     rows = total.shape[0] // 2
-    lanes = out_ref.shape[2]
-    for core in range(2):
-        for chunk in range(total.shape[1] // lanes):
-            out_ref[core, chunk * rows : (chunk + 1) * rows, :] = total[
-                core * rows : (core + 1) * rows, chunk * lanes : (chunk + 1) * lanes
-            ].astype(jnp.bfloat16)
-
-
-def gather_kernel(meta_ref, kept_ref, kept_out_ref, s1, s2, s3, n0, n1, f0, f1, pieces_ref):
-    group = meta_ref[GROUP_HEADS + 1]
+    base = sums_ref.shape[1]
+    lanes = keep_ref.shape[1]
+    first = meta_ref[GROUP_HEADS + 2] == 0
+    keep_ref[:base, :] = jnp.where(first, sums_ref[0], sums_ref[1])
+    give_ref[:base, :] = jnp.where(first, sums_ref[1], sums_ref[0])
+    for chunk in range(total.shape[1] // lanes):
+        part = total[:, chunk * lanes : (chunk + 1) * lanes]
+        place = slice(base + chunk * rows, base + (chunk + 1) * rows)
+        keep_ref[place, :] = jnp.where(first, part[:rows], part[rows:]).astype(jnp.bfloat16)
+        give_ref[place, :] = jnp.where(first, part[rows:], part[:rows]).astype(jnp.bfloat16)
+
+
+def combine_kernel(here_ref, there_ref, after_ref, out_ref):
+    del after_ref
     rows = GROUP_COLS
-
-    @pl.when(group < 3)
+    size = out_ref.shape[1]
+    blank = jnp.zeros((size - rows, out_ref.shape[2]), jnp.bfloat16)
+    for matrix in range(3):
+        place = slice(matrix * rows, (matrix + 1) * rows)
+        out_ref[matrix, :rows, :] = here_ref[place, :] + there_ref[place, :]
+        out_ref[matrix, rows:, :] = blank
+    out_ref[3] = here_ref[3 * rows :, :] + there_ref[3 * rows :, :]
+
+
+def gather_kernel(meta_ref, got_ref, mine_ref, other_ref):
+    rows = GROUP_COLS
+    size = got_ref.shape[1]
+
+    @pl.when(meta_ref[GROUP_HEADS + 1] < 3)
     def _():
-        own = pl.multiple_of(group * rows, rows)
-        pieces_ref[pl.ds(own, rows), :] = kept_ref[pl.ds(own, rows), :]
-        for turn, got in ((1, s1), (2, s2), (3, s3)):
-            source = lax.rem(group - turn + GROUPS, GROUPS)
-            pieces_ref[pl.ds(pl.multiple_of(source * rows, rows), rows), :] = got[...]
-        tail = pieces_ref.shape[0] - GROUPS * rows
-        pieces_ref[GROUPS * rows :, :] = jnp.zeros((tail, kept_ref.shape[1]), jnp.bfloat16)
-
-    @pl.when(group == 3)
+        for group in range(GROUPS):
+            mine_ref[group * rows : (group + 1) * rows, :] = got_ref[group, :rows, :]
+        other_ref[...] = jnp.zeros_like(other_ref)
+
+    @pl.when(meta_ref[GROUP_HEADS + 1] == 3)
     def _():
-        size = kept_out_ref.shape[0]
-        own = meta_ref[GROUP_HEADS] == 1
-        pieces_ref[0:size, :] = n0[...]
-        pieces_ref[size : 2 * size, :] = f0[...]
-        pieces_ref[2 * size : 3 * size, :] = jnp.where(own, kept_out_ref[...], n1[...])
-        pieces_ref[3 * size :, :] = f1[...]
+        first = meta_ref[GROUP_HEADS] == 0
+        for part in range(2):
+            place = slice(part * size, (part + 1) * size)
+            mine_ref[place, :] = jnp.where(first, got_ref[part], got_ref[2 + part])
+            other_ref[place, :] = jnp.where(first, got_ref[2 + part], got_ref[part])
+        tail = mine_ref.shape[0] - 2 * size
+        mine_ref[2 * size :, :] = jnp.zeros((tail, mine_ref.shape[1]), jnp.bfloat16)
 
 
 def input_kernel(tokens_ref, table_ref, query_ref, key_ref, value_ref, rows_ref, out_ref):
-    widened = table_ref[...].astype(jnp.float32)
     vocab = table_ref.shape[0]
     onehot = onehot_columns(tokens_ref[...], vocab)
     embedded = tdot(onehot, table_ref[...])
@@ -481,24 +515,21 @@
     ).astype(jnp.bfloat16)
 
 
-def weight_kernel(meta_ref, table_ref, mine_ref, other_ref, out_ref):
-    side_rows = out_ref.shape[0]
+def weight_kernel(meta_ref, normed_ref, mine_ref, other_ref, near_ref, far_ref, out_ref):
     half_vocab = mine_ref.shape[1]
     first_core = meta_ref[GROUP_HEADS + 2] == 0
 
     @pl.when(meta_ref[GROUP_HEADS + 1] < 3)
     def _():
-        normed = normed_table(table_ref)
-        first = normed[:, :side_rows]
-        second = normed[:, side_rows:]
-        taken = jnp.where(meta_ref[GROUP_HEADS] == 0, first, second)
-        upper = jnp.where(first_core, taken[:half_vocab], taken[half_vocab:])
-        lower = jnp.where(first_core, taken[half_vocab:], taken[:half_vocab])
+        first = normed_ref[:half_vocab, :]
+        second = normed_ref[half_vocab:, :]
+        upper = jnp.where(first_core, first, second)
+        lower = jnp.where(first_core, second, first)
         total = None
         for part, sums_ref in ((upper, mine_ref), (lower, other_ref)):
             term = lax.dot_general(
                 part,
-                sums_ref[: GROUPS * GROUP_COLS, :],
+                sums_ref[...],
                 (((0,), (1,)), ((), ())),
                 preferred_element_type=jnp.float32,
             )
@@ -508,47 +539,40 @@
     @pl.when(meta_ref[GROUP_HEADS + 1] == 3)
     def _():
         rows = GROUP_COLS // 2
-        side = meta_ref[GROUP_HEADS]
-        for core in range(2):
-            for half in range(2):
-                for plane in range(2):
-                    for chunk in range(3):
-                        place = ((2 * half + plane) * 3 + chunk) * rows
-                        here = mine_ref[place : place + rows, :]
-                        there = other_ref[place : place + rows, :]
-                        value = jnp.where(first_core == (core == 0), here, there)
-                        row = half * GROUP_COLS + core * rows
-                        column = jnp.where(side == 0, plane, 1 - plane) * 3 + chunk
-                        lanes = pl.ds(
-                            pl.multiple_of(column * half_vocab, half_vocab), half_vocab
+        first_side = meta_ref[GROUP_HEADS] == 0
+        for half in range(2):
+            for chunk in range(3):
+                place = slice((half * 3 + chunk) * rows, (half * 3 + chunk + 1) * rows)
+                for core in range(2):
+                    same = first_core == (core == 0)
+                    own = jnp.where(same, mine_ref[place, :], other_ref[place, :])
+                    crossed = jnp.where(same, near_ref[place, :], far_ref[place, :])
+                    row = half * GROUP_COLS + core * rows
+                    for side in range(2):
+                        value = jnp.where(first_side == (side == 0), own, crossed)
+                        start = (side * 3 + chunk) * half_vocab
+                        out_ref[row : row + rows, start : start + half_vocab] = value.astype(
+                            jnp.float32
                         )
-                        out_ref[row : row + rows, lanes] = value.astype(jnp.float32)
 
 
 def whole(shape):
     return pl.BlockSpec(shape, lambda *_: (0,) * len(shape))
-
-
-def kernel_call(body, steps, operands, in_specs, outs, out_specs, scratch, flops, moved):
-    return pl.pallas_call(
-        body,
-        grid=(steps,),
-        in_specs=[pl.BlockSpec(memory_space=pltpu.SMEM)] + in_specs
-        if operands[0].ndim == 1
-        else in_specs,
-        out_specs=out_specs,
-        out_shape=outs,
-        scratch_shapes=scratch,
-        compiler_params=pltpu.CompilerParams(
-            dimension_semantics=("arbitrary",), vmem_limit_bytes=VMEM_BYTES
-        ),
-        cost_estimate=pl.CostEstimate(flops=flops, bytes_accessed=moved, transcendentals=0),
-    )(*operands)
 
 
 def swapped(block, axis, bit):
     route = [(i, i ^ bit) for i in range(lax.axis_size(axis))]
     return lax.ppermute(block, axis, route)
+
+
+def rope_table(length):
+    frequency = (10000.0 ** (-2.0 * np.arange(HALF, dtype=np.float32) / HEAD_DIM)).astype(np.float32)
+    angles = frequency[:, None] * np.arange(length, dtype=np.float32)[None, :]
+    angles = angles.astype(np.float64)
+    return (
+        jnp.asarray(np.cos(angles).astype(np.float32)),
+        jnp.asarray(np.sin(angles).astype(np.float32)),
+    )
 
 
 def grouped_device(token_ids, cotangent, table, w_query, w_key, w_value, w_out, window):
@@ -561,158 +585,131 @@
     vocab = table.shape[0]
     blocks = lax.axis_size("seq")
     length = block * blocks
-    early, late = kernel_call(
-        send_kernel,
-        1,
-        (token_ids, cotangent[0], w_out),
-        [whole(token_ids.shape), whole((block, features)), whole(w_out.shape)],
-        [
-            jax.ShapeDtypeStruct((blocks, GROUP_COLS + TOKEN_ROWS, block), jnp.bfloat16),
-            jax.ShapeDtypeStruct((blocks, block, features // 2), jnp.bfloat16),
-        ],
-        [
-            whole((blocks, GROUP_COLS + TOKEN_ROWS, block)),
-            whole((blocks, block, features // 2)),
-        ],
-        [],
-        2 * 10**8,
-        3 * 10**6,
-    )
-    early = lax.all_to_all(early, "seq", split_axis=0, concat_axis=0, tiled=True)
-    late = lax.all_to_all(late, "seq", split_axis=0, concat_axis=0, tiled=True)
-    start = group * GROUP_COLS
-    weights = jnp.concatenate(
-        [lax.dynamic_slice_in_dim(w, start, GROUP_COLS, 1) for w in (w_query, w_key, w_value)],
-        axis=1,
-    )
+    grad_out = cotangent[0]
     meta = jnp.concatenate(
         [
             lax.dynamic_slice_in_dim(window, group * GROUP_HEADS, GROUP_HEADS, 0),
             jnp.stack([side, group, core]).astype(jnp.int32),
         ]
     )
-    frequency = 10000.0 ** (-2.0 * jnp.arange(HALF, dtype=jnp.float32) / HEAD_DIM)
-    angles = frequency[:, None] * jnp.arange(length, dtype=jnp.int32).astype(jnp.float32)[None, :]
-    cosine = jnp.cos(angles)
-    sine_part = jnp.sin(angles)
+    cosine, sine_part = rope_table(length)
+
+    def call(body, operands, outs, scratch=(), steps=1, flops=10**8, moved=10**6, loose=0):
+        spaces = [whole(operand.shape) for operand in operands]
+        for index in range(loose):
+            spaces[-1 - index] = pl.BlockSpec(memory_space=pl.ANY)
+        if operands[0].ndim == 1:
+            spaces[0] = pl.BlockSpec(memory_space=pltpu.SMEM)
+        return pl.pallas_call(
+            body,
+            grid=(steps,),
+            in_specs=spaces,
+            out_specs=[whole(shape) for shape, _ in outs],
+            out_shape=[jax.ShapeDtypeStruct(shape, dtype) for shape, dtype in outs],
+            scratch_shapes=list(scratch),
+            compiler_params=pltpu.CompilerParams(
+                dimension_semantics=("arbitrary",), vmem_limit_bytes=VMEM_BYTES
+            ),
+            cost_estimate=pl.CostEstimate(flops=flops, bytes_accessed=moved, transcendentals=0),
+        )(*operands)
+
+    half = jnp.bfloat16
+    (early,) = call(
+        send_kernel,
+        (token_ids, grad_out, w_out),
+        [((blocks, GROUP_COLS + TOKEN_ROWS, block), half)],
+    )
+    early = lax.all_to_all(early, "seq", split_axis=0, concat_axis=0, tiled=True)
+    late, lookup, normed = call(
+        prepare_kernel,
+        (meta, grad_out, table, w_query, w_key, w_value),
+        [
+            ((blocks, block, features // 2), half),
+            ((2, 3 * GROUP_COLS, vocab), half),
+            ((vocab, features // 2), half),
+        ],
+        [pltpu.VMEM((features, vocab), jnp.float32)],
+        flops=10**9,
+        moved=5 * 10**6,
+    )
+    late = lax.all_to_all(late, "seq", split_axis=0, concat_axis=0, tiled=True)
     heads_shape = (GROUP_HEADS, HEAD_DIM, length)
     rows_shape = (GROUP_HEADS, length, 2 * HEAD_DIM)
-    rows_out = (GROUPS, 3 * GROUP_COLS, block)
-    sums_out = (2, 3 * GROUP_COLS, vocab // 2)
-    rows, sums, attended = kernel_call(
+    rows, sums, attended = call(
         attention_kernel,
-        GROUP_HEADS,
-        (meta, early, table, weights, cosine, sine_part),
+        (meta, early, lookup, cosine, sine_part),
         [
-            whole(early.shape),
-            whole(table.shape),
-            whole(weights.shape),
-            whole(cosine.shape),
-            whole(sine_part.shape),
+            ((GROUPS, 3 * GROUP_COLS, block), half),
+            ((2, 3 * GROUP_COLS, vocab // 2), half),
+            ((GROUP_COLS, length), half),
         ],
         [
-            jax.ShapeDtypeStruct(rows_out, jnp.bfloat16),
-            jax.ShapeDtypeStruct(sums_out, jnp.bfloat16),
-            jax.ShapeDtypeStruct((GROUP_COLS, length), jnp.bfloat16),
-        ],
-        [whole(rows_out), whole(sums_out), whole((GROUP_COLS, length))],
-        [
-            pltpu.VMEM(rows_shape, jnp.bfloat16),
-            pltpu.VMEM((GROUP_HEADS, 2 * HEAD_DIM, length), jnp.bfloat16),
-            pltpu.VMEM(heads_shape, jnp.bfloat16),
-            pltpu.VMEM(rows_shape, jnp.bfloat16),
-            pltpu.VMEM(heads_shape, jnp.bfloat16),
-            pltpu.VMEM(heads_shape, jnp.bfloat16),
-            pltpu.VMEM((vocab, length), jnp.bfloat16),
+            pltpu.VMEM(rows_shape, half),
+            pltpu.VMEM((GROUP_HEADS, 2 * HEAD_DIM, length), half),
+            pltpu.VMEM(heads_shape, half),
+            pltpu.VMEM(rows_shape, half),
+            pltpu.VMEM(heads_shape, half),
+            pltpu.VMEM(heads_shape, half),
+            pltpu.VMEM((vocab, length), half),
             pltpu.VMEM((HEAD_DIM, length), jnp.float32),
             pltpu.VMEM((length, 2 * HEAD_DIM), jnp.float32),
             pltpu.VMEM((length, 2 * HEAD_DIM), jnp.float32),
         ],
-        8 * 10**9,
-        8 * 10**6,
-    )
-    late = late.reshape(length, features // 2)
-    out_shape = (2, 3 * GROUP_COLS // 2, 128)
-    out_sums = kernel_call(
+        steps=GROUP_HEADS,
+        flops=8 * 10**9,
+        moved=8 * 10**6,
+    )
+    planes = [[2 * z + x for z in range(GROUPS)] for x in range(2)]
+
+    def over_plane(chunks):
+        return lax.all_to_all(
+            chunks, "seq", split_axis=0, concat_axis=0, axis_index_groups=planes, tiled=True
+        )
+
+    got_rows = over_plane(rows)
+    lanes = vocab // 2
+    out_rows = 3 * GROUP_COLS // 2
+    packed = 3 * GROUP_COLS + out_rows
+    keep, give = call(
         out_kernel,
-        1,
-        (attended, late),
-        [whole(attended.shape), whole(late.shape)],
-        jax.ShapeDtypeStruct(out_shape, jnp.bfloat16),
-        whole(out_shape),
-        [],
-        3 * 10**8,
-        2 * 10**6,
-    )
-
-    def over_dp(halves):
-        kept = lax.dynamic_index_in_dim(halves, core, 0, keepdims=False)
-        given = lax.dynamic_index_in_dim(halves, 1 - core, 0, keepdims=False)
-        kept = kept + swapped(given, "dp", 1)
-        return kept + swapped(kept, "dp", 2)
-
-    kept = over_dp(sums)
-    kept_out = over_dp(out_sums)
-    planes = [[2 * z + x for z in range(GROUPS)] for x in range(2)]
-    got_rows = lax.all_to_all(
-        rows, "seq", split_axis=0, concat_axis=0, axis_index_groups=planes, tiled=True
-    )
-    grad_input = kernel_call(
+        (meta, attended, late.reshape(length, features // 2), sums),
+        [((packed, lanes), half)] * 2,
+    )
+    here = keep + swapped(give, "dp", 1)
+    there = swapped(here, "dp", 2)
+    (chunks,) = call(
+        combine_kernel, (here, there, got_rows), [((GROUPS, out_rows, lanes), half)], loose=1
+    )
+    mine, other = call(
+        gather_kernel,
+        (meta, over_plane(chunks)),
+        [((GROUPS * GROUP_COLS, lanes), half), ((2 * out_rows, lanes), half)],
+    )
+    (grad_input,) = call(
         input_kernel,
-        1,
         (token_ids, table, w_query, w_key, w_value, got_rows),
+        [((block, features), half)],
+        flops=10**9,
+        moved=5 * 10**6,
+    )
+    last = blocks - 2
+    paired = swapped(mine, "dp", 1)
+    near = lax.ppermute(other, "seq", [(last, last + 1), (last + 1, last)])
+    far = lax.ppermute(
+        other,
+        ("dp", "seq"),
         [
-            whole(token_ids.shape),
-            whole(table.shape),
-            whole(w_query.shape),
-            whole(w_key.shape),
-            whole(w_value.shape),
-            whole(got_rows.shape),
+            (blocks * d + last + x, blocks * (d ^ 1) + last + 1 - x)
+            for d in range(lax.axis_size("dp"))
+            for x in range(2)
         ],
-        jax.ShapeDtypeStruct((block, features), jnp.bfloat16),
-        whole((block, features)),
-        [],
-        10**9,
-        5 * 10**6,
-    )
-    got = []
-    for turn in range(1, GROUPS):
-        route = [
-            (2 * z + x, 2 * ((z + turn) % GROUPS) + x)
-            for z in range(GROUPS)
-            for x in range(2)
-            if (z + turn) % GROUPS != 3
-        ]
-        target = jnp.minimum((group + turn) % GROUPS, 2)
-        piece = lax.dynamic_slice_in_dim(kept, target * GROUP_COLS, GROUP_COLS, 0)
-        got.append(lax.ppermute(piece, "seq", route))
-    for other in range(2):
-        for half in range(2):
-            route = [(2 * (2 * x + half) + (x ^ other), 6 + x) for x in range(2)]
-            route = [(s, t) for s, t in route if s != t]
-            got.append(lax.ppermute(kept_out, "seq", route))
-    pieces = kernel_call(
-        gather_kernel,
-        1,
-        (meta, kept, kept_out, *got),
-        [whole(kept.shape), whole(kept_out.shape)] + [whole(piece.shape) for piece in got],
-        jax.ShapeDtypeStruct((4 * kept_out.shape[0], kept.shape[1]), jnp.bfloat16),
-        whole((4 * kept_out.shape[0], kept.shape[1])),
-        [],
-        10**6,
-        10**6,
-    )
-    others = swapped(pieces, "dp", 1)
-    weight_grads = kernel_call(
+    )
+    (weight_grads,) = call(
         weight_kernel,
-        1,
-        (meta, table, pieces, others),
-        [whole(table.shape), whole(pieces.shape), whole(others.shape)],
-        jax.ShapeDtypeStruct((features // 2, features), jnp.float32),
-        whole((features // 2, features)),
-        [],
-        10**9,
-        5 * 10**6,
+        (meta, normed, mine, paired, near, far),
+        [((features // 2, features), jnp.float32)],
+        flops=10**9,
+        moved=5 * 10**6,
     )
     return (grad_input[None], weight_grads)
 

time: 92.7 us -> 90.5 us (0.976)
  the two profiles are of different devices: /device:TPU:0 before, /device:TPU:26 now
where the time goes in v3:
time: 90.5 us; the launch traced here: 89.8 us
  Pallas kernels  26.2 us (29%)
  starting transfers between devices  26 us (29%)
  waiting for transfers between devices  15.8 us (17%)
  blocking collectives  11.4 us (13%)
  local copies, waits for them, and re-layouts  8.79 us (10%)
    pallas_call x8, Pallas kernels, call(): pl.pallas_call(body, grid=(steps,), in_specs=spaces, out_specs=[whole(sha...  26.2 us
    all_to_all x1, blocking collectives, over_plane(): lax.all_to_all(chunks, 'seq', split_axis=0, concat_axis=0, axis_index_gro...  11.4 us
    unnamed x40, local copies, waits for them, and re-layouts  8.72 us
    all_to_all x1, waiting for transfers between devices, over_plane(): lax.all_to_all(chunks, 'seq', split_axis=0, concat_axis=0, axis_index_gro...  6.72 us
    all_to_all x1, starting transfers between devices, grouped_device(): late = lax.all_to_all(late, 'seq', split_axis=0, concat_axis=0, tiled=True)  6.5 us
    all_to_all x1, starting transfers between devices, grouped_device(): lax.all_to_all(early, 'seq', split_axis=0, concat_axis=0, tiled=True)  6 us
    all_to_all x1, starting transfers between devices, over_plane(): lax.all_to_all(chunks, 'seq', split_axis=0, concat_axis=0, axis_index_gro...  5.81 us
    all_to_all x1, waiting for transfers between devices, grouped_device(): lax.all_to_all(early, 'seq', split_axis=0, concat_axis=0, tiled=True)  4.01 us
  transfers between devices with their start and end apart: 8, of which 5 were waited for; matrix products, arithmetic and copies ran while one was open for 1% of the time, Pallas kernels for 24%

profile of v3, /device:TPU:26, one launch (start us, length us, event | category | flops | bytes accessed | tf_op | source)
XLA Modules:
  0.0 89.8 jit_solution(14703916402059850572)
XLA Ops:
  0.6 1.3 %copy-done.6 = bf16[768,768]{1,0:T(8,128)(2,1)S(1)} copy-done((bf16[768,768]{1,0:T(8,128)(2,1)S(1)}, bf16[768,768]{1,0:T(8,128)(2,1)}, u32[]{:S(2)}) %copy-start.6) | copy-done | bytes 1179672
  1.9 0.9 %copy-done.7 = bf16[1,128,768]{2,1,0:T(8,128)(2,1)S(1)} copy-done((bf16[1,128,768]{2,1,0:T(8,128)(2,1)S(1)}, bf16[1,128,768]{2,1,0:T(8,128)(2,1)}, u32[]{:S(2)}) %copy-start.7) | copy-done | bytes 196632
  3.5 1.2 %shard_map.113 = bf16[8,208,128]{2,1,0:T(8,128)(2,1)} custom-call(s32[1,128]{1,0:T(1,128)S(1)} %copy-done.11, bf16[128,768]{1,0:T(8,128)(2,1)S(1)} %bitcast.6, bf16[768,768]{1,0:T(8,128)(2,1)S(1)} %copy-done.6), custom_call_target="tpu_custom_call" | custom-call | flops 100000000 | bytes 1000000 | tf_op jit(solution)/shard_map/pallas_call | solution.py:603
  4.7 6.0 %all-to-all-start = ((bf16[8,208,128]{2,1,0:T(8,128)(2,1)}), bf16[8,208,128]{2,1,0:T(8,128)(2,1)S(1)}, u32[]{:S(2)}, u32[]{:S(2)}) async-start(bf16[8,208,128]{2,1,0:T(8,128)(2,1)} %shard_map.113), calls=%async_computation | async-start | bytes 851968 | tf_op jit(solution)/shard_map/all_to_all | solution.py:622
  10.9 1.3 %copy-done.2 = bf16[768,768]{1,0:T(8,128)(2,1)S(1)} copy-done((bf16[768,768]{1,0:T(8,128)(2,1)S(1)}, bf16[768,768]{1,0:T(8,128)(2,1)}, u32[]{:S(2)}) %copy-start.2) | copy-done | bytes 1179672
  12.2 1.0 %copy-done.4 = bf16[256,768]{1,0:T(8,128)(2,1)S(1)} copy-done((bf16[256,768]{1,0:T(8,128)(2,1)S(1)}, bf16[256,768]{1,0:T(8,128)(2,1)}, u32[]{:S(2)}) %copy-start.4) | copy-done | bytes 393240
  13.2 2.7 %shard_map.114 = (bf16[8,128,384]{2,1,0:T(8,128)(2,1)}, bf16[2,576,256]{2,1,0:T(8,128)(2,1)S(1)}, bf16[256,384]{1,0:T(8,128)(2,1)S(1)}) custom-call(s32[6]{0:T(128)S(1)} %pad_add_fusion.meta_ref, bf16[128,768]{1,0:T(8,128)(2,1)S(1)} %bitcast.7, bf16[256,768]{1,0:T(8,128)(2,1)S(1)} %copy-done.4, bf16[768,768]{1,0:T(8,128)(2,1)S(1)} %copy-done, ...), custom_call_target="tpu_custom_call" | custom-call | flops 1000000000 | bytes 5000000 | tf_op jit(solution)/shard_map/pallas_call | solution.py:603
  16.7 4.0 %all-to-all-done.early_ref = bf16[8,208,128]{2,1,0:T(8,128)(2,1)S(1)} async-done(((bf16[8,208,128]{2,1,0:T(8,128)(2,1)}), bf16[8,208,128]{2,1,0:T(8,128)(2,1)S(1)}, u32[]{:S(2)}, u32[]{:S(2)}) %all-to-all-start) | async-done | bytes 426016 | tf_op jit(solution)/shard_map/all_to_all | solution.py:622
  20.7 6.5 %all-to-all-start.2 = ((bf16[8,128,384]{2,1,0:T(8,128)(2,1)}), bf16[8,128,384]{2,1,0:T(8,128)(2,1)}, u32[]{:S(2)}, u32[]{:S(2)}) async-start(bf16[8,128,384]{2,1,0:T(8,128)(2,1)} %get-tuple-element.16), calls=%async_computation.2 | async-start | bytes 1572864 | tf_op jit(solution)/shard_map/all_to_all | solution.py:635
  27.3 1.1 %copy-done.14 = bf16[2,576,256]{2,1,0:T(8,128)(2,1)S(1)} copy-done((bf16[2,576,256]{2,1,0:T(8,128)(2,1)S(1)}, bf16[2,576,256]{2,1,0:T(8,128)(2,1)}, u32[]{:S(2)}) %copy-start.14) | copy-done | bytes 589848
  28.3 15.3 %shard_map.115 = (bf16[4,576,128]{2,1,0:T(8,128)(2,1)}, bf16[2,576,128]{2,1,0:T(8,128)(2,1)S(1)}, bf16[192,1024]{1,0:T(8,128)(2,1)S(1)}) custom-call(s32[6]{0:T(128)S(1)} %pad_add_fusion.meta_ref, bf16[8,208,128]{2,1,0:T(8,128)(2,1)S(1)} %all-to-all-done.early_ref, bf16[2,576,256]{2,1,0:T(8,128)(2,1)S(1)} %copy-done.14, f32[32,1024]{1,0:T(8,128)S(1)} %copy-done.18, ...), custom_call_target="tpu_custom_call" | custom-call | flops 8000000000 | bytes 8000000 | tf_op jit(solution)/shard_map/pallas_call | solution.py:603
  44.6 5.8 %all-to-all-start.1 = ((bf16[4,576,128]{2,1,0:T(8,128)(2,1)}), bf16[4,576,128]{2,1,0:T(8,128)(2,1)S(1)}, u32[]{:S(2)}, u32[]{:S(2)}) async-start(bf16[4,576,128]{2,1,0:T(8,128)(2,1)} %get-tuple-element.13), calls=%async_computation.1 | async-start | bytes 1179648 | tf_op jit(solution)/shard_map/all_to_all | solution.py:665
  50.4 1.0 %copy-done.10 = bf16[2,576,128]{2,1,0:T(8,128)(2,1)S(1)} copy-done((bf16[2,576,128]{2,1,0:T(8,128)(2,1)S(1)}, bf16[2,576,128]{2,1,0:T(8,128)(2,1)}, u32[]{:S(2)}) %copy-start.10) | copy-done | bytes 294936
  51.4 1.5 %shard_map.117 = (bf16[864,128]{1,0:T(8,128)(2,1)S(1)}, bf16[864,128]{1,0:T(8,128)(2,1)S(1)}) custom-call(s32[6]{0:T(128)S(1)} %pad_add_fusion.meta_ref, bf16[192,1024]{1,0:T(8,128)(2,1)S(1)} %get-tuple-element.15.attended_ref, bf16[1024,384]{1,0:T(8,128)(2,1)} %bitcast.5.cotangent_ref, bf16[2,576,128]{2,1,0:T(8,128)(2,1)S(1)} %copy-done.10), custom_call_target="tpu_custom_call" | custom-call | flops 100000000 | bytes 1000000 | tf_op jit(solution)/shard_map/pallas_call | solution.py:603
  53.0 1.5 %collective-permute-done = bf16[864,128]{1,0:T(8,128)(2,1)S(1)} collective-permute-done((bf16[864,128]{1,0:T(8,128)(2,1)S(1)}, bf16[864,128]{1,0:T(8,128)(2,1)S(1)}, u32[]{:S(2)}, u32[]{:S(2)}) %collective-permute-start) | collective-permute-done | bytes 221216 | tf_op jit(solution)/shard_map/ppermute | solution.py:565
  55.2 1.5 %collective-permute-start.1 = (bf16[864,128]{1,0:T(8,128)(2,1)}, bf16[864,128]{1,0:T(8,128)(2,1)}, u32[]{:S(2)}, u32[]{:S(2)}) collective-permute-start(bf16[864,128]{1,0:T(8,128)(2,1)} %add.17.here_ref), channel_id=1, source_target_pairs={{0,16},{8,24},{16,0},{24,8},{1,17},{9,25},{17,1},{25,9},{2,18},{10... | collective-permute-start | bytes 663560 | tf_op jit(solution)/shard_map/ppermute | solution.py:565
  56.7 6.7 %all-to-all-done.1.rows_ref.after_ref = bf16[4,576,128]{2,1,0:T(8,128)(2,1)S(1)} async-done(((bf16[4,576,128]{2,1,0:T(8,128)(2,1)}), bf16[4,576,128]{2,1,0:T(8,128)(2,1)S(1)}, u32[]{:S(2)}, u32[]{:S(2)}) %all-to-all-start.1) | async-done | bytes 589856 | tf_op jit(solution)/shard_map/all_to_all | solution.py:665
  63.4 1.2 %shard_map.118 = bf16[4,288,128]{2,1,0:T(8,128)(2,1)S(1)} custom-call(bf16[864,128]{1,0:T(8,128)(2,1)} %add.17.here_ref, bf16[864,128]{1,0:T(8,128)(2,1)} %collective-permute-done.1.there_ref, bf16[4,576,128]{2,1,0:T(8,128)(2,1)S(1)} %all-to-all-done.1.rows_ref.after_ref), custom_call_target="tpu_custom_call" | custom-call | flops 100000000 | bytes 1000000 | tf_op jit(solution)/shard_map/pallas_call | solution.py:603
  64.6 11.4 %all_to_all.20.got_ref = bf16[4,288,128]{2,1,0:T(8,128)(2,1)S(1)} all-to-all(bf16[4,288,128]{2,1,0:T(8,128)(2,1)S(1)} %shard_map.118), channel_id=1, replica_groups={{0,2,4,6},{1,3,5,7},{8,10,12,14},{9,11,13,15},{16,18,20,22},{17,19,21,2..., dimensions={0} | all-to-all | bytes 589824 | tf_op jit(solution)/shard_map/all_to_all | solution.py:665
  76.8 2.4 %collective-permute-start.4 = (bf16[576,128]{1,0:T(8,128)(2,1)S(1)}, bf16[576,128]{1,0:T(8,128)(2,1)S(1)}, u32[]{:S(2)}, u32[]{:S(2)}) collective-permute-start(bf16[576,128]{1,0:T(8,128)(2,1)S(1)} %get-tuple-element.21), channel_id=1, source_target_pairs={{6,15},{7,14},{14,7},{15,6},{22,31},{23,30},{30,23},{31,22}} | collective-permute-start | bytes 442376 | tf_op jit(solution)/shard_map/ppermute | solution.py:698
  79.2 3.6 %collective-permute-start.3 = (bf16[576,128]{1,0:T(8,128)(2,1)S(1)}, bf16[576,128]{1,0:T(8,128)(2,1)S(1)}, u32[]{:S(2)}, u32[]{:S(2)}) collective-permute-start(bf16[576,128]{1,0:T(8,128)(2,1)S(1)} %get-tuple-element.21), channel_id=1, source_target_pairs={{6,7},{7,6},{14,15},{15,14},{22,23},{23,22},{30,31},{31,30}} | collective-permute-start | bytes 442376 | tf_op jit(solution)/shard_map/ppermute | solution.py:697
  82.9 1.9 %shard_map.116 = bf16[128,768]{1,0:T(8,128)(2,1)} custom-call(s32[1,128]{1,0:T(1,128)S(1)} %copy-done.12, bf16[256,768]{1,0:T(8,128)(2,1)S(1)} %copy-done.5, bf16[768,768]{1,0:T(8,128)(2,1)S(1)} %copy-done, bf16[768,768]{1,0:T(8,128)(2,1)S(1)} %copy-done.1, bf16[768,768]{1,0:T(8,128)(2,1)S(1)} %copy-done.3, ...), custom_call_target="tpu_custom_call" | custom-call | flops 1000000000 | bytes 5000000 | tf_op jit(solution)/shard_map/pallas_call | solution.py:603
  84.8 3.3 %collective-permute-done.3.near_ref = bf16[576,128]{1,0:T(8,128)(2,1)S(1)} collective-permute-done((bf16[576,128]{1,0:T(8,128)(2,1)S(1)}, bf16[576,128]{1,0:T(8,128)(2,1)S(1)}, u32[]{:S(2)}, u32[]{:S(2)}) %collective-permute-start.3) | collective-permute-done | bytes 147488 | tf_op jit(solution)/shard_map/ppermute | solution.py:697
  88.1 1.7 %shard_map.120 = f32[384,768]{1,0:T(8,128)} custom-call(s32[6]{0:T(128)S(1)} %pad_add_fusion.meta_ref, bf16[256,384]{1,0:T(8,128)(2,1)S(1)} %copy-done.16, bf16[768,128]{1,0:T(8,128)(2,1)S(1)} %get-tuple-element.20.mine_ref, bf16[768,128]{1,0:T(8,128)(2,1)S(1)} %collective-permute-done.2.other_ref, bf16[576,128]{1,0:T(8,128)(2,1)S(1)} %collective-permute-done.3.near_ref, ...), custom_call_target="tpu_custom_call" | custom-call | flops 1000000000 | bytes 5000000 | tf_op jit(solution)/shard_map/pallas_call | solution.py:603
  (44 shorter events, 4.2 us)
Async XLA Ops:
  0.6 1.3 %copy-start.6 = (bf16[768,768]{1,0:T(8,128)(2,1)S(1)}, bf16[768,768]{1,0:T(8,128)(2,1)}, u32[]{:S(2)}) copy-start(bf16[768,768]{1,0:T(8,128)(2,1)} %out_weights_ref.1) | copy-start | bytes 3538948
  3.5 7.2 %copy-start.19 = (s32[12]{0:T(128)S(1)}, s32[12]{0:T(128)}, u32[]{:S(2)}) copy-start(s32[12]{0:T(128)} %param.17) | copy-start | bytes 148
  3.5 7.4 %copy-start = (bf16[768,768]{1,0:T(8,128)(2,1)S(1)}, bf16[768,768]{1,0:T(8,128)(2,1)}, u32[]{:S(2)}) copy-start(bf16[768,768]{1,0:T(8,128)(2,1)} %query_ref.3) | copy-start | bytes 3538948
  3.5 7.4 %copy-start.1 = (bf16[768,768]{1,0:T(8,128)(2,1)S(1)}, bf16[768,768]{1,0:T(8,128)(2,1)}, u32[]{:S(2)}) copy-start(bf16[768,768]{1,0:T(8,128)(2,1)} %key_ref.3) | copy-start | bytes 3538948
  3.5 7.4 %copy-start.8 = (bf16[1,128,768]{2,1,0:T(8,128)(2,1)S(1)}, bf16[1,128,768]{2,1,0:T(8,128)(2,1)}, u32[]{:S(2)}) copy-start(bf16[1,128,768]{2,1,0:T(8,128)(2,1)} %param.11) | copy-start | bytes 589828
  4.7 16.0 %all-to-all-start = ((bf16[8,208,128]{2,1,0:T(8,128)(2,1)}), bf16[8,208,128]{2,1,0:T(8,128)(2,1)S(1)}, u32[]{:S(2)}, u32[]{:S(2)}) async-start(bf16[8,208,128]{2,1,0:T(8,128)(2,1)} %shard_map.113), calls=%async_computation | async-start | bytes 851968 | tf_op jit(solution)/shard_map/all_to_all | solution.py:622
  10.9 1.3 %copy-start.2 = (bf16[768,768]{1,0:T(8,128)(2,1)S(1)}, bf16[768,768]{1,0:T(8,128)(2,1)}, u32[]{:S(2)}) copy-start(bf16[768,768]{1,0:T(8,128)(2,1)} %value_ref.3) | copy-start | bytes 3538948
  12.2 1.0 %copy-start.4 = (bf16[256,768]{1,0:T(8,128)(2,1)S(1)}, bf16[256,768]{1,0:T(8,128)(2,1)}, u32[]{:S(2)}) copy-start(bf16[256,768]{1,0:T(8,128)(2,1)} %table_ref.3) | copy-start | bytes 1179652
  16.7 10.5 %copy-start.15 = (bf16[256,384]{1,0:T(8,128)(2,1)}, bf16[256,384]{1,0:T(8,128)(2,1)S(1)}, u32[]{:S(2)}) copy-start(bf16[256,384]{1,0:T(8,128)(2,1)S(1)} %get-tuple-element.14.normed_ref) | copy-start | bytes 589828
  16.7 10.5 %copy-start.17 = (f32[32,1024]{1,0:T(8,128)S(1)}, f32[32,1024]{1,0:T(8,128)}, u32[]{:S(2)}) copy-start(f32[32,1024]{1,0:T(8,128)} %constant.46.clone.sine_ref) | copy-start | bytes 393220
  16.7 10.5 %copy-start.18 = (f32[32,1024]{1,0:T(8,128)S(1)}, f32[32,1024]{1,0:T(8,128)}, u32[]{:S(2)}) copy-start(f32[32,1024]{1,0:T(8,128)} %constant.45.clone.cosine_ref) | copy-start | bytes 393220
  20.7 23.9 %all-to-all-start.2 = ((bf16[8,128,384]{2,1,0:T(8,128)(2,1)}), bf16[8,128,384]{2,1,0:T(8,128)(2,1)}, u32[]{:S(2)}, u32[]{:S(2)}) async-start(bf16[8,128,384]{2,1,0:T(8,128)(2,1)} %get-tuple-element.16), calls=%async_computation.2 | async-start | bytes 1572864 | tf_op jit(solution)/shard_map/all_to_all | solution.py:635
  27.3 1.1 %copy-start.14 = (bf16[2,576,256]{2,1,0:T(8,128)(2,1)S(1)}, bf16[2,576,256]{2,1,0:T(8,128)(2,1)}, u32[]{:S(2)}) copy-start(bf16[2,576,256]{2,1,0:T(8,128)(2,1)} %copy-done.13) | copy-start | bytes 1769476
  44.6 18.8 %all-to-all-start.1 = ((bf16[4,576,128]{2,1,0:T(8,128)(2,1)}), bf16[4,576,128]{2,1,0:T(8,128)(2,1)S(1)}, u32[]{:S(2)}, u32[]{:S(2)}) async-start(bf16[4,576,128]{2,1,0:T(8,128)(2,1)} %get-tuple-element.13), calls=%async_computation.1 | async-start | bytes 1179648 | tf_op jit(solution)/shard_map/all_to_all | solution.py:665
  50.4 1.0 %copy-start.10 = (bf16[2,576,128]{2,1,0:T(8,128)(2,1)S(1)}, bf16[2,576,128]{2,1,0:T(8,128)(2,1)}, u32[]{:S(2)}) copy-start(bf16[2,576,128]{2,1,0:T(8,128)(2,1)} %copy-done.9) | copy-start | bytes 884740
  52.9 1.5 %collective-permute-start = (bf16[864,128]{1,0:T(8,128)(2,1)S(1)}, bf16[864,128]{1,0:T(8,128)(2,1)S(1)}, u32[]{:S(2)}, u32[]{:S(2)}) collective-permute-start(bf16[864,128]{1,0:T(8,128)(2,1)S(1)} %get-tuple-element.19), channel_id=1, source_target_pairs={{0,8},{8,0},{16,24},{24,16},{1,9},{9,1},{17,25},{25,17},{2,10},{10... | collective-permute-start | bytes 663560 | tf_op jit(solution)/shard_map/ppermute | solution.py:565
  55.2 27.6 %copy-start.5 = (bf16[256,768]{1,0:T(8,128)(2,1)S(1)}, bf16[256,768]{1,0:T(8,128)(2,1)}, u32[]{:S(2)}) copy-start(bf16[256,768]{1,0:T(8,128)(2,1)} %table_ref.3) | copy-start | bytes 1179652
  55.2 27.7 %copy-start.12 = (s32[1,128]{1,0:T(1,128)S(1)}, s32[1,128]{1,0:T(1,128)}, u32[]{:S(2)}) copy-start(s32[1,128]{1,0:T(1,128)} %tokens_ref.3) | copy-start | bytes 1540
  55.2 8.2 %collective-permute-start.1 = (bf16[864,128]{1,0:T(8,128)(2,1)}, bf16[864,128]{1,0:T(8,128)(2,1)}, u32[]{:S(2)}, u32[]{:S(2)}) collective-permute-start(bf16[864,128]{1,0:T(8,128)(2,1)} %add.17.here_ref), channel_id=1, source_target_pairs={{0,16},{8,24},{16,0},{24,8},{1,17},{9,25},{17,1},{25,9},{2,18},{10... | collective-permute-start | bytes 663560 | tf_op jit(solution)/shard_map/ppermute | solution.py:565
  63.4 19.4 %copy-start.3 = (bf16[768,768]{1,0:T(8,128)(2,1)S(1)}, bf16[768,768]{1,0:T(8,128)(2,1)}, u32[]{:S(2)}) copy-start(bf16[768,768]{1,0:T(8,128)(2,1)} %value_ref.3) | copy-start | bytes 3538948
  76.7 11.4 %collective-permute-start.2 = (bf16[768,128]{1,0:T(8,128)(2,1)S(1)}, bf16[768,128]{1,0:T(8,128)(2,1)S(1)}, u32[]{:S(2)}, u32[]{:S(2)}) collective-permute-start(bf16[768,128]{1,0:T(8,128)(2,1)S(1)} %get-tuple-element.20.mine_ref), channel_id=1, source_target_pairs={{0,8},{8,0},{16,24},{24,16},{1,9},{9,1},{17,25},{25,17},{2,10},{10... | collective-permute-start | bytes 589832 | tf_op jit(solution)/shard_map/ppermute | solution.py:565
  76.8 11.3 %copy-start.16 = (bf16[256,384]{1,0:T(8,128)(2,1)S(1)}, bf16[256,384]{1,0:T(8,128)(2,1)}, u32[]{:S(2)}) copy-start(bf16[256,384]{1,0:T(8,128)(2,1)} %copy-done.15) | copy-start | bytes 589828
  76.8 8.1 %collective-permute-start.4 = (bf16[576,128]{1,0:T(8,128)(2,1)S(1)}, bf16[576,128]{1,0:T(8,128)(2,1)S(1)}, u32[]{:S(2)}, u32[]{:S(2)}) collective-permute-start(bf16[576,128]{1,0:T(8,128)(2,1)S(1)} %get-tuple-element.21), channel_id=1, source_target_pairs={{6,15},{7,14},{14,7},{15,6},{22,31},{23,30},{30,23},{31,22}} | collective-permute-start | bytes 442376 | tf_op jit(solution)/shard_map/ppermute | solution.py:698
  79.2 8.9 %collective-permute-start.3 = (bf16[576,128]{1,0:T(8,128)(2,1)S(1)}, bf16[576,128]{1,0:T(8,128)(2,1)S(1)}, u32[]{:S(2)}, u32[]{:S(2)}) collective-permute-start(bf16[576,128]{1,0:T(8,128)(2,1)S(1)} %get-tuple-element.21), channel_id=1, source_target_pairs={{6,7},{7,6},{14,15},{15,14},{22,23},{23,22},{30,31},{31,30}} | collective-permute-start | bytes 442376 | tf_op jit(solution)/shard_map/ppermute | solution.py:697
  (4 other events, 3.1 us)

commit v4 on v3

--- a/solution.py
+++ b/solution.py
@@ -247,18 +247,19 @@
     return (rows == tokens).astype(jnp.float32).astype(jnp.bfloat16)
 
 
-def send_kernel(tokens_ref, cotangent_ref, out_weights_ref, early_ref):
+def send_kernel(meta_ref, tokens_ref, cotangent_ref, out_weights_ref, *out_refs):
+    early_refs, grads_ref = out_refs[:-1], out_refs[-1]
     grad_att = ndot(out_weights_ref[...], cotangent_ref[...]).astype(jnp.bfloat16)
+    grads_ref[...] = grad_att
     block = tokens_ref.shape[1]
     tokens = jnp.broadcast_to(tokens_ref[...].astype(jnp.float32), (TOKEN_ROWS, block)).astype(
         jnp.bfloat16
     )
-    for target in range(2 * GROUPS):
-        group = target // 2
-        early_ref[target, :GROUP_COLS, :] = grad_att[
-            group * GROUP_COLS : (group + 1) * GROUP_COLS
-        ]
-        early_ref[target, GROUP_COLS:, :] = tokens
+    for turn, early_ref in enumerate(early_refs):
+        group = meta_ref[GROUP_HEADS + 1] ^ turn
+        place = pl.ds(pl.multiple_of(group * GROUP_COLS, GROUP_COLS), GROUP_COLS)
+        early_ref[:GROUP_COLS, :] = grads_ref[place, :]
+        early_ref[GROUP_COLS:, :] = tokens
 
 
 def prepare_kernel(
@@ -268,18 +269,20 @@
     query_ref,
     key_ref,
     value_ref,
-    late_ref,
+    keep_ref,
+    give_ref,
     lookup_ref,
     normed_ref,
     columns_ref,
 ):
-    columns = late_ref.shape[2]
-    for target in range(2 * GROUPS):
-        side = target % 2
-        late_ref[target] = cotangent_ref[:, side * columns : (side + 1) * columns]
+    first = meta_ref[GROUP_HEADS] == 0
+    columns = keep_ref.shape[1]
+    left = cotangent_ref[:, :columns]
+    right = cotangent_ref[:, columns:]
+    keep_ref[...] = jnp.where(first, left, right)
+    give_ref[...] = jnp.where(first, right, left)
     normed = normed_table(table_ref)
-    half = normed.shape[1] // 2
-    normed_ref[...] = jnp.where(meta_ref[GROUP_HEADS] == 0, normed[:, :half], normed[:, half:])
+    normed_ref[...] = jnp.where(first, normed[:, :columns], normed[:, columns:])
     place = pl.ds(pl.multiple_of(meta_ref[GROUP_HEADS + 1] * GROUP_COLS, GROUP_COLS), GROUP_COLS)
     for matrix, weights_ref in enumerate((query_ref, key_ref, value_ref)):
         columns_ref[...] = jnp.dot(
@@ -292,12 +295,30 @@
         lookup_ref[1, rows, :] = (mine - upper.astype(jnp.float32)).astype(jnp.bfloat16)
 
 
+def pair_kernel(meta_ref, keep_ref, got_ref, out_ref):
+    first = meta_ref[GROUP_HEADS] == 0
+    rows = keep_ref.shape[0]
+    out_ref[:rows, :] = jnp.where(first, keep_ref[...], got_ref[...])
+    out_ref[rows:, :] = jnp.where(first, got_ref[...], keep_ref[...])
+
+
 def attention_kernel(
     meta_ref,
-    early_ref,
     lookup_ref,
     cosine_ref,
     sine_ref,
+    *rest,
+):
+    early_refs = rest[: 2 * GROUPS]
+    attention_body(meta_ref, lookup_ref, cosine_ref, sine_ref, early_refs, *rest[2 * GROUPS :])
+
+
+def attention_body(
+    meta_ref,
+    lookup_ref,
+    cosine_ref,
+    sine_ref,
+    early_refs,
     rows_ref,
     sums_ref,
     attended_ref,
@@ -313,8 +334,8 @@
     grad_value_ref,
 ):
     head = pl.program_id(0)
-    blocks, _, block = early_ref.shape
-    length = blocks * block
+    block = early_refs[0].shape[1]
+    length = len(early_refs) * block
     vocab = lookup_ref.shape[2]
     half_vocab = vocab // 2
     cosine = cosine_ref[...]
@@ -323,12 +344,13 @@
 
     @pl.when(head == 0)
     def _():
-        for source in range(blocks):
-            lanes = slice(source * block, (source + 1) * block)
-            tokens = early_ref[source, GROUP_COLS : GROUP_COLS + TOKEN_ROWS, :]
+        own = 2 * meta_ref[GROUP_HEADS + 1] + meta_ref[GROUP_HEADS]
+        for turn, early_ref in enumerate(early_refs):
+            lanes = pl.ds(pl.multiple_of((own ^ turn) * block, block), block)
+            tokens = early_ref[GROUP_COLS : GROUP_COLS + TOKEN_ROWS, :]
             tokens = tokens.astype(jnp.float32)[:1].astype(jnp.int32)
             onehot_ref[:, lanes] = onehot_columns(tokens, vocab)
-            grad_att_ref[:, :, lanes] = early_ref[source, :GROUP_COLS, :].reshape(
+            grad_att_ref[:, :, lanes] = early_ref[:GROUP_COLS, :].reshape(
                 GROUP_HEADS, HEAD_DIM, block
             )
         onehot = onehot_ref[...]
@@ -445,8 +467,19 @@
             rows_ref[target, place, :] = jnp.where(meta_ref[GROUP_HEADS] == 0, even, odd)
 
 
-def out_kernel(meta_ref, attended_ref, cotangent_ref, sums_ref, keep_ref, give_ref):
-    total = jnp.dot(attended_ref[...], cotangent_ref[...], preferred_element_type=jnp.float32)
+def out_kernel(
+    meta_ref, attended_ref, c0_ref, c1_ref, c2_ref, c3_ref, sums_ref, keep_ref, give_ref
+):
+    span = c0_ref.shape[0]
+    total = None
+    for turn, rows_ref in enumerate((c0_ref, c1_ref, c2_ref, c3_ref)):
+        source = meta_ref[GROUP_HEADS + 1] ^ turn
+        part = jnp.dot(
+            attended_ref[:, pl.ds(pl.multiple_of(source * span, span), span)],
+            rows_ref[...],
+            preferred_element_type=jnp.float32,
+        )
+        total = part if total is None else total + part
     rows = total.shape[0] // 2
     base = sums_ref.shape[1]
     lanes = keep_ref.shape[1]
@@ -460,37 +493,36 @@
         give_ref[place, :] = jnp.where(first, part[rows:], part[:rows]).astype(jnp.bfloat16)
 
 
-def combine_kernel(here_ref, there_ref, after_ref, out_ref):
+def combine_kernel(meta_ref, here_ref, there_ref, after_ref, out_ref, *piece_refs):
     del after_ref
     rows = GROUP_COLS
-    size = out_ref.shape[1]
-    blank = jnp.zeros((size - rows, out_ref.shape[2]), jnp.bfloat16)
-    for matrix in range(3):
-        place = slice(matrix * rows, (matrix + 1) * rows)
-        out_ref[matrix, :rows, :] = here_ref[place, :] + there_ref[place, :]
-        out_ref[matrix, rows:, :] = blank
-    out_ref[3] = here_ref[3 * rows :, :] + there_ref[3 * rows :, :]
-
-
-def gather_kernel(meta_ref, got_ref, mine_ref, other_ref):
+    out_ref[...] = here_ref[3 * rows :, :] + there_ref[3 * rows :, :]
+    for turn, piece_ref in enumerate(piece_refs):
+        target = jnp.minimum(meta_ref[GROUP_HEADS + 1] ^ turn, 2)
+        place = pl.ds(pl.multiple_of(target * rows, rows), rows)
+        piece_ref[...] = here_ref[place, :] + there_ref[place, :]
+
+
+def gather_kernel(meta_ref, s0, s1, s2, s3, own_ref, o0, o1, o2, o3, mine_ref):
     rows = GROUP_COLS
-    size = got_ref.shape[1]
-
-    @pl.when(meta_ref[GROUP_HEADS + 1] < 3)
+    group = meta_ref[GROUP_HEADS + 1]
+
+    @pl.when(group < 3)
     def _():
-        for group in range(GROUPS):
-            mine_ref[group * rows : (group + 1) * rows, :] = got_ref[group, :rows, :]
-        other_ref[...] = jnp.zeros_like(other_ref)
-
-    @pl.when(meta_ref[GROUP_HEADS + 1] == 3)
+        for turn, got in enumerate((s0, s1, s2, s3)):
+            source = group ^ turn
+            mine_ref[pl.ds(pl.multiple_of(source * rows, rows), rows), :] = got[...]
+        tail = mine_ref.shape[0] - GROUPS * rows
+        mine_ref[GROUPS * rows :, :] = jnp.zeros((tail, mine_ref.shape[1]), jnp.bfloat16)
+
+    @pl.when(group == 3)
     def _():
-        first = meta_ref[GROUP_HEADS] == 0
-        for part in range(2):
-            place = slice(part * size, (part + 1) * size)
-            mine_ref[place, :] = jnp.where(first, got_ref[part], got_ref[2 + part])
-            other_ref[place, :] = jnp.where(first, got_ref[2 + part], got_ref[part])
-        tail = mine_ref.shape[0] - 2 * size
-        mine_ref[2 * size :, :] = jnp.zeros((tail, mine_ref.shape[1]), jnp.bfloat16)
+        size = own_ref.shape[0]
+        own = meta_ref[GROUP_HEADS] == 1
+        mine_ref[0:size, :] = o0[...]
+        mine_ref[size : 2 * size, :] = o1[...]
+        mine_ref[2 * size : 3 * size, :] = jnp.where(own, own_ref[...], o2[...])
+        mine_ref[3 * size :, :] = o3[...]
 
 
 def input_kernel(tokens_ref, table_ref, query_ref, key_ref, value_ref, rows_ref, out_ref):
@@ -515,7 +547,7 @@
     ).astype(jnp.bfloat16)
 
 
-def weight_kernel(meta_ref, normed_ref, mine_ref, other_ref, near_ref, far_ref, out_ref):
+def weight_kernel(meta_ref, normed_ref, mine_ref, other_ref, out_ref):
     half_vocab = mine_ref.shape[1]
     first_core = meta_ref[GROUP_HEADS + 2] == 0
 
@@ -529,7 +561,7 @@
         for part, sums_ref in ((upper, mine_ref), (lower, other_ref)):
             term = lax.dot_general(
                 part,
-                sums_ref[...],
+                sums_ref[: GROUPS * GROUP_COLS, :],
                 (((0,), (1,)), ((), ())),
                 preferred_element_type=jnp.float32,
             )
@@ -542,14 +574,16 @@
         first_side = meta_ref[GROUP_HEADS] == 0
         for half in range(2):
             for chunk in range(3):
-                place = slice((half * 3 + chunk) * rows, (half * 3 + chunk + 1) * rows)
                 for core in range(2):
                     same = first_core == (core == 0)
-                    own = jnp.where(same, mine_ref[place, :], other_ref[place, :])
-                    crossed = jnp.where(same, near_ref[place, :], far_ref[place, :])
+                    planes = []
+                    for plane in range(2):
+                        start = ((2 * half + plane) * 3 + chunk) * rows
+                        place = slice(start, start + rows)
+                        planes.append(jnp.where(same, mine_ref[place, :], other_ref[place, :]))
                     row = half * GROUP_COLS + core * rows
                     for side in range(2):
-                        value = jnp.where(first_side == (side == 0), own, crossed)
+                        value = jnp.where(first_side, planes[side], planes[1 - side])
                         start = (side * 3 + chunk) * half_vocab
                         out_ref[row : row + rows, start : start + half_vocab] = value.astype(
                             jnp.float32
@@ -594,7 +628,9 @@
     )
     cosine, sine_part = rope_table(length)
 
-    def call(body, operands, outs, scratch=(), steps=1, flops=10**8, moved=10**6, loose=0):
+    def call(
+        body, operands, outs, scratch=(), steps=1, flops=10**8, moved=10**6, loose=0, grant=VMEM_BYTES
+    ):
         spaces = [whole(operand.shape) for operand in operands]
         for index in range(loose):
             spaces[-1 - index] = pl.BlockSpec(memory_space=pl.ANY)
@@ -608,23 +644,28 @@
             out_shape=[jax.ShapeDtypeStruct(shape, dtype) for shape, dtype in outs],
             scratch_shapes=list(scratch),
             compiler_params=pltpu.CompilerParams(
-                dimension_semantics=("arbitrary",), vmem_limit_bytes=VMEM_BYTES
+                dimension_semantics=("arbitrary",), vmem_limit_bytes=grant
             ),
             cost_estimate=pl.CostEstimate(flops=flops, bytes_accessed=moved, transcendentals=0),
         )(*operands)
 
     half = jnp.bfloat16
-    (early,) = call(
+    sent = call(
         send_kernel,
-        (token_ids, grad_out, w_out),
-        [((blocks, GROUP_COLS + TOKEN_ROWS, block), half)],
-    )
-    early = lax.all_to_all(early, "seq", split_axis=0, concat_axis=0, tiled=True)
-    late, lookup, normed = call(
+        (meta, token_ids, grad_out, w_out),
+        [((GROUP_COLS + TOKEN_ROWS, block), half)] * GROUPS,
+        [pltpu.VMEM((features, block), half)],
+        grant=60 * 1024 * 1024,
+    )
+    early = [sent[0]] + [None] * (blocks - 1)
+    for turn in (4, 6, 5, 7, 2, 3, 1):
+        early[turn] = swapped(sent[turn // 2], "seq", turn)
+    keep, give, lookup, normed = call(
         prepare_kernel,
         (meta, grad_out, table, w_query, w_key, w_value),
         [
-            ((blocks, block, features // 2), half),
+            ((block, features // 2), half),
+            ((block, features // 2), half),
             ((2, 3 * GROUP_COLS, vocab), half),
             ((vocab, features // 2), half),
         ],
@@ -632,12 +673,15 @@
         flops=10**9,
         moved=5 * 10**6,
     )
-    late = lax.all_to_all(late, "seq", split_axis=0, concat_axis=0, tiled=True)
+    (late,) = call(
+        pair_kernel, (meta, keep, swapped(give, "seq", 1)), [((2 * block, features // 2), half)]
+    )
+    lates = [late] + [swapped(late, "seq", 2 * turn) for turn in range(1, GROUPS)]
     heads_shape = (GROUP_HEADS, HEAD_DIM, length)
     rows_shape = (GROUP_HEADS, length, 2 * HEAD_DIM)
     rows, sums, attended = call(
         attention_kernel,
-        (meta, early, lookup, cosine, sine_part),
+        (meta, lookup, cosine, sine_part, *early),
         [
             ((GROUPS, 3 * GROUP_COLS, block), half),
             ((2, 3 * GROUP_COLS, vocab // 2), half),
@@ -672,18 +716,29 @@
     packed = 3 * GROUP_COLS + out_rows
     keep, give = call(
         out_kernel,
-        (meta, attended, late.reshape(length, features // 2), sums),
+        (meta, attended, *lates, sums),
         [((packed, lanes), half)] * 2,
     )
     here = keep + swapped(give, "dp", 1)
     there = swapped(here, "dp", 2)
-    (chunks,) = call(
-        combine_kernel, (here, there, got_rows), [((GROUPS, out_rows, lanes), half)], loose=1
-    )
-    mine, other = call(
-        gather_kernel,
-        (meta, over_plane(chunks)),
-        [((GROUPS * GROUP_COLS, lanes), half), ((2 * out_rows, lanes), half)],
+    kept_out, *pieces = call(
+        combine_kernel,
+        (meta, here, there, got_rows),
+        [((out_rows, lanes), half)] + [((GROUP_COLS, lanes), half)] * GROUPS,
+        loose=1,
+    )
+    got = [pieces[0]]
+    for turn in range(1, GROUPS):
+        route = [(i, i ^ (2 * turn)) for i in range(blocks) if (i ^ (2 * turn)) < blocks - 2]
+        got.append(lax.ppermute(pieces[turn], "seq", route))
+    got_out = []
+    for part in range(2):
+        for other in range(2):
+            route = [(2 * (2 * x + part) + (x ^ other), blocks - 2 + x) for x in range(2)]
+            route = [(s, t) for s, t in route if s != t]
+            got_out.append(lax.ppermute(kept_out, "seq", route))
+    (mine,) = call(
+        gather_kernel, (meta, *got, kept_out, *got_out), [((4 * out_rows, lanes), half)]
     )
     (grad_input,) = call(
         input_kernel,
@@ -692,21 +747,9 @@
         flops=10**9,
         moved=5 * 10**6,
     )
-    last = blocks - 2
-    paired = swapped(mine, "dp", 1)
-    near = lax.ppermute(other, "seq", [(last, last + 1), (last + 1, last)])
-    far = lax.ppermute(
-        other,
-        ("dp", "seq"),
-        [
-            (blocks * d + last + x, blocks * (d ^ 1) + last + 1 - x)
-            for d in range(lax.axis_size("dp"))
-            for x in range(2)
-        ],
-    )
     (weight_grads,) = call(
         weight_kernel,
-        (meta, normed, mine, paired, near, far),
+        (meta, normed, mine, swapped(mine, "dp", 1)),
         [((features // 2, features), jnp.float32)],
         flops=10**9,
         moved=5 * 10**6,

time: 90.5 us -> 112 us (1.24)
  the two profiles are of different devices: /device:TPU:26 before, /device:TPU:0 now
where the time goes in v4:
time: 112 us
  waiting for transfers between devices  38.9 us (35%)
  starting transfers between devices  37.1 us (33%)
  Pallas kernels  26.5 us (24%)
  local copies, waits for them, and re-layouts  7.64 us (7%)
    ppermute x14, waiting for transfers between devices, swapped(): return lax.ppermute(block, axis, route)  32.4 us
    pallas_call x9, Pallas kernels, call(): pl.pallas_call(body, grid=(steps,), in_specs=spaces, out_specs=[whole(sha...  26.5 us
    ppermute x14, starting transfers between devices, swapped(): return lax.ppermute(block, axis, route)  20.2 us
    ppermute x4, starting transfers between devices, grouped_device(): got_out.append(lax.ppermute(kept_out, 'seq', route))  8.26 us
    unnamed x34, local copies, waits for them, and re-layouts  6.81 us
    ppermute x3, waiting for transfers between devices, grouped_device(): got.append(lax.ppermute(pieces[turn], 'seq', route))  6.49 us
    ppermute x3, starting transfers between devices, grouped_device(): got.append(lax.ppermute(pieces[turn], 'seq', route))  5.13 us
    all_to_all x1, starting transfers between devices, over_plane(): lax.all_to_all(chunks, 'seq', split_axis=0, concat_axis=0, axis_index_gro...  3.57 us
  transfers between devices with their start and end apart: 22, of which 7 were waited for; matrix products, arithmetic and copies ran while one was open for 0% of the time, Pallas kernels for 5%

profile of v4, /device:TPU:0, one launch (start us, length us, event | category | flops | bytes accessed | tf_op | source)
XLA Modules:
  0.0 111.8 jit_solution(11032913270567151645)
XLA Ops:
  2.2 2.6 %shard_map.114 = (bf16[208,128]{1,0:T(8,128)(2,1)}, bf16[208,128]{1,0:T(8,128)(2,1)}, bf16[208,128]{1,0:T(8,128)(2,1)}, bf16[208,128]{1,0:T(8,128)(2,1)}) custom-call(s32[6]{0:T(128)} %pad_add_fusion.meta_ref, s32[1,128]{1,0:T(1,128)} %tokens_ref.3, bf16[128,768]{1,0:T(8,128)(2,1)} %bitcast.5, bf16[768,768]{1,0:T(8,128)(2,1)} %out_weights_ref.1), custom_call_target="tpu_custom_call" | custom-call | flops 100000000 | bytes 1000000 | tf_op jit(solution)/shard_map/pallas_call | solution.py:639
  4.7 2.9 %collective-permute-start = (bf16[208,128]{1,0:T(8,128)(2,1)}, bf16[208,128]{1,0:T(8,128)(2,1)S(1)}, u32[]{:S(2)}, u32[]{:S(2)}) collective-permute-start(bf16[208,128]{1,0:T(8,128)(2,1)} %get-tuple-element.21.rest_0_), channel_id=1, source_target_pairs={{0,1},{1,0},{2,3},{3,2},{4,5},{5,4},{6,7},{7,6},{8,9},{9,8},{10,11... | collective-permute-start | bytes 159752 | tf_op jit(solution)/shard_map/ppermute | solution.py:599
  7.7 1.6 %collective-permute-start.1 = (bf16[208,128]{1,0:T(8,128)(2,1)}, bf16[208,128]{1,0:T(8,128)(2,1)S(1)}, u32[]{:S(2)}, u32[]{:S(2)}) collective-permute-start(bf16[208,128]{1,0:T(8,128)(2,1)} %get-tuple-element.22), channel_id=1, source_target_pairs={{0,2},{1,3},{2,0},{3,1},{4,6},{5,7},{6,4},{7,5},{8,10},{9,11},{10,... | collective-permute-start | bytes 159752 | tf_op jit(solution)/shard_map/ppermute | solution.py:599
  9.2 3.0 %collective-permute-start.3 = (bf16[208,128]{1,0:T(8,128)(2,1)}, bf16[208,128]{1,0:T(8,128)(2,1)S(1)}, u32[]{:S(2)}, u32[]{:S(2)}) collective-permute-start(bf16[208,128]{1,0:T(8,128)(2,1)} %get-tuple-element.23), channel_id=1, source_target_pairs={{0,4},{1,5},{2,6},{3,7},{4,0},{5,1},{6,2},{7,3},{8,12},{9,13},{10,... | collective-permute-start | bytes 159752 | tf_op jit(solution)/shard_map/ppermute | solution.py:599
  13.5 3.6 %collective-permute-start.5 = (bf16[208,128]{1,0:T(8,128)(2,1)}, bf16[208,128]{1,0:T(8,128)(2,1)S(1)}, u32[]{:S(2)}, u32[]{:S(2)}) collective-permute-start(bf16[208,128]{1,0:T(8,128)(2,1)} %get-tuple-element.24), channel_id=1, source_target_pairs={{0,6},{1,7},{2,4},{3,5},{4,2},{5,3},{6,0},{7,1},{8,14},{9,15},{10,... | collective-permute-start | bytes 159752 | tf_op jit(solution)/shard_map/ppermute | solution.py:599
  20.7 1.9 %shard_map.113 = (bf16[128,384]{1,0:T(8,128)(2,1)S(1)}, bf16[128,384]{1,0:T(8,128)(2,1)S(1)}, bf16[2,576,256]{2,1,0:T(8,128)(2,1)S(1)}, bf16[256,384]{1,0:T(8,128)(2,1)S(1)}) custom-call(s32[6]{0:T(128)S(1)} %copy-done.12, bf16[128,768]{1,0:T(8,128)(2,1)S(1)} %bitcast.6, bf16[256,768]{1,0:T(8,128)(2,1)S(1)} %copy-done.5, bf16[768,768]{1,0:T(8,128)(2,1)S(1)} %copy-done, ...), custom_call_target="tpu_custom_call" | custom-call | flops 1000000000 | bytes 5000000 | tf_op jit(solution)/shard_map/pallas_call | solution.py:639
  22.7 1.5 %collective-permute-done.6.rest_7_ = bf16[208,128]{1,0:T(8,128)(2,1)S(1)} collective-permute-done((bf16[208,128]{1,0:T(8,128)(2,1)}, bf16[208,128]{1,0:T(8,128)(2,1)S(1)}, u32[]{:S(2)}, u32[]{:S(2)}) %collective-permute-start.6) | collective-permute-done | bytes 53280 | tf_op jit(solution)/shard_map/ppermute | solution.py:599
  24.2 15.3 %shard_map.115 = (bf16[4,576,128]{2,1,0:T(8,128)(2,1)}, bf16[2,576,128]{2,1,0:T(8,128)(2,1)S(1)}, bf16[192,1024]{1,0:T(8,128)(2,1)S(1)}) custom-call(s32[6]{0:T(128)S(1)} %copy-done.12, bf16[2,576,256]{2,1,0:T(8,128)(2,1)S(1)} %get-tuple-element.20.lookup_ref, f32[32,1024]{1,0:T(8,128)S(1)} %copy-done.15, f32[32,1024]{1,0:T(8,128)S(1)} %copy-done.16, ...), custom_call_target="tpu_custom_call" | custom-call | flops 8000000000 | bytes 8000000 | tf_op jit(solution)/shard_map/pallas_call | solution.py:639
  39.5 3.6 %all-to-all-start = ((bf16[4,576,128]{2,1,0:T(8,128)(2,1)}), bf16[4,576,128]{2,1,0:T(8,128)(2,1)S(1)}, u32[]{:S(2)}, u32[]{:S(2)}) async-start(bf16[4,576,128]{2,1,0:T(8,128)(2,1)} %get-tuple-element.25), calls=%async_computation | async-start | bytes 1179648 | tf_op jit(solution)/shard_map/all_to_all | solution.py:709
  43.0 1.5 %collective-permute-start.7 = (bf16[128,384]{1,0:T(8,128)(2,1)S(1)}, bf16[128,384]{1,0:T(8,128)(2,1)S(1)}, u32[]{:S(2)}, u32[]{:S(2)}) collective-permute-start(bf16[128,384]{1,0:T(8,128)(2,1)S(1)} %get-tuple-element.29), channel_id=1, source_target_pairs={{0,1},{1,0},{2,3},{3,2},{4,5},{5,4},{6,7},{7,6},{8,9},{9,8},{10,11... | collective-permute-start | bytes 294920 | tf_op jit(solution)/shard_map/ppermute | solution.py:599
  44.5 3.1 %collective-permute-done.7.got_ref = bf16[128,384]{1,0:T(8,128)(2,1)S(1)} collective-permute-done((bf16[128,384]{1,0:T(8,128)(2,1)S(1)}, bf16[128,384]{1,0:T(8,128)(2,1)S(1)}, u32[]{:S(2)}, u32[]{:S(2)}) %collective-permute-start.7) | collective-permute-done | bytes 98336 | tf_op jit(solution)/shard_map/ppermute | solution.py:599
  48.2 3.9 %collective-permute-start.10 = (bf16[256,384]{1,0:T(8,128)(2,1)S(1)}, bf16[256,384]{1,0:T(8,128)(2,1)S(1)}, u32[]{:S(2)}, u32[]{:S(2)}) collective-permute-start(bf16[256,384]{1,0:T(8,128)(2,1)S(1)} %shard_map.117.c0_ref), channel_id=1, source_target_pairs={{0,6},{1,7},{2,4},{3,5},{4,2},{5,3},{6,0},{7,1},{8,14},{9,15},{10,... | collective-permute-start | bytes 589832 | tf_op jit(solution)/shard_map/ppermute | solution.py:599
  52.8 9.6 %collective-permute-done.10.c3_ref = bf16[256,384]{1,0:T(8,128)(2,1)S(1)} collective-permute-done((bf16[256,384]{1,0:T(8,128)(2,1)S(1)}, bf16[256,384]{1,0:T(8,128)(2,1)S(1)}, u32[]{:S(2)}, u32[]{:S(2)}) %collective-permute-start.10) | collective-permute-done | bytes 196640 | tf_op jit(solution)/shard_map/ppermute | solution.py:599
  62.4 11.4 %collective-permute-done.9.c2_ref = bf16[256,384]{1,0:T(8,128)(2,1)S(1)} collective-permute-done((bf16[256,384]{1,0:T(8,128)(2,1)S(1)}, bf16[256,384]{1,0:T(8,128)(2,1)S(1)}, u32[]{:S(2)}, u32[]{:S(2)}) %collective-permute-start.9) | collective-permute-done | bytes 196640 | tf_op jit(solution)/shard_map/ppermute | solution.py:599
  74.8 1.5 %collective-permute-done.11 = bf16[864,128]{1,0:T(8,128)(2,1)S(1)} collective-permute-done((bf16[864,128]{1,0:T(8,128)(2,1)S(1)}, bf16[864,128]{1,0:T(8,128)(2,1)S(1)}, u32[]{:S(2)}, u32[]{:S(2)}) %collective-permute-start.11) | collective-permute-done | bytes 221216 | tf_op jit(solution)/shard_map/ppermute | solution.py:599
  76.4 1.6 %collective-permute-start.12 = (bf16[864,128]{1,0:T(8,128)(2,1)S(1)}, bf16[864,128]{1,0:T(8,128)(2,1)S(1)}, u32[]{:S(2)}, u32[]{:S(2)}) collective-permute-start(bf16[864,128]{1,0:T(8,128)(2,1)S(1)} %add.17.here_ref), channel_id=1, source_target_pairs={{0,16},{8,24},{16,0},{24,8},{1,17},{9,25},{17,1},{25,9},{2,18},{10... | collective-permute-start | bytes 663560 | tf_op jit(solution)/shard_map/ppermute | solution.py:599
  78.6 5.3 %collective-permute-done.12.there_ref = bf16[864,128]{1,0:T(8,128)(2,1)S(1)} collective-permute-done((bf16[864,128]{1,0:T(8,128)(2,1)S(1)}, bf16[864,128]{1,0:T(8,128)(2,1)S(1)}, u32[]{:S(2)}, u32[]{:S(2)}) %collective-permute-start.12) | collective-permute-done | bytes 221216 | tf_op jit(solution)/shard_map/ppermute | solution.py:599
  87.1 1.9 %collective-permute-start.13 = (bf16[192,128]{1,0:T(8,128)(2,1)S(1)}, bf16[192,128]{1,0:T(8,128)(2,1)S(1)}, u32[]{:S(2)}, u32[]{:S(2)}) collective-permute-start(bf16[192,128]{1,0:T(8,128)(2,1)S(1)} %get-tuple-element.34), channel_id=1, source_target_pairs={{0,2},{1,3},{2,0},{3,1},{6,4},{7,5},{8,10},{9,11},{10,8},{11,9},{1... | collective-permute-start | bytes 147464 | tf_op jit(solution)/shard_map/ppermute | solution.py:733
  89.0 1.9 %collective-permute-start.14 = (bf16[192,128]{1,0:T(8,128)(2,1)S(1)}, bf16[192,128]{1,0:T(8,128)(2,1)S(1)}, u32[]{:S(2)}, u32[]{:S(2)}) collective-permute-start(bf16[192,128]{1,0:T(8,128)(2,1)S(1)} %get-tuple-element.35), channel_id=1, source_target_pairs={{0,4},{1,5},{4,0},{5,1},{6,2},{7,3},{8,12},{9,13},{12,8},{13,9},{1... | collective-permute-start | bytes 147464 | tf_op jit(solution)/shard_map/ppermute | solution.py:733
  90.9 6.3 %collective-permute-start.16 = (bf16[288,128]{1,0:T(8,128)(2,1)S(1)}, bf16[288,128]{1,0:T(8,128)(2,1)S(1)}, u32[]{:S(2)}, u32[]{:S(2)}) collective-permute-start(bf16[288,128]{1,0:T(8,128)(2,1)S(1)} %get-tuple-element.37.own_ref), channel_id=1, source_target_pairs={{0,6},{5,7},{8,14},{13,15},{16,22},{21,23},{24,30},{29,31}} | collective-permute-start | bytes 221192 | tf_op jit(solution)/shard_map/ppermute | solution.py:739
  99.3 1.3 %collective-permute-start.15 = (bf16[192,128]{1,0:T(8,128)(2,1)S(1)}, bf16[192,128]{1,0:T(8,128)(2,1)S(1)}, u32[]{:S(2)}, u32[]{:S(2)}) collective-permute-start(bf16[192,128]{1,0:T(8,128)(2,1)S(1)} %get-tuple-element.36), channel_id=1, source_target_pairs={{2,4},{3,5},{4,2},{5,3},{6,0},{7,1},{10,12},{11,13},{12,10},{13,11... | collective-permute-start | bytes 147464 | tf_op jit(solution)/shard_map/ppermute | solution.py:733
  100.6 6.5 %collective-permute-done.15.s3 = bf16[192,128]{1,0:T(8,128)(2,1)S(1)} collective-permute-done((bf16[192,128]{1,0:T(8,128)(2,1)S(1)}, bf16[192,128]{1,0:T(8,128)(2,1)S(1)}, u32[]{:S(2)}, u32[]{:S(2)}) %collective-permute-start.15) | collective-permute-done | bytes 49184 | tf_op jit(solution)/shard_map/ppermute | solution.py:733
  107.8 1.9 %shard_map.116 = bf16[128,768]{1,0:T(8,128)(2,1)} custom-call(s32[1,128]{1,0:T(1,128)S(1)} %copy-done.13, bf16[256,768]{1,0:T(8,128)(2,1)S(1)} %copy-done.6, bf16[768,768]{1,0:T(8,128)(2,1)S(1)} %copy-done, bf16[768,768]{1,0:T(8,128)(2,1)S(1)} %copy-done.2, bf16[768,768]{1,0:T(8,128)(2,1)S(1)} %copy-done.4, ...), custom_call_target="tpu_custom_call" | custom-call | flops 1000000000 | bytes 5000000 | tf_op jit(solution)/shard_map/pallas_call | solution.py:639
  109.7 2.1 %shard_map.121 = f32[384,768]{1,0:T(8,128)} custom-call(s32[6]{0:T(128)S(1)} %copy-done.12, bf16[256,384]{1,0:T(8,128)(2,1)S(1)} %get-tuple-element.26.normed_ref, bf16[1152,128]{1,0:T(8,128)(2,1)S(1)} %shard_map.120.mine_ref, bf16[1152,128]{1,0:T(8,128)(2,1)S(1)} %collective-permute-done.20.other_ref), custom_call_target="tpu_custom_call" | custom-call | flops 1000000000 | bytes 5000000 | tf_op jit(solution)/shard_map/pallas_call | solution.py:639
  (66 shorter events, 15.2 us)
Async XLA Ops:
  4.7 8.8 %collective-permute-start = (bf16[208,128]{1,0:T(8,128)(2,1)}, bf16[208,128]{1,0:T(8,128)(2,1)S(1)}, u32[]{:S(2)}, u32[]{:S(2)}) collective-permute-start(bf16[208,128]{1,0:T(8,128)(2,1)} %get-tuple-element.21.rest_0_), channel_id=1, source_target_pairs={{0,1},{1,0},{2,3},{3,2},{4,5},{5,4},{6,7},{7,6},{8,9},{9,8},{10,11... | collective-permute-start | bytes 159752 | tf_op jit(solution)/shard_map/ppermute | solution.py:599
  7.7 9.5 %collective-permute-start.1 = (bf16[208,128]{1,0:T(8,128)(2,1)}, bf16[208,128]{1,0:T(8,128)(2,1)S(1)}, u32[]{:S(2)}, u32[]{:S(2)}) collective-permute-start(bf16[208,128]{1,0:T(8,128)(2,1)} %get-tuple-element.22), channel_id=1, source_target_pairs={{0,2},{1,3},{2,0},{3,1},{4,6},{5,7},{6,4},{7,5},{8,10},{9,11},{10,... | collective-permute-start | bytes 159752 | tf_op jit(solution)/shard_map/ppermute | solution.py:599
  9.2 13.4 %collective-permute-start.2 = (bf16[208,128]{1,0:T(8,128)(2,1)}, bf16[208,128]{1,0:T(8,128)(2,1)S(1)}, u32[]{:S(2)}, u32[]{:S(2)}) collective-permute-start(bf16[208,128]{1,0:T(8,128)(2,1)} %get-tuple-element.22), channel_id=1, source_target_pairs={{0,3},{1,2},{2,1},{3,0},{4,7},{5,6},{6,5},{7,4},{8,11},{9,10},{10,... | collective-permute-start | bytes 159752 | tf_op jit(solution)/shard_map/ppermute | solution.py:599
  9.2 13.4 %collective-permute-start.3 = (bf16[208,128]{1,0:T(8,128)(2,1)}, bf16[208,128]{1,0:T(8,128)(2,1)S(1)}, u32[]{:S(2)}, u32[]{:S(2)}) collective-permute-start(bf16[208,128]{1,0:T(8,128)(2,1)} %get-tuple-element.23), channel_id=1, source_target_pairs={{0,4},{1,5},{2,6},{3,7},{4,0},{5,1},{6,2},{7,3},{8,12},{9,13},{10,... | collective-permute-start | bytes 159752 | tf_op jit(solution)/shard_map/ppermute | solution.py:599
  12.2 10.4 %collective-permute-start.4 = (bf16[208,128]{1,0:T(8,128)(2,1)}, bf16[208,128]{1,0:T(8,128)(2,1)S(1)}, u32[]{:S(2)}, u32[]{:S(2)}) collective-permute-start(bf16[208,128]{1,0:T(8,128)(2,1)} %get-tuple-element.23), channel_id=1, source_target_pairs={{0,5},{1,4},{2,7},{3,6},{4,1},{5,0},{6,3},{7,2},{8,13},{9,12},{10,... | collective-permute-start | bytes 159752 | tf_op jit(solution)/shard_map/ppermute | solution.py:599
  13.5 9.2 %collective-permute-start.5 = (bf16[208,128]{1,0:T(8,128)(2,1)}, bf16[208,128]{1,0:T(8,128)(2,1)S(1)}, u32[]{:S(2)}, u32[]{:S(2)}) collective-permute-start(bf16[208,128]{1,0:T(8,128)(2,1)} %get-tuple-element.24), channel_id=1, source_target_pairs={{0,6},{1,7},{2,4},{3,5},{4,2},{5,3},{6,0},{7,1},{8,14},{9,15},{10,... | collective-permute-start | bytes 159752 | tf_op jit(solution)/shard_map/ppermute | solution.py:599
  17.1 7.0 %collective-permute-start.6 = (bf16[208,128]{1,0:T(8,128)(2,1)}, bf16[208,128]{1,0:T(8,128)(2,1)S(1)}, u32[]{:S(2)}, u32[]{:S(2)}) collective-permute-start(bf16[208,128]{1,0:T(8,128)(2,1)} %get-tuple-element.24), channel_id=1, source_target_pairs={{0,7},{1,6},{2,5},{3,4},{4,3},{5,2},{6,1},{7,0},{8,15},{9,14},{10,... | collective-permute-start | bytes 159752 | tf_op jit(solution)/shard_map/ppermute | solution.py:599
  39.5 45.1 %all-to-all-start = ((bf16[4,576,128]{2,1,0:T(8,128)(2,1)}), bf16[4,576,128]{2,1,0:T(8,128)(2,1)S(1)}, u32[]{:S(2)}, u32[]{:S(2)}) async-start(bf16[4,576,128]{2,1,0:T(8,128)(2,1)} %get-tuple-element.25), calls=%async_computation | async-start | bytes 1179648 | tf_op jit(solution)/shard_map/all_to_all | solution.py:709
  43.0 4.6 %collective-permute-start.7 = (bf16[128,384]{1,0:T(8,128)(2,1)S(1)}, bf16[128,384]{1,0:T(8,128)(2,1)S(1)}, u32[]{:S(2)}, u32[]{:S(2)}) collective-permute-start(bf16[128,384]{1,0:T(8,128)(2,1)S(1)} %get-tuple-element.29), channel_id=1, source_target_pairs={{0,1},{1,0},{2,3},{3,2},{4,5},{5,4},{6,7},{7,6},{8,9},{9,8},{10,11... | collective-permute-start | bytes 294920 | tf_op jit(solution)/shard_map/ppermute | solution.py:599
  48.2 14.2 %collective-permute-start.10 = (bf16[256,384]{1,0:T(8,128)(2,1)S(1)}, bf16[256,384]{1,0:T(8,128)(2,1)S(1)}, u32[]{:S(2)}, u32[]{:S(2)}) collective-permute-start(bf16[256,384]{1,0:T(8,128)(2,1)S(1)} %shard_map.117.c0_ref), channel_id=1, source_target_pairs={{0,6},{1,7},{2,4},{3,5},{4,2},{5,3},{6,0},{7,1},{8,14},{9,15},{10,... | collective-permute-start | bytes 589832 | tf_op jit(solution)/shard_map/ppermute | solution.py:599
  52.1 10.3 %collective-permute-start.8 = (bf16[256,384]{1,0:T(8,128)(2,1)S(1)}, bf16[256,384]{1,0:T(8,128)(2,1)S(1)}, u32[]{:S(2)}, u32[]{:S(2)}) collective-permute-start(bf16[256,384]{1,0:T(8,128)(2,1)S(1)} %shard_map.117.c0_ref), channel_id=1, source_target_pairs={{0,2},{1,3},{2,0},{3,1},{4,6},{5,7},{6,4},{7,5},{8,10},{9,11},{10,... | collective-permute-start | bytes 589832 | tf_op jit(solution)/shard_map/ppermute | solution.py:599
  52.1 21.7 %collective-permute-start.9 = (bf16[256,384]{1,0:T(8,128)(2,1)S(1)}, bf16[256,384]{1,0:T(8,128)(2,1)S(1)}, u32[]{:S(2)}, u32[]{:S(2)}) collective-permute-start(bf16[256,384]{1,0:T(8,128)(2,1)S(1)} %shard_map.117.c0_ref), channel_id=1, source_target_pairs={{0,4},{1,5},{2,6},{3,7},{4,0},{5,1},{6,2},{7,3},{8,12},{9,13},{10,... | collective-permute-start | bytes 589832 | tf_op jit(solution)/shard_map/ppermute | solution.py:599
  73.8 33.9 %copy-start.6 = (bf16[256,768]{1,0:T(8,128)(2,1)S(1)}, bf16[256,768]{1,0:T(8,128)(2,1)}, u32[]{:S(2)}) copy-start(bf16[256,768]{1,0:T(8,128)(2,1)} %table_ref.3) | copy-start | bytes 1179652
  74.8 1.5 %collective-permute-start.11 = (bf16[864,128]{1,0:T(8,128)(2,1)S(1)}, bf16[864,128]{1,0:T(8,128)(2,1)S(1)}, u32[]{:S(2)}, u32[]{:S(2)}) collective-permute-start(bf16[864,128]{1,0:T(8,128)(2,1)S(1)} %get-tuple-element.32), channel_id=1, source_target_pairs={{0,8},{8,0},{16,24},{24,16},{1,9},{9,1},{17,25},{25,17},{2,10},{10... | collective-permute-start | bytes 663560 | tf_op jit(solution)/shard_map/ppermute | solution.py:599
  76.3 31.4 %copy-start.2 = (bf16[768,768]{1,0:T(8,128)(2,1)S(1)}, bf16[768,768]{1,0:T(8,128)(2,1)}, u32[]{:S(2)}) copy-start(bf16[768,768]{1,0:T(8,128)(2,1)} %key_ref.3) | copy-start | bytes 3538948
  76.4 7.5 %collective-permute-start.12 = (bf16[864,128]{1,0:T(8,128)(2,1)S(1)}, bf16[864,128]{1,0:T(8,128)(2,1)S(1)}, u32[]{:S(2)}, u32[]{:S(2)}) collective-permute-start(bf16[864,128]{1,0:T(8,128)(2,1)S(1)} %add.17.here_ref), channel_id=1, source_target_pairs={{0,16},{8,24},{16,0},{24,8},{1,17},{9,25},{17,1},{25,9},{2,18},{10... | collective-permute-start | bytes 663560 | tf_op jit(solution)/shard_map/ppermute | solution.py:599
  87.1 11.5 %collective-permute-start.13 = (bf16[192,128]{1,0:T(8,128)(2,1)S(1)}, bf16[192,128]{1,0:T(8,128)(2,1)S(1)}, u32[]{:S(2)}, u32[]{:S(2)}) collective-permute-start(bf16[192,128]{1,0:T(8,128)(2,1)S(1)} %get-tuple-element.34), channel_id=1, source_target_pairs={{0,2},{1,3},{2,0},{3,1},{6,4},{7,5},{8,10},{9,11},{10,8},{11,9},{1... | collective-permute-start | bytes 147464 | tf_op jit(solution)/shard_map/ppermute | solution.py:733
  89.0 10.2 %collective-permute-start.14 = (bf16[192,128]{1,0:T(8,128)(2,1)S(1)}, bf16[192,128]{1,0:T(8,128)(2,1)S(1)}, u32[]{:S(2)}, u32[]{:S(2)}) collective-permute-start(bf16[192,128]{1,0:T(8,128)(2,1)S(1)} %get-tuple-element.35), channel_id=1, source_target_pairs={{0,4},{1,5},{4,0},{5,1},{6,2},{7,3},{8,12},{9,13},{12,8},{13,9},{1... | collective-permute-start | bytes 147464 | tf_op jit(solution)/shard_map/ppermute | solution.py:733
  90.9 16.1 %collective-permute-start.16 = (bf16[288,128]{1,0:T(8,128)(2,1)S(1)}, bf16[288,128]{1,0:T(8,128)(2,1)S(1)}, u32[]{:S(2)}, u32[]{:S(2)}) collective-permute-start(bf16[288,128]{1,0:T(8,128)(2,1)S(1)} %get-tuple-element.37.own_ref), channel_id=1, source_target_pairs={{0,6},{5,7},{8,14},{13,15},{16,22},{21,23},{24,30},{29,31}} | collective-permute-start | bytes 221192 | tf_op jit(solution)/shard_map/ppermute | solution.py:739
  97.2 9.8 %collective-permute-start.17 = (bf16[288,128]{1,0:T(8,128)(2,1)S(1)}, bf16[288,128]{1,0:T(8,128)(2,1)S(1)}, u32[]{:S(2)}, u32[]{:S(2)}) collective-permute-start(bf16[288,128]{1,0:T(8,128)(2,1)S(1)} %get-tuple-element.37.own_ref), channel_id=1, source_target_pairs={{1,6},{4,7},{9,14},{12,15},{17,22},{20,23},{25,30},{28,31}} | collective-permute-start | bytes 221192 | tf_op jit(solution)/shard_map/ppermute | solution.py:739
  97.9 9.2 %collective-permute-start.18 = (bf16[288,128]{1,0:T(8,128)(2,1)S(1)}, bf16[288,128]{1,0:T(8,128)(2,1)S(1)}, u32[]{:S(2)}, u32[]{:S(2)}) collective-permute-start(bf16[288,128]{1,0:T(8,128)(2,1)S(1)} %get-tuple-element.37.own_ref), channel_id=1, source_target_pairs={{2,6},{10,14},{18,22},{26,30}} | collective-permute-start | bytes 221192 | tf_op jit(solution)/shard_map/ppermute | solution.py:739
  98.6 8.5 %collective-permute-start.19 = (bf16[288,128]{1,0:T(8,128)(2,1)S(1)}, bf16[288,128]{1,0:T(8,128)(2,1)S(1)}, u32[]{:S(2)}, u32[]{:S(2)}) collective-permute-start(bf16[288,128]{1,0:T(8,128)(2,1)S(1)} %get-tuple-element.37.own_ref), channel_id=1, source_target_pairs={{3,6},{6,7},{11,14},{14,15},{19,22},{22,23},{27,30},{30,31}} | collective-permute-start | bytes 221192 | tf_op jit(solution)/shard_map/ppermute | solution.py:739
  99.3 7.8 %collective-permute-start.15 = (bf16[192,128]{1,0:T(8,128)(2,1)S(1)}, bf16[192,128]{1,0:T(8,128)(2,1)S(1)}, u32[]{:S(2)}, u32[]{:S(2)}) collective-permute-start(bf16[192,128]{1,0:T(8,128)(2,1)S(1)} %get-tuple-element.36), channel_id=1, source_target_pairs={{2,4},{3,5},{4,2},{5,3},{6,0},{7,1},{10,12},{11,13},{12,10},{13,11... | collective-permute-start | bytes 147464 | tf_op jit(solution)/shard_map/ppermute | solution.py:733
  107.7 2.1 %collective-permute-start.20 = (bf16[1152,128]{1,0:T(8,128)(2,1)S(1)}, bf16[1152,128]{1,0:T(8,128)(2,1)S(1)}, u32[]{:S(2)}, u32[]{:S(2)}) collective-permute-start(bf16[1152,128]{1,0:T(8,128)(2,1)S(1)} %shard_map.120.mine_ref), channel_id=1, source_target_pairs={{0,8},{8,0},{16,24},{24,16},{1,9},{9,1},{17,25},{25,17},{2,10},{10... | collective-permute-start | bytes 884744 | tf_op jit(solution)/shard_map/ppermute | solution.py:599
  (15 other events, 117.9 us)

commit v5 on v3

--- a/solution.py
+++ b/solution.py
@@ -247,18 +247,19 @@
     return (rows == tokens).astype(jnp.float32).astype(jnp.bfloat16)
 
 
-def send_kernel(tokens_ref, cotangent_ref, out_weights_ref, early_ref):
+def send_kernel(meta_ref, tokens_ref, cotangent_ref, out_weights_ref, *out_refs):
+    early_refs, grads_ref = out_refs[:-1], out_refs[-1]
     grad_att = ndot(out_weights_ref[...], cotangent_ref[...]).astype(jnp.bfloat16)
+    grads_ref[...] = grad_att
     block = tokens_ref.shape[1]
     tokens = jnp.broadcast_to(tokens_ref[...].astype(jnp.float32), (TOKEN_ROWS, block)).astype(
         jnp.bfloat16
     )
-    for target in range(2 * GROUPS):
-        group = target // 2
-        early_ref[target, :GROUP_COLS, :] = grad_att[
-            group * GROUP_COLS : (group + 1) * GROUP_COLS
-        ]
-        early_ref[target, GROUP_COLS:, :] = tokens
+    for turn, early_ref in enumerate(early_refs):
+        group = meta_ref[GROUP_HEADS + 1] ^ turn
+        place = pl.ds(pl.multiple_of(group * GROUP_COLS, GROUP_COLS), GROUP_COLS)
+        early_ref[:GROUP_COLS, :] = grads_ref[place, :]
+        early_ref[GROUP_COLS:, :] = tokens
 
 
 def prepare_kernel(
@@ -294,41 +295,55 @@
 
 def attention_kernel(
     meta_ref,
-    early_ref,
     lookup_ref,
     cosine_ref,
     sine_ref,
+    *rest,
+):
+    early_refs = rest[: 2 * GROUPS]
+    attention_body(meta_ref, lookup_ref, cosine_ref, sine_ref, early_refs, *rest[2 * GROUPS :])
+
+
+def attention_body(
+    meta_ref,
+    lookup_ref,
+    cosine_ref,
+    sine_ref,
+    early_refs,
     rows_ref,
     sums_ref,
     attended_ref,
     query_key_ref,
     zero_query_ref,
     key_t_ref,
-    value_ref,
     value_t_ref,
     grad_att_ref,
     onehot_ref,
     grad_query_ref,
-    grad_key_ref,
-    grad_value_ref,
+    both_ref,
+    value_grad_ref,
+    probs_ref,
+    scores_ref,
 ):
     head = pl.program_id(0)
-    blocks, _, block = early_ref.shape
-    length = blocks * block
+    block = early_refs[0].shape[1]
+    length = len(early_refs) * block
     vocab = lookup_ref.shape[2]
     half_vocab = vocab // 2
+    half = jnp.bfloat16
     cosine = cosine_ref[...]
     sine_part = sine_ref[...]
-    blank = jnp.zeros((HEAD_DIM, length), jnp.float32)
+    blank = jnp.zeros((HEAD_DIM, length), half)
 
     @pl.when(head == 0)
     def _():
-        for source in range(blocks):
-            lanes = slice(source * block, (source + 1) * block)
-            tokens = early_ref[source, GROUP_COLS : GROUP_COLS + TOKEN_ROWS, :]
+        own = 2 * meta_ref[GROUP_HEADS + 1] + meta_ref[GROUP_HEADS]
+        for turn, early_ref in enumerate(early_refs):
+            lanes = pl.ds(pl.multiple_of((own ^ turn) * block, block), block)
+            tokens = early_ref[GROUP_COLS : GROUP_COLS + TOKEN_ROWS, :]
             tokens = tokens.astype(jnp.float32)[:1].astype(jnp.int32)
             onehot_ref[:, lanes] = onehot_columns(tokens, vocab)
-            grad_att_ref[:, :, lanes] = early_ref[source, :GROUP_COLS, :].reshape(
+            grad_att_ref[:, :, lanes] = early_ref[:GROUP_COLS, :].reshape(
                 GROUP_HEADS, HEAD_DIM, block
             )
         onehot = onehot_ref[...]
@@ -347,22 +362,19 @@
             )
 
         for index in range(GROUP_HEADS):
-            query = turned(chosen(index * HEAD_DIM)) * HEAD_DIM ** (-0.5)
-            keys = turned(chosen(GROUP_COLS + index * HEAD_DIM))
-            values = chosen(2 * GROUP_COLS + index * HEAD_DIM)
-            query_key_ref[index] = jnp.concatenate([query, keys], axis=0).T.astype(jnp.bfloat16)
-            value_ref[index] = jnp.concatenate([values, blank], axis=0).T.astype(jnp.bfloat16)
-            zero_query_ref[index] = jnp.concatenate([blank, query], axis=0).astype(jnp.bfloat16)
-            key_t_ref[index] = keys.astype(jnp.bfloat16)
-            value_t_ref[index] = values.astype(jnp.bfloat16)
+            query = (turned(chosen(index * HEAD_DIM)) * HEAD_DIM ** (-0.5)).astype(half)
+            keys = turned(chosen(GROUP_COLS + index * HEAD_DIM)).astype(half)
+            values = chosen(2 * GROUP_COLS + index * HEAD_DIM).astype(half)
+            query_key_ref[index] = jnp.concatenate([query, keys], axis=0).T
+            zero_query_ref[index] = jnp.concatenate([blank, query], axis=0)
+            key_t_ref[index] = keys
+            value_t_ref[index] = values
 
     width = meta_ref[head]
     grad_att = grad_att_ref[head]
     wide_grad = grad_att.astype(jnp.float32)
-    grad_blank = jnp.concatenate([wide_grad, blank], axis=0).astype(jnp.bfloat16)
-    blank_grad = jnp.concatenate([blank, wide_grad], axis=0).T.astype(jnp.bfloat16)
-    grad_key_ref[...] = jnp.zeros_like(grad_key_ref)
-    grad_value_ref[...] = jnp.zeros_like(grad_value_ref)
+    grad_blank = jnp.concatenate([grad_att, blank], axis=0)
+    value_grad_ref[...] = jnp.concatenate([value_t_ref[head], grad_att], axis=0).T
     distance = lax.broadcasted_iota(jnp.int32, (TILE, TILE), 1) - lax.broadcasted_iota(
         jnp.int32, (TILE, TILE), 0
     )
@@ -386,7 +398,8 @@
         row_max = jnp.max(masked, axis=0, keepdims=True)
         weights = jnp.exp(masked - row_max)
         probs = weights * (1.0 / jnp.sum(weights, axis=0, keepdims=True))
-        rounded = probs.astype(jnp.bfloat16)
+        rounded = probs.astype(half)
+        probs_ref[first : first + count, columns] = rounded
         attended = jnp.dot(
             value_t_ref[head, :, first : first + count], rounded, preferred_element_type=jnp.float32
         )
@@ -395,7 +408,7 @@
         )
         row_term = jnp.sum(attended * wide_grad[:, columns], axis=0, keepdims=True)
         grad_probs = jnp.dot(
-            value_ref[head, first : first + count, :],
+            value_grad_ref[first : first + count, :],
             grad_blank[:, columns],
             preferred_element_type=jnp.float32,
         )
@@ -405,12 +418,22 @@
             grad_scores,
             preferred_element_type=jnp.float32,
         )
-        grad_key_ref[first : first + count, :] += jnp.dot(
-            grad_scores, query_key_ref[head, columns, :], preferred_element_type=jnp.float32
-        )
-        grad_value_ref[first : first + count, :] += jnp.dot(
-            rounded, blank_grad[columns, :], preferred_element_type=jnp.float32
-        )
+        scores_ref[first : first + count, columns] = grad_scores
+    lanes = lax.broadcasted_iota(jnp.int32, (TILE, 2 * HEAD_DIM), 1)
+    for key_tile in range(length // TILE):
+        start = key_tile * TILE
+        stop = min(length, start + TILE + WINDOW)
+        grad_key = jnp.dot(
+            scores_ref[start : start + TILE, start:stop],
+            query_key_ref[head, start:stop, :],
+            preferred_element_type=jnp.float32,
+        )
+        grad_value = jnp.dot(
+            probs_ref[start : start + TILE, start:stop],
+            value_grad_ref[start:stop, :],
+            preferred_element_type=jnp.float32,
+        )
+        both_ref[:, start : start + TILE] = jnp.where(lanes < HEAD_DIM, grad_key, grad_value).T
 
     def turned_back(columns):
         former = columns[:HALF]
@@ -419,8 +442,7 @@
             [former * cosine + latter * sine_part, latter * cosine - former * sine_part], axis=0
         )
 
-    lanes = lax.broadcasted_iota(jnp.int32, grad_key_ref.shape, 1)
-    both = jnp.where(lanes < HEAD_DIM, grad_key_ref[...], grad_value_ref[...]).T
+    both = both_ref[...]
     grads = jnp.concatenate(
         [
             turned_back(grad_query_ref[...] * HEAD_DIM ** (-0.5)),
@@ -460,35 +482,43 @@
         give_ref[place, :] = jnp.where(first, part[rows:], part[:rows]).astype(jnp.bfloat16)
 
 
-def combine_kernel(here_ref, there_ref, after_ref, out_ref):
+def combine_kernel(meta_ref, here_ref, there_ref, after_ref, *piece_refs):
     del after_ref
     rows = GROUP_COLS
-    size = out_ref.shape[1]
-    blank = jnp.zeros((size - rows, out_ref.shape[2]), jnp.bfloat16)
-    for matrix in range(3):
-        place = slice(matrix * rows, (matrix + 1) * rows)
-        out_ref[matrix, :rows, :] = here_ref[place, :] + there_ref[place, :]
-        out_ref[matrix, rows:, :] = blank
-    out_ref[3] = here_ref[3 * rows :, :] + there_ref[3 * rows :, :]
-
-
-def gather_kernel(meta_ref, got_ref, mine_ref, other_ref):
+    for turn, piece_ref in enumerate(piece_refs):
+        target = meta_ref[GROUP_HEADS + 1] ^ turn
+
+        @pl.when(target < 3)
+        def _(piece_ref=piece_ref, target=target):
+            place = pl.ds(pl.multiple_of(target * rows, rows), rows)
+            piece_ref[:rows, :] = here_ref[place, :] + there_ref[place, :]
+            tail = piece_ref.shape[0] - rows
+            piece_ref[rows:, :] = jnp.zeros((tail, piece_ref.shape[1]), jnp.bfloat16)
+
+        @pl.when(target == 3)
+        def _(piece_ref=piece_ref):
+            piece_ref[...] = here_ref[3 * rows :, :] + there_ref[3 * rows :, :]
+
+
+def gather_kernel(meta_ref, g0, g1, g2, g3, mine_ref, other_ref):
     rows = GROUP_COLS
-    size = got_ref.shape[1]
-
-    @pl.when(meta_ref[GROUP_HEADS + 1] < 3)
+    size = g0.shape[0]
+    group = meta_ref[GROUP_HEADS + 1]
+
+    @pl.when(group < 3)
     def _():
-        for group in range(GROUPS):
-            mine_ref[group * rows : (group + 1) * rows, :] = got_ref[group, :rows, :]
+        for turn, got in enumerate((g0, g1, g2, g3)):
+            place = pl.ds(pl.multiple_of((group ^ turn) * rows, rows), rows)
+            mine_ref[place, :] = got[:rows, :]
         other_ref[...] = jnp.zeros_like(other_ref)
 
-    @pl.when(meta_ref[GROUP_HEADS + 1] == 3)
+    @pl.when(group == 3)
     def _():
         first = meta_ref[GROUP_HEADS] == 0
-        for part in range(2):
+        for part, (low, high) in enumerate(((g3, g1), (g2, g0))):
             place = slice(part * size, (part + 1) * size)
-            mine_ref[place, :] = jnp.where(first, got_ref[part], got_ref[2 + part])
-            other_ref[place, :] = jnp.where(first, got_ref[2 + part], got_ref[part])
+            mine_ref[place, :] = jnp.where(first, low[...], high[...])
+            other_ref[place, :] = jnp.where(first, high[...], low[...])
         tail = mine_ref.shape[0] - 2 * size
         mine_ref[2 * size :, :] = jnp.zeros((tail, mine_ref.shape[1]), jnp.bfloat16)
 
@@ -594,7 +624,9 @@
     )
     cosine, sine_part = rope_table(length)
 
-    def call(body, operands, outs, scratch=(), steps=1, flops=10**8, moved=10**6, loose=0):
+    def call(
+        body, operands, outs, scratch=(), steps=1, flops=10**8, moved=10**6, loose=0, grant=VMEM_BYTES
+    ):
         spaces = [whole(operand.shape) for operand in operands]
         for index in range(loose):
             spaces[-1 - index] = pl.BlockSpec(memory_space=pl.ANY)
@@ -608,18 +640,22 @@
             out_shape=[jax.ShapeDtypeStruct(shape, dtype) for shape, dtype in outs],
             scratch_shapes=list(scratch),
             compiler_params=pltpu.CompilerParams(
-                dimension_semantics=("arbitrary",), vmem_limit_bytes=VMEM_BYTES
+                dimension_semantics=("arbitrary",), vmem_limit_bytes=grant
             ),
             cost_estimate=pl.CostEstimate(flops=flops, bytes_accessed=moved, transcendentals=0),
         )(*operands)
 
     half = jnp.bfloat16
-    (early,) = call(
+    sent = call(
         send_kernel,
-        (token_ids, grad_out, w_out),
-        [((blocks, GROUP_COLS + TOKEN_ROWS, block), half)],
-    )
-    early = lax.all_to_all(early, "seq", split_axis=0, concat_axis=0, tiled=True)
+        (meta, token_ids, grad_out, w_out),
+        [((GROUP_COLS + TOKEN_ROWS, block), half)] * GROUPS,
+        [pltpu.VMEM((features, block), half)],
+        grant=60 * 1024 * 1024,
+    )
+    early = [sent[0]] + [None] * (blocks - 1)
+    for turn in (4, 6, 5, 7, 2, 3, 1):
+        early[turn] = swapped(sent[turn // 2], "seq", turn)
     late, lookup, normed = call(
         prepare_kernel,
         (meta, grad_out, table, w_query, w_key, w_value),
@@ -631,13 +667,14 @@
         [pltpu.VMEM((features, vocab), jnp.float32)],
         flops=10**9,
         moved=5 * 10**6,
+        grant=60 * 1024 * 1024,
     )
     late = lax.all_to_all(late, "seq", split_axis=0, concat_axis=0, tiled=True)
     heads_shape = (GROUP_HEADS, HEAD_DIM, length)
     rows_shape = (GROUP_HEADS, length, 2 * HEAD_DIM)
     rows, sums, attended = call(
         attention_kernel,
-        (meta, early, lookup, cosine, sine_part),
+        (meta, lookup, cosine, sine_part, *early),
         [
             ((GROUPS, 3 * GROUP_COLS, block), half),
             ((2, 3 * GROUP_COLS, vocab // 2), half),
@@ -647,13 +684,14 @@
             pltpu.VMEM(rows_shape, half),
             pltpu.VMEM((GROUP_HEADS, 2 * HEAD_DIM, length), half),
             pltpu.VMEM(heads_shape, half),
-            pltpu.VMEM(rows_shape, half),
             pltpu.VMEM(heads_shape, half),
             pltpu.VMEM(heads_shape, half),
             pltpu.VMEM((vocab, length), half),
             pltpu.VMEM((HEAD_DIM, length), jnp.float32),
-            pltpu.VMEM((length, 2 * HEAD_DIM), jnp.float32),
-            pltpu.VMEM((length, 2 * HEAD_DIM), jnp.float32),
+            pltpu.VMEM((2 * HEAD_DIM, length), jnp.float32),
+            pltpu.VMEM((length, 2 * HEAD_DIM), half),
+            pltpu.VMEM((length, length), half),
+            pltpu.VMEM((length, length), half),
         ],
         steps=GROUP_HEADS,
         flops=8 * 10**9,
@@ -677,12 +715,18 @@
     )
     here = keep + swapped(give, "dp", 1)
     there = swapped(here, "dp", 2)
-    (chunks,) = call(
-        combine_kernel, (here, there, got_rows), [((GROUPS, out_rows, lanes), half)], loose=1
-    )
+    pieces = call(
+        combine_kernel,
+        (meta, here, there, got_rows),
+        [((out_rows, lanes), half)] * GROUPS,
+        loose=1,
+    )
+    got = [pieces[0]] + [None] * (GROUPS - 1)
+    for turn in (2, 3, 1):
+        got[turn] = swapped(pieces[turn], "seq", 2 * turn)
     mine, other = call(
         gather_kernel,
-        (meta, over_plane(chunks)),
+        (meta, *got),
         [((GROUPS * GROUP_COLS, lanes), half), ((2 * out_rows, lanes), half)],
     )
     (grad_input,) = call(
@@ -693,13 +737,13 @@
         moved=5 * 10**6,
     )
     last = blocks - 2
+    near = lax.ppermute(other, "seq", [(last, last + 1), (last + 1, last)])
     paired = swapped(mine, "dp", 1)
-    near = lax.ppermute(other, "seq", [(last, last + 1), (last + 1, last)])
     far = lax.ppermute(
-        other,
+        near,
         ("dp", "seq"),
         [
-            (blocks * d + last + x, blocks * (d ^ 1) + last + 1 - x)
+            (blocks * d + last + x, blocks * (d ^ 1) + last + x)
             for d in range(lax.axis_size("dp"))
             for x in range(2)
         ],

time: 90.5 us -> 100 us (1.10)
  the two profiles are of different devices: /device:TPU:26 before, /device:TPU:27 now
where the time goes in v5:
time: 100 us; the launch traced here: 99.6 us
  starting transfers between devices  33.2 us (33%)
  waiting for transfers between devices  32.1 us (32%)
  Pallas kernels  29.1 us (29%)
  local copies, waits for them, and re-layouts  2.84 us (3%)
  other arithmetic  1.4 us (1%)
    pallas_call x8, Pallas kernels, call(): pl.pallas_call(body, grid=(steps,), in_specs=spaces, out_specs=[whole(sha...  29.1 us
    ppermute x13, waiting for transfers between devices, swapped(): return lax.ppermute(block, axis, route)  24.1 us
    ppermute x13, starting transfers between devices, swapped(): return lax.ppermute(block, axis, route)  14.4 us
    all_to_all x1, waiting for transfers between devices, over_plane(): lax.all_to_all(chunks, 'seq', split_axis=0, concat_axis=0, axis_index_gro...  6.87 us
    all_to_all x1, starting transfers between devices, over_plane(): lax.all_to_all(chunks, 'seq', split_axis=0, concat_axis=0, axis_index_gro...  5.89 us
    all_to_all x1, starting transfers between devices, grouped_device(): late = lax.all_to_all(late, 'seq', split_axis=0, concat_axis=0, tiled=True)  5.58 us
    ppermute x1, starting transfers between devices, grouped_device(): lax.ppermute(near, ('dp', 'seq'), [(blocks * d + last + x, blocks * (d ^...  5.45 us
    unnamed x22, local copies, waits for them, and re-layouts  2.11 us
  transfers between devices with their start and end apart: 17, of which 10 were waited for; matrix products, arithmetic and copies ran while one was open for 1% of the time, Pallas kernels for 21%

profile of v5, /device:TPU:27, one launch (start us, length us, event | category | flops | bytes accessed | tf_op | source)
XLA Modules:
  0.0 99.6 jit_solution(9350365781492548167)
XLA Ops:
  2.0 4.6 %shard_map.113 = (bf16[8,128,384]{2,1,0:T(8,128)(2,1)}, bf16[2,576,256]{2,1,0:T(8,128)(2,1)}, bf16[256,384]{1,0:T(8,128)(2,1)}) custom-call(s32[6]{0:T(128)} %pad_add_fusion.meta_ref, bf16[128,768]{1,0:T(8,128)(2,1)} %bitcast.7, bf16[256,768]{1,0:T(8,128)(2,1)} %table_ref.3, bf16[768,768]{1,0:T(8,128)(2,1)} %query_ref.3, bf16[768,768]{1,0:T(8,128)(2,1)} %key_ref.3, ...), custom_call_target="tpu_custom_call" | custom-call | flops 1000000000 | bytes 5000000 | tf_op jit(solution)/shard_map/pallas_call | solution.py:635
  6.7 5.6 %all-to-all-start.1 = ((bf16[8,128,384]{2,1,0:T(8,128)(2,1)}), bf16[8,128,384]{2,1,0:T(8,128)(2,1)S(1)}, u32[]{:S(2)}, u32[]{:S(2)}) async-start(bf16[8,128,384]{2,1,0:T(8,128)(2,1)} %get-tuple-element.28), calls=%async_computation.1 | async-start | bytes 1572864 | tf_op jit(solution)/shard_map/all_to_all | solution.py:672
  12.3 2.5 %shard_map.114 = (bf16[208,128]{1,0:T(8,128)(2,1)}, bf16[208,128]{1,0:T(8,128)(2,1)}, bf16[208,128]{1,0:T(8,128)(2,1)}, bf16[208,128]{1,0:T(8,128)(2,1)}) custom-call(s32[6]{0:T(128)} %pad_add_fusion.meta_ref, s32[1,128]{1,0:T(1,128)} %tokens_ref.3, bf16[128,768]{1,0:T(8,128)(2,1)} %bitcast.8, bf16[768,768]{1,0:T(8,128)(2,1)} %out_weights_ref.1), custom_call_target="tpu_custom_call" | custom-call | flops 100000000 | bytes 1000000 | tf_op jit(solution)/shard_map/pallas_call | solution.py:635
  15.1 1.2 %collective-permute-start.2 = (bf16[208,128]{1,0:T(8,128)(2,1)}, bf16[208,128]{1,0:T(8,128)(2,1)S(1)}, u32[]{:S(2)}, u32[]{:S(2)}) collective-permute-start(bf16[208,128]{1,0:T(8,128)(2,1)} %get-tuple-element.22), channel_id=1, source_target_pairs={{0,3},{1,2},{2,1},{3,0},{4,7},{5,6},{6,5},{7,4},{8,11},{9,10},{10,... | collective-permute-start | bytes 159752 | tf_op jit(solution)/shard_map/ppermute | solution.py:595
  16.3 1.2 %collective-permute-start.1 = (bf16[208,128]{1,0:T(8,128)(2,1)}, bf16[208,128]{1,0:T(8,128)(2,1)S(1)}, u32[]{:S(2)}, u32[]{:S(2)}) collective-permute-start(bf16[208,128]{1,0:T(8,128)(2,1)} %get-tuple-element.22), channel_id=1, source_target_pairs={{0,2},{1,3},{2,0},{3,1},{4,6},{5,7},{6,4},{7,5},{8,10},{9,11},{10,... | collective-permute-start | bytes 159752 | tf_op jit(solution)/shard_map/ppermute | solution.py:595
  17.7 2.1 %collective-permute-start.3 = (bf16[208,128]{1,0:T(8,128)(2,1)}, bf16[208,128]{1,0:T(8,128)(2,1)S(1)}, u32[]{:S(2)}, u32[]{:S(2)}) collective-permute-start(bf16[208,128]{1,0:T(8,128)(2,1)} %get-tuple-element.23), channel_id=1, source_target_pairs={{0,4},{1,5},{2,6},{3,7},{4,0},{5,1},{6,2},{7,3},{8,12},{9,13},{10,... | collective-permute-start | bytes 159752 | tf_op jit(solution)/shard_map/ppermute | solution.py:595
  19.8 1.2 %collective-permute-done.rest_1_ = bf16[208,128]{1,0:T(8,128)(2,1)S(1)} collective-permute-done((bf16[208,128]{1,0:T(8,128)(2,1)}, bf16[208,128]{1,0:T(8,128)(2,1)S(1)}, u32[]{:S(2)}, u32[]{:S(2)}) %collective-permute-start) | collective-permute-done | bytes 53280 | tf_op jit(solution)/shard_map/ppermute | solution.py:595
  21.1 4.4 %collective-permute-done.2.rest_3_ = bf16[208,128]{1,0:T(8,128)(2,1)S(1)} collective-permute-done((bf16[208,128]{1,0:T(8,128)(2,1)}, bf16[208,128]{1,0:T(8,128)(2,1)S(1)}, u32[]{:S(2)}, u32[]{:S(2)}) %collective-permute-start.2) | collective-permute-done | bytes 53280 | tf_op jit(solution)/shard_map/ppermute | solution.py:595
  26.6 9.2 %collective-permute-done.4.rest_5_ = bf16[208,128]{1,0:T(8,128)(2,1)S(1)} collective-permute-done((bf16[208,128]{1,0:T(8,128)(2,1)}, bf16[208,128]{1,0:T(8,128)(2,1)S(1)}, u32[]{:S(2)}, u32[]{:S(2)}) %collective-permute-start.4) | collective-permute-done | bytes 53280 | tf_op jit(solution)/shard_map/ppermute | solution.py:595
  35.8 1.7 %collective-permute-done.3.rest_4_ = bf16[208,128]{1,0:T(8,128)(2,1)S(1)} collective-permute-done((bf16[208,128]{1,0:T(8,128)(2,1)}, bf16[208,128]{1,0:T(8,128)(2,1)S(1)}, u32[]{:S(2)}, u32[]{:S(2)}) %collective-permute-start.3) | collective-permute-done | bytes 53280 | tf_op jit(solution)/shard_map/ppermute | solution.py:595
  38.4 15.6 %shard_map.115 = (bf16[4,576,128]{2,1,0:T(8,128)(2,1)}, bf16[2,576,128]{2,1,0:T(8,128)(2,1)S(1)}, bf16[192,1024]{1,0:T(8,128)(2,1)S(1)}) custom-call(s32[6]{0:T(128)S(1)} %copy-done.4, bf16[2,576,256]{2,1,0:T(8,128)(2,1)S(1)} %copy-done.6, f32[32,1024]{1,0:T(8,128)S(1)} %copy-done.10, f32[32,1024]{1,0:T(8,128)S(1)} %copy-done.9, ...), custom_call_target="tpu_custom_call" | custom-call | flops 8000000000 | bytes 8000000 | tf_op jit(solution)/shard_map/pallas_call | solution.py:635
  54.1 5.9 %all-to-all-start = ((bf16[4,576,128]{2,1,0:T(8,128)(2,1)}), bf16[4,576,128]{2,1,0:T(8,128)(2,1)S(1)}, u32[]{:S(2)}, u32[]{:S(2)}) async-start(bf16[4,576,128]{2,1,0:T(8,128)(2,1)} %get-tuple-element.25), calls=%async_computation | async-start | bytes 1179648 | tf_op jit(solution)/shard_map/all_to_all | solution.py:703
  60.9 1.5 %collective-permute-start.7 = (bf16[864,128]{1,0:T(8,128)(2,1)S(1)}, bf16[864,128]{1,0:T(8,128)(2,1)S(1)}, u32[]{:S(2)}, u32[]{:S(2)}) collective-permute-start(bf16[864,128]{1,0:T(8,128)(2,1)S(1)} %get-tuple-element.31), channel_id=1, source_target_pairs={{0,8},{8,0},{16,24},{24,16},{1,9},{9,1},{17,25},{25,17},{2,10},{10... | collective-permute-start | bytes 663560 | tf_op jit(solution)/shard_map/ppermute | solution.py:595
  64.3 1.2 %collective-permute-start.8 = (bf16[864,128]{1,0:T(8,128)(2,1)}, bf16[864,128]{1,0:T(8,128)(2,1)}, u32[]{:S(2)}, u32[]{:S(2)}) collective-permute-start(bf16[864,128]{1,0:T(8,128)(2,1)} %add.17.here_ref), channel_id=1, source_target_pairs={{0,16},{8,24},{16,0},{24,8},{1,17},{9,25},{17,1},{25,9},{2,18},{10... | collective-permute-start | bytes 663560 | tf_op jit(solution)/shard_map/ppermute | solution.py:595
  65.5 6.9 %all-to-all-done.rows_ref.after_ref = bf16[4,576,128]{2,1,0:T(8,128)(2,1)S(1)} async-done(((bf16[4,576,128]{2,1,0:T(8,128)(2,1)}), bf16[4,576,128]{2,1,0:T(8,128)(2,1)S(1)}, u32[]{:S(2)}, u32[]{:S(2)}) %all-to-all-start) | async-done | bytes 589856 | tf_op jit(solution)/shard_map/all_to_all | solution.py:703
  73.9 3.0 %collective-permute-start.10 = (bf16[288,128]{1,0:T(8,128)(2,1)S(1)}, bf16[288,128]{1,0:T(8,128)(2,1)S(1)}, u32[]{:S(2)}, u32[]{:S(2)}) collective-permute-start(bf16[288,128]{1,0:T(8,128)(2,1)S(1)} %get-tuple-element.34), channel_id=1, source_target_pairs={{0,4},{1,5},{2,6},{3,7},{4,0},{5,1},{6,2},{7,3},{8,12},{9,13},{10,... | collective-permute-start | bytes 221192 | tf_op jit(solution)/shard_map/ppermute | solution.py:595
  77.2 2.3 %collective-permute-done.10.g2 = bf16[288,128]{1,0:T(8,128)(2,1)S(1)} collective-permute-done((bf16[288,128]{1,0:T(8,128)(2,1)S(1)}, bf16[288,128]{1,0:T(8,128)(2,1)S(1)}, u32[]{:S(2)}, u32[]{:S(2)}) %collective-permute-start.10) | collective-permute-done | bytes 73760 | tf_op jit(solution)/shard_map/ppermute | solution.py:595
  79.5 3.1 %collective-permute-done.11.g3 = bf16[288,128]{1,0:T(8,128)(2,1)S(1)} collective-permute-done((bf16[288,128]{1,0:T(8,128)(2,1)S(1)}, bf16[288,128]{1,0:T(8,128)(2,1)S(1)}, u32[]{:S(2)}, u32[]{:S(2)}) %collective-permute-start.11) | collective-permute-done | bytes 73760 | tf_op jit(solution)/shard_map/ppermute | solution.py:595
  83.2 2.0 %collective-permute-start.13 = (bf16[576,128]{1,0:T(8,128)(2,1)S(1)}, bf16[576,128]{1,0:T(8,128)(2,1)S(1)}, u32[]{:S(2)}, u32[]{:S(2)}) collective-permute-start(bf16[576,128]{1,0:T(8,128)(2,1)S(1)} %get-tuple-element.37), channel_id=1, source_target_pairs={{6,7},{7,6},{14,15},{15,14},{22,23},{23,22},{30,31},{31,30}} | collective-permute-start | bytes 442376 | tf_op jit(solution)/shard_map/ppermute | solution.py:740
  85.2 2.7 %collective-permute-start.12 = (bf16[768,128]{1,0:T(8,128)(2,1)S(1)}, bf16[768,128]{1,0:T(8,128)(2,1)S(1)}, u32[]{:S(2)}, u32[]{:S(2)}) collective-permute-start(bf16[768,128]{1,0:T(8,128)(2,1)S(1)} %get-tuple-element.36.mine_ref), channel_id=1, source_target_pairs={{0,8},{8,0},{16,24},{24,16},{1,9},{9,1},{17,25},{25,17},{2,10},{10... | collective-permute-start | bytes 589832 | tf_op jit(solution)/shard_map/ppermute | solution.py:595
  89.1 5.4 %collective-permute-start.14 = (bf16[576,128]{1,0:T(8,128)(2,1)S(1)}, bf16[576,128]{1,0:T(8,128)(2,1)S(1)}, u32[]{:S(2)}, u32[]{:S(2)}) collective-permute-start(bf16[576,128]{1,0:T(8,128)(2,1)S(1)} %collective-permute-done.13.near_ref), channel_id=1, source_target_pairs={{6,14},{7,15},{14,6},{15,7},{22,30},{23,31},{30,22},{31,23}} | collective-permute-start | bytes 442376 | tf_op jit(solution)/shard_map/ppermute | solution.py:742
  94.6 1.3 %copy-done.2 = bf16[768,768]{1,0:T(8,128)(2,1)S(1)} copy-done((bf16[768,768]{1,0:T(8,128)(2,1)S(1)}, bf16[768,768]{1,0:T(8,128)(2,1)}, u32[]{:S(2)}) %copy-start.2) | copy-done | bytes 1179672
  95.9 1.9 %shard_map.116 = bf16[128,768]{1,0:T(8,128)(2,1)} custom-call(s32[1,128]{1,0:T(1,128)S(1)} %copy-done.5, bf16[256,768]{1,0:T(8,128)(2,1)S(1)} %copy-done.3, bf16[768,768]{1,0:T(8,128)(2,1)S(1)} %copy-done, bf16[768,768]{1,0:T(8,128)(2,1)S(1)} %copy-done.1, bf16[768,768]{1,0:T(8,128)(2,1)S(1)} %copy-done.2, ...), custom_call_target="tpu_custom_call" | custom-call | flops 1000000000 | bytes 5000000 | tf_op jit(solution)/shard_map/pallas_call | solution.py:635
  97.9 1.7 %shard_map.120 = f32[384,768]{1,0:T(8,128)} custom-call(s32[6]{0:T(128)S(1)} %copy-done.4, bf16[256,384]{1,0:T(8,128)(2,1)S(1)} %copy-done.7, bf16[768,128]{1,0:T(8,128)(2,1)S(1)} %get-tuple-element.36.mine_ref, bf16[768,128]{1,0:T(8,128)(2,1)S(1)} %collective-permute-done.12.other_ref, bf16[576,128]{1,0:T(8,128)(2,1)S(1)} %collective-permute-done.13.near_ref, ...), custom_call_target="tpu_custom_call" | custom-call | flops 1000000000 | bytes 5000000 | tf_op jit(solution)/shard_map/pallas_call | solution.py:635
  (43 shorter events, 10.3 us)
Async XLA Ops:
  6.7 30.9 %copy-start.6 = (bf16[2,576,256]{2,1,0:T(8,128)(2,1)S(1)}, bf16[2,576,256]{2,1,0:T(8,128)(2,1)}, u32[]{:S(2)}) copy-start(bf16[2,576,256]{2,1,0:T(8,128)(2,1)} %get-tuple-element.20.lookup_ref) | copy-start | bytes 1769476
  6.7 31.0 %copy-start.9 = (f32[32,1024]{1,0:T(8,128)S(1)}, f32[32,1024]{1,0:T(8,128)}, u32[]{:S(2)}) copy-start(f32[32,1024]{1,0:T(8,128)} %constant.46.clone.sine_ref) | copy-start | bytes 393220
  6.7 31.0 %copy-start.10 = (f32[32,1024]{1,0:T(8,128)S(1)}, f32[32,1024]{1,0:T(8,128)}, u32[]{:S(2)}) copy-start(f32[32,1024]{1,0:T(8,128)} %constant.45.clone.cosine_ref) | copy-start | bytes 393220
  6.7 47.4 %all-to-all-start.1 = ((bf16[8,128,384]{2,1,0:T(8,128)(2,1)}), bf16[8,128,384]{2,1,0:T(8,128)(2,1)S(1)}, u32[]{:S(2)}, u32[]{:S(2)}) async-start(bf16[8,128,384]{2,1,0:T(8,128)(2,1)} %get-tuple-element.28), calls=%async_computation.1 | async-start | bytes 1572864 | tf_op jit(solution)/shard_map/all_to_all | solution.py:672
  14.8 6.3 %collective-permute-start = (bf16[208,128]{1,0:T(8,128)(2,1)}, bf16[208,128]{1,0:T(8,128)(2,1)S(1)}, u32[]{:S(2)}, u32[]{:S(2)}) collective-permute-start(bf16[208,128]{1,0:T(8,128)(2,1)} %get-tuple-element.21.rest_0_), channel_id=1, source_target_pairs={{0,1},{1,0},{2,3},{3,2},{4,5},{5,4},{6,7},{7,6},{8,9},{9,8},{10,11... | collective-permute-start | bytes 159752 | tf_op jit(solution)/shard_map/ppermute | solution.py:595
  15.1 10.4 %collective-permute-start.2 = (bf16[208,128]{1,0:T(8,128)(2,1)}, bf16[208,128]{1,0:T(8,128)(2,1)S(1)}, u32[]{:S(2)}, u32[]{:S(2)}) collective-permute-start(bf16[208,128]{1,0:T(8,128)(2,1)} %get-tuple-element.22), channel_id=1, source_target_pairs={{0,3},{1,2},{2,1},{3,0},{4,7},{5,6},{6,5},{7,4},{8,11},{9,10},{10,... | collective-permute-start | bytes 159752 | tf_op jit(solution)/shard_map/ppermute | solution.py:595
  16.3 10.4 %collective-permute-start.1 = (bf16[208,128]{1,0:T(8,128)(2,1)}, bf16[208,128]{1,0:T(8,128)(2,1)S(1)}, u32[]{:S(2)}, u32[]{:S(2)}) collective-permute-start(bf16[208,128]{1,0:T(8,128)(2,1)} %get-tuple-element.22), channel_id=1, source_target_pairs={{0,2},{1,3},{2,0},{3,1},{4,6},{5,7},{6,4},{7,5},{8,10},{9,11},{10,... | collective-permute-start | bytes 159752 | tf_op jit(solution)/shard_map/ppermute | solution.py:595
  17.5 18.4 %collective-permute-start.4 = (bf16[208,128]{1,0:T(8,128)(2,1)}, bf16[208,128]{1,0:T(8,128)(2,1)S(1)}, u32[]{:S(2)}, u32[]{:S(2)}) collective-permute-start(bf16[208,128]{1,0:T(8,128)(2,1)} %get-tuple-element.23), channel_id=1, source_target_pairs={{0,5},{1,4},{2,7},{3,6},{4,1},{5,0},{6,3},{7,2},{8,13},{9,12},{10,... | collective-permute-start | bytes 159752 | tf_op jit(solution)/shard_map/ppermute | solution.py:595
  17.7 19.9 %collective-permute-start.3 = (bf16[208,128]{1,0:T(8,128)(2,1)}, bf16[208,128]{1,0:T(8,128)(2,1)S(1)}, u32[]{:S(2)}, u32[]{:S(2)}) collective-permute-start(bf16[208,128]{1,0:T(8,128)(2,1)} %get-tuple-element.23), channel_id=1, source_target_pairs={{0,4},{1,5},{2,6},{3,7},{4,0},{5,1},{6,2},{7,3},{8,12},{9,13},{10,... | collective-permute-start | bytes 159752 | tf_op jit(solution)/shard_map/ppermute | solution.py:595
  21.1 16.5 %collective-permute-start.6 = (bf16[208,128]{1,0:T(8,128)(2,1)}, bf16[208,128]{1,0:T(8,128)(2,1)S(1)}, u32[]{:S(2)}, u32[]{:S(2)}) collective-permute-start(bf16[208,128]{1,0:T(8,128)(2,1)} %get-tuple-element.24), channel_id=1, source_target_pairs={{0,7},{1,6},{2,5},{3,4},{4,3},{5,2},{6,1},{7,0},{8,15},{9,14},{10,... | collective-permute-start | bytes 159752 | tf_op jit(solution)/shard_map/ppermute | solution.py:595
  25.5 12.1 %collective-permute-start.5 = (bf16[208,128]{1,0:T(8,128)(2,1)}, bf16[208,128]{1,0:T(8,128)(2,1)S(1)}, u32[]{:S(2)}, u32[]{:S(2)}) collective-permute-start(bf16[208,128]{1,0:T(8,128)(2,1)} %get-tuple-element.24), channel_id=1, source_target_pairs={{0,6},{1,7},{2,4},{3,5},{4,2},{5,3},{6,0},{7,1},{8,14},{9,15},{10,... | collective-permute-start | bytes 159752 | tf_op jit(solution)/shard_map/ppermute | solution.py:595
  54.1 18.4 %all-to-all-start = ((bf16[4,576,128]{2,1,0:T(8,128)(2,1)}), bf16[4,576,128]{2,1,0:T(8,128)(2,1)S(1)}, u32[]{:S(2)}, u32[]{:S(2)}) async-start(bf16[4,576,128]{2,1,0:T(8,128)(2,1)} %get-tuple-element.25), calls=%async_computation | async-start | bytes 1179648 | tf_op jit(solution)/shard_map/all_to_all | solution.py:703
  60.0 34.6 %copy-start.1 = (bf16[768,768]{1,0:T(8,128)(2,1)S(1)}, bf16[768,768]{1,0:T(8,128)(2,1)}, u32[]{:S(2)}) copy-start(bf16[768,768]{1,0:T(8,128)(2,1)} %key_ref.3) | copy-start | bytes 3538948
  60.9 33.7 %copy-start = (bf16[768,768]{1,0:T(8,128)(2,1)S(1)}, bf16[768,768]{1,0:T(8,128)(2,1)}, u32[]{:S(2)}) copy-start(bf16[768,768]{1,0:T(8,128)(2,1)} %query_ref.3) | copy-start | bytes 3538948
  60.9 33.7 %copy-start.3 = (bf16[256,768]{1,0:T(8,128)(2,1)S(1)}, bf16[256,768]{1,0:T(8,128)(2,1)}, u32[]{:S(2)}) copy-start(bf16[256,768]{1,0:T(8,128)(2,1)} %table_ref.3) | copy-start | bytes 1179652
  60.9 33.7 %copy-start.5 = (s32[1,128]{1,0:T(1,128)S(1)}, s32[1,128]{1,0:T(1,128)}, u32[]{:S(2)}) copy-start(s32[1,128]{1,0:T(1,128)} %tokens_ref.3) | copy-start | bytes 1540
  60.9 2.6 %collective-permute-start.7 = (bf16[864,128]{1,0:T(8,128)(2,1)S(1)}, bf16[864,128]{1,0:T(8,128)(2,1)S(1)}, u32[]{:S(2)}, u32[]{:S(2)}) collective-permute-start(bf16[864,128]{1,0:T(8,128)(2,1)S(1)} %get-tuple-element.31), channel_id=1, source_target_pairs={{0,8},{8,0},{16,24},{24,16},{1,9},{9,1},{17,25},{25,17},{2,10},{10... | collective-permute-start | bytes 663560 | tf_op jit(solution)/shard_map/ppermute | solution.py:595
  64.3 8.1 %collective-permute-start.8 = (bf16[864,128]{1,0:T(8,128)(2,1)}, bf16[864,128]{1,0:T(8,128)(2,1)}, u32[]{:S(2)}, u32[]{:S(2)}) collective-permute-start(bf16[864,128]{1,0:T(8,128)(2,1)} %add.17.here_ref), channel_id=1, source_target_pairs={{0,16},{8,24},{16,0},{24,8},{1,17},{9,25},{17,1},{25,9},{2,18},{10... | collective-permute-start | bytes 663560 | tf_op jit(solution)/shard_map/ppermute | solution.py:595
  73.6 3.6 %collective-permute-start.9 = (bf16[288,128]{1,0:T(8,128)(2,1)S(1)}, bf16[288,128]{1,0:T(8,128)(2,1)S(1)}, u32[]{:S(2)}, u32[]{:S(2)}) collective-permute-start(bf16[288,128]{1,0:T(8,128)(2,1)S(1)} %get-tuple-element.33), channel_id=1, source_target_pairs={{0,2},{1,3},{2,0},{3,1},{4,6},{5,7},{6,4},{7,5},{8,10},{9,11},{10,... | collective-permute-start | bytes 221192 | tf_op jit(solution)/shard_map/ppermute | solution.py:595
  73.9 5.6 %collective-permute-start.10 = (bf16[288,128]{1,0:T(8,128)(2,1)S(1)}, bf16[288,128]{1,0:T(8,128)(2,1)S(1)}, u32[]{:S(2)}, u32[]{:S(2)}) collective-permute-start(bf16[288,128]{1,0:T(8,128)(2,1)S(1)} %get-tuple-element.34), channel_id=1, source_target_pairs={{0,4},{1,5},{2,6},{3,7},{4,0},{5,1},{6,2},{7,3},{8,12},{9,13},{10,... | collective-permute-start | bytes 221192 | tf_op jit(solution)/shard_map/ppermute | solution.py:595
  76.9 5.8 %collective-permute-start.11 = (bf16[288,128]{1,0:T(8,128)(2,1)S(1)}, bf16[288,128]{1,0:T(8,128)(2,1)S(1)}, u32[]{:S(2)}, u32[]{:S(2)}) collective-permute-start(bf16[288,128]{1,0:T(8,128)(2,1)S(1)} %get-tuple-element.35), channel_id=1, source_target_pairs={{0,6},{1,7},{2,4},{3,5},{4,2},{5,3},{6,0},{7,1},{8,14},{9,15},{10,... | collective-permute-start | bytes 221192 | tf_op jit(solution)/shard_map/ppermute | solution.py:595
  83.2 5.9 %collective-permute-start.13 = (bf16[576,128]{1,0:T(8,128)(2,1)S(1)}, bf16[576,128]{1,0:T(8,128)(2,1)S(1)}, u32[]{:S(2)}, u32[]{:S(2)}) collective-permute-start(bf16[576,128]{1,0:T(8,128)(2,1)S(1)} %get-tuple-element.37), channel_id=1, source_target_pairs={{6,7},{7,6},{14,15},{15,14},{22,23},{23,22},{30,31},{31,30}} | collective-permute-start | bytes 442376 | tf_op jit(solution)/shard_map/ppermute | solution.py:740
  85.2 12.6 %collective-permute-start.12 = (bf16[768,128]{1,0:T(8,128)(2,1)S(1)}, bf16[768,128]{1,0:T(8,128)(2,1)S(1)}, u32[]{:S(2)}, u32[]{:S(2)}) collective-permute-start(bf16[768,128]{1,0:T(8,128)(2,1)S(1)} %get-tuple-element.36.mine_ref), channel_id=1, source_target_pairs={{0,8},{8,0},{16,24},{24,16},{1,9},{9,1},{17,25},{25,17},{2,10},{10... | collective-permute-start | bytes 589832 | tf_op jit(solution)/shard_map/ppermute | solution.py:595
  89.1 8.7 %collective-permute-start.14 = (bf16[576,128]{1,0:T(8,128)(2,1)S(1)}, bf16[576,128]{1,0:T(8,128)(2,1)S(1)}, u32[]{:S(2)}, u32[]{:S(2)}) collective-permute-start(bf16[576,128]{1,0:T(8,128)(2,1)S(1)} %collective-permute-done.13.near_ref), channel_id=1, source_target_pairs={{6,14},{7,15},{14,6},{15,7},{22,30},{23,31},{30,22},{31,23}} | collective-permute-start | bytes 442376 | tf_op jit(solution)/shard_map/ppermute | solution.py:742
  (4 other events, 35.0 us)

commit v6 on v5

--- a/solution.py
+++ b/solution.py
@@ -227,6 +227,7 @@
 GROUP_COLS = GROUP_HEADS * HEAD_DIM
 TILE = 256
 TOKEN_ROWS = 16
+STRIP = 8
 HALF = HEAD_DIM // 2
 VMEM_BYTES = 48 * 1024 * 1024
 
@@ -247,7 +248,7 @@
     return (rows == tokens).astype(jnp.float32).astype(jnp.bfloat16)
 
 
-def send_kernel(meta_ref, tokens_ref, cotangent_ref, out_weights_ref, *out_refs):
+def send_kernel(spot_ref, tokens_ref, cotangent_ref, out_weights_ref, *out_refs):
     early_refs, grads_ref = out_refs[:-1], out_refs[-1]
     grad_att = ndot(out_weights_ref[...], cotangent_ref[...]).astype(jnp.bfloat16)
     grads_ref[...] = grad_att
@@ -256,10 +257,14 @@
         jnp.bfloat16
     )
     for turn, early_ref in enumerate(early_refs):
-        group = meta_ref[GROUP_HEADS + 1] ^ turn
+        group = spot_ref[1] ^ turn
         place = pl.ds(pl.multiple_of(group * GROUP_COLS, GROUP_COLS), GROUP_COLS)
         early_ref[:GROUP_COLS, :] = grads_ref[place, :]
         early_ref[GROUP_COLS:, :] = tokens
+
+
+def gate_kernel(*refs):
+    del refs
 
 
 def prepare_kernel(
@@ -313,27 +318,32 @@
     rows_ref,
     sums_ref,
     attended_ref,
-    query_key_ref,
-    zero_query_ref,
+    value_key_ref,
+    query_t_ref,
     key_t_ref,
     value_t_ref,
     grad_att_ref,
     onehot_ref,
+    onehot_rows_ref,
     grad_query_ref,
     both_ref,
-    value_grad_ref,
+    scaled_ref,
     probs_ref,
     scores_ref,
+    right_ref,
+    products_ref,
+    inverse_ref,
+    term_ref,
 ):
     head = pl.program_id(0)
     block = early_refs[0].shape[1]
     length = len(early_refs) * block
+    tiles = length // TILE
     vocab = lookup_ref.shape[2]
     half_vocab = vocab // 2
     half = jnp.bfloat16
     cosine = cosine_ref[...]
     sine_part = sine_ref[...]
-    blank = jnp.zeros((HEAD_DIM, length), half)
 
     @pl.when(head == 0)
     def _():
@@ -347,12 +357,15 @@
                 GROUP_HEADS, HEAD_DIM, block
             )
         onehot = onehot_ref[...]
-
-        def chosen(start):
-            rows = slice(start, start + HEAD_DIM)
-            return jnp.dot(
-                lookup_ref[0, rows, :], onehot, preferred_element_type=jnp.float32
-            ) + jnp.dot(lookup_ref[1, rows, :], onehot, preferred_element_type=jnp.float32)
+        onehot_rows_ref[...] = onehot.T
+        size = 3 * GROUP_COLS
+        chosen = jnp.dot(
+            lookup_ref[...].reshape(2 * size, vocab), onehot, preferred_element_type=jnp.float32
+        )
+
+        def picked(start):
+            lower = start + size
+            return chosen[start : start + HEAD_DIM] + chosen[lower : lower + HEAD_DIM]
 
         def turned(columns):
             former = columns[:HALF]
@@ -362,79 +375,118 @@
             )
 
         for index in range(GROUP_HEADS):
-            query = (turned(chosen(index * HEAD_DIM)) * HEAD_DIM ** (-0.5)).astype(half)
-            keys = turned(chosen(GROUP_COLS + index * HEAD_DIM)).astype(half)
-            values = chosen(2 * GROUP_COLS + index * HEAD_DIM).astype(half)
-            query_key_ref[index] = jnp.concatenate([query, keys], axis=0).T
-            zero_query_ref[index] = jnp.concatenate([blank, query], axis=0)
+            query = turned(picked(index * HEAD_DIM)) * HEAD_DIM ** (-0.5)
+            keys = turned(picked(GROUP_COLS + index * HEAD_DIM)).astype(half)
+            values = picked(2 * GROUP_COLS + index * HEAD_DIM).astype(half)
+            value_key_ref[index] = jnp.concatenate([values, keys], axis=0).T
+            query_t_ref[index] = query.astype(half)
             key_t_ref[index] = keys
             value_t_ref[index] = values
 
     width = meta_ref[head]
     grad_att = grad_att_ref[head]
-    wide_grad = grad_att.astype(jnp.float32)
-    grad_blank = jnp.concatenate([grad_att, blank], axis=0)
-    value_grad_ref[...] = jnp.concatenate([value_t_ref[head], grad_att], axis=0).T
-    distance = lax.broadcasted_iota(jnp.int32, (TILE, TILE), 1) - lax.broadcasted_iota(
-        jnp.int32, (TILE, TILE), 0
-    )
-    for query_tile in range(length // TILE):
-        first, count = key_span(query_tile)
-        columns = slice(query_tile * TILE, (query_tile + 1) * TILE)
-        scores = jnp.dot(
-            query_key_ref[head, first : first + count, :],
-            zero_query_ref[head, :, columns],
+    query_t = query_t_ref[head]
+    blank = jnp.zeros((HEAD_DIM, TILE), half)
+    base = lax.broadcasted_iota(jnp.int32, (STRIP, TILE), 1) - lax.broadcasted_iota(
+        jnp.int32, (STRIP, TILE), 0
+    )
+    for tile in range(tiles):
+        columns = slice(tile * TILE, (tile + 1) * TILE)
+        right_ref[tile, :HEAD_DIM, :TILE] = grad_att[:, columns]
+        right_ref[tile, HEAD_DIM:, :TILE] = blank
+        right_ref[tile, :HEAD_DIM, TILE:] = blank
+        right_ref[tile, HEAD_DIM:, TILE:] = query_t[:, columns]
+
+    def multiply(tile):
+        first, count = key_span(tile)
+        products_ref[tile, :count, :] = jnp.dot(
+            value_key_ref[head, first : first + count, :],
+            right_ref[tile],
             preferred_element_type=jnp.float32,
         )
-        masked = []
-        for key_tile in range(count // TILE):
-            offset = query_tile * TILE - first - key_tile * TILE
-            allowed = distance < width - offset
-            if offset == 0:
-                allowed = allowed & (distance >= 0)
-            part = scores[key_tile * TILE : (key_tile + 1) * TILE]
-            masked.append(jnp.where(allowed, part, -1e30))
-        masked = jnp.concatenate(masked, axis=0)
-        row_max = jnp.max(masked, axis=0, keepdims=True)
-        weights = jnp.exp(masked - row_max)
-        probs = weights * (1.0 / jnp.sum(weights, axis=0, keepdims=True))
-        rounded = probs.astype(half)
-        probs_ref[first : first + count, columns] = rounded
-        attended = jnp.dot(
-            value_t_ref[head, :, first : first + count], rounded, preferred_element_type=jnp.float32
+
+    def forward(tile):
+        first, count = key_span(tile)
+        columns = slice(tile * TILE, (tile + 1) * TILE)
+        row_max = None
+        for row in range(0, count, STRIP):
+            offset = tile * TILE - first - row
+            allowed = base < width - offset
+            if offset - STRIP < 0:
+                allowed = allowed & (base >= -offset)
+            masked = jnp.where(allowed, products_ref[tile, row : row + STRIP, TILE:], -1e30)
+            products_ref[tile, row : row + STRIP, TILE:] = masked
+            row_max = masked if row_max is None else jnp.maximum(row_max, masked)
+        row_max = jnp.max(row_max, axis=0, keepdims=True)
+        total = None
+        for row in range(0, count, 2 * STRIP):
+            weights = jnp.exp(products_ref[tile, row : row + 2 * STRIP, TILE:] - row_max)
+            total = weights if total is None else total + weights
+            probs_ref[first + row : first + row + 2 * STRIP, columns] = weights.astype(half)
+        inverse = 1.0 / jnp.sum(total, axis=0, keepdims=True)
+        attended = inverse * jnp.dot(
+            value_t_ref[head, :, first : first + count],
+            probs_ref[first : first + count, columns],
+            preferred_element_type=jnp.float32,
         )
         attended_ref[pl.ds(pl.multiple_of(head * HEAD_DIM, HEAD_DIM), HEAD_DIM), columns] = (
-            attended.astype(jnp.bfloat16)
-        )
-        row_term = jnp.sum(attended * wide_grad[:, columns], axis=0, keepdims=True)
-        grad_probs = jnp.dot(
-            value_grad_ref[first : first + count, :],
-            grad_blank[:, columns],
+            attended.astype(half)
+        )
+        wide_grad = grad_att[:, columns].astype(jnp.float32)
+        inverse_ref[:, columns] = inverse
+        term_ref[:, columns] = jnp.sum(attended * wide_grad, axis=0, keepdims=True)
+        scaled_ref[columns, :] = jnp.concatenate(
+            [
+                (inverse * query_t[:, columns].astype(jnp.float32)).astype(half),
+                (inverse * wide_grad).astype(half),
+            ],
+            axis=0,
+        ).T
+
+    def backward(tile):
+        first, count = key_span(tile)
+        columns = slice(tile * TILE, (tile + 1) * TILE)
+        row_term = term_ref[:, columns]
+        for row in range(0, count, 2 * STRIP):
+            strip = slice(first + row, first + row + 2 * STRIP)
+            scores_ref[strip, columns] = (
+                probs_ref[strip, columns].astype(jnp.float32)
+                * (products_ref[tile, row : row + 2 * STRIP, :TILE] - row_term)
+            ).astype(half)
+        grad_query_ref[:, columns] = inverse_ref[:, columns] * jnp.dot(
+            key_t_ref[head, :, first : first + count],
+            scores_ref[first : first + count, columns],
             preferred_element_type=jnp.float32,
         )
-        grad_scores = (probs * (grad_probs - row_term)).astype(jnp.bfloat16)
-        grad_query_ref[:, columns] = jnp.dot(
-            key_t_ref[head, :, first : first + count],
-            grad_scores,
-            preferred_element_type=jnp.float32,
-        )
-        scores_ref[first : first + count, columns] = grad_scores
+
     lanes = lax.broadcasted_iota(jnp.int32, (TILE, 2 * HEAD_DIM), 1)
-    for key_tile in range(length // TILE):
-        start = key_tile * TILE
+
+    def collect(tile):
+        start = tile * TILE
         stop = min(length, start + TILE + WINDOW)
         grad_key = jnp.dot(
             scores_ref[start : start + TILE, start:stop],
-            query_key_ref[head, start:stop, :],
+            scaled_ref[start:stop, :],
             preferred_element_type=jnp.float32,
         )
         grad_value = jnp.dot(
             probs_ref[start : start + TILE, start:stop],
-            value_grad_ref[start:stop, :],
+            scaled_ref[start:stop, :],
             preferred_element_type=jnp.float32,
         )
         both_ref[:, start : start + TILE] = jnp.where(lanes < HEAD_DIM, grad_key, grad_value).T
 
+    reach = WINDOW // TILE
+    for step in range(tiles + 3 + reach):
+        if step < tiles:
+            multiply(step)
+        if 0 <= step - 1 < tiles:
+            forward(step - 1)
+        if 0 <= step - 2 < tiles:
+            backward(step - 2)
+        ready = step - 3 - reach
+        if 0 <= ready < tiles:
+            collect(ready)
     def turned_back(columns):
         former = columns[:HALF]
         latter = columns[HALF:]
@@ -450,8 +502,8 @@
             both[HEAD_DIM:],
         ],
         axis=0,
-    ).astype(jnp.bfloat16)
-    sums = ndot(grads, onehot_ref[...]).astype(jnp.bfloat16)
+    ).astype(half)
+    sums = jnp.dot(grads, onehot_rows_ref[...], preferred_element_type=jnp.float32).astype(half)
     for matrix in range(3):
         rows = slice(matrix * HEAD_DIM, (matrix + 1) * HEAD_DIM)
         place = pl.ds(
@@ -482,45 +534,44 @@
         give_ref[place, :] = jnp.where(first, part[rows:], part[:rows]).astype(jnp.bfloat16)
 
 
-def combine_kernel(meta_ref, here_ref, there_ref, after_ref, *piece_refs):
+def core_kernel(keep_ref, got_ref, here_ref, out_ref):
+    here_ref[...] = keep_ref[...] + got_ref[...]
+    base = here_ref.shape[0] - out_ref.shape[0]
+    out_ref[...] = here_ref[base:, :]
+
+
+def combine_kernel(meta_ref, here_ref, there_ref, near_ref, far_ref, out_ref, *piece_refs):
+    rows = GROUP_COLS
+    for turn, piece_ref in enumerate(piece_refs):
+        target = jnp.minimum(meta_ref[GROUP_HEADS + 1] ^ turn, 2)
+        place = pl.ds(pl.multiple_of(target * rows, rows), rows)
+        piece_ref[...] = here_ref[place, :] + there_ref[place, :]
+    own = here_ref[3 * rows :, :] + there_ref[3 * rows :, :]
+    other = near_ref[...] + far_ref[...]
+    first = meta_ref[GROUP_HEADS] == 0
+    size = own.shape[0]
+    out_ref[:size, :] = jnp.where(first, own, other)
+    out_ref[size:, :] = jnp.where(first, other, own)
+
+
+def gather_kernel(meta_ref, s0, s1, s2, s3, own_ref, o0, o1, after_ref, mine_ref):
     del after_ref
     rows = GROUP_COLS
-    for turn, piece_ref in enumerate(piece_refs):
-        target = meta_ref[GROUP_HEADS + 1] ^ turn
-
-        @pl.when(target < 3)
-        def _(piece_ref=piece_ref, target=target):
-            place = pl.ds(pl.multiple_of(target * rows, rows), rows)
-            piece_ref[:rows, :] = here_ref[place, :] + there_ref[place, :]
-            tail = piece_ref.shape[0] - rows
-            piece_ref[rows:, :] = jnp.zeros((tail, piece_ref.shape[1]), jnp.bfloat16)
-
-        @pl.when(target == 3)
-        def _(piece_ref=piece_ref):
-            piece_ref[...] = here_ref[3 * rows :, :] + there_ref[3 * rows :, :]
-
-
-def gather_kernel(meta_ref, g0, g1, g2, g3, mine_ref, other_ref):
-    rows = GROUP_COLS
-    size = g0.shape[0]
+    size = own_ref.shape[0]
     group = meta_ref[GROUP_HEADS + 1]
 
     @pl.when(group < 3)
     def _():
-        for turn, got in enumerate((g0, g1, g2, g3)):
+        for turn, got in enumerate((s0, s1, s2, s3)):
             place = pl.ds(pl.multiple_of((group ^ turn) * rows, rows), rows)
-            mine_ref[place, :] = got[:rows, :]
-        other_ref[...] = jnp.zeros_like(other_ref)
+            mine_ref[place, :] = got[...]
+        tail = mine_ref.shape[0] - GROUPS * rows
+        mine_ref[GROUPS * rows :, :] = jnp.zeros((tail, mine_ref.shape[1]), jnp.bfloat16)
 
     @pl.when(group == 3)
     def _():
-        first = meta_ref[GROUP_HEADS] == 0
-        for part, (low, high) in enumerate(((g3, g1), (g2, g0))):
-            place = slice(part * size, (part + 1) * size)
-            mine_ref[place, :] = jnp.where(first, low[...], high[...])
-            other_ref[place, :] = jnp.where(first, high[...], low[...])
-        tail = mine_ref.shape[0] - 2 * size
-        mine_ref[2 * size :, :] = jnp.zeros((tail, mine_ref.shape[1]), jnp.bfloat16)
+        mine_ref[:size, :] = o0[...]
+        mine_ref[size:, :] = jnp.where(meta_ref[GROUP_HEADS] == 0, o1[...], own_ref[...])
 
 
 def input_kernel(tokens_ref, table_ref, query_ref, key_ref, value_ref, rows_ref, out_ref):
@@ -545,7 +596,7 @@
     ).astype(jnp.bfloat16)
 
 
-def weight_kernel(meta_ref, normed_ref, mine_ref, other_ref, near_ref, far_ref, out_ref):
+def weight_kernel(meta_ref, normed_ref, mine_ref, other_ref, out_ref):
     half_vocab = mine_ref.shape[1]
     first_core = meta_ref[GROUP_HEADS + 2] == 0
 
@@ -559,7 +610,7 @@
         for part, sums_ref in ((upper, mine_ref), (lower, other_ref)):
             term = lax.dot_general(
                 part,
-                sums_ref[...],
+                sums_ref[: GROUPS * GROUP_COLS, :],
                 (((0,), (1,)), ((), ())),
                 preferred_element_type=jnp.float32,
             )
@@ -569,21 +620,18 @@
     @pl.when(meta_ref[GROUP_HEADS + 1] == 3)
     def _():
         rows = GROUP_COLS // 2
-        first_side = meta_ref[GROUP_HEADS] == 0
         for half in range(2):
-            for chunk in range(3):
-                place = slice((half * 3 + chunk) * rows, (half * 3 + chunk + 1) * rows)
+            for column in range(6):
+                start = (half * 6 + column) * rows
                 for core in range(2):
                     same = first_core == (core == 0)
-                    own = jnp.where(same, mine_ref[place, :], other_ref[place, :])
-                    crossed = jnp.where(same, near_ref[place, :], far_ref[place, :])
+                    value = jnp.where(
+                        same, mine_ref[start : start + rows, :], other_ref[start : start + rows, :]
+                    )
                     row = half * GROUP_COLS + core * rows
-                    for side in range(2):
-                        value = jnp.where(first_side == (side == 0), own, crossed)
-                        start = (side * 3 + chunk) * half_vocab
-                        out_ref[row : row + rows, start : start + half_vocab] = value.astype(
-                            jnp.float32
-                        )
+                    out_ref[
+                        row : row + rows, column * half_vocab : (column + 1) * half_vocab
+                    ] = value.astype(jnp.float32)
 
 
 def whole(shape):
@@ -622,6 +670,7 @@
             jnp.stack([side, group, core]).astype(jnp.int32),
         ]
     )
+    spot = jnp.stack([side, group, core]).astype(jnp.int32)
     cosine, sine_part = rope_table(length)
 
     def call(
@@ -648,7 +697,7 @@
     half = jnp.bfloat16
     sent = call(
         send_kernel,
-        (meta, token_ids, grad_out, w_out),
+        (spot, token_ids, grad_out, w_out),
         [((GROUP_COLS + TOKEN_ROWS, block), half)] * GROUPS,
         [pltpu.VMEM((features, block), half)],
         grant=60 * 1024 * 1024,
@@ -669,6 +718,13 @@
         moved=5 * 10**6,
         grant=60 * 1024 * 1024,
     )
+    late = pl.pallas_call(
+        gate_kernel,
+        in_specs=[pl.BlockSpec(memory_space=pl.ANY)] * blocks,
+        out_specs=pl.BlockSpec(memory_space=pl.ANY),
+        out_shape=jax.ShapeDtypeStruct(late.shape, half),
+        input_output_aliases={0: 0},
+    )(late, *early[1:])
     late = lax.all_to_all(late, "seq", split_axis=0, concat_axis=0, tiled=True)
     heads_shape = (GROUP_HEADS, HEAD_DIM, length)
     rows_shape = (GROUP_HEADS, length, 2 * HEAD_DIM)
@@ -682,16 +738,21 @@
         ],
         [
             pltpu.VMEM(rows_shape, half),
-            pltpu.VMEM((GROUP_HEADS, 2 * HEAD_DIM, length), half),
+            pltpu.VMEM(heads_shape, half),
             pltpu.VMEM(heads_shape, half),
             pltpu.VMEM(heads_shape, half),
             pltpu.VMEM(heads_shape, half),
             pltpu.VMEM((vocab, length), half),
+            pltpu.VMEM((length, vocab), half),
             pltpu.VMEM((HEAD_DIM, length), jnp.float32),
             pltpu.VMEM((2 * HEAD_DIM, length), jnp.float32),
             pltpu.VMEM((length, 2 * HEAD_DIM), half),
             pltpu.VMEM((length, length), half),
             pltpu.VMEM((length, length), half),
+            pltpu.VMEM((length // TILE, 2 * HEAD_DIM, 2 * TILE), half),
+            pltpu.VMEM((length // TILE, WINDOW + TILE, 2 * TILE), jnp.float32),
+            pltpu.VMEM((1, length), jnp.float32),
+            pltpu.VMEM((1, length), jnp.float32),
         ],
         steps=GROUP_HEADS,
         flops=8 * 10**9,
@@ -713,22 +774,37 @@
         (meta, attended, late.reshape(length, features // 2), sums),
         [((packed, lanes), half)] * 2,
     )
-    here = keep + swapped(give, "dp", 1)
+    here, here_out = call(
+        core_kernel,
+        (keep, swapped(give, "dp", 1)),
+        [((packed, lanes), half), ((out_rows, lanes), half)],
+    )
     there = swapped(here, "dp", 2)
-    pieces = call(
+    inward = [(2 * z + 1 - z // 2, 2 * z + z // 2) for z in range(GROUPS)]
+    near = lax.ppermute(here_out, "seq", inward)
+    far = lax.ppermute(
+        here_out,
+        ("dp", "seq"),
+        [
+            (blocks * d + source, blocks * (d ^ 2) + target)
+            for d in range(lax.axis_size("dp"))
+            for source, target in inward
+        ],
+    )
+    full_out, *pieces = call(
         combine_kernel,
-        (meta, here, there, got_rows),
-        [((out_rows, lanes), half)] * GROUPS,
-        loose=1,
-    )
+        (meta, here, there, near, far),
+        [((2 * out_rows, lanes), half)] + [((GROUP_COLS, lanes), half)] * GROUPS,
+    )
+    last = blocks - 2
+    got_out = [
+        lax.ppermute(full_out, "seq", [(0, last), (last - 1, last + 1)]),
+        lax.ppermute(full_out, "seq", [(2, last)]),
+    ]
     got = [pieces[0]] + [None] * (GROUPS - 1)
     for turn in (2, 3, 1):
-        got[turn] = swapped(pieces[turn], "seq", 2 * turn)
-    mine, other = call(
-        gather_kernel,
-        (meta, *got),
-        [((GROUPS * GROUP_COLS, lanes), half), ((2 * out_rows, lanes), half)],
-    )
+        route = [(i, i ^ (2 * turn)) for i in range(blocks) if (i ^ (2 * turn)) < last]
+        got[turn] = lax.ppermute(pieces[turn], "seq", route)
     (grad_input,) = call(
         input_kernel,
         (token_ids, table, w_query, w_key, w_value, got_rows),
@@ -736,21 +812,15 @@
         flops=10**9,
         moved=5 * 10**6,
     )
-    last = blocks - 2
-    near = lax.ppermute(other, "seq", [(last, last + 1), (last + 1, last)])
-    paired = swapped(mine, "dp", 1)
-    far = lax.ppermute(
-        near,
-        ("dp", "seq"),
-        [
-            (blocks * d + last + x, blocks * (d ^ 1) + last + x)
-            for d in range(lax.axis_size("dp"))
-            for x in range(2)
-        ],
+    (mine,) = call(
+        gather_kernel,
+        (meta, *got, full_out, *got_out, grad_input),
+        [((4 * out_rows, lanes), half)],
+        loose=1,
     )
     (weight_grads,) = call(
         weight_kernel,
-        (meta, normed, mine, paired, near, far),
+        (meta, normed, mine, swapped(mine, "dp", 1)),
         [((features // 2, features), jnp.float32)],
         flops=10**9,
         moved=5 * 10**6,

time: 100 us -> 95.2 us (0.952)
  the two profiles are of different devices: /device:TPU:27 before, /device:TPU:0 now
where the time goes in v6:
time: 95.2 us; the launch traced here: 94.5 us
  starting transfers between devices  38.2 us (40%)
  Pallas kernels  26.7 us (28%)
  waiting for transfers between devices  19.4 us (20%)
  local copies, waits for them, and re-layouts  7.83 us (8%)
  other arithmetic  1.26 us (1%)
  between operations  1.08 us (1%)
    pallas_call x9, Pallas kernels, call(): pl.pallas_call(body, grid=(steps,), in_specs=spaces, out_specs=[whole(sha...  26.7 us
    ppermute x10, starting transfers between devices, swapped(): return lax.ppermute(block, axis, route)  15.4 us
    unnamed x70, local copies, waits for them, and re-layouts  7.75 us
    ppermute x10, waiting for transfers between devices, swapped(): return lax.ppermute(block, axis, route)  6.8 us
    ppermute x3, starting transfers between devices, grouped_device(): got[turn] = lax.ppermute(pieces[turn], 'seq', route)  5.66 us
    ppermute x1, waiting for transfers between devices, grouped_device(): lax.ppermute(here_out, ('dp', 'seq'), [(blocks * d + source, blocks * (d...  5.14 us
    ppermute x1, starting transfers between devices, grouped_device(): lax.ppermute(full_out, 'seq', [(0, last), (last - 1, last + 1)])  5.13 us
    all_to_all x1, waiting for transfers between devices, grouped_device(): late = lax.all_to_all(late, 'seq', split_axis=0, concat_axis=0, tiled=True)  4.71 us
  transfers between devices with their start and end apart: 19, of which 8 were waited for; matrix products, arithmetic and copies ran while one was open for 1% of the time, Pallas kernels for 22%

profile of v6, /device:TPU:0, one launch (start us, length us, event | category | flops | bytes accessed | tf_op | source)
XLA Modules:
  0.0 94.5 jit_solution(4554142890801707377)
XLA Ops:
  1.3 2.5 %shard_map.114 = (bf16[208,128]{1,0:T(8,128)(2,1)}, bf16[208,128]{1,0:T(8,128)(2,1)}, bf16[208,128]{1,0:T(8,128)(2,1)}, bf16[208,128]{1,0:T(8,128)(2,1)}) custom-call(s32[3]{0:T(128)} %pad_add_fusion.1.spot_ref, s32[1,128]{1,0:T(1,128)} %tokens_ref.3, bf16[128,768]{1,0:T(8,128)(2,1)} %bitcast.8, bf16[768,768]{1,0:T(8,128)(2,1)} %out_weights_ref.1), custom_call_target="tpu_custom_call" | custom-call | flops 100000000 | bytes 1000000 | tf_op jit(solution)/shard_map/pallas_call | solution.py:684
  3.8 3.0 %collective-permute-start.1 = (bf16[208,128]{1,0:T(8,128)(2,1)}, bf16[208,128]{1,0:T(8,128)(2,1)S(1)}, u32[]{:S(2)}, u32[]{:S(2)}) collective-permute-start(bf16[208,128]{1,0:T(8,128)(2,1)} %get-tuple-element.23), channel_id=1, source_target_pairs={{0,2},{1,3},{2,0},{3,1},{4,6},{5,7},{6,4},{7,5},{8,10},{9,11},{10,... | collective-permute-start | bytes 159752 | tf_op jit(solution)/shard_map/ppermute | solution.py:643
  6.8 1.4 %collective-permute-start.2 = (bf16[208,128]{1,0:T(8,128)(2,1)}, bf16[208,128]{1,0:T(8,128)(2,1)S(1)}, u32[]{:S(2)}, u32[]{:S(2)}) collective-permute-start(bf16[208,128]{1,0:T(8,128)(2,1)} %get-tuple-element.23), channel_id=1, source_target_pairs={{0,3},{1,2},{2,1},{3,0},{4,7},{5,6},{6,5},{7,4},{8,11},{9,10},{10,... | collective-permute-start | bytes 159752 | tf_op jit(solution)/shard_map/ppermute | solution.py:643
  8.2 2.6 %collective-permute-start.3 = (bf16[208,128]{1,0:T(8,128)(2,1)}, bf16[208,128]{1,0:T(8,128)(2,1)S(1)}, u32[]{:S(2)}, u32[]{:S(2)}) collective-permute-start(bf16[208,128]{1,0:T(8,128)(2,1)} %get-tuple-element.24), channel_id=1, source_target_pairs={{0,4},{1,5},{2,6},{3,7},{4,0},{5,1},{6,2},{7,3},{8,12},{9,13},{10,... | collective-permute-start | bytes 159752 | tf_op jit(solution)/shard_map/ppermute | solution.py:643
  10.8 1.8 %collective-permute-start = (bf16[208,128]{1,0:T(8,128)(2,1)}, bf16[208,128]{1,0:T(8,128)(2,1)S(1)}, u32[]{:S(2)}, u32[]{:S(2)}) collective-permute-start(bf16[208,128]{1,0:T(8,128)(2,1)} %get-tuple-element.22.rest_0_), channel_id=1, source_target_pairs={{0,1},{1,0},{2,3},{3,2},{4,5},{5,4},{6,7},{7,6},{8,9},{9,8},{10,11... | collective-permute-start | bytes 159752 | tf_op jit(solution)/shard_map/ppermute | solution.py:643
  13.3 2.4 %collective-permute-done.rest_1_.refs_1_ = bf16[208,128]{1,0:T(8,128)(2,1)S(1)} collective-permute-done((bf16[208,128]{1,0:T(8,128)(2,1)}, bf16[208,128]{1,0:T(8,128)(2,1)S(1)}, u32[]{:S(2)}, u32[]{:S(2)}) %collective-permute-start) | collective-permute-done | bytes 53280 | tf_op jit(solution)/shard_map/ppermute | solution.py:643
  15.7 4.0 %collective-permute-start.5 = (bf16[208,128]{1,0:T(8,128)(2,1)}, bf16[208,128]{1,0:T(8,128)(2,1)S(1)}, u32[]{:S(2)}, u32[]{:S(2)}) collective-permute-start(bf16[208,128]{1,0:T(8,128)(2,1)} %get-tuple-element.25), channel_id=1, source_target_pairs={{0,6},{1,7},{2,4},{3,5},{4,2},{5,3},{6,0},{7,1},{8,14},{9,15},{10,... | collective-permute-start | bytes 159752 | tf_op jit(solution)/shard_map/ppermute | solution.py:643
  20.6 4.6 %shard_map.113 = (bf16[8,128,384]{2,1,0:T(8,128)(2,1)}, bf16[2,576,256]{2,1,0:T(8,128)(2,1)}, bf16[256,384]{1,0:T(8,128)(2,1)}) custom-call(s32[6]{0:T(128)} %pad_add_fusion.meta_ref, bf16[128,768]{1,0:T(8,128)(2,1)} %bitcast.9, bf16[256,768]{1,0:T(8,128)(2,1)} %table_ref.3, bf16[768,768]{1,0:T(8,128)(2,1)} %query_ref.3, bf16[768,768]{1,0:T(8,128)(2,1)} %key_ref.3, ...), custom_call_target="tpu_custom_call" | custom-call | flops 1000000000 | bytes 5000000 | tf_op jit(solution)/shard_map/pallas_call | solution.py:684
  25.3 1.4 %collective-permute-done.6.rest_7_.refs_7_ = bf16[208,128]{1,0:T(8,128)(2,1)S(1)} collective-permute-done((bf16[208,128]{1,0:T(8,128)(2,1)}, bf16[208,128]{1,0:T(8,128)(2,1)S(1)}, u32[]{:S(2)}, u32[]{:S(2)}) %collective-permute-start.6) | collective-permute-done | bytes 53280 | tf_op jit(solution)/shard_map/ppermute | solution.py:643
  27.4 3.8 %all-to-all-start.1 = ((bf16[8,128,384]{2,1,0:T(8,128)(2,1)}), bf16[8,128,384]{2,1,0:T(8,128)(2,1)S(1)}, u32[]{:S(2)}, u32[]{:S(2)}) async-start(bf16[8,128,384]{2,1,0:T(8,128)(2,1)} %shard_map.117), calls=%async_computation.1 | async-start | bytes 1572864 | tf_op jit(solution)/shard_map/all_to_all | solution.py:728
  31.4 11.0 %shard_map.115 = (bf16[4,576,128]{2,1,0:T(8,128)(2,1)}, bf16[2,576,128]{2,1,0:T(8,128)(2,1)S(1)}, bf16[192,1024]{1,0:T(8,128)(2,1)S(1)}) custom-call(s32[6]{0:T(128)S(1)} %copy-done.27, bf16[2,576,256]{2,1,0:T(8,128)(2,1)S(1)} %copy-done.29, f32[32,1024]{1,0:T(8,128)S(1)} %copy-done.32, f32[32,1024]{1,0:T(8,128)S(1)} %copy-done.33, ...), custom_call_target="tpu_custom_call" | custom-call | flops 8000000000 | bytes 8000000 | tf_op jit(solution)/shard_map/pallas_call | solution.py:684
  43.8 4.7 %all-to-all-done.1 = bf16[8,128,384]{2,1,0:T(8,128)(2,1)S(1)} async-done(((bf16[8,128,384]{2,1,0:T(8,128)(2,1)}), bf16[8,128,384]{2,1,0:T(8,128)(2,1)S(1)}, u32[]{:S(2)}, u32[]{:S(2)}) %all-to-all-start.1) | async-done | bytes 786464 | tf_op jit(solution)/shard_map/all_to_all | solution.py:728
  48.5 4.3 %all-to-all-start = ((bf16[4,576,128]{2,1,0:T(8,128)(2,1)}), bf16[4,576,128]{2,1,0:T(8,128)(2,1)}, u32[]{:S(2)}, u32[]{:S(2)}) async-start(bf16[4,576,128]{2,1,0:T(8,128)(2,1)} %get-tuple-element.26), calls=%async_computation | async-start | bytes 1179648 | tf_op jit(solution)/shard_map/all_to_all | solution.py:764
  56.9 1.5 %collective-permute-done.7.got_ref = bf16[864,128]{1,0:T(8,128)(2,1)S(1)} collective-permute-done((bf16[864,128]{1,0:T(8,128)(2,1)S(1)}, bf16[864,128]{1,0:T(8,128)(2,1)S(1)}, u32[]{:S(2)}, u32[]{:S(2)}) %collective-permute-start.7) | collective-permute-done | bytes 221216 | tf_op jit(solution)/shard_map/ppermute | solution.py:643
  58.5 1.6 %collective-permute-start.8 = (bf16[864,128]{1,0:T(8,128)(2,1)S(1)}, bf16[864,128]{1,0:T(8,128)(2,1)S(1)}, u32[]{:S(2)}, u32[]{:S(2)}) collective-permute-start(bf16[864,128]{1,0:T(8,128)(2,1)S(1)} %get-tuple-element.33.here_ref), channel_id=1, source_target_pairs={{0,16},{8,24},{16,0},{24,8},{1,17},{9,25},{17,1},{25,9},{2,18},{10... | collective-permute-start | bytes 663560 | tf_op jit(solution)/shard_map/ppermute | solution.py:643
  62.6 5.1 %collective-permute-done.10.far_ref = bf16[288,128]{1,0:T(8,128)(2,1)S(1)} collective-permute-done((bf16[288,128]{1,0:T(8,128)(2,1)S(1)}, bf16[288,128]{1,0:T(8,128)(2,1)S(1)}, u32[]{:S(2)}, u32[]{:S(2)}) %collective-permute-start.10) | collective-permute-done | bytes 73760 | tf_op jit(solution)/shard_map/ppermute | solution.py:785
  67.8 1.3 %shard_map.120 = (bf16[576,128]{1,0:T(8,128)(2,1)}, bf16[192,128]{1,0:T(8,128)(2,1)S(1)}, bf16[192,128]{1,0:T(8,128)(2,1)}, bf16[192,128]{1,0:T(8,128)(2,1)}, bf16[192,128]{1,0:T(8,128)(2,1)}) custom-call(s32[6]{0:T(128)S(1)} %copy-done.27, bf16[864,128]{1,0:T(8,128)(2,1)S(1)} %get-tuple-element.33.here_ref, ...), custom_call_target="tpu_custom_call" | custom-call | flops 100000000 | bytes 1000000 | tf_op jit(solution)/shard_map/pallas_call | solution.py:684
  69.7 5.1 %collective-permute-start.14 = (bf16[576,128]{1,0:T(8,128)(2,1)}, bf16[576,128]{1,0:T(8,128)(2,1)}, u32[]{:S(2)}, u32[]{:S(2)}) collective-permute-start(bf16[576,128]{1,0:T(8,128)(2,1)} %get-tuple-element.39.own_ref), channel_id=1, source_target_pairs={{0,6},{5,7},{8,14},{13,15},{16,22},{21,23},{24,30},{29,31}} | collective-permute-start | bytes 442376 | tf_op jit(solution)/shard_map/ppermute | solution.py:801
  76.2 2.4 %collective-permute-start.11 = (bf16[192,128]{1,0:T(8,128)(2,1)}, bf16[192,128]{1,0:T(8,128)(2,1)}, u32[]{:S(2)}, u32[]{:S(2)}) collective-permute-start(bf16[192,128]{1,0:T(8,128)(2,1)} %get-tuple-element.36), channel_id=1, source_target_pairs={{0,2},{1,3},{2,0},{3,1},{6,4},{7,5},{8,10},{9,11},{10,8},{11,9},{1... | collective-permute-start | bytes 147464 | tf_op jit(solution)/shard_map/ppermute | solution.py:807
  78.6 1.9 %collective-permute-start.12 = (bf16[192,128]{1,0:T(8,128)(2,1)}, bf16[192,128]{1,0:T(8,128)(2,1)}, u32[]{:S(2)}, u32[]{:S(2)}) collective-permute-start(bf16[192,128]{1,0:T(8,128)(2,1)} %get-tuple-element.37), channel_id=1, source_target_pairs={{0,4},{1,5},{4,0},{5,1},{6,2},{7,3},{8,12},{9,13},{12,8},{13,9},{1... | collective-permute-start | bytes 147464 | tf_op jit(solution)/shard_map/ppermute | solution.py:807
  82.9 3.1 %shard_map.116.after_ref = bf16[128,768]{1,0:T(8,128)(2,1)} custom-call(s32[1,128]{1,0:T(1,128)S(1)} %copy-done.28, bf16[256,768]{1,0:T(8,128)(2,1)S(1)} %copy-done.5, bf16[768,768]{1,0:T(8,128)(2,1)S(1)} %copy-done, bf16[768,768]{1,0:T(8,128)(2,1)S(1)} %copy-done.1, bf16[768,768]{1,0:T(8,128)(2,1)S(1)} %copy-done.2, bf16[4,576,128]{2,1,0:T(8,128)(2,1)} %all-to-all-done.rows_ref), custom_call_target="tpu_custom_call" | custom-call | flops 1000000000 | bytes 5000000 | tf_op jit(solution)/shard_map/pallas_call | solution.py:684
  87.1 1.5 %collective-permute-done.13.s3 = bf16[192,128]{1,0:T(8,128)(2,1)} collective-permute-done((bf16[192,128]{1,0:T(8,128)(2,1)}, bf16[192,128]{1,0:T(8,128)(2,1)}, u32[]{:S(2)}, u32[]{:S(2)}) %collective-permute-start.13) | collective-permute-done | bytes 49184 | tf_op jit(solution)/shard_map/ppermute | solution.py:807
  90.9 1.6 %collective-permute-done.16.other_ref = bf16[1152,128]{1,0:T(8,128)(2,1)S(1)} collective-permute-done((bf16[1152,128]{1,0:T(8,128)(2,1)S(1)}, bf16[1152,128]{1,0:T(8,128)(2,1)S(1)}, u32[]{:S(2)}, u32[]{:S(2)}) %collective-permute-start.16) | collective-permute-done | bytes 294944 | tf_op jit(solution)/shard_map/ppermute | solution.py:643
  92.4 2.1 %shard_map.122 = f32[384,768]{1,0:T(8,128)} custom-call(s32[6]{0:T(128)S(1)} %copy-done.27, bf16[256,384]{1,0:T(8,128)(2,1)S(1)} %copy-done.30, bf16[1152,128]{1,0:T(8,128)(2,1)S(1)} %shard_map.121.mine_ref, bf16[1152,128]{1,0:T(8,128)(2,1)S(1)} %collective-permute-done.16.other_ref), custom_call_target="tpu_custom_call" | custom-call | flops 1000000000 | bytes 5000000 | tf_op jit(solution)/shard_map/pallas_call | solution.py:684
  (97 shorter events, 18.7 us)
Async XLA Ops:
  0.6 12.0 %copy-start.34 = (s32[12]{0:T(128)S(1)}, s32[12]{0:T(128)}, u32[]{:S(2)}) copy-start(s32[12]{0:T(128)} %param.17) | copy-start | bytes 148
  3.8 15.9 %collective-permute-start.1 = (bf16[208,128]{1,0:T(8,128)(2,1)}, bf16[208,128]{1,0:T(8,128)(2,1)S(1)}, u32[]{:S(2)}, u32[]{:S(2)}) collective-permute-start(bf16[208,128]{1,0:T(8,128)(2,1)} %get-tuple-element.23), channel_id=1, source_target_pairs={{0,2},{1,3},{2,0},{3,1},{4,6},{5,7},{6,4},{7,5},{8,10},{9,11},{10,... | collective-permute-start | bytes 159752 | tf_op jit(solution)/shard_map/ppermute | solution.py:643
  6.8 18.4 %collective-permute-start.2 = (bf16[208,128]{1,0:T(8,128)(2,1)}, bf16[208,128]{1,0:T(8,128)(2,1)S(1)}, u32[]{:S(2)}, u32[]{:S(2)}) collective-permute-start(bf16[208,128]{1,0:T(8,128)(2,1)} %get-tuple-element.23), channel_id=1, source_target_pairs={{0,3},{1,2},{2,1},{3,0},{4,7},{5,6},{6,5},{7,4},{8,11},{9,10},{10,... | collective-permute-start | bytes 159752 | tf_op jit(solution)/shard_map/ppermute | solution.py:643
  8.2 17.1 %collective-permute-start.3 = (bf16[208,128]{1,0:T(8,128)(2,1)}, bf16[208,128]{1,0:T(8,128)(2,1)S(1)}, u32[]{:S(2)}, u32[]{:S(2)}) collective-permute-start(bf16[208,128]{1,0:T(8,128)(2,1)} %get-tuple-element.24), channel_id=1, source_target_pairs={{0,4},{1,5},{2,6},{3,7},{4,0},{5,1},{6,2},{7,3},{8,12},{9,13},{10,... | collective-permute-start | bytes 159752 | tf_op jit(solution)/shard_map/ppermute | solution.py:643
  10.8 14.5 %collective-permute-start.4 = (bf16[208,128]{1,0:T(8,128)(2,1)}, bf16[208,128]{1,0:T(8,128)(2,1)S(1)}, u32[]{:S(2)}, u32[]{:S(2)}) collective-permute-start(bf16[208,128]{1,0:T(8,128)(2,1)} %get-tuple-element.24), channel_id=1, source_target_pairs={{0,5},{1,4},{2,7},{3,6},{4,1},{5,0},{6,3},{7,2},{8,13},{9,12},{10,... | collective-permute-start | bytes 159752 | tf_op jit(solution)/shard_map/ppermute | solution.py:643
  10.8 4.9 %collective-permute-start = (bf16[208,128]{1,0:T(8,128)(2,1)}, bf16[208,128]{1,0:T(8,128)(2,1)S(1)}, u32[]{:S(2)}, u32[]{:S(2)}) collective-permute-start(bf16[208,128]{1,0:T(8,128)(2,1)} %get-tuple-element.22.rest_0_), channel_id=1, source_target_pairs={{0,1},{1,0},{2,3},{3,2},{4,5},{5,4},{6,7},{7,6},{8,9},{9,8},{10,11... | collective-permute-start | bytes 159752 | tf_op jit(solution)/shard_map/ppermute | solution.py:643
  15.7 9.6 %collective-permute-start.5 = (bf16[208,128]{1,0:T(8,128)(2,1)}, bf16[208,128]{1,0:T(8,128)(2,1)S(1)}, u32[]{:S(2)}, u32[]{:S(2)}) collective-permute-start(bf16[208,128]{1,0:T(8,128)(2,1)} %get-tuple-element.25), channel_id=1, source_target_pairs={{0,6},{1,7},{2,4},{3,5},{4,2},{5,3},{6,0},{7,1},{8,14},{9,15},{10,... | collective-permute-start | bytes 159752 | tf_op jit(solution)/shard_map/ppermute | solution.py:643
  19.7 7.0 %collective-permute-start.6 = (bf16[208,128]{1,0:T(8,128)(2,1)}, bf16[208,128]{1,0:T(8,128)(2,1)S(1)}, u32[]{:S(2)}, u32[]{:S(2)}) collective-permute-start(bf16[208,128]{1,0:T(8,128)(2,1)} %get-tuple-element.25), channel_id=1, source_target_pairs={{0,7},{1,6},{2,5},{3,4},{4,3},{5,2},{6,1},{7,0},{8,15},{9,14},{10,... | collective-permute-start | bytes 159752 | tf_op jit(solution)/shard_map/ppermute | solution.py:643
  27.4 21.1 %all-to-all-start.1 = ((bf16[8,128,384]{2,1,0:T(8,128)(2,1)}), bf16[8,128,384]{2,1,0:T(8,128)(2,1)S(1)}, u32[]{:S(2)}, u32[]{:S(2)}) async-start(bf16[8,128,384]{2,1,0:T(8,128)(2,1)} %shard_map.117), calls=%async_computation.1 | async-start | bytes 1572864 | tf_op jit(solution)/shard_map/all_to_all | solution.py:728
  48.5 33.4 %copy-start.2 = (bf16[768,768]{1,0:T(8,128)(2,1)S(1)}, bf16[768,768]{1,0:T(8,128)(2,1)}, u32[]{:S(2)}) copy-start(bf16[768,768]{1,0:T(8,128)(2,1)} %value_ref.3) | copy-start | bytes 3538948
  48.5 33.4 %all-to-all-start = ((bf16[4,576,128]{2,1,0:T(8,128)(2,1)}), bf16[4,576,128]{2,1,0:T(8,128)(2,1)}, u32[]{:S(2)}, u32[]{:S(2)}) async-start(bf16[4,576,128]{2,1,0:T(8,128)(2,1)} %get-tuple-element.26), calls=%async_computation | async-start | bytes 1179648 | tf_op jit(solution)/shard_map/all_to_all | solution.py:764
  55.9 26.0 %copy-start = (bf16[768,768]{1,0:T(8,128)(2,1)S(1)}, bf16[768,768]{1,0:T(8,128)(2,1)}, u32[]{:S(2)}) copy-start(bf16[768,768]{1,0:T(8,128)(2,1)} %query_ref.3) | copy-start | bytes 3538948
  55.9 26.0 %copy-start.1 = (bf16[768,768]{1,0:T(8,128)(2,1)S(1)}, bf16[768,768]{1,0:T(8,128)(2,1)}, u32[]{:S(2)}) copy-start(bf16[768,768]{1,0:T(8,128)(2,1)} %key_ref.3) | copy-start | bytes 3538948
  55.9 26.0 %copy-start.28 = (s32[1,128]{1,0:T(1,128)S(1)}, s32[1,128]{1,0:T(1,128)}, u32[]{:S(2)}) copy-start(s32[1,128]{1,0:T(1,128)} %tokens_ref.3) | copy-start | bytes 1540
  56.8 1.5 %collective-permute-start.7 = (bf16[864,128]{1,0:T(8,128)(2,1)S(1)}, bf16[864,128]{1,0:T(8,128)(2,1)S(1)}, u32[]{:S(2)}, u32[]{:S(2)}) collective-permute-start(bf16[864,128]{1,0:T(8,128)(2,1)S(1)} %get-tuple-element.32), channel_id=1, source_target_pairs={{0,8},{8,0},{16,24},{24,16},{1,9},{9,1},{17,25},{25,17},{2,10},{10... | collective-permute-start | bytes 663560 | tf_op jit(solution)/shard_map/ppermute | solution.py:643
  58.5 9.3 %collective-permute-start.8 = (bf16[864,128]{1,0:T(8,128)(2,1)S(1)}, bf16[864,128]{1,0:T(8,128)(2,1)S(1)}, u32[]{:S(2)}, u32[]{:S(2)}) collective-permute-start(bf16[864,128]{1,0:T(8,128)(2,1)S(1)} %get-tuple-element.33.here_ref), channel_id=1, source_target_pairs={{0,16},{8,24},{16,0},{24,8},{1,17},{9,25},{17,1},{25,9},{2,18},{10... | collective-permute-start | bytes 663560 | tf_op jit(solution)/shard_map/ppermute | solution.py:643
  60.0 7.7 %collective-permute-start.10 = (bf16[288,128]{1,0:T(8,128)(2,1)S(1)}, bf16[288,128]{1,0:T(8,128)(2,1)S(1)}, u32[]{:S(2)}, u32[]{:S(2)}) collective-permute-start(bf16[288,128]{1,0:T(8,128)(2,1)S(1)} %get-tuple-element.34), channel_id=1, source_target_pairs={{1,16},{3,18},{4,21},{6,23},{9,24},{11,26},{12,29},{14,31},{17,0},... | collective-permute-start | bytes 221192 | tf_op jit(solution)/shard_map/ppermute | solution.py:785
  61.3 6.5 %collective-permute-start.9 = (bf16[288,128]{1,0:T(8,128)(2,1)S(1)}, bf16[288,128]{1,0:T(8,128)(2,1)S(1)}, u32[]{:S(2)}, u32[]{:S(2)}) collective-permute-start(bf16[288,128]{1,0:T(8,128)(2,1)S(1)} %get-tuple-element.34), channel_id=1, source_target_pairs={{1,0},{3,2},{4,5},{6,7},{9,8},{11,10},{12,13},{14,15},{17,16},{19,... | collective-permute-start | bytes 221192 | tf_op jit(solution)/shard_map/ppermute | solution.py:784
  69.7 18.9 %collective-permute-start.14 = (bf16[576,128]{1,0:T(8,128)(2,1)}, bf16[576,128]{1,0:T(8,128)(2,1)}, u32[]{:S(2)}, u32[]{:S(2)}) collective-permute-start(bf16[576,128]{1,0:T(8,128)(2,1)} %get-tuple-element.39.own_ref), channel_id=1, source_target_pairs={{0,6},{5,7},{8,14},{13,15},{16,22},{21,23},{24,30},{29,31}} | collective-permute-start | bytes 442376 | tf_op jit(solution)/shard_map/ppermute | solution.py:801
  74.9 13.8 %collective-permute-start.15 = (bf16[576,128]{1,0:T(8,128)(2,1)}, bf16[576,128]{1,0:T(8,128)(2,1)}, u32[]{:S(2)}, u32[]{:S(2)}) collective-permute-start(bf16[576,128]{1,0:T(8,128)(2,1)} %get-tuple-element.39.own_ref), channel_id=1, source_target_pairs={{2,6},{10,14},{18,22},{26,30}} | collective-permute-start | bytes 442376 | tf_op jit(solution)/shard_map/ppermute | solution.py:802
  76.2 9.8 %collective-permute-start.11 = (bf16[192,128]{1,0:T(8,128)(2,1)}, bf16[192,128]{1,0:T(8,128)(2,1)}, u32[]{:S(2)}, u32[]{:S(2)}) collective-permute-start(bf16[192,128]{1,0:T(8,128)(2,1)} %get-tuple-element.36), channel_id=1, source_target_pairs={{0,2},{1,3},{2,0},{3,1},{6,4},{7,5},{8,10},{9,11},{10,8},{11,9},{1... | collective-permute-start | bytes 147464 | tf_op jit(solution)/shard_map/ppermute | solution.py:807
  78.6 8.5 %collective-permute-start.12 = (bf16[192,128]{1,0:T(8,128)(2,1)}, bf16[192,128]{1,0:T(8,128)(2,1)}, u32[]{:S(2)}, u32[]{:S(2)}) collective-permute-start(bf16[192,128]{1,0:T(8,128)(2,1)} %get-tuple-element.37), channel_id=1, source_target_pairs={{0,4},{1,5},{4,0},{5,1},{6,2},{7,3},{8,12},{9,13},{12,8},{13,9},{1... | collective-permute-start | bytes 147464 | tf_op jit(solution)/shard_map/ppermute | solution.py:807
  80.6 8.1 %collective-permute-start.13 = (bf16[192,128]{1,0:T(8,128)(2,1)}, bf16[192,128]{1,0:T(8,128)(2,1)}, u32[]{:S(2)}, u32[]{:S(2)}) collective-permute-start(bf16[192,128]{1,0:T(8,128)(2,1)} %get-tuple-element.38), channel_id=1, source_target_pairs={{2,4},{3,5},{4,2},{5,3},{6,0},{7,1},{10,12},{11,13},{12,10},{13,11... | collective-permute-start | bytes 147464 | tf_op jit(solution)/shard_map/ppermute | solution.py:807
  90.8 1.6 %collective-permute-start.16 = (bf16[1152,128]{1,0:T(8,128)(2,1)S(1)}, bf16[1152,128]{1,0:T(8,128)(2,1)S(1)}, u32[]{:S(2)}, u32[]{:S(2)}) collective-permute-start(bf16[1152,128]{1,0:T(8,128)(2,1)S(1)} %shard_map.121.mine_ref), channel_id=1, source_target_pairs={{0,8},{8,0},{16,24},{24,16},{1,9},{9,1},{17,25},{25,17},{2,10},{10... | collective-permute-start | bytes 884744 | tf_op jit(solution)/shard_map/ppermute | solution.py:643
  (30 other events, 95.5 us)

commit v7 on v6

--- a/solution.py
+++ b/solution.py
@@ -263,10 +263,6 @@
         early_ref[GROUP_COLS:, :] = tokens
 
 
-def gate_kernel(*refs):
-    del refs
-
-
 def prepare_kernel(
     meta_ref,
     cotangent_ref,
@@ -274,11 +270,14 @@
     query_ref,
     key_ref,
     value_ref,
+    first_ref,
+    second_ref,
     late_ref,
     lookup_ref,
     normed_ref,
     columns_ref,
 ):
+    del first_ref, second_ref
     columns = late_ref.shape[2]
     for target in range(2 * GROUPS):
         side = target % 2
@@ -534,44 +533,52 @@
         give_ref[place, :] = jnp.where(first, part[rows:], part[:rows]).astype(jnp.bfloat16)
 
 
-def core_kernel(keep_ref, got_ref, here_ref, out_ref):
-    here_ref[...] = keep_ref[...] + got_ref[...]
-    base = here_ref.shape[0] - out_ref.shape[0]
-    out_ref[...] = here_ref[base:, :]
-
-
-def combine_kernel(meta_ref, here_ref, there_ref, near_ref, far_ref, out_ref, *piece_refs):
+def combine_kernel(meta_ref, here_ref, there_ref, after_ref, *piece_refs):
+    del after_ref
     rows = GROUP_COLS
     for turn, piece_ref in enumerate(piece_refs):
-        target = jnp.minimum(meta_ref[GROUP_HEADS + 1] ^ turn, 2)
-        place = pl.ds(pl.multiple_of(target * rows, rows), rows)
-        piece_ref[...] = here_ref[place, :] + there_ref[place, :]
-    own = here_ref[3 * rows :, :] + there_ref[3 * rows :, :]
-    other = near_ref[...] + far_ref[...]
-    first = meta_ref[GROUP_HEADS] == 0
-    size = own.shape[0]
-    out_ref[:size, :] = jnp.where(first, own, other)
-    out_ref[size:, :] = jnp.where(first, other, own)
-
-
-def gather_kernel(meta_ref, s0, s1, s2, s3, own_ref, o0, o1, after_ref, mine_ref):
+        target = meta_ref[GROUP_HEADS + 1] ^ turn
+
+        @pl.when(target < 3)
+        def _(piece_ref=piece_ref, target=target):
+            place = pl.ds(pl.multiple_of(target * rows, rows), rows)
+            piece_ref[:rows, :] = here_ref[place, :] + there_ref[place, :]
+            tail = piece_ref.shape[0] - rows
+            piece_ref[rows:, :] = jnp.zeros((tail, piece_ref.shape[1]), jnp.bfloat16)
+
+        @pl.when(target == 3)
+        def _(piece_ref=piece_ref):
+            piece_ref[...] = here_ref[3 * rows :, :] + there_ref[3 * rows :, :]
+
+
+def cross_kernel(meta_ref, low_ref, high_ref, out_ref):
+    out_ref[...] = jnp.where(meta_ref[GROUP_HEADS] == 0, low_ref[...], high_ref[...])
+
+
+def gather_kernel(meta_ref, g0, g1, g2, g3, early_ref, late_ref, after_ref, mine_ref):
     del after_ref
     rows = GROUP_COLS
-    size = own_ref.shape[0]
+    size = g0.shape[0]
     group = meta_ref[GROUP_HEADS + 1]
+    first = meta_ref[GROUP_HEADS] == 0
 
     @pl.when(group < 3)
     def _():
-        for turn, got in enumerate((s0, s1, s2, s3)):
+        for turn, got in enumerate((g0, g1, g2, g3)):
             place = pl.ds(pl.multiple_of((group ^ turn) * rows, rows), rows)
-            mine_ref[place, :] = got[...]
+            mine_ref[place, :] = got[:rows, :]
         tail = mine_ref.shape[0] - GROUPS * rows
         mine_ref[GROUPS * rows :, :] = jnp.zeros((tail, mine_ref.shape[1]), jnp.bfloat16)
 
-    @pl.when(group == 3)
+    @pl.when((group == 3) & first)
     def _():
-        mine_ref[:size, :] = o0[...]
-        mine_ref[size:, :] = jnp.where(meta_ref[GROUP_HEADS] == 0, o1[...], own_ref[...])
+        for place, piece in enumerate((g3, late_ref, g2, early_ref)):
+            mine_ref[place * size : (place + 1) * size, :] = piece[...]
+
+    @pl.when((group == 3) & jnp.logical_not(first))
+    def _():
+        for place, piece in enumerate((late_ref, g1, early_ref, g0)):
+            mine_ref[place * size : (place + 1) * size, :] = piece[...]
 
 
 def input_kernel(tokens_ref, table_ref, query_ref, key_ref, value_ref, rows_ref, out_ref):
@@ -674,11 +681,13 @@
     cosine, sine_part = rope_table(length)
 
     def call(
-        body, operands, outs, scratch=(), steps=1, flops=10**8, moved=10**6, loose=0, grant=VMEM_BYTES
+        body, operands, outs, scratch=(), steps=1, flops=10**8, moved=10**6, loose=0, peeked=0, grant=VMEM_BYTES
     ):
         spaces = [whole(operand.shape) for operand in operands]
         for index in range(loose):
             spaces[-1 - index] = pl.BlockSpec(memory_space=pl.ANY)
+        for index in range(peeked):
+            spaces[-1 - index] = whole((16, 128))
         if operands[0].ndim == 1:
             spaces[0] = pl.BlockSpec(memory_space=pltpu.SMEM)
         return pl.pallas_call(
@@ -707,7 +716,7 @@
         early[turn] = swapped(sent[turn // 2], "seq", turn)
     late, lookup, normed = call(
         prepare_kernel,
-        (meta, grad_out, table, w_query, w_key, w_value),
+        (meta, grad_out, table, w_query, w_key, w_value, early[1], early[2]),
         [
             ((blocks, block, features // 2), half),
             ((2, 3 * GROUP_COLS, vocab), half),
@@ -716,15 +725,9 @@
         [pltpu.VMEM((features, vocab), jnp.float32)],
         flops=10**9,
         moved=5 * 10**6,
+        peeked=2,
         grant=60 * 1024 * 1024,
     )
-    late = pl.pallas_call(
-        gate_kernel,
-        in_specs=[pl.BlockSpec(memory_space=pl.ANY)] * blocks,
-        out_specs=pl.BlockSpec(memory_space=pl.ANY),
-        out_shape=jax.ShapeDtypeStruct(late.shape, half),
-        input_output_aliases={0: 0},
-    )(late, *early[1:])
     late = lax.all_to_all(late, "seq", split_axis=0, concat_axis=0, tiled=True)
     heads_shape = (GROUP_HEADS, HEAD_DIM, length)
     rows_shape = (GROUP_HEADS, length, 2 * HEAD_DIM)
@@ -774,37 +777,17 @@
         (meta, attended, late.reshape(length, features // 2), sums),
         [((packed, lanes), half)] * 2,
     )
-    here, here_out = call(
-        core_kernel,
-        (keep, swapped(give, "dp", 1)),
-        [((packed, lanes), half), ((out_rows, lanes), half)],
-    )
+    here = keep + swapped(give, "dp", 1)
     there = swapped(here, "dp", 2)
-    inward = [(2 * z + 1 - z // 2, 2 * z + z // 2) for z in range(GROUPS)]
-    near = lax.ppermute(here_out, "seq", inward)
-    far = lax.ppermute(
-        here_out,
-        ("dp", "seq"),
-        [
-            (blocks * d + source, blocks * (d ^ 2) + target)
-            for d in range(lax.axis_size("dp"))
-            for source, target in inward
-        ],
-    )
-    full_out, *pieces = call(
+    pieces = call(
         combine_kernel,
-        (meta, here, there, near, far),
-        [((2 * out_rows, lanes), half)] + [((GROUP_COLS, lanes), half)] * GROUPS,
-    )
-    last = blocks - 2
-    got_out = [
-        lax.ppermute(full_out, "seq", [(0, last), (last - 1, last + 1)]),
-        lax.ppermute(full_out, "seq", [(2, last)]),
-    ]
+        (meta, here, there, got_rows),
+        [((out_rows, lanes), half)] * GROUPS,
+        loose=1,
+    )
     got = [pieces[0]] + [None] * (GROUPS - 1)
     for turn in (2, 3, 1):
-        route = [(i, i ^ (2 * turn)) for i in range(blocks) if (i ^ (2 * turn)) < last]
-        got[turn] = lax.ppermute(pieces[turn], "seq", route)
+        got[turn] = swapped(pieces[turn], "seq", 2 * turn)
     (grad_input,) = call(
         input_kernel,
         (token_ids, table, w_query, w_key, w_value, got_rows),
@@ -812,9 +795,15 @@
         flops=10**9,
         moved=5 * 10**6,
     )
+    last = blocks - 2
+    between = [(last, last + 1), (last + 1, last)]
+    crossed = []
+    for low, high in ((got[0], got[2]), (got[1], got[3])):
+        (piece,) = call(cross_kernel, (meta, low, high), [(low.shape, half)])
+        crossed.append(lax.ppermute(piece, "seq", between))
     (mine,) = call(
         gather_kernel,
-        (meta, *got, full_out, *got_out, grad_input),
+        (meta, *got, *crossed, grad_input),
         [((4 * out_rows, lanes), half)],
         loose=1,
     )

time: 95.2 us -> 98.6 us (1.036)
  waiting for transfers between devices: 19.4 us -> 34.2 us
  starting transfers between devices: 38.2 us -> 31.1 us
  local copies, waits for them, and re-layouts: 7.83 us -> 2.96 us
    ppermute x10 -> x13, waiting for transfers between devices: 6.8 us -> 24.2 us  [swapped(): return lax.ppermute(block, axis, route)]
    ppermute x7 -> x2, starting transfers between devices: 14.7 us -> 1.33 us  [grouped_device(): crossed.append(lax.ppermute(piece, 'seq', between))]
    all_to_all x1, waiting for transfers between devices: 0.01 us -> 10 us  [over_plane(): lax.all_to_all(chunks, 'seq', split_axis=0, concat_axis=0, axis_index_gro...]
    ppermute x7 -> x2, waiting for transfers between devices: 7.86 us -> 0.01 us  [grouped_device(): crossed.append(lax.ppermute(piece, 'seq', between))]
    ppermute x10 -> x13, starting transfers between devices: 15.4 us -> 21.2 us  [swapped(): return lax.ppermute(block, axis, route)]
    unnamed x70 -> x40, local copies, waits for them, and re-layouts: 7.75 us -> 2.89 us
    all_to_all x1, waiting for transfers between devices: 4.71 us -> 0.01 us  [grouped_device(): late = lax.all_to_all(late, 'seq', split_axis=0, concat_axis=0, tiled=True)]
    all_to_all x1, starting transfers between devices: 3.83 us -> 5.07 us  [grouped_device(): late = lax.all_to_all(late, 'seq', split_axis=0, concat_axis=0, tiled=True)]
  transfers between devices with their start and end apart: 19 -> 17, of which waited for: 8 -> 8; matrix products, arithmetic and copies ran while one was open for 1% -> 1% of each run, Pallas kernels for 22% -> 15%
where the time goes in v7:
time: 98.6 us; the launch traced here: 97.1 us
  waiting for transfers between devices  34.2 us (35%)
  starting transfers between devices  31.1 us (32%)
  Pallas kernels  25.9 us (26%)
  local copies, waits for them, and re-layouts  2.96 us (3%)
  other arithmetic  2.01 us (2%)
    pallas_call x10, Pallas kernels, call(): pl.pallas_call(body, grid=(steps,), in_specs=spaces, out_specs=[whole(sha...  25.9 us
    ppermute x13, waiting for transfers between devices, swapped(): return lax.ppermute(block, axis, route)  24.2 us
    ppermute x13, starting transfers between devices, swapped(): return lax.ppermute(block, axis, route)  21.2 us
    all_to_all x1, waiting for transfers between devices, over_plane(): lax.all_to_all(chunks, 'seq', split_axis=0, concat_axis=0, axis_index_gro...  10 us
    all_to_all x1, starting transfers between devices, grouped_device(): late = lax.all_to_all(late, 'seq', split_axis=0, concat_axis=0, tiled=True)  5.07 us
    all_to_all x1, starting transfers between devices, over_plane(): lax.all_to_all(chunks, 'seq', split_axis=0, concat_axis=0, axis_index_gro...  3.48 us
    unnamed x40, local copies, waits for them, and re-layouts  2.89 us
  transfers between devices with their start and end apart: 17, of which 8 were waited for; matrix products, arithmetic and copies ran while one was open for 1% of the time, Pallas kernels for 15%

profile of v7, /device:TPU:0, one launch (start us, length us, event | category | flops | bytes accessed | tf_op | source)
XLA Modules:
  0.0 97.1 jit_solution(15931649286790628259)
XLA Ops:
  1.3 2.6 %shard_map.113 = (bf16[208,128]{1,0:T(8,128)(2,1)}, bf16[208,128]{1,0:T(8,128)(2,1)}, bf16[208,128]{1,0:T(8,128)(2,1)}, bf16[208,128]{1,0:T(8,128)(2,1)}) custom-call(s32[3]{0:T(128)} %pad_add_fusion.1.spot_ref, s32[1,128]{1,0:T(1,128)} %tokens_ref.3, bf16[128,768]{1,0:T(8,128)(2,1)} %bitcast.8, bf16[768,768]{1,0:T(8,128)(2,1)} %out_weights_ref.1), custom_call_target="tpu_custom_call" | custom-call | flops 100000000 | bytes 1000000 | tf_op jit(solution)/shard_map/pallas_call | solution.py:693
  3.9 2.9 %collective-permute-start = (bf16[208,128]{1,0:T(8,128)(2,1)}, bf16[208,128]{1,0:T(8,128)(2,1)S(1)}, u32[]{:S(2)}, u32[]{:S(2)}) collective-permute-start(bf16[208,128]{1,0:T(8,128)(2,1)} %get-tuple-element.18.rest_0_), channel_id=1, source_target_pairs={{0,1},{1,0},{2,3},{3,2},{4,5},{5,4},{6,7},{7,6},{8,9},{9,8},{10,11... | collective-permute-start | bytes 159752 | tf_op jit(solution)/shard_map/ppermute | solution.py:650
  6.8 1.6 %collective-permute-start.1 = (bf16[208,128]{1,0:T(8,128)(2,1)}, bf16[208,128]{1,0:T(8,128)(2,1)S(1)}, u32[]{:S(2)}, u32[]{:S(2)}) collective-permute-start(bf16[208,128]{1,0:T(8,128)(2,1)} %get-tuple-element.19), channel_id=1, source_target_pairs={{0,2},{1,3},{2,0},{3,1},{4,6},{5,7},{6,4},{7,5},{8,10},{9,11},{10,... | collective-permute-start | bytes 159752 | tf_op jit(solution)/shard_map/ppermute | solution.py:650
  9.1 2.0 %collective-permute-done.1.second_ref.rest_2_ = bf16[208,128]{1,0:T(8,128)(2,1)S(1)} collective-permute-done((bf16[208,128]{1,0:T(8,128)(2,1)}, bf16[208,128]{1,0:T(8,128)(2,1)S(1)}, u32[]{:S(2)}, u32[]{:S(2)}) %collective-permute-start.1) | collective-permute-done | bytes 53280 | tf_op jit(solution)/shard_map/ppermute | solution.py:650
  11.8 4.6 %shard_map.114 = (bf16[8,128,384]{2,1,0:T(8,128)(2,1)}, bf16[2,576,256]{2,1,0:T(8,128)(2,1)}, bf16[256,384]{1,0:T(8,128)(2,1)}) custom-call(s32[6]{0:T(128)} %pad_add_fusion.meta_ref, bf16[128,768]{1,0:T(8,128)(2,1)} %bitcast.9, bf16[256,768]{1,0:T(8,128)(2,1)} %table_ref.3, bf16[768,768]{1,0:T(8,128)(2,1)} %query_ref.3, bf16[768,768]{1,0:T(8,128)(2,1)} %key_ref.3, ...), custom_call_target="tpu_custom_call" | custom-call | flops 1000000000 | bytes 5000000 | tf_op jit(solution)/shard_map/pallas_call | solution.py:693
  16.5 5.1 %all-to-all-start.1 = ((bf16[8,128,384]{2,1,0:T(8,128)(2,1)}), bf16[8,128,384]{2,1,0:T(8,128)(2,1)S(1)}, u32[]{:S(2)}, u32[]{:S(2)}) async-start(bf16[8,128,384]{2,1,0:T(8,128)(2,1)} %get-tuple-element.26), calls=%async_computation.1 | async-start | bytes 1572864 | tf_op jit(solution)/shard_map/all_to_all | solution.py:731
  21.6 2.9 %collective-permute-start.2 = (bf16[208,128]{1,0:T(8,128)(2,1)S(1)}, bf16[208,128]{1,0:T(8,128)(2,1)S(1)}, u32[]{:S(2)}, u32[]{:S(2)}) collective-permute-start(bf16[208,128]{1,0:T(8,128)(2,1)S(1)} %copy-done.18), channel_id=1, source_target_pairs={{0,3},{1,2},{2,1},{3,0},{4,7},{5,6},{6,5},{7,4},{8,11},{9,10},{10,... | collective-permute-start | bytes 159752 | tf_op jit(solution)/shard_map/ppermute | solution.py:650
  24.5 2.4 %collective-permute-start.4 = (bf16[208,128]{1,0:T(8,128)(2,1)S(1)}, bf16[208,128]{1,0:T(8,128)(2,1)S(1)}, u32[]{:S(2)}, u32[]{:S(2)}) collective-permute-start(bf16[208,128]{1,0:T(8,128)(2,1)S(1)} %copy-done.17), channel_id=1, source_target_pairs={{0,5},{1,4},{2,7},{3,6},{4,1},{5,0},{6,3},{7,2},{8,13},{9,12},{10,... | collective-permute-start | bytes 159752 | tf_op jit(solution)/shard_map/ppermute | solution.py:650
  27.4 3.3 %collective-permute-start.6 = (bf16[208,128]{1,0:T(8,128)(2,1)S(1)}, bf16[208,128]{1,0:T(8,128)(2,1)S(1)}, u32[]{:S(2)}, u32[]{:S(2)}) collective-permute-start(bf16[208,128]{1,0:T(8,128)(2,1)S(1)} %copy-done.16), channel_id=1, source_target_pairs={{0,7},{1,6},{2,5},{3,4},{4,3},{5,2},{6,1},{7,0},{8,15},{9,14},{10,... | collective-permute-start | bytes 159752 | tf_op jit(solution)/shard_map/ppermute | solution.py:650
  30.7 1.5 %collective-permute-start.5 = (bf16[208,128]{1,0:T(8,128)(2,1)S(1)}, bf16[208,128]{1,0:T(8,128)(2,1)S(1)}, u32[]{:S(2)}, u32[]{:S(2)}) collective-permute-start(bf16[208,128]{1,0:T(8,128)(2,1)S(1)} %copy-done.16), channel_id=1, source_target_pairs={{0,6},{1,7},{2,4},{3,5},{4,2},{5,3},{6,0},{7,1},{8,14},{9,15},{10,... | collective-permute-start | bytes 159752 | tf_op jit(solution)/shard_map/ppermute | solution.py:650
  32.1 4.6 %collective-permute-done.2.rest_3_ = bf16[208,128]{1,0:T(8,128)(2,1)S(1)} collective-permute-done((bf16[208,128]{1,0:T(8,128)(2,1)S(1)}, bf16[208,128]{1,0:T(8,128)(2,1)S(1)}, u32[]{:S(2)}, u32[]{:S(2)}) %collective-permute-start.2) | collective-permute-done | bytes 53280 | tf_op jit(solution)/shard_map/ppermute | solution.py:650
  36.8 11.9 %collective-permute-done.4.rest_5_ = bf16[208,128]{1,0:T(8,128)(2,1)S(1)} collective-permute-done((bf16[208,128]{1,0:T(8,128)(2,1)S(1)}, bf16[208,128]{1,0:T(8,128)(2,1)S(1)}, u32[]{:S(2)}, u32[]{:S(2)}) %collective-permute-start.4) | collective-permute-done | bytes 53280 | tf_op jit(solution)/shard_map/ppermute | solution.py:650
  48.8 11.0 %shard_map.115 = (bf16[4,576,128]{2,1,0:T(8,128)(2,1)}, bf16[2,576,128]{2,1,0:T(8,128)(2,1)S(1)}, bf16[192,1024]{1,0:T(8,128)(2,1)S(1)}) custom-call(s32[6]{0:T(128)S(1)} %copy-done.9, bf16[2,576,256]{2,1,0:T(8,128)(2,1)S(1)} %copy-done.11, f32[32,1024]{1,0:T(8,128)S(1)} %copy-done.15, f32[32,1024]{1,0:T(8,128)S(1)} %copy-done.14, ...), custom_call_target="tpu_custom_call" | custom-call | flops 8000000000 | bytes 8000000 | tf_op jit(solution)/shard_map/pallas_call | solution.py:693
  59.7 3.5 %all-to-all-start = ((bf16[4,576,128]{2,1,0:T(8,128)(2,1)}), bf16[4,576,128]{2,1,0:T(8,128)(2,1)S(1)}, u32[]{:S(2)}, u32[]{:S(2)}) async-start(bf16[4,576,128]{2,1,0:T(8,128)(2,1)} %get-tuple-element.23), calls=%async_computation | async-start | bytes 1179648 | tf_op jit(solution)/shard_map/all_to_all | solution.py:767
  64.2 1.5 %collective-permute-done.7 = bf16[864,128]{1,0:T(8,128)(2,1)S(1)} collective-permute-done((bf16[864,128]{1,0:T(8,128)(2,1)S(1)}, bf16[864,128]{1,0:T(8,128)(2,1)S(1)}, u32[]{:S(2)}, u32[]{:S(2)}) %collective-permute-start.7) | collective-permute-done | bytes 221216 | tf_op jit(solution)/shard_map/ppermute | solution.py:650
  66.4 1.5 %collective-permute-start.8 = (bf16[864,128]{1,0:T(8,128)(2,1)}, bf16[864,128]{1,0:T(8,128)(2,1)}, u32[]{:S(2)}, u32[]{:S(2)}) collective-permute-start(bf16[864,128]{1,0:T(8,128)(2,1)} %add.17.here_ref), channel_id=1, source_target_pairs={{0,16},{8,24},{16,0},{24,8},{1,17},{9,25},{17,1},{25,9},{2,18},{10... | collective-permute-start | bytes 663560 | tf_op jit(solution)/shard_map/ppermute | solution.py:650
  68.0 10.0 %all-to-all-done.rows_ref.after_ref = bf16[4,576,128]{2,1,0:T(8,128)(2,1)S(1)} async-done(((bf16[4,576,128]{2,1,0:T(8,128)(2,1)}), bf16[4,576,128]{2,1,0:T(8,128)(2,1)S(1)}, u32[]{:S(2)}, u32[]{:S(2)}) %all-to-all-start) | async-done | bytes 589856 | tf_op jit(solution)/shard_map/all_to_all | solution.py:767
  79.2 2.0 %collective-permute-start.9 = (bf16[288,128]{1,0:T(8,128)(2,1)S(1)}, bf16[288,128]{1,0:T(8,128)(2,1)S(1)}, u32[]{:S(2)}, u32[]{:S(2)}) collective-permute-start(bf16[288,128]{1,0:T(8,128)(2,1)S(1)} %get-tuple-element.31), channel_id=1, source_target_pairs={{0,2},{1,3},{2,0},{3,1},{4,6},{5,7},{6,4},{7,5},{8,10},{9,11},{10,... | collective-permute-start | bytes 221192 | tf_op jit(solution)/shard_map/ppermute | solution.py:650
  81.2 2.4 %collective-permute-start.11 = (bf16[288,128]{1,0:T(8,128)(2,1)S(1)}, bf16[288,128]{1,0:T(8,128)(2,1)S(1)}, u32[]{:S(2)}, u32[]{:S(2)}) collective-permute-start(bf16[288,128]{1,0:T(8,128)(2,1)S(1)} %get-tuple-element.33), channel_id=1, source_target_pairs={{0,6},{1,7},{2,4},{3,5},{4,2},{5,3},{6,0},{7,1},{8,14},{9,15},{10,... | collective-permute-start | bytes 221192 | tf_op jit(solution)/shard_map/ppermute | solution.py:650
  83.6 2.1 %collective-permute-done.10.high_ref.g2 = bf16[288,128]{1,0:T(8,128)(2,1)S(1)} collective-permute-done((bf16[288,128]{1,0:T(8,128)(2,1)S(1)}, bf16[288,128]{1,0:T(8,128)(2,1)S(1)}, u32[]{:S(2)}, u32[]{:S(2)}) %collective-permute-start.10) | collective-permute-done | bytes 73760 | tf_op jit(solution)/shard_map/ppermute | solution.py:650
  88.7 1.3 %copy-done.2 = bf16[768,768]{1,0:T(8,128)(2,1)S(1)} copy-done((bf16[768,768]{1,0:T(8,128)(2,1)S(1)}, bf16[768,768]{1,0:T(8,128)(2,1)}, u32[]{:S(2)}) %copy-start.2) | copy-done | bytes 1179672
  89.9 1.9 %shard_map.116.after_ref = bf16[128,768]{1,0:T(8,128)(2,1)} custom-call(s32[1,128]{1,0:T(1,128)S(1)} %copy-done.10, bf16[256,768]{1,0:T(8,128)(2,1)S(1)} %copy-done.3, bf16[768,768]{1,0:T(8,128)(2,1)S(1)} %copy-done, bf16[768,768]{1,0:T(8,128)(2,1)S(1)} %copy-done.1, bf16[768,768]{1,0:T(8,128)(2,1)S(1)} %copy-done.2, ...), custom_call_target="tpu_custom_call" | custom-call | flops 1000000000 | bytes 5000000 | tf_op jit(solution)/shard_map/pallas_call | solution.py:693
  93.5 1.6 %collective-permute-done.14.other_ref = bf16[1152,128]{1,0:T(8,128)(2,1)S(1)} collective-permute-done((bf16[1152,128]{1,0:T(8,128)(2,1)S(1)}, bf16[1152,128]{1,0:T(8,128)(2,1)S(1)}, u32[]{:S(2)}, u32[]{:S(2)}) %collective-permute-start.14) | collective-permute-done | bytes 294944 | tf_op jit(solution)/shard_map/ppermute | solution.py:650
  95.1 2.1 %shard_map.122 = f32[384,768]{1,0:T(8,128)} custom-call(s32[6]{0:T(128)S(1)} %copy-done.9, bf16[256,384]{1,0:T(8,128)(2,1)S(1)} %copy-done.12, bf16[1152,128]{1,0:T(8,128)(2,1)S(1)} %shard_map.121.mine_ref, bf16[1152,128]{1,0:T(8,128)(2,1)S(1)} %collective-permute-done.14.other_ref), custom_call_target="tpu_custom_call" | custom-call | flops 1000000000 | bytes 5000000 | tf_op jit(solution)/shard_map/pallas_call | solution.py:693
  (64 shorter events, 10.1 us)
Async XLA Ops:
  3.9 5.3 %collective-permute-start = (bf16[208,128]{1,0:T(8,128)(2,1)}, bf16[208,128]{1,0:T(8,128)(2,1)S(1)}, u32[]{:S(2)}, u32[]{:S(2)}) collective-permute-start(bf16[208,128]{1,0:T(8,128)(2,1)} %get-tuple-element.18.rest_0_), channel_id=1, source_target_pairs={{0,1},{1,0},{2,3},{3,2},{4,5},{5,4},{6,7},{7,6},{8,9},{9,8},{10,11... | collective-permute-start | bytes 159752 | tf_op jit(solution)/shard_map/ppermute | solution.py:650
  6.8 4.3 %collective-permute-start.1 = (bf16[208,128]{1,0:T(8,128)(2,1)}, bf16[208,128]{1,0:T(8,128)(2,1)S(1)}, u32[]{:S(2)}, u32[]{:S(2)}) collective-permute-start(bf16[208,128]{1,0:T(8,128)(2,1)} %get-tuple-element.19), channel_id=1, source_target_pairs={{0,2},{1,3},{2,0},{3,1},{4,6},{5,7},{6,4},{7,5},{8,10},{9,11},{10,... | collective-permute-start | bytes 159752 | tf_op jit(solution)/shard_map/ppermute | solution.py:650
  16.4 32.3 %copy-start.6 = (bf16[208,128]{1,0:T(8,128)(2,1)S(1)}, bf16[208,128]{1,0:T(8,128)(2,1)}, u32[]{:S(2)}) copy-start(bf16[208,128]{1,0:T(8,128)(2,1)} %copy-done.5) | copy-start | bytes 159748
  16.4 32.3 %copy-start.8 = (bf16[208,128]{1,0:T(8,128)(2,1)S(1)}, bf16[208,128]{1,0:T(8,128)(2,1)}, u32[]{:S(2)}) copy-start(bf16[208,128]{1,0:T(8,128)(2,1)} %copy-done.7) | copy-start | bytes 159748
  16.4 32.3 %copy-start.9 = (s32[6]{0:T(128)S(1)}, s32[6]{0:T(128)}, u32[]{:S(2)}) copy-start(s32[6]{0:T(128)} %pad_add_fusion.meta_ref) | copy-start | bytes 76
  16.4 32.3 %copy-start.11 = (bf16[2,576,256]{2,1,0:T(8,128)(2,1)S(1)}, bf16[2,576,256]{2,1,0:T(8,128)(2,1)}, u32[]{:S(2)}) copy-start(bf16[2,576,256]{2,1,0:T(8,128)(2,1)} %get-tuple-element.20.lookup_ref) | copy-start | bytes 1769476
  16.4 32.3 %copy-start.13 = (bf16[208,128]{1,0:T(8,128)(2,1)S(1)}, bf16[208,128]{1,0:T(8,128)(2,1)}, u32[]{:S(2)}) copy-start(bf16[208,128]{1,0:T(8,128)(2,1)} %get-tuple-element.18.rest_0_) | copy-start | bytes 159748
  16.4 32.3 %copy-start.14 = (f32[32,1024]{1,0:T(8,128)S(1)}, f32[32,1024]{1,0:T(8,128)}, u32[]{:S(2)}) copy-start(f32[32,1024]{1,0:T(8,128)} %constant.46.clone.sine_ref) | copy-start | bytes 393220
  16.5 32.3 %copy-start.15 = (f32[32,1024]{1,0:T(8,128)S(1)}, f32[32,1024]{1,0:T(8,128)}, u32[]{:S(2)}) copy-start(f32[32,1024]{1,0:T(8,128)} %constant.45.clone.cosine_ref) | copy-start | bytes 393220
  16.5 43.2 %all-to-all-start.1 = ((bf16[8,128,384]{2,1,0:T(8,128)(2,1)}), bf16[8,128,384]{2,1,0:T(8,128)(2,1)S(1)}, u32[]{:S(2)}, u32[]{:S(2)}) async-start(bf16[8,128,384]{2,1,0:T(8,128)(2,1)} %get-tuple-element.26), calls=%async_computation.1 | async-start | bytes 1572864 | tf_op jit(solution)/shard_map/all_to_all | solution.py:731
  21.6 15.2 %collective-permute-start.2 = (bf16[208,128]{1,0:T(8,128)(2,1)S(1)}, bf16[208,128]{1,0:T(8,128)(2,1)S(1)}, u32[]{:S(2)}, u32[]{:S(2)}) collective-permute-start(bf16[208,128]{1,0:T(8,128)(2,1)S(1)} %copy-done.18), channel_id=1, source_target_pairs={{0,3},{1,2},{2,1},{3,0},{4,7},{5,6},{6,5},{7,4},{8,11},{9,10},{10,... | collective-permute-start | bytes 159752 | tf_op jit(solution)/shard_map/ppermute | solution.py:650
  24.5 24.2 %collective-permute-start.4 = (bf16[208,128]{1,0:T(8,128)(2,1)S(1)}, bf16[208,128]{1,0:T(8,128)(2,1)S(1)}, u32[]{:S(2)}, u32[]{:S(2)}) collective-permute-start(bf16[208,128]{1,0:T(8,128)(2,1)S(1)} %copy-done.17), channel_id=1, source_target_pairs={{0,5},{1,4},{2,7},{3,6},{4,1},{5,0},{6,3},{7,2},{8,13},{9,12},{10,... | collective-permute-start | bytes 159752 | tf_op jit(solution)/shard_map/ppermute | solution.py:650
  26.8 21.8 %collective-permute-start.3 = (bf16[208,128]{1,0:T(8,128)(2,1)S(1)}, bf16[208,128]{1,0:T(8,128)(2,1)S(1)}, u32[]{:S(2)}, u32[]{:S(2)}) collective-permute-start(bf16[208,128]{1,0:T(8,128)(2,1)S(1)} %copy-done.17), channel_id=1, source_target_pairs={{0,4},{1,5},{2,6},{3,7},{4,0},{5,1},{6,2},{7,3},{8,12},{9,13},{10,... | collective-permute-start | bytes 159752 | tf_op jit(solution)/shard_map/ppermute | solution.py:650
  27.4 21.3 %collective-permute-start.6 = (bf16[208,128]{1,0:T(8,128)(2,1)S(1)}, bf16[208,128]{1,0:T(8,128)(2,1)S(1)}, u32[]{:S(2)}, u32[]{:S(2)}) collective-permute-start(bf16[208,128]{1,0:T(8,128)(2,1)S(1)} %copy-done.16), channel_id=1, source_target_pairs={{0,7},{1,6},{2,5},{3,4},{4,3},{5,2},{6,1},{7,0},{8,15},{9,14},{10,... | collective-permute-start | bytes 159752 | tf_op jit(solution)/shard_map/ppermute | solution.py:650
  30.7 18.0 %collective-permute-start.5 = (bf16[208,128]{1,0:T(8,128)(2,1)S(1)}, bf16[208,128]{1,0:T(8,128)(2,1)S(1)}, u32[]{:S(2)}, u32[]{:S(2)}) collective-permute-start(bf16[208,128]{1,0:T(8,128)(2,1)S(1)} %copy-done.16), channel_id=1, source_target_pairs={{0,6},{1,7},{2,4},{3,5},{4,2},{5,3},{6,0},{7,1},{8,14},{9,15},{10,... | collective-permute-start | bytes 159752 | tf_op jit(solution)/shard_map/ppermute | solution.py:650
  59.7 18.3 %all-to-all-start = ((bf16[4,576,128]{2,1,0:T(8,128)(2,1)}), bf16[4,576,128]{2,1,0:T(8,128)(2,1)S(1)}, u32[]{:S(2)}, u32[]{:S(2)}) async-start(bf16[4,576,128]{2,1,0:T(8,128)(2,1)} %get-tuple-element.23), calls=%async_computation | async-start | bytes 1179648 | tf_op jit(solution)/shard_map/all_to_all | solution.py:767
  64.2 1.5 %collective-permute-start.7 = (bf16[864,128]{1,0:T(8,128)(2,1)S(1)}, bf16[864,128]{1,0:T(8,128)(2,1)S(1)}, u32[]{:S(2)}, u32[]{:S(2)}) collective-permute-start(bf16[864,128]{1,0:T(8,128)(2,1)S(1)} %get-tuple-element.29), channel_id=1, source_target_pairs={{0,8},{8,0},{16,24},{24,16},{1,9},{9,1},{17,25},{25,17},{2,10},{10... | collective-permute-start | bytes 663560 | tf_op jit(solution)/shard_map/ppermute | solution.py:650
  66.4 11.5 %collective-permute-start.8 = (bf16[864,128]{1,0:T(8,128)(2,1)}, bf16[864,128]{1,0:T(8,128)(2,1)}, u32[]{:S(2)}, u32[]{:S(2)}) collective-permute-start(bf16[864,128]{1,0:T(8,128)(2,1)} %add.17.here_ref), channel_id=1, source_target_pairs={{0,16},{8,24},{16,0},{24,8},{1,17},{9,25},{17,1},{25,9},{2,18},{10... | collective-permute-start | bytes 663560 | tf_op jit(solution)/shard_map/ppermute | solution.py:650
  79.1 6.6 %collective-permute-start.10 = (bf16[288,128]{1,0:T(8,128)(2,1)S(1)}, bf16[288,128]{1,0:T(8,128)(2,1)S(1)}, u32[]{:S(2)}, u32[]{:S(2)}) collective-permute-start(bf16[288,128]{1,0:T(8,128)(2,1)S(1)} %get-tuple-element.32), channel_id=1, source_target_pairs={{0,4},{1,5},{2,6},{3,7},{4,0},{5,1},{6,2},{7,3},{8,12},{9,13},{10,... | collective-permute-start | bytes 221192 | tf_op jit(solution)/shard_map/ppermute | solution.py:650
  79.2 7.7 %collective-permute-start.9 = (bf16[288,128]{1,0:T(8,128)(2,1)S(1)}, bf16[288,128]{1,0:T(8,128)(2,1)S(1)}, u32[]{:S(2)}, u32[]{:S(2)}) collective-permute-start(bf16[288,128]{1,0:T(8,128)(2,1)S(1)} %get-tuple-element.31), channel_id=1, source_target_pairs={{0,2},{1,3},{2,0},{3,1},{4,6},{5,7},{6,4},{7,5},{8,10},{9,11},{10,... | collective-permute-start | bytes 221192 | tf_op jit(solution)/shard_map/ppermute | solution.py:650
  81.2 6.2 %collective-permute-start.11 = (bf16[288,128]{1,0:T(8,128)(2,1)S(1)}, bf16[288,128]{1,0:T(8,128)(2,1)S(1)}, u32[]{:S(2)}, u32[]{:S(2)}) collective-permute-start(bf16[288,128]{1,0:T(8,128)(2,1)S(1)} %get-tuple-element.33), channel_id=1, source_target_pairs={{0,6},{1,7},{2,4},{3,5},{4,2},{5,3},{6,0},{7,1},{8,14},{9,15},{10,... | collective-permute-start | bytes 221192 | tf_op jit(solution)/shard_map/ppermute | solution.py:650
  86.3 5.6 %collective-permute-start.12 = (bf16[288,128]{1,0:T(8,128)(2,1)S(1)}, bf16[288,128]{1,0:T(8,128)(2,1)S(1)}, u32[]{:S(2)}, u32[]{:S(2)}) collective-permute-start(bf16[288,128]{1,0:T(8,128)(2,1)S(1)} %shard_map.119), channel_id=1, source_target_pairs={{6,7},{7,6},{14,15},{15,14},{22,23},{23,22},{30,31},{31,30}} | collective-permute-start | bytes 221192 | tf_op jit(solution)/shard_map/ppermute | solution.py:803
  88.0 3.9 %collective-permute-start.13 = (bf16[288,128]{1,0:T(8,128)(2,1)S(1)}, bf16[288,128]{1,0:T(8,128)(2,1)S(1)}, u32[]{:S(2)}, u32[]{:S(2)}) collective-permute-start(bf16[288,128]{1,0:T(8,128)(2,1)S(1)} %shard_map.120), channel_id=1, source_target_pairs={{6,7},{7,6},{14,15},{15,14},{22,23},{23,22},{30,31},{31,30}} | collective-permute-start | bytes 221192 | tf_op jit(solution)/shard_map/ppermute | solution.py:803
  93.4 1.6 %collective-permute-start.14 = (bf16[1152,128]{1,0:T(8,128)(2,1)S(1)}, bf16[1152,128]{1,0:T(8,128)(2,1)S(1)}, u32[]{:S(2)}, u32[]{:S(2)}) collective-permute-start(bf16[1152,128]{1,0:T(8,128)(2,1)S(1)} %shard_map.121.mine_ref), channel_id=1, source_target_pairs={{0,8},{8,0},{16,24},{24,16},{1,9},{9,1},{17,25},{25,17},{2,10},{10... | collective-permute-start | bytes 884744 | tf_op jit(solution)/shard_map/ppermute | solution.py:650
  (13 other events, 136.3 us)

commit v8 on v7

--- a/solution.py
+++ b/solution.py
@@ -230,6 +230,7 @@
 STRIP = 8
 HALF = HEAD_DIM // 2
 VMEM_BYTES = 48 * 1024 * 1024
+LARGE_BYTES = 60 * 1024 * 1024
 
 
 def key_span(query_tile):
@@ -263,6 +264,22 @@
         early_ref[GROUP_COLS:, :] = tokens
 
 
+def gate_kernel(*refs):
+    del refs
+
+
+def gated(block, *others):
+    return pl.pallas_call(
+        gate_kernel,
+        grid=(1,),
+        in_specs=[pl.BlockSpec(memory_space=pl.ANY)] + [whole((16, 128))] * len(others),
+        out_specs=pl.BlockSpec(memory_space=pl.ANY),
+        out_shape=jax.ShapeDtypeStruct(block.shape, block.dtype),
+        input_output_aliases={0: 0},
+        compiler_params=pltpu.CompilerParams(vmem_limit_bytes=LARGE_BYTES),
+    )(block, *others)
+
+
 def prepare_kernel(
     meta_ref,
     cotangent_ref,
@@ -270,14 +287,11 @@
     query_ref,
     key_ref,
     value_ref,
-    first_ref,
-    second_ref,
     late_ref,
     lookup_ref,
     normed_ref,
     columns_ref,
 ):
-    del first_ref, second_ref
     columns = late_ref.shape[2]
     for target in range(2 * GROUPS):
         side = target % 2
@@ -315,6 +329,7 @@
     sine_ref,
     early_refs,
     rows_ref,
+    tail_ref,
     sums_ref,
     attended_ref,
     value_key_ref,
@@ -503,6 +518,7 @@
         axis=0,
     ).astype(half)
     sums = jnp.dot(grads, onehot_rows_ref[...], preferred_element_type=jnp.float32).astype(half)
+    tail = pl.multiple_of(head * HEAD_DIM, HEAD_DIM)
     for matrix in range(3):
         rows = slice(matrix * HEAD_DIM, (matrix + 1) * HEAD_DIM)
         place = pl.ds(
@@ -515,7 +531,11 @@
             start = target * 2 * block
             even = grads[rows, start : start + block]
             odd = grads[rows, start + block : start + 2 * block]
-            rows_ref[target, place, :] = jnp.where(meta_ref[GROUP_HEADS] == 0, even, odd)
+            mine = jnp.where(meta_ref[GROUP_HEADS] == 0, even, odd)
+            if matrix < 2:
+                rows_ref[target, place, :] = mine
+            else:
+                tail_ref[target, pl.ds(tail, HEAD_DIM), :] = mine
 
 
 def out_kernel(meta_ref, attended_ref, cotangent_ref, sums_ref, keep_ref, give_ref):
@@ -555,8 +575,7 @@
     out_ref[...] = jnp.where(meta_ref[GROUP_HEADS] == 0, low_ref[...], high_ref[...])
 
 
-def gather_kernel(meta_ref, g0, g1, g2, g3, early_ref, late_ref, after_ref, mine_ref):
-    del after_ref
+def gather_kernel(meta_ref, g0, g1, g2, g3, early_ref, late_ref, mine_ref):
     rows = GROUP_COLS
     size = g0.shape[0]
     group = meta_ref[GROUP_HEADS + 1]
@@ -581,16 +600,19 @@
             mine_ref[place * size : (place + 1) * size, :] = piece[...]
 
 
-def input_kernel(tokens_ref, table_ref, query_ref, key_ref, value_ref, rows_ref, out_ref):
+def input_kernel(
+    tokens_ref, table_ref, query_ref, key_ref, value_ref, rows_ref, tail_ref, out_ref
+):
     vocab = table_ref.shape[0]
     onehot = onehot_columns(tokens_ref[...], vocab)
     embedded = tdot(onehot, table_ref[...])
     inv_rms = lax.rsqrt(jnp.mean(embedded * embedded, axis=1, keepdims=True) + EPSILON)
     grad_normed = None
     for matrix, weights in enumerate((query_ref, key_ref, value_ref)):
+        place = slice(matrix * GROUP_COLS, (matrix + 1) * GROUP_COLS)
         columns = jnp.concatenate(
             [
-                rows_ref[group, matrix * GROUP_COLS : (matrix + 1) * GROUP_COLS, :]
+                rows_ref[group, place, :] if matrix < 2 else tail_ref[group]
                 for group in range(GROUPS)
             ],
             axis=0,
@@ -681,13 +703,11 @@
     cosine, sine_part = rope_table(length)
 
     def call(
-        body, operands, outs, scratch=(), steps=1, flops=10**8, moved=10**6, loose=0, peeked=0, grant=VMEM_BYTES
+        body, operands, outs, scratch=(), steps=1, flops=10**8, moved=10**6, loose=0, grant=VMEM_BYTES
     ):
         spaces = [whole(operand.shape) for operand in operands]
         for index in range(loose):
             spaces[-1 - index] = pl.BlockSpec(memory_space=pl.ANY)
-        for index in range(peeked):
-            spaces[-1 - index] = whole((16, 128))
         if operands[0].ndim == 1:
             spaces[0] = pl.BlockSpec(memory_space=pltpu.SMEM)
         return pl.pallas_call(
@@ -709,14 +729,14 @@
         (spot, token_ids, grad_out, w_out),
         [((GROUP_COLS + TOKEN_ROWS, block), half)] * GROUPS,
         [pltpu.VMEM((features, block), half)],
-        grant=60 * 1024 * 1024,
+        grant=LARGE_BYTES,
     )
     early = [sent[0]] + [None] * (blocks - 1)
     for turn in (4, 6, 5, 7, 2, 3, 1):
         early[turn] = swapped(sent[turn // 2], "seq", turn)
     late, lookup, normed = call(
         prepare_kernel,
-        (meta, grad_out, table, w_query, w_key, w_value, early[1], early[2]),
+        (meta, grad_out, table, w_query, w_key, w_value),
         [
             ((blocks, block, features // 2), half),
             ((2, 3 * GROUP_COLS, vocab), half),
@@ -725,17 +745,18 @@
         [pltpu.VMEM((features, vocab), jnp.float32)],
         flops=10**9,
         moved=5 * 10**6,
-        peeked=2,
-        grant=60 * 1024 * 1024,
-    )
+        grant=LARGE_BYTES,
+    )
+    late = gated(late, *early[1:])
     late = lax.all_to_all(late, "seq", split_axis=0, concat_axis=0, tiled=True)
     heads_shape = (GROUP_HEADS, HEAD_DIM, length)
     rows_shape = (GROUP_HEADS, length, 2 * HEAD_DIM)
-    rows, sums, attended = call(
+    rows, tail, sums, attended = call(
         attention_kernel,
         (meta, lookup, cosine, sine_part, *early),
         [
-            ((GROUPS, 3 * GROUP_COLS, block), half),
+            ((GROUPS, 2 * GROUP_COLS, block), half),
+            ((GROUPS, GROUP_COLS, block), half),
             ((2, 3 * GROUP_COLS, vocab // 2), half),
             ((GROUP_COLS, length), half),
         ],
@@ -788,9 +809,10 @@
     got = [pieces[0]] + [None] * (GROUPS - 1)
     for turn in (2, 3, 1):
         got[turn] = swapped(pieces[turn], "seq", 2 * turn)
+    got_tail = over_plane(gated(tail, got[2]))
     (grad_input,) = call(
         input_kernel,
-        (token_ids, table, w_query, w_key, w_value, got_rows),
+        (token_ids, table, w_query, w_key, w_value, got_rows, got_tail),
         [((block, features), half)],
         flops=10**9,
         moved=5 * 10**6,
@@ -803,9 +825,8 @@
         crossed.append(lax.ppermute(piece, "seq", between))
     (mine,) = call(
         gather_kernel,
-        (meta, *got, *crossed, grad_input),
+        (meta, *got, *crossed),
         [((4 * out_rows, lanes), half)],
-        loose=1,
     )
     (weight_grads,) = call(
         weight_kernel,

time: 98.6 us -> 104 us (1.055)
  the two profiles are of different devices: /device:TPU:0 before, /device:TPU:25 now
where the time goes in v8:
time: 104 us; the launch traced here: 103 us
  starting transfers between devices  45 us (43%)
  Pallas kernels  30 us (29%)
  waiting for transfers between devices  16.7 us (16%)
  local copies, waits for them, and re-layouts  8.97 us (9%)
  other arithmetic  1.28 us (1%)
    pallas_call x10, Pallas kernels, call(): pl.pallas_call(body, grid=(steps,), in_specs=spaces, out_specs=[whole(sha...  28.6 us
    ppermute x13, starting transfers between devices, swapped(): return lax.ppermute(block, axis, route)  26 us
    ppermute x13, waiting for transfers between devices, swapped(): return lax.ppermute(block, axis, route)  9.12 us
    all_to_all x2, starting transfers between devices, over_plane(): lax.all_to_all(chunks, 'seq', split_axis=0, concat_axis=0, axis_index_gro...  9.06 us
    unnamed x70, local copies, waits for them, and re-layouts  8.9 us
    ppermute x2, starting transfers between devices, grouped_device(): crossed.append(lax.ppermute(piece, 'seq', between))  5.28 us
    all_to_all x1, starting transfers between devices, grouped_device(): late = lax.all_to_all(late, 'seq', split_axis=0, concat_axis=0, tiled=True)  4.68 us
    all_to_all x1, waiting for transfers between devices, grouped_device(): late = lax.all_to_all(late, 'seq', split_axis=0, concat_axis=0, tiled=True)  4.09 us
  transfers between devices with their start and end apart: 18, of which 6 were waited for; matrix products, arithmetic and copies ran while one was open for 1% of the time, Pallas kernels for 23%

profile of v8, /device:TPU:25, one launch (start us, length us, event | category | flops | bytes accessed | tf_op | source)
XLA Modules:
  0.0 103.0 jit_solution(14719096289121756046)
XLA Ops:
  1.2 2.6 %shard_map.114 = (bf16[208,128]{1,0:T(8,128)(2,1)}, bf16[208,128]{1,0:T(8,128)(2,1)}, bf16[208,128]{1,0:T(8,128)(2,1)}, bf16[208,128]{1,0:T(8,128)(2,1)}) custom-call(s32[3]{0:T(128)} %pad_add_fusion.1.spot_ref, s32[1,128]{1,0:T(1,128)} %tokens_ref.3, bf16[128,768]{1,0:T(8,128)(2,1)} %bitcast.7, bf16[768,768]{1,0:T(8,128)(2,1)} %out_weights_ref.1), custom_call_target="tpu_custom_call" | custom-call | flops 100000000 | bytes 1000000 | tf_op jit(solution)/shard_map/pallas_call | solution.py:713
  4.0 2.2 %collective-permute-start.2 = (bf16[208,128]{1,0:T(8,128)(2,1)}, bf16[208,128]{1,0:T(8,128)(2,1)S(1)}, u32[]{:S(2)}, u32[]{:S(2)}) collective-permute-start(bf16[208,128]{1,0:T(8,128)(2,1)} %get-tuple-element.21), channel_id=1, source_target_pairs={{0,3},{1,2},{2,1},{3,0},{4,7},{5,6},{6,5},{7,4},{8,11},{9,10},{10,... | collective-permute-start | bytes 159752 | tf_op jit(solution)/shard_map/ppermute | solution.py:672
  6.2 2.3 %collective-permute-start.4 = (bf16[208,128]{1,0:T(8,128)(2,1)}, bf16[208,128]{1,0:T(8,128)(2,1)S(1)}, u32[]{:S(2)}, u32[]{:S(2)}) collective-permute-start(bf16[208,128]{1,0:T(8,128)(2,1)} %get-tuple-element.22), channel_id=1, source_target_pairs={{0,5},{1,4},{2,7},{3,6},{4,1},{5,0},{6,3},{7,2},{8,13},{9,12},{10,... | collective-permute-start | bytes 159752 | tf_op jit(solution)/shard_map/ppermute | solution.py:672
  10.5 1.2 %collective-permute-done.rest_1_.refs_1_ = bf16[208,128]{1,0:T(8,128)(2,1)S(1)} collective-permute-done((bf16[208,128]{1,0:T(8,128)(2,1)}, bf16[208,128]{1,0:T(8,128)(2,1)S(1)}, u32[]{:S(2)}, u32[]{:S(2)}) %collective-permute-start) | collective-permute-done | bytes 53280 | tf_op jit(solution)/shard_map/ppermute | solution.py:672
  11.9 4.4 %collective-permute-start.6 = (bf16[208,128]{1,0:T(8,128)(2,1)}, bf16[208,128]{1,0:T(8,128)(2,1)S(1)}, u32[]{:S(2)}, u32[]{:S(2)}) collective-permute-start(bf16[208,128]{1,0:T(8,128)(2,1)} %get-tuple-element.23), channel_id=1, source_target_pairs={{0,7},{1,6},{2,5},{3,4},{4,3},{5,2},{6,1},{7,0},{8,15},{9,14},{10,... | collective-permute-start | bytes 159752 | tf_op jit(solution)/shard_map/ppermute | solution.py:672
  16.3 4.6 %shard_map.113 = (bf16[8,128,384]{2,1,0:T(8,128)(2,1)}, bf16[2,576,256]{2,1,0:T(8,128)(2,1)}, bf16[256,384]{1,0:T(8,128)(2,1)}) custom-call(s32[6]{0:T(128)} %pad_add_fusion.meta_ref, bf16[128,768]{1,0:T(8,128)(2,1)} %bitcast.8, bf16[256,768]{1,0:T(8,128)(2,1)} %table_ref.3, bf16[768,768]{1,0:T(8,128)(2,1)} %query_ref.3, bf16[768,768]{1,0:T(8,128)(2,1)} %key_ref.3, ...), custom_call_target="tpu_custom_call" | custom-call | flops 1000000000 | bytes 5000000 | tf_op jit(solution)/shard_map/pallas_call | solution.py:713
  22.5 4.7 %all-to-all-start.1 = ((bf16[8,128,384]{2,1,0:T(8,128)(2,1)}), bf16[8,128,384]{2,1,0:T(8,128)(2,1)S(1)}, u32[]{:S(2)}, u32[]{:S(2)}) async-start(bf16[8,128,384]{2,1,0:T(8,128)(2,1)} %shard_map.116), calls=%async_computation.1 | async-start | bytes 1572864 | tf_op jit(solution)/shard_map/all_to_all | solution.py:751
  27.3 10.9 %shard_map.115 = (bf16[4,384,128]{2,1,0:T(8,128)(2,1)}, bf16[4,192,128]{2,1,0:T(8,128)(2,1)S(1)}, bf16[2,576,128]{2,1,0:T(8,128)(2,1)S(1)}, bf16[192,1024]{1,0:T(8,128)(2,1)S(1)}) custom-call(s32[6]{0:T(128)S(1)} %copy-done.27, bf16[2,576,256]{2,1,0:T(8,128)(2,1)S(1)} %copy-done.29, f32[32,1024]{1,0:T(8,128)S(1)} %copy-done.32, f32[32,1024]{1,0:T(8,128)S(1)} %copy-done.33, ...), custom_call_target="tpu_custom_call" | custom-call | flops 8000000000 | bytes 8000000 | tf_op jit(solution)/shard_map/pallas_call | solution.py:713
  38.8 4.1 %all-to-all-done.1 = bf16[8,128,384]{2,1,0:T(8,128)(2,1)S(1)} async-done(((bf16[8,128,384]{2,1,0:T(8,128)(2,1)}), bf16[8,128,384]{2,1,0:T(8,128)(2,1)S(1)}, u32[]{:S(2)}, u32[]{:S(2)}) %all-to-all-start.1) | async-done | bytes 786464 | tf_op jit(solution)/shard_map/all_to_all | solution.py:751
  42.9 4.5 %all-to-all-start = ((bf16[4,384,128]{2,1,0:T(8,128)(2,1)}), bf16[4,384,128]{2,1,0:T(8,128)(2,1)S(1)}, u32[]{:S(2)}, u32[]{:S(2)}) async-start(bf16[4,384,128]{2,1,0:T(8,128)(2,1)} %get-tuple-element.24), calls=%async_computation | async-start | bytes 786432 | tf_op jit(solution)/shard_map/all_to_all | solution.py:788
  48.4 4.7 %collective-permute-start.7 = (bf16[864,128]{1,0:T(8,128)(2,1)S(1)}, bf16[864,128]{1,0:T(8,128)(2,1)S(1)}, u32[]{:S(2)}, u32[]{:S(2)}) collective-permute-start(bf16[864,128]{1,0:T(8,128)(2,1)S(1)} %get-tuple-element.30), channel_id=1, source_target_pairs={{0,8},{8,0},{16,24},{24,16},{1,9},{9,1},{17,25},{25,17},{2,10},{10... | collective-permute-start | bytes 663560 | tf_op jit(solution)/shard_map/ppermute | solution.py:672
  54.3 1.3 %collective-permute-start.8 = (bf16[864,128]{1,0:T(8,128)(2,1)S(1)}, bf16[864,128]{1,0:T(8,128)(2,1)S(1)}, u32[]{:S(2)}, u32[]{:S(2)}) collective-permute-start(bf16[864,128]{1,0:T(8,128)(2,1)S(1)} %add.17.here_ref), channel_id=1, source_target_pairs={{0,16},{8,24},{16,0},{24,8},{1,17},{9,25},{17,1},{25,9},{2,18},{10... | collective-permute-start | bytes 663560 | tf_op jit(solution)/shard_map/ppermute | solution.py:672
  55.6 5.4 %collective-permute-done.8.there_ref = bf16[864,128]{1,0:T(8,128)(2,1)S(1)} collective-permute-done((bf16[864,128]{1,0:T(8,128)(2,1)S(1)}, bf16[864,128]{1,0:T(8,128)(2,1)S(1)}, u32[]{:S(2)}, u32[]{:S(2)}) %collective-permute-start.8) | collective-permute-done | bytes 221216 | tf_op jit(solution)/shard_map/ppermute | solution.py:672
  61.0 1.3 %shard_map.118 = (bf16[288,128]{1,0:T(8,128)(2,1)S(1)}, bf16[288,128]{1,0:T(8,128)(2,1)}, bf16[288,128]{1,0:T(8,128)(2,1)S(1)}, bf16[288,128]{1,0:T(8,128)(2,1)}) custom-call(s32[6]{0:T(128)S(1)} %copy-done.27, bf16[864,128]{1,0:T(8,128)(2,1)S(1)} %add.17.here_ref, bf16[864,128]{1,0:T(8,128)(2,1)S(1)} %collective-permute-done.8.there_ref, ...), custom_call_target="tpu_custom_call" | custom-call | flops 100000000 | bytes 1000000 | tf_op jit(solution)/shard_map/pallas_call | solution.py:713
  64.0 3.3 %collective-permute-start.11 = (bf16[288,128]{1,0:T(8,128)(2,1)}, bf16[288,128]{1,0:T(8,128)(2,1)}, u32[]{:S(2)}, u32[]{:S(2)}) collective-permute-start(bf16[288,128]{1,0:T(8,128)(2,1)} %get-tuple-element.35), channel_id=1, source_target_pairs={{0,6},{1,7},{2,4},{3,5},{4,2},{5,3},{6,0},{7,1},{8,14},{9,15},{10,... | collective-permute-start | bytes 221192 | tf_op jit(solution)/shard_map/ppermute | solution.py:672
  67.2 1.3 %collective-permute-done.9.refs_1_.high_ref.g2 = bf16[288,128]{1,0:T(8,128)(2,1)S(1)} collective-permute-done((bf16[288,128]{1,0:T(8,128)(2,1)S(1)}, bf16[288,128]{1,0:T(8,128)(2,1)S(1)}, u32[]{:S(2)}, u32[]{:S(2)}) %collective-permute-start.9) | collective-permute-done | bytes 73760 | tf_op jit(solution)/shard_map/ppermute | solution.py:672
  69.9 4.5 %all-to-all-start.2 = ((bf16[4,192,128]{2,1,0:T(8,128)(2,1)}), bf16[4,192,128]{2,1,0:T(8,128)(2,1)}, u32[]{:S(2)}, u32[]{:S(2)}) async-start(bf16[4,192,128]{2,1,0:T(8,128)(2,1)} %shard_map.119), calls=%async_computation.2 | async-start | bytes 393216 | tf_op jit(solution)/shard_map/all_to_all | solution.py:788
  75.4 2.9 %collective-permute-start.13 = (bf16[288,128]{1,0:T(8,128)(2,1)S(1)}, bf16[288,128]{1,0:T(8,128)(2,1)S(1)}, u32[]{:S(2)}, u32[]{:S(2)}) collective-permute-start(bf16[288,128]{1,0:T(8,128)(2,1)S(1)} %shard_map.122), channel_id=1, source_target_pairs={{6,7},{7,6},{14,15},{15,14},{22,23},{23,22},{30,31},{31,30}} | collective-permute-start | bytes 221192 | tf_op jit(solution)/shard_map/ppermute | solution.py:825
  80.6 2.4 %collective-permute-start.12 = (bf16[288,128]{1,0:T(8,128)(2,1)S(1)}, bf16[288,128]{1,0:T(8,128)(2,1)S(1)}, u32[]{:S(2)}, u32[]{:S(2)}) collective-permute-start(bf16[288,128]{1,0:T(8,128)(2,1)S(1)} %shard_map.121), channel_id=1, source_target_pairs={{6,7},{7,6},{14,15},{15,14},{22,23},{23,22},{30,31},{31,30}} | collective-permute-start | bytes 221192 | tf_op jit(solution)/shard_map/ppermute | solution.py:825
  83.0 3.5 %collective-permute-done.12.early_ref = bf16[288,128]{1,0:T(8,128)(2,1)S(1)} collective-permute-done((bf16[288,128]{1,0:T(8,128)(2,1)S(1)}, bf16[288,128]{1,0:T(8,128)(2,1)S(1)}, u32[]{:S(2)}, u32[]{:S(2)}) %collective-permute-start.12) | collective-permute-done | bytes 73760 | tf_op jit(solution)/shard_map/ppermute | solution.py:825
  88.3 1.7 %shard_map.123.mine_ref = bf16[1152,128]{1,0:T(8,128)(2,1)} custom-call(s32[6]{0:T(128)S(1)} %copy-done.27, bf16[288,128]{1,0:T(8,128)(2,1)S(1)} %copy-done.12, bf16[288,128]{1,0:T(8,128)(2,1)} %collective-permute-done.10.low_ref.g1, bf16[288,128]{1,0:T(8,128)(2,1)S(1)} %copy-done.9, bf16[288,128]{1,0:T(8,128)(2,1)} %collective-permute-done.11.high_ref.g3, ...), custom_call_target="tpu_custom_call" | custom-call | flops 100000000 | bytes 1000000 | tf_op jit(solution)/shard_map/pallas_call | solution.py:713
  90.0 5.9 %collective-permute-start.14 = (bf16[1152,128]{1,0:T(8,128)(2,1)}, bf16[1152,128]{1,0:T(8,128)(2,1)}, u32[]{:S(2)}, u32[]{:S(2)}) collective-permute-start(bf16[1152,128]{1,0:T(8,128)(2,1)} %shard_map.123.mine_ref), channel_id=1, source_target_pairs={{0,8},{8,0},{16,24},{24,16},{1,9},{9,1},{17,25},{25,17},{2,10},{10... | collective-permute-start | bytes 884744 | tf_op jit(solution)/shard_map/ppermute | solution.py:672
  97.8 2.9 %shard_map.120 = bf16[128,768]{1,0:T(8,128)(2,1)} custom-call(s32[1,128]{1,0:T(1,128)S(1)} %copy-done.28, bf16[256,768]{1,0:T(8,128)(2,1)S(1)} %copy-done.5, bf16[768,768]{1,0:T(8,128)(2,1)S(1)} %copy-done, bf16[768,768]{1,0:T(8,128)(2,1)S(1)} %copy-done.1, bf16[768,768]{1,0:T(8,128)(2,1)S(1)} %copy-done.2, bf16[4,384,128]{2,1,0:T(8,128)(2,1)S(1)} %copy-done.4, ...), custom_call_target="tpu_custom_call" | custom-call | flops 1000000000 | bytes 5000000 | tf_op jit(solution)/shard_map/pallas_call | solution.py:713
  100.8 2.2 %shard_map.124 = f32[384,768]{1,0:T(8,128)} custom-call(s32[6]{0:T(128)S(1)} %copy-done.27, bf16[256,384]{1,0:T(8,128)(2,1)S(1)} %copy-done.30, bf16[1152,128]{1,0:T(8,128)(2,1)} %shard_map.123.mine_ref, bf16[1152,128]{1,0:T(8,128)(2,1)} %collective-permute-done.14.other_ref), custom_call_target="tpu_custom_call" | custom-call | flops 1000000000 | bytes 5000000 | tf_op jit(solution)/shard_map/pallas_call | solution.py:713
  (98 shorter events, 17.2 us)
Async XLA Ops:
  0.6 9.1 %copy-start.34 = (s32[12]{0:T(128)S(1)}, s32[12]{0:T(128)}, u32[]{:S(2)}) copy-start(s32[12]{0:T(128)} %param.17) | copy-start | bytes 148
  3.8 8.2 %collective-permute-start.1 = (bf16[208,128]{1,0:T(8,128)(2,1)}, bf16[208,128]{1,0:T(8,128)(2,1)S(1)}, u32[]{:S(2)}, u32[]{:S(2)}) collective-permute-start(bf16[208,128]{1,0:T(8,128)(2,1)} %get-tuple-element.21), channel_id=1, source_target_pairs={{0,2},{1,3},{2,0},{3,1},{4,6},{5,7},{6,4},{7,5},{8,10},{9,11},{10,... | collective-permute-start | bytes 159752 | tf_op jit(solution)/shard_map/ppermute | solution.py:672
  4.0 17.0 %collective-permute-start.2 = (bf16[208,128]{1,0:T(8,128)(2,1)}, bf16[208,128]{1,0:T(8,128)(2,1)S(1)}, u32[]{:S(2)}, u32[]{:S(2)}) collective-permute-start(bf16[208,128]{1,0:T(8,128)(2,1)} %get-tuple-element.21), channel_id=1, source_target_pairs={{0,3},{1,2},{2,1},{3,0},{4,7},{5,6},{6,5},{7,4},{8,11},{9,10},{10,... | collective-permute-start | bytes 159752 | tf_op jit(solution)/shard_map/ppermute | solution.py:672
  6.2 14.8 %collective-permute-start.3 = (bf16[208,128]{1,0:T(8,128)(2,1)}, bf16[208,128]{1,0:T(8,128)(2,1)S(1)}, u32[]{:S(2)}, u32[]{:S(2)}) collective-permute-start(bf16[208,128]{1,0:T(8,128)(2,1)} %get-tuple-element.22), channel_id=1, source_target_pairs={{0,4},{1,5},{2,6},{3,7},{4,0},{5,1},{6,2},{7,3},{8,12},{9,13},{10,... | collective-permute-start | bytes 159752 | tf_op jit(solution)/shard_map/ppermute | solution.py:672
  6.2 14.7 %collective-permute-start.4 = (bf16[208,128]{1,0:T(8,128)(2,1)}, bf16[208,128]{1,0:T(8,128)(2,1)S(1)}, u32[]{:S(2)}, u32[]{:S(2)}) collective-permute-start(bf16[208,128]{1,0:T(8,128)(2,1)} %get-tuple-element.22), channel_id=1, source_target_pairs={{0,5},{1,4},{2,7},{3,6},{4,1},{5,0},{6,3},{7,2},{8,13},{9,12},{10,... | collective-permute-start | bytes 159752 | tf_op jit(solution)/shard_map/ppermute | solution.py:672
  8.5 3.2 %collective-permute-start = (bf16[208,128]{1,0:T(8,128)(2,1)}, bf16[208,128]{1,0:T(8,128)(2,1)S(1)}, u32[]{:S(2)}, u32[]{:S(2)}) collective-permute-start(bf16[208,128]{1,0:T(8,128)(2,1)} %get-tuple-element.20.rest_0_), channel_id=1, source_target_pairs={{0,1},{1,0},{2,3},{3,2},{4,5},{5,4},{6,7},{7,6},{8,9},{9,8},{10,11... | collective-permute-start | bytes 159752 | tf_op jit(solution)/shard_map/ppermute | solution.py:672
  11.7 9.2 %copy-start.21 = (bf16[208,128]{1,0:T(8,128)(2,1)}, bf16[208,128]{1,0:T(8,128)(2,1)S(1)}, u32[]{:S(2)}) copy-start(bf16[208,128]{1,0:T(8,128)(2,1)S(1)} %collective-permute-done.rest_1_.refs_1_) | copy-start | bytes 159748
  11.7 9.3 %collective-permute-start.5 = (bf16[208,128]{1,0:T(8,128)(2,1)}, bf16[208,128]{1,0:T(8,128)(2,1)S(1)}, u32[]{:S(2)}, u32[]{:S(2)}) collective-permute-start(bf16[208,128]{1,0:T(8,128)(2,1)} %get-tuple-element.23), channel_id=1, source_target_pairs={{0,6},{1,7},{2,4},{3,5},{4,2},{5,3},{6,0},{7,1},{8,14},{9,15},{10,... | collective-permute-start | bytes 159752 | tf_op jit(solution)/shard_map/ppermute | solution.py:672
  11.9 9.1 %collective-permute-start.6 = (bf16[208,128]{1,0:T(8,128)(2,1)}, bf16[208,128]{1,0:T(8,128)(2,1)S(1)}, u32[]{:S(2)}, u32[]{:S(2)}) collective-permute-start(bf16[208,128]{1,0:T(8,128)(2,1)} %get-tuple-element.23), channel_id=1, source_target_pairs={{0,7},{1,6},{2,5},{3,4},{4,3},{5,2},{6,1},{7,0},{8,15},{9,14},{10,... | collective-permute-start | bytes 159752 | tf_op jit(solution)/shard_map/ppermute | solution.py:672
  22.5 20.4 %all-to-all-start.1 = ((bf16[8,128,384]{2,1,0:T(8,128)(2,1)}), bf16[8,128,384]{2,1,0:T(8,128)(2,1)S(1)}, u32[]{:S(2)}, u32[]{:S(2)}) async-start(bf16[8,128,384]{2,1,0:T(8,128)(2,1)} %shard_map.116), calls=%async_computation.1 | async-start | bytes 1572864 | tf_op jit(solution)/shard_map/all_to_all | solution.py:751
  42.9 12.7 %all-to-all-start = ((bf16[4,384,128]{2,1,0:T(8,128)(2,1)}), bf16[4,384,128]{2,1,0:T(8,128)(2,1)S(1)}, u32[]{:S(2)}, u32[]{:S(2)}) async-start(bf16[4,384,128]{2,1,0:T(8,128)(2,1)} %get-tuple-element.24), calls=%async_computation | async-start | bytes 786432 | tf_op jit(solution)/shard_map/all_to_all | solution.py:788
  48.4 5.8 %collective-permute-start.7 = (bf16[864,128]{1,0:T(8,128)(2,1)S(1)}, bf16[864,128]{1,0:T(8,128)(2,1)S(1)}, u32[]{:S(2)}, u32[]{:S(2)}) collective-permute-start(bf16[864,128]{1,0:T(8,128)(2,1)S(1)} %get-tuple-element.30), channel_id=1, source_target_pairs={{0,8},{8,0},{16,24},{24,16},{1,9},{9,1},{17,25},{25,17},{2,10},{10... | collective-permute-start | bytes 663560 | tf_op jit(solution)/shard_map/ppermute | solution.py:672
  54.2 41.6 %copy-start.28 = (s32[1,128]{1,0:T(1,128)S(1)}, s32[1,128]{1,0:T(1,128)}, u32[]{:S(2)}) copy-start(s32[1,128]{1,0:T(1,128)} %tokens_ref.3) | copy-start | bytes 1540
  54.2 41.6 %copy-start.2 = (bf16[768,768]{1,0:T(8,128)(2,1)S(1)}, bf16[768,768]{1,0:T(8,128)(2,1)}, u32[]{:S(2)}) copy-start(bf16[768,768]{1,0:T(8,128)(2,1)} %value_ref.3) | copy-start | bytes 3538948
  54.3 6.7 %collective-permute-start.8 = (bf16[864,128]{1,0:T(8,128)(2,1)S(1)}, bf16[864,128]{1,0:T(8,128)(2,1)S(1)}, u32[]{:S(2)}, u32[]{:S(2)}) collective-permute-start(bf16[864,128]{1,0:T(8,128)(2,1)S(1)} %add.17.here_ref), channel_id=1, source_target_pairs={{0,16},{8,24},{16,0},{24,8},{1,17},{9,25},{17,1},{25,9},{2,18},{10... | collective-permute-start | bytes 663560 | tf_op jit(solution)/shard_map/ppermute | solution.py:672
  61.0 34.8 %copy-start.1 = (bf16[768,768]{1,0:T(8,128)(2,1)S(1)}, bf16[768,768]{1,0:T(8,128)(2,1)}, u32[]{:S(2)}) copy-start(bf16[768,768]{1,0:T(8,128)(2,1)} %key_ref.3) | copy-start | bytes 3538948
  63.7 32.2 %copy-start = (bf16[768,768]{1,0:T(8,128)(2,1)S(1)}, bf16[768,768]{1,0:T(8,128)(2,1)}, u32[]{:S(2)}) copy-start(bf16[768,768]{1,0:T(8,128)(2,1)} %query_ref.3) | copy-start | bytes 3538948
  63.7 4.9 %collective-permute-start.9 = (bf16[288,128]{1,0:T(8,128)(2,1)S(1)}, bf16[288,128]{1,0:T(8,128)(2,1)S(1)}, u32[]{:S(2)}, u32[]{:S(2)}) collective-permute-start(bf16[288,128]{1,0:T(8,128)(2,1)S(1)} %get-tuple-element.31), channel_id=1, source_target_pairs={{0,4},{1,5},{2,6},{3,7},{4,0},{5,1},{6,2},{7,3},{8,12},{9,13},{10,... | collective-permute-start | bytes 221192 | tf_op jit(solution)/shard_map/ppermute | solution.py:672
  63.9 10.4 %collective-permute-start.10 = (bf16[288,128]{1,0:T(8,128)(2,1)}, bf16[288,128]{1,0:T(8,128)(2,1)}, u32[]{:S(2)}, u32[]{:S(2)}) collective-permute-start(bf16[288,128]{1,0:T(8,128)(2,1)} %get-tuple-element.34), channel_id=1, source_target_pairs={{0,2},{1,3},{2,0},{3,1},{4,6},{5,7},{6,4},{7,5},{8,10},{9,11},{10,... | collective-permute-start | bytes 221192 | tf_op jit(solution)/shard_map/ppermute | solution.py:672
  64.0 10.4 %collective-permute-start.11 = (bf16[288,128]{1,0:T(8,128)(2,1)}, bf16[288,128]{1,0:T(8,128)(2,1)}, u32[]{:S(2)}, u32[]{:S(2)}) collective-permute-start(bf16[288,128]{1,0:T(8,128)(2,1)} %get-tuple-element.35), channel_id=1, source_target_pairs={{0,6},{1,7},{2,4},{3,5},{4,2},{5,3},{6,0},{7,1},{8,14},{9,15},{10,... | collective-permute-start | bytes 221192 | tf_op jit(solution)/shard_map/ppermute | solution.py:672
  69.9 26.0 %all-to-all-start.2 = ((bf16[4,192,128]{2,1,0:T(8,128)(2,1)}), bf16[4,192,128]{2,1,0:T(8,128)(2,1)}, u32[]{:S(2)}, u32[]{:S(2)}) async-start(bf16[4,192,128]{2,1,0:T(8,128)(2,1)} %shard_map.119), calls=%async_computation.2 | async-start | bytes 393216 | tf_op jit(solution)/shard_map/all_to_all | solution.py:788
  75.4 7.6 %collective-permute-start.13 = (bf16[288,128]{1,0:T(8,128)(2,1)S(1)}, bf16[288,128]{1,0:T(8,128)(2,1)S(1)}, u32[]{:S(2)}, u32[]{:S(2)}) collective-permute-start(bf16[288,128]{1,0:T(8,128)(2,1)S(1)} %shard_map.122), channel_id=1, source_target_pairs={{6,7},{7,6},{14,15},{15,14},{22,23},{23,22},{30,31},{31,30}} | collective-permute-start | bytes 221192 | tf_op jit(solution)/shard_map/ppermute | solution.py:825
  80.6 5.9 %collective-permute-start.12 = (bf16[288,128]{1,0:T(8,128)(2,1)S(1)}, bf16[288,128]{1,0:T(8,128)(2,1)S(1)}, u32[]{:S(2)}, u32[]{:S(2)}) collective-permute-start(bf16[288,128]{1,0:T(8,128)(2,1)S(1)} %shard_map.121), channel_id=1, source_target_pairs={{6,7},{7,6},{14,15},{15,14},{22,23},{23,22},{30,31},{31,30}} | collective-permute-start | bytes 221192 | tf_op jit(solution)/shard_map/ppermute | solution.py:825
  90.0 10.8 %collective-permute-start.14 = (bf16[1152,128]{1,0:T(8,128)(2,1)}, bf16[1152,128]{1,0:T(8,128)(2,1)}, u32[]{:S(2)}, u32[]{:S(2)}) collective-permute-start(bf16[1152,128]{1,0:T(8,128)(2,1)} %shard_map.123.mine_ref), channel_id=1, source_target_pairs={{0,8},{8,0},{16,24},{24,16},{1,9},{9,1},{17,25},{25,17},{2,10},{10... | collective-permute-start | bytes 884744 | tf_op jit(solution)/shard_map/ppermute | solution.py:672
  (29 other events, 80.8 us)

commit v9 on v7

--- a/solution.py
+++ b/solution.py
@@ -229,7 +229,9 @@
 TOKEN_ROWS = 16
 STRIP = 8
 HALF = HEAD_DIM // 2
-VMEM_BYTES = 48 * 1024 * 1024
+VMEM_BYTES = 40 * 1024 * 1024
+MIDDLE_BYTES = 24 * 1024 * 1024
+SMALL_BYTES = 12 * 1024 * 1024
 
 
 def key_span(query_tile):
@@ -263,25 +265,24 @@
         early_ref[GROUP_COLS:, :] = tokens
 
 
+def late_kernel(cotangent_ref, *rest):
+    late_ref = rest[-1]
+    columns = late_ref.shape[2]
+    for target in range(2 * GROUPS):
+        side = target % 2
+        late_ref[target] = cotangent_ref[:, side * columns : (side + 1) * columns]
+
+
 def prepare_kernel(
     meta_ref,
-    cotangent_ref,
     table_ref,
     query_ref,
     key_ref,
     value_ref,
-    first_ref,
-    second_ref,
-    late_ref,
     lookup_ref,
     normed_ref,
     columns_ref,
 ):
-    del first_ref, second_ref
-    columns = late_ref.shape[2]
-    for target in range(2 * GROUPS):
-        side = target % 2
-        late_ref[target] = cotangent_ref[:, side * columns : (side + 1) * columns]
     normed = normed_table(table_ref)
     half = normed.shape[1] // 2
     normed_ref[...] = jnp.where(meta_ref[GROUP_HEADS] == 0, normed[:, :half], normed[:, half:])
@@ -305,7 +306,8 @@
     *rest,
 ):
     early_refs = rest[: 2 * GROUPS]
-    attention_body(meta_ref, lookup_ref, cosine_ref, sine_ref, early_refs, *rest[2 * GROUPS :])
+    rest = rest[2 * GROUPS + 1 :]
+    attention_body(meta_ref, lookup_ref, cosine_ref, sine_ref, early_refs, *rest)
 
 
 def attention_body(
@@ -314,7 +316,10 @@
     cosine_ref,
     sine_ref,
     early_refs,
-    rows_ref,
+    own_rows_ref,
+    rows1_ref,
+    rows2_ref,
+    rows3_ref,
     sums_ref,
     attended_ref,
     value_key_ref,
@@ -333,6 +338,7 @@
     products_ref,
     inverse_ref,
     term_ref,
+    grads_ref,
 ):
     head = pl.program_id(0)
     block = early_refs[0].shape[1]
@@ -502,6 +508,7 @@
         ],
         axis=0,
     ).astype(half)
+    grads_ref[...] = grads
     sums = jnp.dot(grads, onehot_rows_ref[...], preferred_element_type=jnp.float32).astype(half)
     for matrix in range(3):
         rows = slice(matrix * HEAD_DIM, (matrix + 1) * HEAD_DIM)
@@ -511,14 +518,13 @@
         for core in range(2):
             lane = core * half_vocab
             sums_ref[core, place, :] = sums[rows, lane : lane + half_vocab]
-        for target in range(GROUPS):
-            start = target * 2 * block
-            even = grads[rows, start : start + block]
-            odd = grads[rows, start + block : start + 2 * block]
-            rows_ref[target, place, :] = jnp.where(meta_ref[GROUP_HEADS] == 0, even, odd)
-
-
-def out_kernel(meta_ref, attended_ref, cotangent_ref, sums_ref, keep_ref, give_ref):
+        for turn, rows_ref in enumerate((own_rows_ref, rows1_ref, rows2_ref, rows3_ref)):
+            target = 2 * (meta_ref[GROUP_HEADS + 1] ^ turn) + meta_ref[GROUP_HEADS]
+            rows_ref[place, :] = grads_ref[rows, pl.ds(pl.multiple_of(target * block, block), block)]
+
+
+def out_kernel(meta_ref, attended_ref, cotangent_ref, sums_ref, after_ref, keep_ref, give_ref):
+    del after_ref
     total = jnp.dot(attended_ref[...], cotangent_ref[...], preferred_element_type=jnp.float32)
     rows = total.shape[0] // 2
     base = sums_ref.shape[1]
@@ -533,8 +539,8 @@
         give_ref[place, :] = jnp.where(first, part[rows:], part[:rows]).astype(jnp.bfloat16)
 
 
-def combine_kernel(meta_ref, here_ref, there_ref, after_ref, *piece_refs):
-    del after_ref
+def combine_kernel(meta_ref, here_ref, there_ref, *rest):
+    piece_refs = rest[-GROUPS:]
     rows = GROUP_COLS
     for turn, piece_ref in enumerate(piece_refs):
         target = meta_ref[GROUP_HEADS + 1] ^ turn
@@ -551,12 +557,12 @@
             piece_ref[...] = here_ref[3 * rows :, :] + there_ref[3 * rows :, :]
 
 
-def cross_kernel(meta_ref, low_ref, high_ref, out_ref):
+def cross_kernel(meta_ref, low_ref, high_ref, after_ref, out_ref):
+    del after_ref
     out_ref[...] = jnp.where(meta_ref[GROUP_HEADS] == 0, low_ref[...], high_ref[...])
 
 
-def gather_kernel(meta_ref, g0, g1, g2, g3, early_ref, late_ref, after_ref, mine_ref):
-    del after_ref
+def gather_kernel(meta_ref, g0, g1, g2, g3, early_ref, late_ref, mine_ref):
     rows = GROUP_COLS
     size = g0.shape[0]
     group = meta_ref[GROUP_HEADS + 1]
@@ -581,21 +587,34 @@
             mine_ref[place * size : (place + 1) * size, :] = piece[...]
 
 
-def input_kernel(tokens_ref, table_ref, query_ref, key_ref, value_ref, rows_ref, out_ref):
-    vocab = table_ref.shape[0]
-    onehot = onehot_columns(tokens_ref[...], vocab)
+def input_kernel(
+    meta_ref,
+    tokens_ref,
+    table_ref,
+    query_ref,
+    key_ref,
+    value_ref,
+    own_ref,
+    first_ref,
+    second_ref,
+    third_ref,
+    out_ref,
+    columns_ref,
+):
+    group = meta_ref[GROUP_HEADS + 1]
+    for turn, got in enumerate((own_ref, first_ref, second_ref, third_ref)):
+        source = group ^ turn
+        for matrix in range(3):
+            columns_ref[
+                matrix, pl.ds(pl.multiple_of(source * GROUP_COLS, GROUP_COLS), GROUP_COLS), :
+            ] = got[matrix * GROUP_COLS : (matrix + 1) * GROUP_COLS, :]
+    onehot = onehot_columns(tokens_ref[...], table_ref.shape[0])
     embedded = tdot(onehot, table_ref[...])
     inv_rms = lax.rsqrt(jnp.mean(embedded * embedded, axis=1, keepdims=True) + EPSILON)
     grad_normed = None
     for matrix, weights in enumerate((query_ref, key_ref, value_ref)):
-        columns = jnp.concatenate(
-            [
-                rows_ref[group, matrix * GROUP_COLS : (matrix + 1) * GROUP_COLS, :]
-                for group in range(GROUPS)
-            ],
-            axis=0,
-        )
-        part = ndot(columns.astype(jnp.float32).T.astype(jnp.bfloat16), weights[...])
+        columns = columns_ref[matrix].astype(jnp.float32).T.astype(jnp.bfloat16)
+        part = ndot(columns, weights[...])
         grad_normed = part if grad_normed is None else grad_normed + part
     scaled = embedded * inv_rms
     out_ref[...] = (
@@ -681,13 +700,11 @@
     cosine, sine_part = rope_table(length)
 
     def call(
-        body, operands, outs, scratch=(), steps=1, flops=10**8, moved=10**6, loose=0, peeked=0, grant=VMEM_BYTES
+        body, operands, outs, scratch=(), steps=1, flops=10**8, moved=10**6, loose=0, grant=VMEM_BYTES
     ):
         spaces = [whole(operand.shape) for operand in operands]
         for index in range(loose):
             spaces[-1 - index] = pl.BlockSpec(memory_space=pl.ANY)
-        for index in range(peeked):
-            spaces[-1 - index] = whole((16, 128))
         if operands[0].ndim == 1:
             spaces[0] = pl.BlockSpec(memory_space=pltpu.SMEM)
         return pl.pallas_call(
@@ -714,28 +731,31 @@
     early = [sent[0]] + [None] * (blocks - 1)
     for turn in (4, 6, 5, 7, 2, 3, 1):
         early[turn] = swapped(sent[turn // 2], "seq", turn)
-    late, lookup, normed = call(
+    lookup, normed = call(
         prepare_kernel,
-        (meta, grad_out, table, w_query, w_key, w_value, early[1], early[2]),
-        [
-            ((blocks, block, features // 2), half),
-            ((2, 3 * GROUP_COLS, vocab), half),
-            ((vocab, features // 2), half),
-        ],
+        (meta, table, w_query, w_key, w_value),
+        [((2, 3 * GROUP_COLS, vocab), half), ((vocab, features // 2), half)],
         [pltpu.VMEM((features, vocab), jnp.float32)],
         flops=10**9,
         moved=5 * 10**6,
-        peeked=2,
         grant=60 * 1024 * 1024,
     )
+    (late,) = call(
+        late_kernel,
+        (grad_out, lookup, *early[1:]),
+        [((blocks, block, features // 2), half)],
+        loose=blocks,
+        grant=SMALL_BYTES,
+    )
+    chunks = late
     late = lax.all_to_all(late, "seq", split_axis=0, concat_axis=0, tiled=True)
     heads_shape = (GROUP_HEADS, HEAD_DIM, length)
     rows_shape = (GROUP_HEADS, length, 2 * HEAD_DIM)
-    rows, sums, attended = call(
+    *rows, sums, attended = call(
         attention_kernel,
-        (meta, lookup, cosine, sine_part, *early),
+        (meta, lookup, cosine, sine_part, *early, chunks),
         [
-            ((GROUPS, 3 * GROUP_COLS, block), half),
+            *[((3 * GROUP_COLS, block), half)] * GROUPS,
             ((2, 3 * GROUP_COLS, vocab // 2), half),
             ((GROUP_COLS, length), half),
         ],
@@ -756,61 +776,68 @@
             pltpu.VMEM((length // TILE, WINDOW + TILE, 2 * TILE), jnp.float32),
             pltpu.VMEM((1, length), jnp.float32),
             pltpu.VMEM((1, length), jnp.float32),
+            pltpu.VMEM((3 * HEAD_DIM, length), half),
         ],
+        loose=1,
         steps=GROUP_HEADS,
         flops=8 * 10**9,
         moved=8 * 10**6,
     )
-    planes = [[2 * z + x for z in range(GROUPS)] for x in range(2)]
-
-    def over_plane(chunks):
-        return lax.all_to_all(
-            chunks, "seq", split_axis=0, concat_axis=0, axis_index_groups=planes, tiled=True
-        )
-
-    got_rows = over_plane(rows)
+    got_rows = [rows[0]] + [swapped(rows[turn], "seq", 2 * turn) for turn in (1, 2, 3)]
     lanes = vocab // 2
     out_rows = 3 * GROUP_COLS // 2
     packed = 3 * GROUP_COLS + out_rows
     keep, give = call(
         out_kernel,
-        (meta, attended, late.reshape(length, features // 2), sums),
+        (meta, attended, late.reshape(length, features // 2), sums, got_rows[1]),
         [((packed, lanes), half)] * 2,
+        loose=1,
+        grant=SMALL_BYTES,
     )
     here = keep + swapped(give, "dp", 1)
     there = swapped(here, "dp", 2)
     pieces = call(
         combine_kernel,
-        (meta, here, there, got_rows),
+        (meta, here, there, *got_rows[1:]),
         [((out_rows, lanes), half)] * GROUPS,
-        loose=1,
+        loose=GROUPS - 1,
+        grant=SMALL_BYTES,
     )
     got = [pieces[0]] + [None] * (GROUPS - 1)
     for turn in (2, 3, 1):
         got[turn] = swapped(pieces[turn], "seq", 2 * turn)
     (grad_input,) = call(
         input_kernel,
-        (token_ids, table, w_query, w_key, w_value, got_rows),
+        (meta, token_ids, table, w_query, w_key, w_value, *got_rows),
         [((block, features), half)],
+        [pltpu.VMEM((3, features, block), half)],
         flops=10**9,
         moved=5 * 10**6,
+        grant=MIDDLE_BYTES,
     )
     last = blocks - 2
     between = [(last, last + 1), (last + 1, last)]
     crossed = []
     for low, high in ((got[0], got[2]), (got[1], got[3])):
-        (piece,) = call(cross_kernel, (meta, low, high), [(low.shape, half)])
+        (piece,) = call(
+            cross_kernel,
+            (meta, low, high, grad_input),
+            [(low.shape, half)],
+            loose=1,
+            grant=SMALL_BYTES,
+        )
         crossed.append(lax.ppermute(piece, "seq", between))
     (mine,) = call(
         gather_kernel,
-        (meta, *got, *crossed, grad_input),
+        (meta, *got, *crossed),
         [((4 * out_rows, lanes), half)],
-        loose=1,
+        grant=SMALL_BYTES,
     )
     (weight_grads,) = call(
         weight_kernel,
         (meta, normed, mine, swapped(mine, "dp", 1)),
         [((features // 2, features), jnp.float32)],
+        grant=SMALL_BYTES,
         flops=10**9,
         moved=5 * 10**6,
     )

time: 98.6 us -> 99.4 us (level)
  the two profiles are of different devices: /device:TPU:0 before, /device:TPU:25 now
where the time goes in v9:
time: 99.4 us; the launch traced here: 98.8 us
  starting transfers between devices  38.6 us (39%)
  Pallas kernels  25.4 us (26%)
  waiting for transfers between devices  22.1 us (22%)
  local copies, waits for them, and re-layouts  10.5 us (11%)
  other arithmetic  1.28 us (1%)
    ppermute x16, starting transfers between devices, swapped(): return lax.ppermute(block, axis, route)  28.7 us
    pallas_call x11, Pallas kernels, call(): pl.pallas_call(body, grid=(steps,), in_specs=spaces, out_specs=[whole(sha...  25.4 us
    ppermute x16, waiting for transfers between devices, swapped(): return lax.ppermute(block, axis, route)  19.2 us
    unnamed x54, local copies, waits for them, and re-layouts  10.4 us
    ppermute x2, starting transfers between devices, grouped_device(): crossed.append(lax.ppermute(piece, 'seq', between))  5.28 us
    all_to_all x1, starting transfers between devices, grouped_device(): late = lax.all_to_all(late, 'seq', split_axis=0, concat_axis=0, tiled=True)  4.67 us
    ppermute x2, waiting for transfers between devices, grouped_device(): crossed.append(lax.ppermute(piece, 'seq', between))  2.88 us
  transfers between devices with their start and end apart: 19, of which 7 were waited for; matrix products, arithmetic and copies ran while one was open for 1% of the time, Pallas kernels for 18%

profile of v9, /device:TPU:25, one launch (start us, length us, event | category | flops | bytes accessed | tf_op | source)
XLA Modules:
  0.0 98.8 jit_solution(7741955586074920207)
XLA Ops:
  1.2 2.6 %shard_map.114 = (bf16[208,128]{1,0:T(8,128)(2,1)}, bf16[208,128]{1,0:T(8,128)(2,1)}, bf16[208,128]{1,0:T(8,128)(2,1)}, bf16[208,128]{1,0:T(8,128)(2,1)}) custom-call(s32[3]{0:T(128)} %pad_add_fusion.1.spot_ref, s32[1,128]{1,0:T(1,128)} %tokens_ref.3, bf16[128,768]{1,0:T(8,128)(2,1)} %bitcast.8, bf16[768,768]{1,0:T(8,128)(2,1)} %out_weights_ref.1), custom_call_target="tpu_custom_call" | custom-call | flops 100000000 | bytes 1000000 | tf_op jit(solution)/shard_map/pallas_call | solution.py:710
  4.0 2.2 %collective-permute-start.2 = (bf16[208,128]{1,0:T(8,128)(2,1)}, bf16[208,128]{1,0:T(8,128)(2,1)S(1)}, u32[]{:S(2)}, u32[]{:S(2)}) collective-permute-start(bf16[208,128]{1,0:T(8,128)(2,1)} %get-tuple-element.22), channel_id=1, source_target_pairs={{0,3},{1,2},{2,1},{3,0},{4,7},{5,6},{6,5},{7,4},{8,11},{9,10},{10,... | collective-permute-start | bytes 159752 | tf_op jit(solution)/shard_map/ppermute | solution.py:669
  6.2 2.3 %collective-permute-start.4 = (bf16[208,128]{1,0:T(8,128)(2,1)}, bf16[208,128]{1,0:T(8,128)(2,1)S(1)}, u32[]{:S(2)}, u32[]{:S(2)}) collective-permute-start(bf16[208,128]{1,0:T(8,128)(2,1)} %get-tuple-element.23), channel_id=1, source_target_pairs={{0,5},{1,4},{2,7},{3,6},{4,1},{5,0},{6,3},{7,2},{8,13},{9,12},{10,... | collective-permute-start | bytes 159752 | tf_op jit(solution)/shard_map/ppermute | solution.py:669
  8.5 1.2 %collective-permute-start = (bf16[208,128]{1,0:T(8,128)(2,1)}, bf16[208,128]{1,0:T(8,128)(2,1)S(1)}, u32[]{:S(2)}, u32[]{:S(2)}) collective-permute-start(bf16[208,128]{1,0:T(8,128)(2,1)} %get-tuple-element.21.rest_0_), channel_id=1, source_target_pairs={{0,1},{1,0},{2,3},{3,2},{4,5},{5,4},{6,7},{7,6},{8,9},{9,8},{10,11... | collective-permute-start | bytes 159752 | tf_op jit(solution)/shard_map/ppermute | solution.py:669
  10.5 1.2 %collective-permute-done.rest_1_ = bf16[208,128]{1,0:T(8,128)(2,1)S(1)} collective-permute-done((bf16[208,128]{1,0:T(8,128)(2,1)}, bf16[208,128]{1,0:T(8,128)(2,1)S(1)}, u32[]{:S(2)}, u32[]{:S(2)}) %collective-permute-start) | collective-permute-done | bytes 53280 | tf_op jit(solution)/shard_map/ppermute | solution.py:669
  11.9 4.4 %collective-permute-start.6 = (bf16[208,128]{1,0:T(8,128)(2,1)}, bf16[208,128]{1,0:T(8,128)(2,1)S(1)}, u32[]{:S(2)}, u32[]{:S(2)}) collective-permute-start(bf16[208,128]{1,0:T(8,128)(2,1)} %get-tuple-element.24), channel_id=1, source_target_pairs={{0,7},{1,6},{2,5},{3,4},{4,3},{5,2},{6,1},{7,0},{8,15},{9,14},{10,... | collective-permute-start | bytes 159752 | tf_op jit(solution)/shard_map/ppermute | solution.py:669
  16.3 4.3 %shard_map.113 = (bf16[2,576,256]{2,1,0:T(8,128)(2,1)}, bf16[256,384]{1,0:T(8,128)(2,1)}) custom-call(s32[6]{0:T(128)} %pad_add_fusion.meta_ref, bf16[256,768]{1,0:T(8,128)(2,1)} %table_ref.3, bf16[768,768]{1,0:T(8,128)(2,1)} %query_ref.3, bf16[768,768]{1,0:T(8,128)(2,1)} %key_ref.3, bf16[768,768]{1,0:T(8,128)(2,1)} %value_ref.3), custom_call_target="tpu_custom_call" | custom-call | flops 1000000000 | bytes 5000000 | tf_op jit(solution)/shard_map/pallas_call | solution.py:710
  23.9 4.7 %all-to-all-start = ((bf16[8,128,384]{2,1,0:T(8,128)(2,1)}), bf16[8,128,384]{2,1,0:T(8,128)(2,1)S(1)}, u32[]{:S(2)}, u32[]{:S(2)}) async-start(bf16[8,128,384]{2,1,0:T(8,128)(2,1)} %shard_map.115.rest_8_), calls=%async_computation | async-start | bytes 1572864 | tf_op jit(solution)/shard_map/all_to_all | solution.py:751
  34.4 10.2 %shard_map.116 = (bf16[576,128]{1,0:T(8,128)(2,1)S(1)}, bf16[576,128]{1,0:T(8,128)(2,1)S(1)}, bf16[576,128]{1,0:T(8,128)(2,1)S(1)}, bf16[576,128]{1,0:T(8,128)(2...) custom-call(s32[6]{0:T(128)S(1)} %copy-done.16, bf16[2,576,256]{2,1,0:T(8,128)(2,1)S(1)} %copy-done.7, ...), custom_call_target="tpu_custom_call" | custom-call | flops 8000000000 | bytes 8000000 | tf_op jit(solution)/shard_map/pallas_call | solution.py:710
  46.2 3.7 %collective-permute-done.7.first_ref.after_ref.rest_0_ = bf16[576,128]{1,0:T(8,128)(2,1)S(1)} collective-permute-done((bf16[576,128]{1,0:T(8,128)(2,1)S(1)}, bf16[576,128]{1,0:T(8,128)(2,1)S(1)}, u32[]{:S(2)}, u32[]{:S(2)}) %collective-permute-start.7) | collective-permute-done | bytes 147488 | tf_op jit(solution)/shard_map/ppermute | solution.py:669
  50.9 5.7 %collective-permute-start.10 = (bf16[864,128]{1,0:T(8,128)(2,1)S(1)}, bf16[864,128]{1,0:T(8,128)(2,1)S(1)}, u32[]{:S(2)}, u32[]{:S(2)}) collective-permute-start(bf16[864,128]{1,0:T(8,128)(2,1)S(1)} %get-tuple-element.33), channel_id=1, source_target_pairs={{0,8},{8,0},{16,24},{24,16},{1,9},{9,1},{17,25},{25,17},{2,10},{10... | collective-permute-start | bytes 663560 | tf_op jit(solution)/shard_map/ppermute | solution.py:669
  56.6 1.1 %collective-permute-done.10 = bf16[864,128]{1,0:T(8,128)(2,1)S(1)} collective-permute-done((bf16[864,128]{1,0:T(8,128)(2,1)S(1)}, bf16[864,128]{1,0:T(8,128)(2,1)S(1)}, u32[]{:S(2)}, u32[]{:S(2)}) %collective-permute-start.10) | collective-permute-done | bytes 221216 | tf_op jit(solution)/shard_map/ppermute | solution.py:669
  57.8 1.3 %collective-permute-start.11 = (bf16[864,128]{1,0:T(8,128)(2,1)S(1)}, bf16[864,128]{1,0:T(8,128)(2,1)S(1)}, u32[]{:S(2)}, u32[]{:S(2)}) collective-permute-start(bf16[864,128]{1,0:T(8,128)(2,1)S(1)} %add.17.here_ref), channel_id=1, source_target_pairs={{0,16},{8,24},{16,0},{24,8},{1,17},{9,25},{17,1},{25,9},{2,18},{10... | collective-permute-start | bytes 663560 | tf_op jit(solution)/shard_map/ppermute | solution.py:669
  59.3 2.1 %collective-permute-start.9 = (bf16[576,128]{1,0:T(8,128)(2,1)S(1)}, bf16[576,128]{1,0:T(8,128)(2,1)S(1)}, u32[]{:S(2)}, u32[]{:S(2)}) collective-permute-start(bf16[576,128]{1,0:T(8,128)(2,1)S(1)} %copy-done.20), channel_id=1, source_target_pairs={{0,6},{1,7},{2,4},{3,5},{4,2},{5,3},{6,0},{7,1},{8,14},{9,15},{10,... | collective-permute-start | bytes 442376 | tf_op jit(solution)/shard_map/ppermute | solution.py:669
  61.5 10.6 %collective-permute-done.8.second_ref.rest_1_ = bf16[576,128]{1,0:T(8,128)(2,1)S(1)} collective-permute-done((bf16[576,128]{1,0:T(8,128)(2,1)S(1)}, bf16[576,128]{1,0:T(8,128)(2,1)S(1)}, u32[]{:S(2)}, u32[]{:S(2)}) %collective-permute-start.8) | collective-permute-done | bytes 147488 | tf_op jit(solution)/shard_map/ppermute | solution.py:669
  72.7 3.5 %collective-permute-start.12 = (bf16[288,128]{1,0:T(8,128)(2,1)S(1)}, bf16[288,128]{1,0:T(8,128)(2,1)S(1)}, u32[]{:S(2)}, u32[]{:S(2)}) collective-permute-start(bf16[288,128]{1,0:T(8,128)(2,1)S(1)} %get-tuple-element.35), channel_id=1, source_target_pairs={{0,2},{1,3},{2,0},{3,1},{4,6},{5,7},{6,4},{7,5},{8,10},{9,11},{10,... | collective-permute-start | bytes 221192 | tf_op jit(solution)/shard_map/ppermute | solution.py:669
  77.5 2.5 %shard_map.117.after_ref = bf16[128,768]{1,0:T(8,128)(2,1)} custom-call(s32[6]{0:T(128)S(1)} %copy-done.16, s32[1,128]{1,0:T(1,128)S(1)} %copy-done.17, bf16[256,768]{1,0:T(8,128)(2,1)S(1)} %copy-done.4, bf16[768,768]{1,0:T(8,128)(2,1)S(1)} %copy-done, bf16[768,768]{1,0:T(8,128)(2,1)S(1)} %copy-done.1, bf16[768,768]{1,0:T(8,128)(2,1)S(1)} %copy-done.2, ...), custom_call_target="tpu_custom_call" | custom-call | flops 1000000000 | bytes 5000000 | tf_op jit(solution)/shard_map/pallas_call | solution.py:710
  80.1 1.3 %collective-permute-done.14.high_ref.g3 = bf16[288,128]{1,0:T(8,128)(2,1)S(1)} collective-permute-done((bf16[288,128]{1,0:T(8,128)(2,1)S(1)}, bf16[288,128]{1,0:T(8,128)(2,1)S(1)}, u32[]{:S(2)}, u32[]{:S(2)}) %collective-permute-start.14) | collective-permute-done | bytes 73760 | tf_op jit(solution)/shard_map/ppermute | solution.py:669
  82.8 3.1 %collective-permute-start.16 = (bf16[288,128]{1,0:T(8,128)(2,1)S(1)}, bf16[288,128]{1,0:T(8,128)(2,1)S(1)}, u32[]{:S(2)}, u32[]{:S(2)}) collective-permute-start(bf16[288,128]{1,0:T(8,128)(2,1)S(1)} %shard_map.121), channel_id=1, source_target_pairs={{6,7},{7,6},{14,15},{15,14},{22,23},{23,22},{30,31},{31,30}} | collective-permute-start | bytes 221192 | tf_op jit(solution)/shard_map/ppermute | solution.py:829
  86.5 2.2 %collective-permute-start.15 = (bf16[288,128]{1,0:T(8,128)(2,1)S(1)}, bf16[288,128]{1,0:T(8,128)(2,1)S(1)}, u32[]{:S(2)}, u32[]{:S(2)}) collective-permute-start(bf16[288,128]{1,0:T(8,128)(2,1)S(1)} %shard_map.120), channel_id=1, source_target_pairs={{6,7},{7,6},{14,15},{15,14},{22,23},{23,22},{30,31},{31,30}} | collective-permute-start | bytes 221192 | tf_op jit(solution)/shard_map/ppermute | solution.py:829
  88.7 2.9 %collective-permute-done.15.early_ref = bf16[288,128]{1,0:T(8,128)(2,1)S(1)} collective-permute-done((bf16[288,128]{1,0:T(8,128)(2,1)S(1)}, bf16[288,128]{1,0:T(8,128)(2,1)S(1)}, u32[]{:S(2)}, u32[]{:S(2)}) %collective-permute-start.15) | collective-permute-done | bytes 73760 | tf_op jit(solution)/shard_map/ppermute | solution.py:829
  92.2 3.8 %collective-permute-start.17 = (bf16[1152,128]{1,0:T(8,128)(2,1)S(1)}, bf16[1152,128]{1,0:T(8,128)(2,1)S(1)}, u32[]{:S(2)}, u32[]{:S(2)}) collective-permute-start(bf16[1152,128]{1,0:T(8,128)(2,1)S(1)} %shard_map.122.mine_ref), channel_id=1, source_target_pairs={{0,8},{8,0},{16,24},{24,16},{1,9},{9,1},{17,25},{25,17},{2,10},{10... | collective-permute-start | bytes 884744 | tf_op jit(solution)/shard_map/ppermute | solution.py:669
  96.0 1.2 %collective-permute-done.17.other_ref = bf16[1152,128]{1,0:T(8,128)(2,1)S(1)} collective-permute-done((bf16[1152,128]{1,0:T(8,128)(2,1)S(1)}, bf16[1152,128]{1,0:T(8,128)(2,1)S(1)}, u32[]{:S(2)}, u32[]{:S(2)}) %collective-permute-start.17) | collective-permute-done | bytes 294944 | tf_op jit(solution)/shard_map/ppermute | solution.py:669
  97.2 1.6 %shard_map.123 = f32[384,768]{1,0:T(8,128)} custom-call(s32[6]{0:T(128)S(1)} %copy-done.16, bf16[256,384]{1,0:T(8,128)(2,1)S(1)} %copy-done.18, bf16[1152,128]{1,0:T(8,128)(2,1)S(1)} %shard_map.122.mine_ref, bf16[1152,128]{1,0:T(8,128)(2,1)S(1)} %collective-permute-done.17.other_ref), custom_call_target="tpu_custom_call" | custom-call | flops 1000000000 | bytes 5000000 | tf_op jit(solution)/shard_map/pallas_call | solution.py:710
  (83 shorter events, 18.2 us)
Async XLA Ops:
  3.8 8.2 %collective-permute-start.1 = (bf16[208,128]{1,0:T(8,128)(2,1)}, bf16[208,128]{1,0:T(8,128)(2,1)S(1)}, u32[]{:S(2)}, u32[]{:S(2)}) collective-permute-start(bf16[208,128]{1,0:T(8,128)(2,1)} %get-tuple-element.22), channel_id=1, source_target_pairs={{0,2},{1,3},{2,0},{3,1},{4,6},{5,7},{6,4},{7,5},{8,10},{9,11},{10,... | collective-permute-start | bytes 159752 | tf_op jit(solution)/shard_map/ppermute | solution.py:669
  4.0 16.6 %collective-permute-start.2 = (bf16[208,128]{1,0:T(8,128)(2,1)}, bf16[208,128]{1,0:T(8,128)(2,1)S(1)}, u32[]{:S(2)}, u32[]{:S(2)}) collective-permute-start(bf16[208,128]{1,0:T(8,128)(2,1)} %get-tuple-element.22), channel_id=1, source_target_pairs={{0,3},{1,2},{2,1},{3,0},{4,7},{5,6},{6,5},{7,4},{8,11},{9,10},{10,... | collective-permute-start | bytes 159752 | tf_op jit(solution)/shard_map/ppermute | solution.py:669
  6.2 14.4 %collective-permute-start.3 = (bf16[208,128]{1,0:T(8,128)(2,1)}, bf16[208,128]{1,0:T(8,128)(2,1)S(1)}, u32[]{:S(2)}, u32[]{:S(2)}) collective-permute-start(bf16[208,128]{1,0:T(8,128)(2,1)} %get-tuple-element.23), channel_id=1, source_target_pairs={{0,4},{1,5},{2,6},{3,7},{4,0},{5,1},{6,2},{7,3},{8,12},{9,13},{10,... | collective-permute-start | bytes 159752 | tf_op jit(solution)/shard_map/ppermute | solution.py:669
  6.2 14.3 %collective-permute-start.4 = (bf16[208,128]{1,0:T(8,128)(2,1)}, bf16[208,128]{1,0:T(8,128)(2,1)S(1)}, u32[]{:S(2)}, u32[]{:S(2)}) collective-permute-start(bf16[208,128]{1,0:T(8,128)(2,1)} %get-tuple-element.23), channel_id=1, source_target_pairs={{0,5},{1,4},{2,7},{3,6},{4,1},{5,0},{6,3},{7,2},{8,13},{9,12},{10,... | collective-permute-start | bytes 159752 | tf_op jit(solution)/shard_map/ppermute | solution.py:669
  8.5 3.2 %collective-permute-start = (bf16[208,128]{1,0:T(8,128)(2,1)}, bf16[208,128]{1,0:T(8,128)(2,1)S(1)}, u32[]{:S(2)}, u32[]{:S(2)}) collective-permute-start(bf16[208,128]{1,0:T(8,128)(2,1)} %get-tuple-element.21.rest_0_), channel_id=1, source_target_pairs={{0,1},{1,0},{2,3},{3,2},{4,5},{5,4},{6,7},{7,6},{8,9},{9,8},{10,11... | collective-permute-start | bytes 159752 | tf_op jit(solution)/shard_map/ppermute | solution.py:669
  11.7 8.9 %collective-permute-start.5 = (bf16[208,128]{1,0:T(8,128)(2,1)}, bf16[208,128]{1,0:T(8,128)(2,1)S(1)}, u32[]{:S(2)}, u32[]{:S(2)}) collective-permute-start(bf16[208,128]{1,0:T(8,128)(2,1)} %get-tuple-element.24), channel_id=1, source_target_pairs={{0,6},{1,7},{2,4},{3,5},{4,2},{5,3},{6,0},{7,1},{8,14},{9,15},{10,... | collective-permute-start | bytes 159752 | tf_op jit(solution)/shard_map/ppermute | solution.py:669
  11.9 8.7 %collective-permute-start.6 = (bf16[208,128]{1,0:T(8,128)(2,1)}, bf16[208,128]{1,0:T(8,128)(2,1)S(1)}, u32[]{:S(2)}, u32[]{:S(2)}) collective-permute-start(bf16[208,128]{1,0:T(8,128)(2,1)} %get-tuple-element.24), channel_id=1, source_target_pairs={{0,7},{1,6},{2,5},{3,4},{4,3},{5,2},{6,1},{7,0},{8,15},{9,14},{10,... | collective-permute-start | bytes 159752 | tf_op jit(solution)/shard_map/ppermute | solution.py:669
  23.9 26.1 %all-to-all-start = ((bf16[8,128,384]{2,1,0:T(8,128)(2,1)}), bf16[8,128,384]{2,1,0:T(8,128)(2,1)S(1)}, u32[]{:S(2)}, u32[]{:S(2)}) async-start(bf16[8,128,384]{2,1,0:T(8,128)(2,1)} %shard_map.115.rest_8_), calls=%async_computation | async-start | bytes 1572864 | tf_op jit(solution)/shard_map/all_to_all | solution.py:751
  34.4 43.1 %copy-start.2 = (bf16[768,768]{1,0:T(8,128)(2,1)S(1)}, bf16[768,768]{1,0:T(8,128)(2,1)}, u32[]{:S(2)}) copy-start(bf16[768,768]{1,0:T(8,128)(2,1)} %value_ref.3) | copy-start | bytes 3538948
  46.0 4.0 %collective-permute-start.7 = (bf16[576,128]{1,0:T(8,128)(2,1)S(1)}, bf16[576,128]{1,0:T(8,128)(2,1)S(1)}, u32[]{:S(2)}, u32[]{:S(2)}) collective-permute-start(bf16[576,128]{1,0:T(8,128)(2,1)S(1)} %get-tuple-element.26), channel_id=1, source_target_pairs={{0,2},{1,3},{2,0},{3,1},{4,6},{5,7},{6,4},{7,5},{8,10},{9,11},{10,... | collective-permute-start | bytes 442376 | tf_op jit(solution)/shard_map/ppermute | solution.py:669
  50.0 27.5 %copy-start.1 = (bf16[768,768]{1,0:T(8,128)(2,1)S(1)}, bf16[768,768]{1,0:T(8,128)(2,1)}, u32[]{:S(2)}) copy-start(bf16[768,768]{1,0:T(8,128)(2,1)} %key_ref.3) | copy-start | bytes 3538948
  50.0 27.5 %copy-start.4 = (bf16[256,768]{1,0:T(8,128)(2,1)S(1)}, bf16[256,768]{1,0:T(8,128)(2,1)}, u32[]{:S(2)}) copy-start(bf16[256,768]{1,0:T(8,128)(2,1)} %table_ref.3) | copy-start | bytes 1179652
  50.9 26.6 %copy-start = (bf16[768,768]{1,0:T(8,128)(2,1)S(1)}, bf16[768,768]{1,0:T(8,128)(2,1)}, u32[]{:S(2)}) copy-start(bf16[768,768]{1,0:T(8,128)(2,1)} %query_ref.3) | copy-start | bytes 3538948
  50.9 26.6 %copy-start.17 = (s32[1,128]{1,0:T(1,128)S(1)}, s32[1,128]{1,0:T(1,128)}, u32[]{:S(2)}) copy-start(s32[1,128]{1,0:T(1,128)} %tokens_ref.3) | copy-start | bytes 1540
  50.9 6.8 %collective-permute-start.10 = (bf16[864,128]{1,0:T(8,128)(2,1)S(1)}, bf16[864,128]{1,0:T(8,128)(2,1)S(1)}, u32[]{:S(2)}, u32[]{:S(2)}) collective-permute-start(bf16[864,128]{1,0:T(8,128)(2,1)S(1)} %get-tuple-element.33), channel_id=1, source_target_pairs={{0,8},{8,0},{16,24},{24,16},{1,9},{9,1},{17,25},{25,17},{2,10},{10... | collective-permute-start | bytes 663560 | tf_op jit(solution)/shard_map/ppermute | solution.py:669
  57.8 14.3 %collective-permute-start.11 = (bf16[864,128]{1,0:T(8,128)(2,1)S(1)}, bf16[864,128]{1,0:T(8,128)(2,1)S(1)}, u32[]{:S(2)}, u32[]{:S(2)}) collective-permute-start(bf16[864,128]{1,0:T(8,128)(2,1)S(1)} %add.17.here_ref), channel_id=1, source_target_pairs={{0,16},{8,24},{16,0},{24,8},{1,17},{9,25},{17,1},{25,9},{2,18},{10... | collective-permute-start | bytes 663560 | tf_op jit(solution)/shard_map/ppermute | solution.py:669
  59.1 13.0 %collective-permute-start.8 = (bf16[576,128]{1,0:T(8,128)(2,1)S(1)}, bf16[576,128]{1,0:T(8,128)(2,1)S(1)}, u32[]{:S(2)}, u32[]{:S(2)}) collective-permute-start(bf16[576,128]{1,0:T(8,128)(2,1)S(1)} %copy-done.22), channel_id=1, source_target_pairs={{0,4},{1,5},{2,6},{3,7},{4,0},{5,1},{6,2},{7,3},{8,12},{9,13},{10,... | collective-permute-start | bytes 442376 | tf_op jit(solution)/shard_map/ppermute | solution.py:669
  59.3 12.7 %collective-permute-start.9 = (bf16[576,128]{1,0:T(8,128)(2,1)S(1)}, bf16[576,128]{1,0:T(8,128)(2,1)S(1)}, u32[]{:S(2)}, u32[]{:S(2)}) collective-permute-start(bf16[576,128]{1,0:T(8,128)(2,1)S(1)} %copy-done.20), channel_id=1, source_target_pairs={{0,6},{1,7},{2,4},{3,5},{4,2},{5,3},{6,0},{7,1},{8,14},{9,15},{10,... | collective-permute-start | bytes 442376 | tf_op jit(solution)/shard_map/ppermute | solution.py:669
  72.7 7.3 %collective-permute-start.12 = (bf16[288,128]{1,0:T(8,128)(2,1)S(1)}, bf16[288,128]{1,0:T(8,128)(2,1)S(1)}, u32[]{:S(2)}, u32[]{:S(2)}) collective-permute-start(bf16[288,128]{1,0:T(8,128)(2,1)S(1)} %get-tuple-element.35), channel_id=1, source_target_pairs={{0,2},{1,3},{2,0},{3,1},{4,6},{5,7},{6,4},{7,5},{8,10},{9,11},{10,... | collective-permute-start | bytes 221192 | tf_op jit(solution)/shard_map/ppermute | solution.py:669
  76.2 5.1 %collective-permute-start.14 = (bf16[288,128]{1,0:T(8,128)(2,1)S(1)}, bf16[288,128]{1,0:T(8,128)(2,1)S(1)}, u32[]{:S(2)}, u32[]{:S(2)}) collective-permute-start(bf16[288,128]{1,0:T(8,128)(2,1)S(1)} %get-tuple-element.37), channel_id=1, source_target_pairs={{0,6},{1,7},{2,4},{3,5},{4,2},{5,3},{6,0},{7,1},{8,14},{9,15},{10,... | collective-permute-start | bytes 221192 | tf_op jit(solution)/shard_map/ppermute | solution.py:669
  76.4 9.5 %collective-permute-start.13 = (bf16[288,128]{1,0:T(8,128)(2,1)S(1)}, bf16[288,128]{1,0:T(8,128)(2,1)S(1)}, u32[]{:S(2)}, u32[]{:S(2)}) collective-permute-start(bf16[288,128]{1,0:T(8,128)(2,1)S(1)} %get-tuple-element.36), channel_id=1, source_target_pairs={{0,4},{1,5},{2,6},{3,7},{4,0},{5,1},{6,2},{7,3},{8,12},{9,13},{10,... | collective-permute-start | bytes 221192 | tf_op jit(solution)/shard_map/ppermute | solution.py:669
  82.8 5.9 %collective-permute-start.16 = (bf16[288,128]{1,0:T(8,128)(2,1)S(1)}, bf16[288,128]{1,0:T(8,128)(2,1)S(1)}, u32[]{:S(2)}, u32[]{:S(2)}) collective-permute-start(bf16[288,128]{1,0:T(8,128)(2,1)S(1)} %shard_map.121), channel_id=1, source_target_pairs={{6,7},{7,6},{14,15},{15,14},{22,23},{23,22},{30,31},{31,30}} | collective-permute-start | bytes 221192 | tf_op jit(solution)/shard_map/ppermute | solution.py:829
  86.5 5.1 %collective-permute-start.15 = (bf16[288,128]{1,0:T(8,128)(2,1)S(1)}, bf16[288,128]{1,0:T(8,128)(2,1)S(1)}, u32[]{:S(2)}, u32[]{:S(2)}) collective-permute-start(bf16[288,128]{1,0:T(8,128)(2,1)S(1)} %shard_map.120), channel_id=1, source_target_pairs={{6,7},{7,6},{14,15},{15,14},{22,23},{23,22},{30,31},{31,30}} | collective-permute-start | bytes 221192 | tf_op jit(solution)/shard_map/ppermute | solution.py:829
  92.2 5.0 %collective-permute-start.17 = (bf16[1152,128]{1,0:T(8,128)(2,1)S(1)}, bf16[1152,128]{1,0:T(8,128)(2,1)S(1)}, u32[]{:S(2)}, u32[]{:S(2)}) collective-permute-start(bf16[1152,128]{1,0:T(8,128)(2,1)S(1)} %shard_map.122.mine_ref), channel_id=1, source_target_pairs={{0,8},{8,0},{16,24},{24,16},{1,9},{9,1},{17,25},{25,17},{2,10},{10... | collective-permute-start | bytes 884744 | tf_op jit(solution)/shard_map/ppermute | solution.py:669
  (22 other events, 92.1 us)

commit v10 on v7

--- a/solution.py
+++ b/solution.py
@@ -263,25 +263,24 @@
         early_ref[GROUP_COLS:, :] = tokens
 
 
+def late_kernel(cotangent_ref, *rest):
+    late_ref = rest[-1]
+    columns = late_ref.shape[2]
+    for target in range(2 * GROUPS):
+        side = target % 2
+        late_ref[target] = cotangent_ref[:, side * columns : (side + 1) * columns]
+
+
 def prepare_kernel(
     meta_ref,
-    cotangent_ref,
     table_ref,
     query_ref,
     key_ref,
     value_ref,
-    first_ref,
-    second_ref,
-    late_ref,
     lookup_ref,
     normed_ref,
     columns_ref,
 ):
-    del first_ref, second_ref
-    columns = late_ref.shape[2]
-    for target in range(2 * GROUPS):
-        side = target % 2
-        late_ref[target] = cotangent_ref[:, side * columns : (side + 1) * columns]
     normed = normed_table(table_ref)
     half = normed.shape[1] // 2
     normed_ref[...] = jnp.where(meta_ref[GROUP_HEADS] == 0, normed[:, :half], normed[:, half:])
@@ -533,7 +532,13 @@
         give_ref[place, :] = jnp.where(first, part[rows:], part[:rows]).astype(jnp.bfloat16)
 
 
-def combine_kernel(meta_ref, here_ref, there_ref, after_ref, *piece_refs):
+def core_kernel(keep_ref, got_ref, here_ref, out_ref):
+    here_ref[...] = keep_ref[...] + got_ref[...]
+    base = here_ref.shape[0] - out_ref.shape[0]
+    out_ref[...] = here_ref[base:, :]
+
+
+def combine_kernel(meta_ref, here_ref, there_ref, near_ref, far_ref, after_ref, *piece_refs):
     del after_ref
     rows = GROUP_COLS
     for turn, piece_ref in enumerate(piece_refs):
@@ -548,19 +553,16 @@
 
         @pl.when(target == 3)
         def _(piece_ref=piece_ref):
-            piece_ref[...] = here_ref[3 * rows :, :] + there_ref[3 * rows :, :]
-
-
-def cross_kernel(meta_ref, low_ref, high_ref, out_ref):
-    out_ref[...] = jnp.where(meta_ref[GROUP_HEADS] == 0, low_ref[...], high_ref[...])
-
-
-def gather_kernel(meta_ref, g0, g1, g2, g3, early_ref, late_ref, after_ref, mine_ref):
+            stays = meta_ref[GROUP_HEADS + 1] // 2 == meta_ref[GROUP_HEADS]
+            own = here_ref[3 * rows :, :] + there_ref[3 * rows :, :]
+            piece_ref[...] = jnp.where(stays, own, near_ref[...] + far_ref[...])
+
+
+def gather_kernel(meta_ref, g0, g1, g2, g3, after_ref, mine_ref):
     del after_ref
     rows = GROUP_COLS
     size = g0.shape[0]
     group = meta_ref[GROUP_HEADS + 1]
-    first = meta_ref[GROUP_HEADS] == 0
 
     @pl.when(group < 3)
     def _():
@@ -570,14 +572,9 @@
         tail = mine_ref.shape[0] - GROUPS * rows
         mine_ref[GROUPS * rows :, :] = jnp.zeros((tail, mine_ref.shape[1]), jnp.bfloat16)
 
-    @pl.when((group == 3) & first)
+    @pl.when(group == 3)
     def _():
-        for place, piece in enumerate((g3, late_ref, g2, early_ref)):
-            mine_ref[place * size : (place + 1) * size, :] = piece[...]
-
-    @pl.when((group == 3) & jnp.logical_not(first))
-    def _():
-        for place, piece in enumerate((late_ref, g1, early_ref, g0)):
+        for place, piece in enumerate((g3, g1, g2, g0)):
             mine_ref[place * size : (place + 1) * size, :] = piece[...]
 
 
@@ -681,13 +678,11 @@
     cosine, sine_part = rope_table(length)
 
     def call(
-        body, operands, outs, scratch=(), steps=1, flops=10**8, moved=10**6, loose=0, peeked=0, grant=VMEM_BYTES
+        body, operands, outs, scratch=(), steps=1, flops=10**8, moved=10**6, loose=0, grant=VMEM_BYTES
     ):
         spaces = [whole(operand.shape) for operand in operands]
         for index in range(loose):
             spaces[-1 - index] = pl.BlockSpec(memory_space=pl.ANY)
-        for index in range(peeked):
-            spaces[-1 - index] = whole((16, 128))
         if operands[0].ndim == 1:
             spaces[0] = pl.BlockSpec(memory_space=pltpu.SMEM)
         return pl.pallas_call(
@@ -714,19 +709,20 @@
     early = [sent[0]] + [None] * (blocks - 1)
     for turn in (4, 6, 5, 7, 2, 3, 1):
         early[turn] = swapped(sent[turn // 2], "seq", turn)
-    late, lookup, normed = call(
+    lookup, normed = call(
         prepare_kernel,
-        (meta, grad_out, table, w_query, w_key, w_value, early[1], early[2]),
-        [
-            ((blocks, block, features // 2), half),
-            ((2, 3 * GROUP_COLS, vocab), half),
-            ((vocab, features // 2), half),
-        ],
+        (meta, table, w_query, w_key, w_value),
+        [((2, 3 * GROUP_COLS, vocab), half), ((vocab, features // 2), half)],
         [pltpu.VMEM((features, vocab), jnp.float32)],
         flops=10**9,
         moved=5 * 10**6,
-        peeked=2,
         grant=60 * 1024 * 1024,
+    )
+    (late,) = call(
+        late_kernel,
+        (grad_out, lookup, *early[1:]),
+        [((blocks, block, features // 2), half)],
+        loose=blocks,
     )
     late = lax.all_to_all(late, "seq", split_axis=0, concat_axis=0, tiled=True)
     heads_shape = (GROUP_HEADS, HEAD_DIM, length)
@@ -777,11 +773,26 @@
         (meta, attended, late.reshape(length, features // 2), sums),
         [((packed, lanes), half)] * 2,
     )
-    here = keep + swapped(give, "dp", 1)
+    here, here_out = call(
+        core_kernel,
+        (keep, swapped(give, "dp", 1)),
+        [((packed, lanes), half), ((out_rows, lanes), half)],
+    )
     there = swapped(here, "dp", 2)
+    astray = [(i, i ^ 5) for i in range(blocks) if i // 4 != i % 2]
+    near = lax.ppermute(here_out, "seq", astray)
+    far = lax.ppermute(
+        here_out,
+        ("dp", "seq"),
+        [
+            (blocks * d + source, blocks * (d ^ 2) + target)
+            for d in range(lax.axis_size("dp"))
+            for source, target in astray
+        ],
+    )
     pieces = call(
         combine_kernel,
-        (meta, here, there, got_rows),
+        (meta, here, there, near, far, got_rows),
         [((out_rows, lanes), half)] * GROUPS,
         loose=1,
     )
@@ -795,15 +806,9 @@
         flops=10**9,
         moved=5 * 10**6,
     )
-    last = blocks - 2
-    between = [(last, last + 1), (last + 1, last)]
-    crossed = []
-    for low, high in ((got[0], got[2]), (got[1], got[3])):
-        (piece,) = call(cross_kernel, (meta, low, high), [(low.shape, half)])
-        crossed.append(lax.ppermute(piece, "seq", between))
     (mine,) = call(
         gather_kernel,
-        (meta, *got, *crossed, grad_input),
+        (meta, *got, grad_input),
         [((4 * out_rows, lanes), half)],
         loose=1,
     )

time: 98.6 us -> 89.5 us (0.908); the launches traced: 97.1 us -> 89 us
  waiting for transfers between devices: 34.2 us -> 25.2 us
  starting transfers between devices: 31.1 us -> 32.1 us
    ppermute x13, waiting for transfers between devices: 24.2 us -> 9.49 us  [swapped(): return lax.ppermute(block, axis, route)]
    all_to_all x1, waiting for transfers between devices: 0.01 us -> 6.45 us  [grouped_device(): late = lax.all_to_all(late, 'seq', split_axis=0, concat_axis=0, tiled=True)]
    ppermute x13, starting transfers between devices: 21.2 us -> 23.6 us  [swapped(): return lax.ppermute(block, axis, route)]
    all_to_all x1, starting transfers between devices: 5.07 us -> 3.72 us  [grouped_device(): late = lax.all_to_all(late, 'seq', split_axis=0, concat_axis=0, tiled=True)]
    unnamed x40 -> x30, local copies, waits for them, and re-layouts: 2.89 us -> 3.32 us
  transfers between devices with their start and end apart: 17 -> 17, of which waited for: 8 -> 8; matrix products, arithmetic and copies ran while one was open for 1% -> 1% of each run, Pallas kernels for 15% -> 21%
where the time goes in v10:
time: 89.5 us; the launch traced here: 89 us
  starting transfers between devices  32.1 us (36%)
  Pallas kernels  26.2 us (29%)
  waiting for transfers between devices  25.2 us (28%)
  local copies, waits for them, and re-layouts  3.39 us (4%)
  other arithmetic  1.25 us (1%)
    pallas_call x10, Pallas kernels, call(): pl.pallas_call(body, grid=(steps,), in_specs=spaces, out_specs=[whole(sha...  26.2 us
    ppermute x13, starting transfers between devices, swapped(): return lax.ppermute(block, axis, route)  23.6 us
    ppermute x13, waiting for transfers between devices, swapped(): return lax.ppermute(block, axis, route)  9.49 us
    all_to_all x1, waiting for transfers between devices, over_plane(): lax.all_to_all(chunks, 'seq', split_axis=0, concat_axis=0, axis_index_gro...  9.24 us
    all_to_all x1, waiting for transfers between devices, grouped_device(): late = lax.all_to_all(late, 'seq', split_axis=0, concat_axis=0, tiled=True)  6.45 us
    all_to_all x1, starting transfers between devices, grouped_device(): late = lax.all_to_all(late, 'seq', split_axis=0, concat_axis=0, tiled=True)  3.72 us
    all_to_all x1, starting transfers between devices, over_plane(): lax.all_to_all(chunks, 'seq', split_axis=0, concat_axis=0, axis_index_gro...  3.48 us
    unnamed x30, local copies, waits for them, and re-layouts  3.32 us
  transfers between devices with their start and end apart: 17, of which 8 were waited for; matrix products, arithmetic and copies ran while one was open for 1% of the time, Pallas kernels for 21%

profile of v10, /device:TPU:0, one launch (start us, length us, event | category | flops | bytes accessed | tf_op | source)
XLA Modules:
  0.0 89.0 jit_solution(3348800947147745533)
XLA Ops:
  1.3 2.6 %shard_map.114 = (bf16[208,128]{1,0:T(8,128)(2,1)}, bf16[208,128]{1,0:T(8,128)(2,1)}, bf16[208,128]{1,0:T(8,128)(2,1)}, bf16[208,128]{1,0:T(8,128)(2,1)}) custom-call(s32[3]{0:T(128)} %pad_add_fusion.1.spot_ref, s32[1,128]{1,0:T(1,128)} %tokens_ref.3, bf16[128,768]{1,0:T(8,128)(2,1)} %bitcast.8, bf16[768,768]{1,0:T(8,128)(2,1)} %out_weights_ref.1), custom_call_target="tpu_custom_call" | custom-call | flops 100000000 | bytes 1000000 | tf_op jit(solution)/shard_map/pallas_call | solution.py:688
  3.8 4.0 %collective-permute-start.2 = (bf16[208,128]{1,0:T(8,128)(2,1)}, bf16[208,128]{1,0:T(8,128)(2,1)S(1)}, u32[]{:S(2)}, u32[]{:S(2)}) collective-permute-start(bf16[208,128]{1,0:T(8,128)(2,1)} %get-tuple-element.21), channel_id=1, source_target_pairs={{0,3},{1,2},{2,1},{3,0},{4,7},{5,6},{6,5},{7,4},{8,11},{9,10},{10,... | collective-permute-start | bytes 159752 | tf_op jit(solution)/shard_map/ppermute | solution.py:647
  8.2 2.6 %collective-permute-start.4 = (bf16[208,128]{1,0:T(8,128)(2,1)}, bf16[208,128]{1,0:T(8,128)(2,1)S(1)}, u32[]{:S(2)}, u32[]{:S(2)}) collective-permute-start(bf16[208,128]{1,0:T(8,128)(2,1)} %get-tuple-element.22), channel_id=1, source_target_pairs={{0,5},{1,4},{2,7},{3,6},{4,1},{5,0},{6,3},{7,2},{8,13},{9,12},{10,... | collective-permute-start | bytes 159752 | tf_op jit(solution)/shard_map/ppermute | solution.py:647
  10.8 1.8 %collective-permute-start = (bf16[208,128]{1,0:T(8,128)(2,1)}, bf16[208,128]{1,0:T(8,128)(2,1)S(1)}, u32[]{:S(2)}, u32[]{:S(2)}) collective-permute-start(bf16[208,128]{1,0:T(8,128)(2,1)} %get-tuple-element.20.rest_0_), channel_id=1, source_target_pairs={{0,1},{1,0},{2,3},{3,2},{4,5},{5,4},{6,7},{7,6},{8,9},{9,8},{10,11... | collective-permute-start | bytes 159752 | tf_op jit(solution)/shard_map/ppermute | solution.py:647
  13.3 1.8 %collective-permute-done.rest_1_ = bf16[208,128]{1,0:T(8,128)(2,1)S(1)} collective-permute-done((bf16[208,128]{1,0:T(8,128)(2,1)}, bf16[208,128]{1,0:T(8,128)(2,1)S(1)}, u32[]{:S(2)}, u32[]{:S(2)}) %collective-permute-start) | collective-permute-done | bytes 53280 | tf_op jit(solution)/shard_map/ppermute | solution.py:647
  15.2 5.0 %collective-permute-start.6 = (bf16[208,128]{1,0:T(8,128)(2,1)}, bf16[208,128]{1,0:T(8,128)(2,1)S(1)}, u32[]{:S(2)}, u32[]{:S(2)}) collective-permute-start(bf16[208,128]{1,0:T(8,128)(2,1)} %get-tuple-element.23), channel_id=1, source_target_pairs={{0,7},{1,6},{2,5},{3,4},{4,3},{5,2},{6,1},{7,0},{8,15},{9,14},{10,... | collective-permute-start | bytes 159752 | tf_op jit(solution)/shard_map/ppermute | solution.py:647
  20.2 4.3 %shard_map.113 = (bf16[2,576,256]{2,1,0:T(8,128)(2,1)}, bf16[256,384]{1,0:T(8,128)(2,1)}) custom-call(s32[6]{0:T(128)} %pad_add_fusion.meta_ref, bf16[256,768]{1,0:T(8,128)(2,1)} %table_ref.3, bf16[768,768]{1,0:T(8,128)(2,1)} %query_ref.3, bf16[768,768]{1,0:T(8,128)(2,1)} %key_ref.3, bf16[768,768]{1,0:T(8,128)(2,1)} %value_ref.3), custom_call_target="tpu_custom_call" | custom-call | flops 1000000000 | bytes 5000000 | tf_op jit(solution)/shard_map/pallas_call | solution.py:688
  24.5 1.7 %collective-permute-done.5.rest_6_ = bf16[208,128]{1,0:T(8,128)(2,1)S(1)} collective-permute-done((bf16[208,128]{1,0:T(8,128)(2,1)}, bf16[208,128]{1,0:T(8,128)(2,1)S(1)}, u32[]{:S(2)}, u32[]{:S(2)}) %collective-permute-start.5) | collective-permute-done | bytes 53280 | tf_op jit(solution)/shard_map/ppermute | solution.py:647
  26.3 1.1 %copy-done.6 = bf16[2,576,256]{2,1,0:T(8,128)(2,1)S(1)} copy-done((bf16[2,576,256]{2,1,0:T(8,128)(2,1)S(1)}, bf16[2,576,256]{2,1,0:T(8,128)(2,1)}, u32[]{:S(2)}) %copy-start.6) | copy-done | bytes 589848
  27.3 0.9 %shard_map.117 = bf16[8,128,384]{2,1,0:T(8,128)(2,1)} custom-call(bf16[128,768]{1,0:T(8,128)(2,1)S(1)} %bitcast.9, bf16[2,576,256]{2,1,0:T(8,128)(2,1)S(1)} %copy-done.6, bf16[208,128]{1,0:T(8,128)(2,1)S(1)} %collective-permute-done.rest_1_, bf16[208,128]{1,0:T(8,128)(2,1)S(1)} %collective-permute-done.1.rest_2_, ...), custom_call_target="tpu_custom_call" | custom-call | flops 100000000 | bytes 1000000 | tf_op jit(solution)/shard_map/pallas_call | solution.py:688
  28.3 3.7 %all-to-all-start.1 = ((bf16[8,128,384]{2,1,0:T(8,128)(2,1)}), bf16[8,128,384]{2,1,0:T(8,128)(2,1)S(1)}, u32[]{:S(2)}, u32[]{:S(2)}) async-start(bf16[8,128,384]{2,1,0:T(8,128)(2,1)} %shard_map.117), calls=%async_computation.1 | async-start | bytes 1572864 | tf_op jit(solution)/shard_map/all_to_all | solution.py:727
  32.1 10.9 %shard_map.115 = (bf16[4,576,128]{2,1,0:T(8,128)(2,1)}, bf16[2,576,128]{2,1,0:T(8,128)(2,1)S(1)}, bf16[192,1024]{1,0:T(8,128)(2,1)S(1)}) custom-call(s32[6]{0:T(128)S(1)} %copy-done.8, bf16[2,576,256]{2,1,0:T(8,128)(2,1)S(1)} %copy-done.7, f32[32,1024]{1,0:T(8,128)S(1)} %copy-done.13, f32[32,1024]{1,0:T(8,128)S(1)} %copy-done.12, ...), custom_call_target="tpu_custom_call" | custom-call | flops 8000000000 | bytes 8000000 | tf_op jit(solution)/shard_map/pallas_call | solution.py:688
  43.0 6.5 %all-to-all-done.1 = bf16[8,128,384]{2,1,0:T(8,128)(2,1)S(1)} async-done(((bf16[8,128,384]{2,1,0:T(8,128)(2,1)}), bf16[8,128,384]{2,1,0:T(8,128)(2,1)S(1)}, u32[]{:S(2)}, u32[]{:S(2)}) %all-to-all-start.1) | async-done | bytes 786464 | tf_op jit(solution)/shard_map/all_to_all | solution.py:727
  49.5 3.5 %all-to-all-start = ((bf16[4,576,128]{2,1,0:T(8,128)(2,1)}), bf16[4,576,128]{2,1,0:T(8,128)(2,1)S(1)}, u32[]{:S(2)}, u32[]{:S(2)}) async-start(bf16[4,576,128]{2,1,0:T(8,128)(2,1)} %get-tuple-element.24), calls=%async_computation | async-start | bytes 1179648 | tf_op jit(solution)/shard_map/all_to_all | solution.py:763
  54.0 1.5 %collective-permute-done.7.got_ref = bf16[864,128]{1,0:T(8,128)(2,1)S(1)} collective-permute-done((bf16[864,128]{1,0:T(8,128)(2,1)S(1)}, bf16[864,128]{1,0:T(8,128)(2,1)S(1)}, u32[]{:S(2)}, u32[]{:S(2)}) %collective-permute-start.7) | collective-permute-done | bytes 221216 | tf_op jit(solution)/shard_map/ppermute | solution.py:647
  56.2 1.6 %collective-permute-start.8 = (bf16[864,128]{1,0:T(8,128)(2,1)}, bf16[864,128]{1,0:T(8,128)(2,1)}, u32[]{:S(2)}, u32[]{:S(2)}) collective-permute-start(bf16[864,128]{1,0:T(8,128)(2,1)} %get-tuple-element.30.here_ref), channel_id=1, source_target_pairs={{0,16},{8,24},{16,0},{24,8},{1,17},{9,25},{17,1},{25,9},{2,18},{10... | collective-permute-start | bytes 663560 | tf_op jit(solution)/shard_map/ppermute | solution.py:647
  59.2 9.2 %all-to-all-done.rows_ref.after_ref = bf16[4,576,128]{2,1,0:T(8,128)(2,1)S(1)} async-done(((bf16[4,576,128]{2,1,0:T(8,128)(2,1)}), bf16[4,576,128]{2,1,0:T(8,128)(2,1)S(1)}, u32[]{:S(2)}, u32[]{:S(2)}) %all-to-all-start) | async-done | bytes 589856 | tf_op jit(solution)/shard_map/all_to_all | solution.py:763
  68.4 1.2 %shard_map.120 = (bf16[288,128]{1,0:T(8,128)(2,1)S(1)}, bf16[288,128]{1,0:T(8,128)(2,1)S(1)}, bf16[288,128]{1,0:T(8,128)(2,1)S(1)}, bf16[288,128]{1,0:T(8,128)(2,1)S(1)}) custom-call(s32[6]{0:T(128)S(1)} %copy-done.8, bf16[864,128]{1,0:T(8,128)(2,1)} %get-tuple-element.30.here_ref, bf16[864,128]{1,0:T(8,128)(2,1)} %collective-permute-done.8.there_ref, ...), custom_call_target="tpu_custom_call" | custom-call | flops 100000000 | bytes 1000000 | tf_op jit(solution)/shard_map/pallas_call | solution.py:688
  69.7 8.0 %collective-permute-start.12 = (bf16[288,128]{1,0:T(8,128)(2,1)S(1)}, bf16[288,128]{1,0:T(8,128)(2,1)S(1)}, u32[]{:S(2)}, u32[]{:S(2)}) collective-permute-start(bf16[288,128]{1,0:T(8,128)(2,1)S(1)} %get-tuple-element.34), channel_id=1, source_target_pairs={{0,4},{1,5},{2,6},{3,7},{4,0},{5,1},{6,2},{7,3},{8,12},{9,13},{10,... | collective-permute-start | bytes 221192 | tf_op jit(solution)/shard_map/ppermute | solution.py:647
  77.7 1.3 %copy-done.2 = bf16[768,768]{1,0:T(8,128)(2,1)S(1)} copy-done((bf16[768,768]{1,0:T(8,128)(2,1)S(1)}, bf16[768,768]{1,0:T(8,128)(2,1)}, u32[]{:S(2)}) %copy-start.2) | copy-done | bytes 1179672
  79.0 1.9 %shard_map.116.after_ref = bf16[128,768]{1,0:T(8,128)(2,1)} custom-call(s32[1,128]{1,0:T(1,128)S(1)} %copy-done.9, bf16[256,768]{1,0:T(8,128)(2,1)S(1)} %copy-done.3, bf16[768,768]{1,0:T(8,128)(2,1)S(1)} %copy-done, bf16[768,768]{1,0:T(8,128)(2,1)S(1)} %copy-done.1, bf16[768,768]{1,0:T(8,128)(2,1)S(1)} %copy-done.2, ...), custom_call_target="tpu_custom_call" | custom-call | flops 1000000000 | bytes 5000000 | tf_op jit(solution)/shard_map/pallas_call | solution.py:688
  81.6 2.2 %collective-permute-done.13.g3 = bf16[288,128]{1,0:T(8,128)(2,1)S(1)} collective-permute-done((bf16[288,128]{1,0:T(8,128)(2,1)S(1)}, bf16[288,128]{1,0:T(8,128)(2,1)S(1)}, u32[]{:S(2)}, u32[]{:S(2)}) %collective-permute-start.13) | collective-permute-done | bytes 73760 | tf_op jit(solution)/shard_map/ppermute | solution.py:647
  85.4 1.6 %collective-permute-done.14.other_ref = bf16[1152,128]{1,0:T(8,128)(2,1)S(1)} collective-permute-done((bf16[1152,128]{1,0:T(8,128)(2,1)S(1)}, bf16[1152,128]{1,0:T(8,128)(2,1)S(1)}, u32[]{:S(2)}, u32[]{:S(2)}) %collective-permute-start.14) | collective-permute-done | bytes 294944 | tf_op jit(solution)/shard_map/ppermute | solution.py:647
  87.0 2.1 %shard_map.122 = f32[384,768]{1,0:T(8,128)} custom-call(s32[6]{0:T(128)S(1)} %copy-done.8, bf16[256,384]{1,0:T(8,128)(2,1)S(1)} %copy-done.10, bf16[1152,128]{1,0:T(8,128)(2,1)S(1)} %shard_map.121.mine_ref, bf16[1152,128]{1,0:T(8,128)(2,1)S(1)} %collective-permute-done.14.other_ref), custom_call_target="tpu_custom_call" | custom-call | flops 1000000000 | bytes 5000000 | tf_op jit(solution)/shard_map/pallas_call | solution.py:688
  (53 shorter events, 7.4 us)
Async XLA Ops:
  0.6 12.0 %copy-start.14 = (s32[12]{0:T(128)S(1)}, s32[12]{0:T(128)}, u32[]{:S(2)}) copy-start(s32[12]{0:T(128)} %param.17) | copy-start | bytes 148
  3.8 16.3 %collective-permute-start.2 = (bf16[208,128]{1,0:T(8,128)(2,1)}, bf16[208,128]{1,0:T(8,128)(2,1)S(1)}, u32[]{:S(2)}, u32[]{:S(2)}) collective-permute-start(bf16[208,128]{1,0:T(8,128)(2,1)} %get-tuple-element.21), channel_id=1, source_target_pairs={{0,3},{1,2},{2,1},{3,0},{4,7},{5,6},{6,5},{7,4},{8,11},{9,10},{10,... | collective-permute-start | bytes 159752 | tf_op jit(solution)/shard_map/ppermute | solution.py:647
  7.8 16.7 %collective-permute-start.1 = (bf16[208,128]{1,0:T(8,128)(2,1)}, bf16[208,128]{1,0:T(8,128)(2,1)S(1)}, u32[]{:S(2)}, u32[]{:S(2)}) collective-permute-start(bf16[208,128]{1,0:T(8,128)(2,1)} %get-tuple-element.21), channel_id=1, source_target_pairs={{0,2},{1,3},{2,0},{3,1},{4,6},{5,7},{6,4},{7,5},{8,10},{9,11},{10,... | collective-permute-start | bytes 159752 | tf_op jit(solution)/shard_map/ppermute | solution.py:647
  8.2 16.3 %collective-permute-start.4 = (bf16[208,128]{1,0:T(8,128)(2,1)}, bf16[208,128]{1,0:T(8,128)(2,1)S(1)}, u32[]{:S(2)}, u32[]{:S(2)}) collective-permute-start(bf16[208,128]{1,0:T(8,128)(2,1)} %get-tuple-element.22), channel_id=1, source_target_pairs={{0,5},{1,4},{2,7},{3,6},{4,1},{5,0},{6,3},{7,2},{8,13},{9,12},{10,... | collective-permute-start | bytes 159752 | tf_op jit(solution)/shard_map/ppermute | solution.py:647
  10.8 13.7 %collective-permute-start.3 = (bf16[208,128]{1,0:T(8,128)(2,1)}, bf16[208,128]{1,0:T(8,128)(2,1)S(1)}, u32[]{:S(2)}, u32[]{:S(2)}) collective-permute-start(bf16[208,128]{1,0:T(8,128)(2,1)} %get-tuple-element.22), channel_id=1, source_target_pairs={{0,4},{1,5},{2,6},{3,7},{4,0},{5,1},{6,2},{7,3},{8,12},{9,13},{10,... | collective-permute-start | bytes 159752 | tf_op jit(solution)/shard_map/ppermute | solution.py:647
  10.8 4.3 %collective-permute-start = (bf16[208,128]{1,0:T(8,128)(2,1)}, bf16[208,128]{1,0:T(8,128)(2,1)S(1)}, u32[]{:S(2)}, u32[]{:S(2)}) collective-permute-start(bf16[208,128]{1,0:T(8,128)(2,1)} %get-tuple-element.20.rest_0_), channel_id=1, source_target_pairs={{0,1},{1,0},{2,3},{3,2},{4,5},{5,4},{6,7},{7,6},{8,9},{9,8},{10,11... | collective-permute-start | bytes 159752 | tf_op jit(solution)/shard_map/ppermute | solution.py:647
  15.2 11.1 %copy-start.5 = (bf16[1,128,768]{2,1,0:T(8,128)(2,1)S(1)}, bf16[1,128,768]{2,1,0:T(8,128)(2,1)}, u32[]{:S(2)}) copy-start(bf16[1,128,768]{2,1,0:T(8,128)(2,1)} %param.11) | copy-start | bytes 589828
  15.2 9.4 %collective-permute-start.6 = (bf16[208,128]{1,0:T(8,128)(2,1)}, bf16[208,128]{1,0:T(8,128)(2,1)S(1)}, u32[]{:S(2)}, u32[]{:S(2)}) collective-permute-start(bf16[208,128]{1,0:T(8,128)(2,1)} %get-tuple-element.23), channel_id=1, source_target_pairs={{0,7},{1,6},{2,5},{3,4},{4,3},{5,2},{6,1},{7,0},{8,15},{9,14},{10,... | collective-permute-start | bytes 159752 | tf_op jit(solution)/shard_map/ppermute | solution.py:647
  20.1 6.1 %collective-permute-start.5 = (bf16[208,128]{1,0:T(8,128)(2,1)}, bf16[208,128]{1,0:T(8,128)(2,1)S(1)}, u32[]{:S(2)}, u32[]{:S(2)}) collective-permute-start(bf16[208,128]{1,0:T(8,128)(2,1)} %get-tuple-element.23), channel_id=1, source_target_pairs={{0,6},{1,7},{2,4},{3,5},{4,2},{5,3},{6,0},{7,1},{8,14},{9,15},{10,... | collective-permute-start | bytes 159752 | tf_op jit(solution)/shard_map/ppermute | solution.py:647
  28.3 21.1 %all-to-all-start.1 = ((bf16[8,128,384]{2,1,0:T(8,128)(2,1)}), bf16[8,128,384]{2,1,0:T(8,128)(2,1)S(1)}, u32[]{:S(2)}, u32[]{:S(2)}) async-start(bf16[8,128,384]{2,1,0:T(8,128)(2,1)} %shard_map.117), calls=%async_computation.1 | async-start | bytes 1572864 | tf_op jit(solution)/shard_map/all_to_all | solution.py:727
  49.5 19.0 %all-to-all-start = ((bf16[4,576,128]{2,1,0:T(8,128)(2,1)}), bf16[4,576,128]{2,1,0:T(8,128)(2,1)S(1)}, u32[]{:S(2)}, u32[]{:S(2)}) async-start(bf16[4,576,128]{2,1,0:T(8,128)(2,1)} %get-tuple-element.24), calls=%async_computation | async-start | bytes 1179648 | tf_op jit(solution)/shard_map/all_to_all | solution.py:763
  52.9 24.7 %copy-start.1 = (bf16[768,768]{1,0:T(8,128)(2,1)S(1)}, bf16[768,768]{1,0:T(8,128)(2,1)}, u32[]{:S(2)}) copy-start(bf16[768,768]{1,0:T(8,128)(2,1)} %key_ref.3) | copy-start | bytes 3538948
  53.9 23.8 %copy-start = (bf16[768,768]{1,0:T(8,128)(2,1)S(1)}, bf16[768,768]{1,0:T(8,128)(2,1)}, u32[]{:S(2)}) copy-start(bf16[768,768]{1,0:T(8,128)(2,1)} %query_ref.3) | copy-start | bytes 3538948
  53.9 23.8 %copy-start.3 = (bf16[256,768]{1,0:T(8,128)(2,1)S(1)}, bf16[256,768]{1,0:T(8,128)(2,1)}, u32[]{:S(2)}) copy-start(bf16[256,768]{1,0:T(8,128)(2,1)} %table_ref.3) | copy-start | bytes 1179652
  53.9 23.8 %copy-start.9 = (s32[1,128]{1,0:T(1,128)S(1)}, s32[1,128]{1,0:T(1,128)}, u32[]{:S(2)}) copy-start(s32[1,128]{1,0:T(1,128)} %tokens_ref.3) | copy-start | bytes 1540
  53.9 1.5 %collective-permute-start.7 = (bf16[864,128]{1,0:T(8,128)(2,1)S(1)}, bf16[864,128]{1,0:T(8,128)(2,1)S(1)}, u32[]{:S(2)}, u32[]{:S(2)}) collective-permute-start(bf16[864,128]{1,0:T(8,128)(2,1)S(1)} %get-tuple-element.29), channel_id=1, source_target_pairs={{0,8},{8,0},{16,24},{24,16},{1,9},{9,1},{17,25},{25,17},{2,10},{10... | collective-permute-start | bytes 663560 | tf_op jit(solution)/shard_map/ppermute | solution.py:647
  56.2 12.2 %collective-permute-start.8 = (bf16[864,128]{1,0:T(8,128)(2,1)}, bf16[864,128]{1,0:T(8,128)(2,1)}, u32[]{:S(2)}, u32[]{:S(2)}) collective-permute-start(bf16[864,128]{1,0:T(8,128)(2,1)} %get-tuple-element.30.here_ref), channel_id=1, source_target_pairs={{0,16},{8,24},{16,0},{24,8},{1,17},{9,25},{17,1},{25,9},{2,18},{10... | collective-permute-start | bytes 663560 | tf_op jit(solution)/shard_map/ppermute | solution.py:647
  57.8 10.6 %collective-permute-start.10 = (bf16[288,128]{1,0:T(8,128)(2,1)}, bf16[288,128]{1,0:T(8,128)(2,1)S(1)}, u32[]{:S(2)}, u32[]{:S(2)}) collective-permute-start(bf16[288,128]{1,0:T(8,128)(2,1)} %get-tuple-element.31), channel_id=1, source_target_pairs={{1,20},{3,22},{4,17},{6,19},{9,28},{11,30},{12,25},{14,27},{17,4},... | collective-permute-start | bytes 221192 | tf_op jit(solution)/shard_map/ppermute | solution.py:784
  58.5 9.9 %collective-permute-start.9 = (bf16[288,128]{1,0:T(8,128)(2,1)}, bf16[288,128]{1,0:T(8,128)(2,1)S(1)}, u32[]{:S(2)}, u32[]{:S(2)}) collective-permute-start(bf16[288,128]{1,0:T(8,128)(2,1)} %get-tuple-element.31), channel_id=1, source_target_pairs={{1,4},{3,6},{4,1},{6,3},{9,12},{11,14},{12,9},{14,11},{17,20},{19,... | collective-permute-start | bytes 221192 | tf_op jit(solution)/shard_map/ppermute | solution.py:783
  69.6 11.3 %collective-permute-start.11 = (bf16[288,128]{1,0:T(8,128)(2,1)S(1)}, bf16[288,128]{1,0:T(8,128)(2,1)S(1)}, u32[]{:S(2)}, u32[]{:S(2)}) collective-permute-start(bf16[288,128]{1,0:T(8,128)(2,1)S(1)} %get-tuple-element.33), channel_id=1, source_target_pairs={{0,2},{1,3},{2,0},{3,1},{4,6},{5,7},{6,4},{7,5},{8,10},{9,11},{10,... | collective-permute-start | bytes 221192 | tf_op jit(solution)/shard_map/ppermute | solution.py:647
  69.7 11.9 %collective-permute-start.12 = (bf16[288,128]{1,0:T(8,128)(2,1)S(1)}, bf16[288,128]{1,0:T(8,128)(2,1)S(1)}, u32[]{:S(2)}, u32[]{:S(2)}) collective-permute-start(bf16[288,128]{1,0:T(8,128)(2,1)S(1)} %get-tuple-element.34), channel_id=1, source_target_pairs={{0,4},{1,5},{2,6},{3,7},{4,0},{5,1},{6,2},{7,3},{8,12},{9,13},{10,... | collective-permute-start | bytes 221192 | tf_op jit(solution)/shard_map/ppermute | solution.py:647
  77.7 6.2 %collective-permute-start.13 = (bf16[288,128]{1,0:T(8,128)(2,1)S(1)}, bf16[288,128]{1,0:T(8,128)(2,1)S(1)}, u32[]{:S(2)}, u32[]{:S(2)}) collective-permute-start(bf16[288,128]{1,0:T(8,128)(2,1)S(1)} %get-tuple-element.35), channel_id=1, source_target_pairs={{0,6},{1,7},{2,4},{3,5},{4,2},{5,3},{6,0},{7,1},{8,14},{9,15},{10,... | collective-permute-start | bytes 221192 | tf_op jit(solution)/shard_map/ppermute | solution.py:647
  79.0 8.0 %copy-start.10 = (bf16[256,384]{1,0:T(8,128)(2,1)S(1)}, bf16[256,384]{1,0:T(8,128)(2,1)}, u32[]{:S(2)}) copy-start(bf16[256,384]{1,0:T(8,128)(2,1)} %get-tuple-element.25.normed_ref) | copy-start | bytes 589828
  85.3 1.6 %collective-permute-start.14 = (bf16[1152,128]{1,0:T(8,128)(2,1)S(1)}, bf16[1152,128]{1,0:T(8,128)(2,1)S(1)}, u32[]{:S(2)}, u32[]{:S(2)}) collective-permute-start(bf16[1152,128]{1,0:T(8,128)(2,1)S(1)} %shard_map.121.mine_ref), channel_id=1, source_target_pairs={{0,8},{8,0},{16,24},{24,16},{1,9},{9,1},{17,25},{25,17},{2,10},{10... | collective-permute-start | bytes 884744 | tf_op jit(solution)/shard_map/ppermute | solution.py:647
  (8 other events, 22.0 us)

commit v11 on v6

--- a/solution.py
+++ b/solution.py
@@ -263,26 +263,24 @@
         early_ref[GROUP_COLS:, :] = tokens
 
 
-def gate_kernel(*refs):
-    del refs
+def late_kernel(cotangent_ref, *rest):
+    late_ref = rest[-1]
+    columns = late_ref.shape[2]
+    for target in range(2 * GROUPS):
+        side = target % 2
+        late_ref[target] = cotangent_ref[:, side * columns : (side + 1) * columns]
 
 
 def prepare_kernel(
     meta_ref,
-    cotangent_ref,
     table_ref,
     query_ref,
     key_ref,
     value_ref,
-    late_ref,
     lookup_ref,
     normed_ref,
     columns_ref,
 ):
-    columns = late_ref.shape[2]
-    for target in range(2 * GROUPS):
-        side = target % 2
-        late_ref[target] = cotangent_ref[:, side * columns : (side + 1) * columns]
     normed = normed_table(table_ref)
     half = normed.shape[1] // 2
     normed_ref[...] = jnp.where(meta_ref[GROUP_HEADS] == 0, normed[:, :half], normed[:, half:])
@@ -540,7 +538,10 @@
     out_ref[...] = here_ref[base:, :]
 
 
-def combine_kernel(meta_ref, here_ref, there_ref, near_ref, far_ref, out_ref, *piece_refs):
+def combine_kernel(
+    meta_ref, here_ref, there_ref, near_ref, far_ref, after_ref, out_ref, *piece_refs
+):
+    del after_ref
     rows = GROUP_COLS
     for turn, piece_ref in enumerate(piece_refs):
         target = jnp.minimum(meta_ref[GROUP_HEADS + 1] ^ turn, 2)
@@ -705,26 +706,21 @@
     early = [sent[0]] + [None] * (blocks - 1)
     for turn in (4, 6, 5, 7, 2, 3, 1):
         early[turn] = swapped(sent[turn // 2], "seq", turn)
-    late, lookup, normed = call(
+    lookup, normed = call(
         prepare_kernel,
-        (meta, grad_out, table, w_query, w_key, w_value),
-        [
-            ((blocks, block, features // 2), half),
-            ((2, 3 * GROUP_COLS, vocab), half),
-            ((vocab, features // 2), half),
-        ],
+        (meta, table, w_query, w_key, w_value),
+        [((2, 3 * GROUP_COLS, vocab), half), ((vocab, features // 2), half)],
         [pltpu.VMEM((features, vocab), jnp.float32)],
         flops=10**9,
         moved=5 * 10**6,
         grant=60 * 1024 * 1024,
     )
-    late = pl.pallas_call(
-        gate_kernel,
-        in_specs=[pl.BlockSpec(memory_space=pl.ANY)] * blocks,
-        out_specs=pl.BlockSpec(memory_space=pl.ANY),
-        out_shape=jax.ShapeDtypeStruct(late.shape, half),
-        input_output_aliases={0: 0},
-    )(late, *early[1:])
+    (late,) = call(
+        late_kernel,
+        (grad_out, lookup, *early[1:]),
+        [((blocks, block, features // 2), half)],
+        loose=blocks,
+    )
     late = lax.all_to_all(late, "seq", split_axis=0, concat_axis=0, tiled=True)
     heads_shape = (GROUP_HEADS, HEAD_DIM, length)
     rows_shape = (GROUP_HEADS, length, 2 * HEAD_DIM)
@@ -793,8 +789,9 @@
     )
     full_out, *pieces = call(
         combine_kernel,
-        (meta, here, there, near, far),
+        (meta, here, there, near, far, got_rows),
         [((2 * out_rows, lanes), half)] + [((GROUP_COLS, lanes), half)] * GROUPS,
+        loose=1,
     )
     last = blocks - 2
     got_out = [
@@ -803,8 +800,7 @@
     ]
     got = [pieces[0]] + [None] * (GROUPS - 1)
     for turn in (2, 3, 1):
-        route = [(i, i ^ (2 * turn)) for i in range(blocks) if (i ^ (2 * turn)) < last]
-        got[turn] = lax.ppermute(pieces[turn], "seq", route)
+        got[turn] = swapped(pieces[turn], "seq", 2 * turn)
     (grad_input,) = call(
         input_kernel,
         (token_ids, table, w_query, w_key, w_value, got_rows),

time: 95.2 us -> 86.2 us (0.905)
  local copies, waits for them, and re-layouts: 7.83 us -> 3.38 us
  starting transfers between devices: 38.2 us -> 35.4 us
    ppermute x3 -> x0, starting transfers between devices: 5.66 us -> none  [grouped_device(): got[turn] = lax.ppermute(pieces[turn], 'seq', route)]
    all_to_all x1, waiting for transfers between devices: 0.01 us -> 5.54 us  [over_plane(): lax.all_to_all(chunks, 'seq', split_axis=0, concat_axis=0, axis_index_gro...]
    ppermute x1, waiting for transfers between devices: 5.14 us -> 0.01 us  [grouped_device(): lax.ppermute(here_out, ('dp', 'seq'), [(blocks * d + source, blocks * (d...]
    ppermute x10 -> x13, starting transfers between devices: 15.4 us -> 20 us  [swapped(): return lax.ppermute(block, axis, route)]
    unnamed x70 -> x30, local copies, waits for them, and re-layouts: 7.75 us -> 3.31 us
    ppermute x3 -> x0, waiting for transfers between devices: 2.68 us -> none  [grouped_device(): got[turn] = lax.ppermute(pieces[turn], 'seq', route)]
    all_to_all x1, waiting for transfers between devices: 4.71 us -> 6.45 us  [grouped_device(): late = lax.all_to_all(late, 'seq', split_axis=0, concat_axis=0, tiled=True)]
    pallas_call x9 -> x10, Pallas kernels: 26.7 us -> 26.1 us  [call(): pl.pallas_call(body, grid=(steps,), in_specs=spaces, out_specs=[whole(sha...]
  transfers between devices with their start and end apart: 19 -> 19, of which waited for: 8 -> 6; matrix products, arithmetic and copies ran while one was open for 1% -> 1% of each run, Pallas kernels for 22% -> 22%
where the time goes in v11:
time: 86.2 us; the launch traced here: 85.7 us
  starting transfers between devices  35.4 us (41%)
  Pallas kernels  26.1 us (30%)
  waiting for transfers between devices  18.7 us (22%)
  local copies, waits for them, and re-layouts  3.38 us (4%)
  other arithmetic  1.19 us (1%)
  between operations  0.92 us (1%)
    pallas_call x10, Pallas kernels, call(): pl.pallas_call(body, grid=(steps,), in_specs=spaces, out_specs=[whole(sha...  26.1 us
    ppermute x13, starting transfers between devices, swapped(): return lax.ppermute(block, axis, route)  20 us
    ppermute x13, waiting for transfers between devices, swapped(): return lax.ppermute(block, axis, route)  6.68 us
    all_to_all x1, waiting for transfers between devices, grouped_device(): late = lax.all_to_all(late, 'seq', split_axis=0, concat_axis=0, tiled=True)  6.45 us
    all_to_all x1, waiting for transfers between devices, over_plane(): lax.all_to_all(chunks, 'seq', split_axis=0, concat_axis=0, axis_index_gro...  5.54 us
    ppermute x1, starting transfers between devices, grouped_device(): lax.ppermute(full_out, 'seq', [(0, last), (last - 1, last + 1)])  5 us
    all_to_all x1, starting transfers between devices, grouped_device(): late = lax.all_to_all(late, 'seq', split_axis=0, concat_axis=0, tiled=True)  3.71 us
    all_to_all x1, starting transfers between devices, over_plane(): lax.all_to_all(chunks, 'seq', split_axis=0, concat_axis=0, axis_index_gro...  3.48 us
  transfers between devices with their start and end apart: 19, of which 6 were waited for; matrix products, arithmetic and copies ran while one was open for 1% of the time, Pallas kernels for 22%

profile of v11, /device:TPU:0, one launch (start us, length us, event | category | flops | bytes accessed | tf_op | source)
XLA Modules:
  0.0 85.7 jit_solution(16405870067814773099)
XLA Ops:
  1.3 2.5 %shard_map.114 = (bf16[208,128]{1,0:T(8,128)(2,1)}, bf16[208,128]{1,0:T(8,128)(2,1)}, bf16[208,128]{1,0:T(8,128)(2,1)}, bf16[208,128]{1,0:T(8,128)(2,1)}) custom-call(s32[3]{0:T(128)} %pad_add_fusion.1.spot_ref, s32[1,128]{1,0:T(1,128)} %tokens_ref.3, bf16[128,768]{1,0:T(8,128)(2,1)} %bitcast.8, bf16[768,768]{1,0:T(8,128)(2,1)} %out_weights_ref.1), custom_call_target="tpu_custom_call" | custom-call | flops 100000000 | bytes 1000000 | tf_op jit(solution)/shard_map/pallas_call | solution.py:685
  3.8 4.0 %collective-permute-start.2 = (bf16[208,128]{1,0:T(8,128)(2,1)}, bf16[208,128]{1,0:T(8,128)(2,1)S(1)}, u32[]{:S(2)}, u32[]{:S(2)}) collective-permute-start(bf16[208,128]{1,0:T(8,128)(2,1)} %get-tuple-element.22), channel_id=1, source_target_pairs={{0,3},{1,2},{2,1},{3,0},{4,7},{5,6},{6,5},{7,4},{8,11},{9,10},{10,... | collective-permute-start | bytes 159752 | tf_op jit(solution)/shard_map/ppermute | solution.py:644
  8.2 2.6 %collective-permute-start.4 = (bf16[208,128]{1,0:T(8,128)(2,1)}, bf16[208,128]{1,0:T(8,128)(2,1)S(1)}, u32[]{:S(2)}, u32[]{:S(2)}) collective-permute-start(bf16[208,128]{1,0:T(8,128)(2,1)} %get-tuple-element.23), channel_id=1, source_target_pairs={{0,5},{1,4},{2,7},{3,6},{4,1},{5,0},{6,3},{7,2},{8,13},{9,12},{10,... | collective-permute-start | bytes 159752 | tf_op jit(solution)/shard_map/ppermute | solution.py:644
  10.8 1.8 %collective-permute-start = (bf16[208,128]{1,0:T(8,128)(2,1)}, bf16[208,128]{1,0:T(8,128)(2,1)S(1)}, u32[]{:S(2)}, u32[]{:S(2)}) collective-permute-start(bf16[208,128]{1,0:T(8,128)(2,1)} %get-tuple-element.21.rest_0_), channel_id=1, source_target_pairs={{0,1},{1,0},{2,3},{3,2},{4,5},{5,4},{6,7},{7,6},{8,9},{9,8},{10,11... | collective-permute-start | bytes 159752 | tf_op jit(solution)/shard_map/ppermute | solution.py:644
  13.3 1.9 %collective-permute-done.rest_1_ = bf16[208,128]{1,0:T(8,128)(2,1)S(1)} collective-permute-done((bf16[208,128]{1,0:T(8,128)(2,1)}, bf16[208,128]{1,0:T(8,128)(2,1)S(1)}, u32[]{:S(2)}, u32[]{:S(2)}) %collective-permute-start) | collective-permute-done | bytes 53280 | tf_op jit(solution)/shard_map/ppermute | solution.py:644
  15.2 5.0 %collective-permute-start.6 = (bf16[208,128]{1,0:T(8,128)(2,1)}, bf16[208,128]{1,0:T(8,128)(2,1)S(1)}, u32[]{:S(2)}, u32[]{:S(2)}) collective-permute-start(bf16[208,128]{1,0:T(8,128)(2,1)} %get-tuple-element.24), channel_id=1, source_target_pairs={{0,7},{1,6},{2,5},{3,4},{4,3},{5,2},{6,1},{7,0},{8,15},{9,14},{10,... | collective-permute-start | bytes 159752 | tf_op jit(solution)/shard_map/ppermute | solution.py:644
  20.2 4.3 %shard_map.113 = (bf16[2,576,256]{2,1,0:T(8,128)(2,1)}, bf16[256,384]{1,0:T(8,128)(2,1)}) custom-call(s32[6]{0:T(128)} %pad_add_fusion.meta_ref, bf16[256,768]{1,0:T(8,128)(2,1)} %table_ref.3, bf16[768,768]{1,0:T(8,128)(2,1)} %query_ref.3, bf16[768,768]{1,0:T(8,128)(2,1)} %key_ref.3, bf16[768,768]{1,0:T(8,128)(2,1)} %value_ref.3), custom_call_target="tpu_custom_call" | custom-call | flops 1000000000 | bytes 5000000 | tf_op jit(solution)/shard_map/pallas_call | solution.py:685
  24.5 1.7 %collective-permute-done.5.rest_6_ = bf16[208,128]{1,0:T(8,128)(2,1)S(1)} collective-permute-done((bf16[208,128]{1,0:T(8,128)(2,1)}, bf16[208,128]{1,0:T(8,128)(2,1)S(1)}, u32[]{:S(2)}, u32[]{:S(2)}) %collective-permute-start.5) | collective-permute-done | bytes 53280 | tf_op jit(solution)/shard_map/ppermute | solution.py:644
  28.3 3.7 %all-to-all-start.1 = ((bf16[8,128,384]{2,1,0:T(8,128)(2,1)}), bf16[8,128,384]{2,1,0:T(8,128)(2,1)S(1)}, u32[]{:S(2)}, u32[]{:S(2)}) async-start(bf16[8,128,384]{2,1,0:T(8,128)(2,1)} %shard_map.117), calls=%async_computation.1 | async-start | bytes 1572864 | tf_op jit(solution)/shard_map/all_to_all | solution.py:724
  32.1 10.9 %shard_map.115 = (bf16[4,576,128]{2,1,0:T(8,128)(2,1)}, bf16[2,576,128]{2,1,0:T(8,128)(2,1)S(1)}, bf16[192,1024]{1,0:T(8,128)(2,1)S(1)}) custom-call(s32[6]{0:T(128)S(1)} %copy-done.8, bf16[2,576,256]{2,1,0:T(8,128)(2,1)S(1)} %copy-done.7, f32[32,1024]{1,0:T(8,128)S(1)} %copy-done.13, f32[32,1024]{1,0:T(8,128)S(1)} %copy-done.12, ...), custom_call_target="tpu_custom_call" | custom-call | flops 8000000000 | bytes 8000000 | tf_op jit(solution)/shard_map/pallas_call | solution.py:685
  43.0 6.4 %all-to-all-done.1 = bf16[8,128,384]{2,1,0:T(8,128)(2,1)S(1)} async-done(((bf16[8,128,384]{2,1,0:T(8,128)(2,1)}), bf16[8,128,384]{2,1,0:T(8,128)(2,1)S(1)}, u32[]{:S(2)}, u32[]{:S(2)}) %all-to-all-start.1) | async-done | bytes 786464 | tf_op jit(solution)/shard_map/all_to_all | solution.py:724
  49.5 3.5 %all-to-all-start = ((bf16[4,576,128]{2,1,0:T(8,128)(2,1)}), bf16[4,576,128]{2,1,0:T(8,128)(2,1)S(1)}, u32[]{:S(2)}, u32[]{:S(2)}) async-start(bf16[4,576,128]{2,1,0:T(8,128)(2,1)} %get-tuple-element.25), calls=%async_computation | async-start | bytes 1179648 | tf_op jit(solution)/shard_map/all_to_all | solution.py:760
  54.0 1.5 %collective-permute-done.7.got_ref = bf16[864,128]{1,0:T(8,128)(2,1)S(1)} collective-permute-done((bf16[864,128]{1,0:T(8,128)(2,1)S(1)}, bf16[864,128]{1,0:T(8,128)(2,1)S(1)}, u32[]{:S(2)}, u32[]{:S(2)}) %collective-permute-start.7) | collective-permute-done | bytes 221216 | tf_op jit(solution)/shard_map/ppermute | solution.py:644
  56.2 1.6 %collective-permute-start.8 = (bf16[864,128]{1,0:T(8,128)(2,1)}, bf16[864,128]{1,0:T(8,128)(2,1)}, u32[]{:S(2)}, u32[]{:S(2)}) collective-permute-start(bf16[864,128]{1,0:T(8,128)(2,1)} %get-tuple-element.31.here_ref), channel_id=1, source_target_pairs={{0,16},{8,24},{16,0},{24,8},{1,17},{9,25},{17,1},{25,9},{2,18},{10... | collective-permute-start | bytes 663560 | tf_op jit(solution)/shard_map/ppermute | solution.py:644
  57.8 1.3 %collective-permute-start.10 = (bf16[288,128]{1,0:T(8,128)(2,1)}, bf16[288,128]{1,0:T(8,128)(2,1)S(1)}, u32[]{:S(2)}, u32[]{:S(2)}) collective-permute-start(bf16[288,128]{1,0:T(8,128)(2,1)} %get-tuple-element.32), channel_id=1, source_target_pairs={{1,16},{3,18},{4,21},{6,23},{9,24},{11,26},{12,29},{14,31},{17,0},... | collective-permute-start | bytes 221192 | tf_op jit(solution)/shard_map/ppermute | solution.py:781
  59.1 1.3 %collective-permute-start.9 = (bf16[288,128]{1,0:T(8,128)(2,1)}, bf16[288,128]{1,0:T(8,128)(2,1)S(1)}, u32[]{:S(2)}, u32[]{:S(2)}) collective-permute-start(bf16[288,128]{1,0:T(8,128)(2,1)} %get-tuple-element.32), channel_id=1, source_target_pairs={{1,0},{3,2},{4,5},{6,7},{9,8},{11,10},{12,13},{14,15},{17,16},{19,... | collective-permute-start | bytes 221192 | tf_op jit(solution)/shard_map/ppermute | solution.py:780
  60.4 5.5 %all-to-all-done.rows_ref.after_ref = bf16[4,576,128]{2,1,0:T(8,128)(2,1)S(1)} async-done(((bf16[4,576,128]{2,1,0:T(8,128)(2,1)}), bf16[4,576,128]{2,1,0:T(8,128)(2,1)S(1)}, u32[]{:S(2)}, u32[]{:S(2)}) %all-to-all-start) | async-done | bytes 589856 | tf_op jit(solution)/shard_map/all_to_all | solution.py:760
  66.0 1.1 %shard_map.120 = (bf16[576,128]{1,0:T(8,128)(2,1)S(1)}, bf16[192,128]{1,0:T(8,128)(2,1)S(1)}, bf16[192,128]{1,0:T(8,128)(2,1)S(1)}, bf16[192,128]{1,0:T(8,128)(2,1)S(1)}, bf16[192,128]{1,0:T(8,128)(2,1)S(1)}) custom-call(s32[6]{0:T(128)S(1)} %copy-done.8, bf16[864,128]{1,0:T(8,128)(2,1)} %get-tuple-element.31.here_ref, ...), custom_call_target="tpu_custom_call" | custom-call | flops 100000000 | bytes 1000000 | tf_op jit(solution)/shard_map/pallas_call | solution.py:685
  67.8 5.0 %collective-permute-start.14 = (bf16[576,128]{1,0:T(8,128)(2,1)S(1)}, bf16[576,128]{1,0:T(8,128)(2,1)S(1)}, u32[]{:S(2)}, u32[]{:S(2)}) collective-permute-start(bf16[576,128]{1,0:T(8,128)(2,1)S(1)} %get-tuple-element.37.own_ref), channel_id=1, source_target_pairs={{0,6},{5,7},{8,14},{13,15},{16,22},{21,23},{24,30},{29,31}} | collective-permute-start | bytes 442376 | tf_op jit(solution)/shard_map/ppermute | solution.py:798
  73.0 4.3 %collective-permute-start.13 = (bf16[192,128]{1,0:T(8,128)(2,1)S(1)}, bf16[192,128]{1,0:T(8,128)(2,1)S(1)}, u32[]{:S(2)}, u32[]{:S(2)}) collective-permute-start(bf16[192,128]{1,0:T(8,128)(2,1)S(1)} %get-tuple-element.36), channel_id=1, source_target_pairs={{0,6},{1,7},{2,4},{3,5},{4,2},{5,3},{6,0},{7,1},{8,14},{9,15},{10,... | collective-permute-start | bytes 147464 | tf_op jit(solution)/shard_map/ppermute | solution.py:644
  77.3 1.3 %copy-done.2 = bf16[768,768]{1,0:T(8,128)(2,1)S(1)} copy-done((bf16[768,768]{1,0:T(8,128)(2,1)S(1)}, bf16[768,768]{1,0:T(8,128)(2,1)}, u32[]{:S(2)}) %copy-start.2) | copy-done | bytes 1179672
  78.5 1.9 %shard_map.116.after_ref = bf16[128,768]{1,0:T(8,128)(2,1)} custom-call(s32[1,128]{1,0:T(1,128)S(1)} %copy-done.9, bf16[256,768]{1,0:T(8,128)(2,1)S(1)} %copy-done.3, bf16[768,768]{1,0:T(8,128)(2,1)S(1)} %copy-done, bf16[768,768]{1,0:T(8,128)(2,1)S(1)} %copy-done.1, bf16[768,768]{1,0:T(8,128)(2,1)S(1)} %copy-done.2, ...), custom_call_target="tpu_custom_call" | custom-call | flops 1000000000 | bytes 5000000 | tf_op jit(solution)/shard_map/pallas_call | solution.py:685
  82.1 1.6 %collective-permute-done.16.other_ref = bf16[1152,128]{1,0:T(8,128)(2,1)S(1)} collective-permute-done((bf16[1152,128]{1,0:T(8,128)(2,1)S(1)}, bf16[1152,128]{1,0:T(8,128)(2,1)S(1)}, u32[]{:S(2)}, u32[]{:S(2)}) %collective-permute-start.16) | collective-permute-done | bytes 294944 | tf_op jit(solution)/shard_map/ppermute | solution.py:644
  83.7 2.1 %shard_map.122 = f32[384,768]{1,0:T(8,128)} custom-call(s32[6]{0:T(128)S(1)} %copy-done.8, bf16[256,384]{1,0:T(8,128)(2,1)S(1)} %copy-done.10, bf16[1152,128]{1,0:T(8,128)(2,1)S(1)} %shard_map.121.mine_ref, bf16[1152,128]{1,0:T(8,128)(2,1)S(1)} %collective-permute-done.16.other_ref), custom_call_target="tpu_custom_call" | custom-call | flops 1000000000 | bytes 5000000 | tf_op jit(solution)/shard_map/pallas_call | solution.py:685
  (57 shorter events, 8.1 us)
Async XLA Ops:
  0.6 12.0 %copy-start.14 = (s32[12]{0:T(128)S(1)}, s32[12]{0:T(128)}, u32[]{:S(2)}) copy-start(s32[12]{0:T(128)} %param.17) | copy-start | bytes 148
  3.8 16.3 %collective-permute-start.2 = (bf16[208,128]{1,0:T(8,128)(2,1)}, bf16[208,128]{1,0:T(8,128)(2,1)S(1)}, u32[]{:S(2)}, u32[]{:S(2)}) collective-permute-start(bf16[208,128]{1,0:T(8,128)(2,1)} %get-tuple-element.22), channel_id=1, source_target_pairs={{0,3},{1,2},{2,1},{3,0},{4,7},{5,6},{6,5},{7,4},{8,11},{9,10},{10,... | collective-permute-start | bytes 159752 | tf_op jit(solution)/shard_map/ppermute | solution.py:644
  7.8 16.7 %collective-permute-start.1 = (bf16[208,128]{1,0:T(8,128)(2,1)}, bf16[208,128]{1,0:T(8,128)(2,1)S(1)}, u32[]{:S(2)}, u32[]{:S(2)}) collective-permute-start(bf16[208,128]{1,0:T(8,128)(2,1)} %get-tuple-element.22), channel_id=1, source_target_pairs={{0,2},{1,3},{2,0},{3,1},{4,6},{5,7},{6,4},{7,5},{8,10},{9,11},{10,... | collective-permute-start | bytes 159752 | tf_op jit(solution)/shard_map/ppermute | solution.py:644
  8.2 16.3 %collective-permute-start.4 = (bf16[208,128]{1,0:T(8,128)(2,1)}, bf16[208,128]{1,0:T(8,128)(2,1)S(1)}, u32[]{:S(2)}, u32[]{:S(2)}) collective-permute-start(bf16[208,128]{1,0:T(8,128)(2,1)} %get-tuple-element.23), channel_id=1, source_target_pairs={{0,5},{1,4},{2,7},{3,6},{4,1},{5,0},{6,3},{7,2},{8,13},{9,12},{10,... | collective-permute-start | bytes 159752 | tf_op jit(solution)/shard_map/ppermute | solution.py:644
  10.8 13.7 %collective-permute-start.3 = (bf16[208,128]{1,0:T(8,128)(2,1)}, bf16[208,128]{1,0:T(8,128)(2,1)S(1)}, u32[]{:S(2)}, u32[]{:S(2)}) collective-permute-start(bf16[208,128]{1,0:T(8,128)(2,1)} %get-tuple-element.23), channel_id=1, source_target_pairs={{0,4},{1,5},{2,6},{3,7},{4,0},{5,1},{6,2},{7,3},{8,12},{9,13},{10,... | collective-permute-start | bytes 159752 | tf_op jit(solution)/shard_map/ppermute | solution.py:644
  10.8 4.3 %collective-permute-start = (bf16[208,128]{1,0:T(8,128)(2,1)}, bf16[208,128]{1,0:T(8,128)(2,1)S(1)}, u32[]{:S(2)}, u32[]{:S(2)}) collective-permute-start(bf16[208,128]{1,0:T(8,128)(2,1)} %get-tuple-element.21.rest_0_), channel_id=1, source_target_pairs={{0,1},{1,0},{2,3},{3,2},{4,5},{5,4},{6,7},{7,6},{8,9},{9,8},{10,11... | collective-permute-start | bytes 159752 | tf_op jit(solution)/shard_map/ppermute | solution.py:644
  15.2 9.4 %collective-permute-start.6 = (bf16[208,128]{1,0:T(8,128)(2,1)}, bf16[208,128]{1,0:T(8,128)(2,1)S(1)}, u32[]{:S(2)}, u32[]{:S(2)}) collective-permute-start(bf16[208,128]{1,0:T(8,128)(2,1)} %get-tuple-element.24), channel_id=1, source_target_pairs={{0,7},{1,6},{2,5},{3,4},{4,3},{5,2},{6,1},{7,0},{8,15},{9,14},{10,... | collective-permute-start | bytes 159752 | tf_op jit(solution)/shard_map/ppermute | solution.py:644
  20.1 6.1 %collective-permute-start.5 = (bf16[208,128]{1,0:T(8,128)(2,1)}, bf16[208,128]{1,0:T(8,128)(2,1)S(1)}, u32[]{:S(2)}, u32[]{:S(2)}) collective-permute-start(bf16[208,128]{1,0:T(8,128)(2,1)} %get-tuple-element.24), channel_id=1, source_target_pairs={{0,6},{1,7},{2,4},{3,5},{4,2},{5,3},{6,0},{7,1},{8,14},{9,15},{10,... | collective-permute-start | bytes 159752 | tf_op jit(solution)/shard_map/ppermute | solution.py:644
  28.3 21.1 %all-to-all-start.1 = ((bf16[8,128,384]{2,1,0:T(8,128)(2,1)}), bf16[8,128,384]{2,1,0:T(8,128)(2,1)S(1)}, u32[]{:S(2)}, u32[]{:S(2)}) async-start(bf16[8,128,384]{2,1,0:T(8,128)(2,1)} %shard_map.117), calls=%async_computation.1 | async-start | bytes 1572864 | tf_op jit(solution)/shard_map/all_to_all | solution.py:724
  49.5 16.5 %all-to-all-start = ((bf16[4,576,128]{2,1,0:T(8,128)(2,1)}), bf16[4,576,128]{2,1,0:T(8,128)(2,1)S(1)}, u32[]{:S(2)}, u32[]{:S(2)}) async-start(bf16[4,576,128]{2,1,0:T(8,128)(2,1)} %get-tuple-element.25), calls=%async_computation | async-start | bytes 1179648 | tf_op jit(solution)/shard_map/all_to_all | solution.py:760
  52.9 24.3 %copy-start.1 = (bf16[768,768]{1,0:T(8,128)(2,1)S(1)}, bf16[768,768]{1,0:T(8,128)(2,1)}, u32[]{:S(2)}) copy-start(bf16[768,768]{1,0:T(8,128)(2,1)} %key_ref.3) | copy-start | bytes 3538948
  53.9 23.4 %copy-start = (bf16[768,768]{1,0:T(8,128)(2,1)S(1)}, bf16[768,768]{1,0:T(8,128)(2,1)}, u32[]{:S(2)}) copy-start(bf16[768,768]{1,0:T(8,128)(2,1)} %query_ref.3) | copy-start | bytes 3538948
  53.9 23.4 %copy-start.3 = (bf16[256,768]{1,0:T(8,128)(2,1)S(1)}, bf16[256,768]{1,0:T(8,128)(2,1)}, u32[]{:S(2)}) copy-start(bf16[256,768]{1,0:T(8,128)(2,1)} %table_ref.3) | copy-start | bytes 1179652
  53.9 23.4 %copy-start.9 = (s32[1,128]{1,0:T(1,128)S(1)}, s32[1,128]{1,0:T(1,128)}, u32[]{:S(2)}) copy-start(s32[1,128]{1,0:T(1,128)} %tokens_ref.3) | copy-start | bytes 1540
  53.9 1.5 %collective-permute-start.7 = (bf16[864,128]{1,0:T(8,128)(2,1)S(1)}, bf16[864,128]{1,0:T(8,128)(2,1)S(1)}, u32[]{:S(2)}, u32[]{:S(2)}) collective-permute-start(bf16[864,128]{1,0:T(8,128)(2,1)S(1)} %get-tuple-element.30), channel_id=1, source_target_pairs={{0,8},{8,0},{16,24},{24,16},{1,9},{9,1},{17,25},{25,17},{2,10},{10... | collective-permute-start | bytes 663560 | tf_op jit(solution)/shard_map/ppermute | solution.py:644
  56.2 9.7 %collective-permute-start.8 = (bf16[864,128]{1,0:T(8,128)(2,1)}, bf16[864,128]{1,0:T(8,128)(2,1)}, u32[]{:S(2)}, u32[]{:S(2)}) collective-permute-start(bf16[864,128]{1,0:T(8,128)(2,1)} %get-tuple-element.31.here_ref), channel_id=1, source_target_pairs={{0,16},{8,24},{16,0},{24,8},{1,17},{9,25},{17,1},{25,9},{2,18},{10... | collective-permute-start | bytes 663560 | tf_op jit(solution)/shard_map/ppermute | solution.py:644
  57.8 8.1 %collective-permute-start.10 = (bf16[288,128]{1,0:T(8,128)(2,1)}, bf16[288,128]{1,0:T(8,128)(2,1)S(1)}, u32[]{:S(2)}, u32[]{:S(2)}) collective-permute-start(bf16[288,128]{1,0:T(8,128)(2,1)} %get-tuple-element.32), channel_id=1, source_target_pairs={{1,16},{3,18},{4,21},{6,23},{9,24},{11,26},{12,29},{14,31},{17,0},... | collective-permute-start | bytes 221192 | tf_op jit(solution)/shard_map/ppermute | solution.py:781
  59.1 6.8 %collective-permute-start.9 = (bf16[288,128]{1,0:T(8,128)(2,1)}, bf16[288,128]{1,0:T(8,128)(2,1)S(1)}, u32[]{:S(2)}, u32[]{:S(2)}) collective-permute-start(bf16[288,128]{1,0:T(8,128)(2,1)} %get-tuple-element.32), channel_id=1, source_target_pairs={{1,0},{3,2},{4,5},{6,7},{9,8},{11,10},{12,13},{14,15},{17,16},{19,... | collective-permute-start | bytes 221192 | tf_op jit(solution)/shard_map/ppermute | solution.py:780
  67.1 13.4 %collective-permute-start.15 = (bf16[576,128]{1,0:T(8,128)(2,1)S(1)}, bf16[576,128]{1,0:T(8,128)(2,1)S(1)}, u32[]{:S(2)}, u32[]{:S(2)}) collective-permute-start(bf16[576,128]{1,0:T(8,128)(2,1)S(1)} %get-tuple-element.37.own_ref), channel_id=1, source_target_pairs={{2,6},{10,14},{18,22},{26,30}} | collective-permute-start | bytes 442376 | tf_op jit(solution)/shard_map/ppermute | solution.py:799
  67.8 12.7 %collective-permute-start.14 = (bf16[576,128]{1,0:T(8,128)(2,1)S(1)}, bf16[576,128]{1,0:T(8,128)(2,1)S(1)}, u32[]{:S(2)}, u32[]{:S(2)}) collective-permute-start(bf16[576,128]{1,0:T(8,128)(2,1)S(1)} %get-tuple-element.37.own_ref), channel_id=1, source_target_pairs={{0,6},{5,7},{8,14},{13,15},{16,22},{21,23},{24,30},{29,31}} | collective-permute-start | bytes 442376 | tf_op jit(solution)/shard_map/ppermute | solution.py:798
  72.8 7.7 %collective-permute-start.11 = (bf16[192,128]{1,0:T(8,128)(2,1)S(1)}, bf16[192,128]{1,0:T(8,128)(2,1)S(1)}, u32[]{:S(2)}, u32[]{:S(2)}) collective-permute-start(bf16[192,128]{1,0:T(8,128)(2,1)S(1)} %get-tuple-element.34), channel_id=1, source_target_pairs={{0,2},{1,3},{2,0},{3,1},{4,6},{5,7},{6,4},{7,5},{8,10},{9,11},{10,... | collective-permute-start | bytes 147464 | tf_op jit(solution)/shard_map/ppermute | solution.py:644
  72.9 7.6 %collective-permute-start.12 = (bf16[192,128]{1,0:T(8,128)(2,1)S(1)}, bf16[192,128]{1,0:T(8,128)(2,1)S(1)}, u32[]{:S(2)}, u32[]{:S(2)}) collective-permute-start(bf16[192,128]{1,0:T(8,128)(2,1)S(1)} %get-tuple-element.35), channel_id=1, source_target_pairs={{0,4},{1,5},{2,6},{3,7},{4,0},{5,1},{6,2},{7,3},{8,12},{9,13},{10,... | collective-permute-start | bytes 147464 | tf_op jit(solution)/shard_map/ppermute | solution.py:644
  73.0 7.5 %collective-permute-start.13 = (bf16[192,128]{1,0:T(8,128)(2,1)S(1)}, bf16[192,128]{1,0:T(8,128)(2,1)S(1)}, u32[]{:S(2)}, u32[]{:S(2)}) collective-permute-start(bf16[192,128]{1,0:T(8,128)(2,1)S(1)} %get-tuple-element.36), channel_id=1, source_target_pairs={{0,6},{1,7},{2,4},{3,5},{4,2},{5,3},{6,0},{7,1},{8,14},{9,15},{10,... | collective-permute-start | bytes 147464 | tf_op jit(solution)/shard_map/ppermute | solution.py:644
  82.0 1.6 %collective-permute-start.16 = (bf16[1152,128]{1,0:T(8,128)(2,1)S(1)}, bf16[1152,128]{1,0:T(8,128)(2,1)S(1)}, u32[]{:S(2)}, u32[]{:S(2)}) collective-permute-start(bf16[1152,128]{1,0:T(8,128)(2,1)S(1)} %shard_map.121.mine_ref), channel_id=1, source_target_pairs={{0,8},{8,0},{16,24},{24,16},{1,9},{9,1},{17,25},{25,17},{2,10},{10... | collective-permute-start | bytes 884744 | tf_op jit(solution)/shard_map/ppermute | solution.py:644
  (10 other events, 38.3 us)

commit v12 on v11

--- a/solution.py
+++ b/solution.py
@@ -232,6 +232,10 @@
 VMEM_BYTES = 48 * 1024 * 1024
 
 
+def mirrored(bits):
+    return 2 * (bits % 2) + bits // 2 % 2
+
+
 def key_span(query_tile):
     first = max(0, query_tile - WINDOW // TILE)
     return (first * TILE, (query_tile - first + 1) * TILE)
@@ -257,7 +261,7 @@
         jnp.bfloat16
     )
     for turn, early_ref in enumerate(early_refs):
-        group = spot_ref[1] ^ turn
+        group = spot_ref[0] ^ turn
         place = pl.ds(pl.multiple_of(group * GROUP_COLS, GROUP_COLS), GROUP_COLS)
         early_ref[:GROUP_COLS, :] = grads_ref[place, :]
         early_ref[GROUP_COLS:, :] = tokens
@@ -267,7 +271,7 @@
     late_ref = rest[-1]
     columns = late_ref.shape[2]
     for target in range(2 * GROUPS):
-        side = target % 2
+        side = target // GROUPS
         late_ref[target] = cotangent_ref[:, side * columns : (side + 1) * columns]
 
 
@@ -284,7 +288,7 @@
     normed = normed_table(table_ref)
     half = normed.shape[1] // 2
     normed_ref[...] = jnp.where(meta_ref[GROUP_HEADS] == 0, normed[:, :half], normed[:, half:])
-    place = pl.ds(pl.multiple_of(meta_ref[GROUP_HEADS + 1] * GROUP_COLS, GROUP_COLS), GROUP_COLS)
+    place = pl.ds(pl.multiple_of(meta_ref[GROUP_HEADS + 3] * GROUP_COLS, GROUP_COLS), GROUP_COLS)
     for matrix, weights_ref in enumerate((query_ref, key_ref, value_ref)):
         columns_ref[...] = jnp.dot(
             normed, weights_ref[...], preferred_element_type=jnp.float32
@@ -511,10 +515,10 @@
             lane = core * half_vocab
             sums_ref[core, place, :] = sums[rows, lane : lane + half_vocab]
         for target in range(GROUPS):
-            start = target * 2 * block
-            even = grads[rows, start : start + block]
-            odd = grads[rows, start + block : start + 2 * block]
-            rows_ref[target, place, :] = jnp.where(meta_ref[GROUP_HEADS] == 0, even, odd)
+            start = target * block
+            near = grads[rows, start : start + block]
+            far = grads[rows, start + GROUPS * block : start + (GROUPS + 1) * block]
+            rows_ref[target, place, :] = jnp.where(meta_ref[GROUP_HEADS + 1] < 2, near, far)
 
 
 def out_kernel(meta_ref, attended_ref, cotangent_ref, sums_ref, keep_ref, give_ref):
@@ -532,47 +536,33 @@
         give_ref[place, :] = jnp.where(first, part[rows:], part[:rows]).astype(jnp.bfloat16)
 
 
-def core_kernel(keep_ref, got_ref, here_ref, out_ref):
-    here_ref[...] = keep_ref[...] + got_ref[...]
-    base = here_ref.shape[0] - out_ref.shape[0]
-    out_ref[...] = here_ref[base:, :]
-
-
-def combine_kernel(
-    meta_ref, here_ref, there_ref, near_ref, far_ref, after_ref, out_ref, *piece_refs
-):
+def combine_kernel(meta_ref, here_ref, there_ref, after_ref, out_ref, *piece_refs):
     del after_ref
     rows = GROUP_COLS
     for turn, piece_ref in enumerate(piece_refs):
-        target = jnp.minimum(meta_ref[GROUP_HEADS + 1] ^ turn, 2)
+        target = jnp.minimum(meta_ref[GROUP_HEADS + 1] ^ (turn // 2), 2)
         place = pl.ds(pl.multiple_of(target * rows, rows), rows)
         piece_ref[...] = here_ref[place, :] + there_ref[place, :]
-    own = here_ref[3 * rows :, :] + there_ref[3 * rows :, :]
-    other = near_ref[...] + far_ref[...]
-    first = meta_ref[GROUP_HEADS] == 0
-    size = own.shape[0]
-    out_ref[:size, :] = jnp.where(first, own, other)
-    out_ref[size:, :] = jnp.where(first, other, own)
-
-
-def gather_kernel(meta_ref, s0, s1, s2, s3, own_ref, o0, o1, after_ref, mine_ref):
+    out_ref[...] = here_ref[3 * rows :, :] + there_ref[3 * rows :, :]
+
+
+def gather_kernel(meta_ref, s0, s1, s2, s3, own_ref, o0, o1, o2, after_ref, mine_ref):
     del after_ref
     rows = GROUP_COLS
     size = own_ref.shape[0]
-    group = meta_ref[GROUP_HEADS + 1]
-
-    @pl.when(group < 3)
+
+    @pl.when(meta_ref[GROUP_HEADS + 1] < 3)
     def _():
         for turn, got in enumerate((s0, s1, s2, s3)):
-            place = pl.ds(pl.multiple_of((group ^ turn) * rows, rows), rows)
-            mine_ref[place, :] = got[...]
+            source = meta_ref[GROUP_HEADS + 3] ^ mirrored(turn)
+            mine_ref[pl.ds(pl.multiple_of(source * rows, rows), rows), :] = got[...]
         tail = mine_ref.shape[0] - GROUPS * rows
         mine_ref[GROUPS * rows :, :] = jnp.zeros((tail, mine_ref.shape[1]), jnp.bfloat16)
 
-    @pl.when(group == 3)
+    @pl.when(meta_ref[GROUP_HEADS + 1] == 3)
     def _():
-        mine_ref[:size, :] = o0[...]
-        mine_ref[size:, :] = jnp.where(meta_ref[GROUP_HEADS] == 0, o1[...], own_ref[...])
+        for place, piece in enumerate((o0, o2, o1, own_ref)):
+            mine_ref[place * size : (place + 1) * size, :] = piece[...]
 
 
 def input_kernel(tokens_ref, table_ref, query_ref, key_ref, value_ref, rows_ref, out_ref):
@@ -585,7 +575,7 @@
         columns = jnp.concatenate(
             [
                 rows_ref[group, matrix * GROUP_COLS : (matrix + 1) * GROUP_COLS, :]
-                for group in range(GROUPS)
+                for group in map(mirrored, range(GROUPS))
             ],
             axis=0,
         )
@@ -657,8 +647,9 @@
 def grouped_device(token_ids, cotangent, table, w_query, w_key, w_value, w_out, window):
     place = lax.axis_index("seq")
     core = lax.axis_index("dp") % 2
-    group = place // 2
     side = place % 2
+    level = place // 2
+    group = 2 * side + level % 2
     block = token_ids.shape[1]
     features = table.shape[1]
     vocab = table.shape[0]
@@ -668,10 +659,10 @@
     meta = jnp.concatenate(
         [
             lax.dynamic_slice_in_dim(window, group * GROUP_HEADS, GROUP_HEADS, 0),
-            jnp.stack([side, group, core]).astype(jnp.int32),
+            jnp.stack([side, level, core, group]).astype(jnp.int32),
         ]
     )
-    spot = jnp.stack([side, group, core]).astype(jnp.int32)
+    spot = jnp.stack([group]).astype(jnp.int32)
     cosine, sine_part = rope_table(length)
 
     def call(
@@ -705,7 +696,7 @@
     )
     early = [sent[0]] + [None] * (blocks - 1)
     for turn in (4, 6, 5, 7, 2, 3, 1):
-        early[turn] = swapped(sent[turn // 2], "seq", turn)
+        early[turn] = swapped(sent[mirrored(turn)], "seq", turn)
     lookup, normed = call(
         prepare_kernel,
         (meta, table, w_query, w_key, w_value),
@@ -754,7 +745,7 @@
         flops=8 * 10**9,
         moved=8 * 10**6,
     )
-    planes = [[2 * z + x for z in range(GROUPS)] for x in range(2)]
+    planes = [[GROUPS * z + x for x in range(GROUPS)] for z in range(2)]
 
     def over_plane(chunks):
         return lax.all_to_all(
@@ -770,37 +761,19 @@
         (meta, attended, late.reshape(length, features // 2), sums),
         [((packed, lanes), half)] * 2,
     )
-    here, here_out = call(
-        core_kernel,
-        (keep, swapped(give, "dp", 1)),
-        [((packed, lanes), half), ((out_rows, lanes), half)],
-    )
+    here = keep + swapped(give, "dp", 1)
     there = swapped(here, "dp", 2)
-    inward = [(2 * z + 1 - z // 2, 2 * z + z // 2) for z in range(GROUPS)]
-    near = lax.ppermute(here_out, "seq", inward)
-    far = lax.ppermute(
-        here_out,
-        ("dp", "seq"),
-        [
-            (blocks * d + source, blocks * (d ^ 2) + target)
-            for d in range(lax.axis_size("dp"))
-            for source, target in inward
-        ],
-    )
-    full_out, *pieces = call(
+    kept_out, *pieces = call(
         combine_kernel,
-        (meta, here, there, near, far, got_rows),
-        [((2 * out_rows, lanes), half)] + [((GROUP_COLS, lanes), half)] * GROUPS,
+        (meta, here, there, got_rows),
+        [((out_rows, lanes), half)] + [((GROUP_COLS, lanes), half)] * GROUPS,
         loose=1,
     )
     last = blocks - 2
+    got = [pieces[0]] + [swapped(pieces[turn], "seq", turn) for turn in (1, 2, 3)]
     got_out = [
-        lax.ppermute(full_out, "seq", [(0, last), (last - 1, last + 1)]),
-        lax.ppermute(full_out, "seq", [(2, last)]),
+        lax.ppermute(kept_out, "seq", [(2 * z, last), (2 * z + 1, last + 1)]) for z in range(3)
     ]
-    got = [pieces[0]] + [None] * (GROUPS - 1)
-    for turn in (2, 3, 1):
-        got[turn] = swapped(pieces[turn], "seq", 2 * turn)
     (grad_input,) = call(
         input_kernel,
         (token_ids, table, w_query, w_key, w_value, got_rows),
@@ -810,7 +783,7 @@
     )
     (mine,) = call(
         gather_kernel,
-        (meta, *got, full_out, *got_out, grad_input),
+        (meta, *got, kept_out, *got_out, grad_input),
         [((4 * out_rows, lanes), half)],
         loose=1,
     )

time: 86.2 us -> 81.7 us (0.948)
  starting transfers between devices: 35.4 us -> 32.2 us
    all_to_all x1, waiting for transfers between devices: 5.54 us -> 2.27 us  [over_plane(): lax.all_to_all(chunks, 'seq', split_axis=0, concat_axis=0, axis_index_gro...]
    ppermute x4 -> x3, starting transfers between devices: 8.25 us -> 6.01 us  [grouped_device(): lax.ppermute(kept_out, 'seq', [(2 * z, last), (2 * z + 1, last + 1)])]
    ppermute x13, starting transfers between devices: 20 us -> 18.2 us  [swapped(): return lax.ppermute(block, axis, route)]
    all_to_all x1, waiting for transfers between devices: 6.45 us -> 7.95 us  [grouped_device(): late = lax.all_to_all(late, 'seq', split_axis=0, concat_axis=0, tiled=True)]
    ppermute x13, waiting for transfers between devices: 6.68 us -> 7.8 us  [swapped(): return lax.ppermute(block, axis, route)]
    pallas_call x10 -> x9, Pallas kernels: 26.1 us -> 25.3 us  [call(): pl.pallas_call(body, grid=(steps,), in_specs=spaces, out_specs=[whole(sha...]
  transfers between devices with their start and end apart: 19 -> 18, of which waited for: 6 -> 6; matrix products, arithmetic and copies ran while one was open for 1% -> 2% of each run, Pallas kernels for 22% -> 22%
where the time goes in v12:
time: 81.7 us; the launch traced here: 81.2 us
  starting transfers between devices  32.2 us (39%)
  Pallas kernels  25.3 us (31%)
  waiting for transfers between devices  18 us (22%)
  local copies, waits for them, and re-layouts  4.01 us (5%)
  between operations  0.92 us (1%)
    pallas_call x9, Pallas kernels, call(): pl.pallas_call(body, grid=(steps,), in_specs=spaces, out_specs=[whole(sha...  25.3 us
    ppermute x13, starting transfers between devices, swapped(): return lax.ppermute(block, axis, route)  18.2 us
    all_to_all x1, waiting for transfers between devices, grouped_device(): late = lax.all_to_all(late, 'seq', split_axis=0, concat_axis=0, tiled=True)  7.95 us
    ppermute x13, waiting for transfers between devices, swapped(): return lax.ppermute(block, axis, route)  7.8 us
    ppermute x3, starting transfers between devices, grouped_device(): lax.ppermute(kept_out, 'seq', [(2 * z, last), (2 * z + 1, last + 1)])  6.01 us
    all_to_all x1, starting transfers between devices, grouped_device(): late = lax.all_to_all(late, 'seq', split_axis=0, concat_axis=0, tiled=True)  4.43 us
    all_to_all x1, starting transfers between devices, over_plane(): lax.all_to_all(chunks, 'seq', split_axis=0, concat_axis=0, axis_index_gro...  3.48 us
    unnamed x30, local copies, waits for them, and re-layouts  3.31 us
  transfers between devices with their start and end apart: 18, of which 6 were waited for; matrix products, arithmetic and copies ran while one was open for 2% of the time, Pallas kernels for 22%

profile of v12, /device:TPU:0, one launch (start us, length us, event | category | flops | bytes accessed | tf_op | source)
XLA Modules:
  0.0 81.2 jit_solution(18070595671197211942)
XLA Ops:
  0.7 2.5 %shard_map.114 = (bf16[208,128]{1,0:T(8,128)(2,1)}, bf16[208,128]{1,0:T(8,128)(2,1)}, bf16[208,128]{1,0:T(8,128)(2,1)}, bf16[208,128]{1,0:T(8,128)(2,1)}) custom-call(s32[1]{0:T(128)} %bitcast.3.spot_ref, s32[1,128]{1,0:T(1,128)} %tokens_ref.3, bf16[128,768]{1,0:T(8,128)(2,1)} %bitcast.9, bf16[768,768]{1,0:T(8,128)(2,1)} %out_weights_ref.1), custom_call_target="tpu_custom_call" | custom-call | flops 100000000 | bytes 1000000 | tf_op jit(solution)/shard_map/pallas_call | solution.py:676
  3.2 4.0 %collective-permute-start.3 = (bf16[208,128]{1,0:T(8,128)(2,1)}, bf16[208,128]{1,0:T(8,128)(2,1)S(1)}, u32[]{:S(2)}, u32[]{:S(2)}) collective-permute-start(bf16[208,128]{1,0:T(8,128)(2,1)} %get-tuple-element.19.rest_0_), channel_id=1, source_target_pairs={{0,4},{1,5},{2,6},{3,7},{4,0},{5,1},{6,2},{7,3},{8,12},{9,13},{10,... | collective-permute-start | bytes 159752 | tf_op jit(solution)/shard_map/ppermute | solution.py:634
  7.3 1.3 %collective-permute-start.4 = (bf16[208,128]{1,0:T(8,128)(2,1)}, bf16[208,128]{1,0:T(8,128)(2,1)S(1)}, u32[]{:S(2)}, u32[]{:S(2)}) collective-permute-start(bf16[208,128]{1,0:T(8,128)(2,1)} %get-tuple-element.20), channel_id=1, source_target_pairs={{0,5},{1,4},{2,7},{3,6},{4,1},{5,0},{6,3},{7,2},{8,13},{9,12},{10,... | collective-permute-start | bytes 159752 | tf_op jit(solution)/shard_map/ppermute | solution.py:634
  8.8 3.9 %collective-permute-start.5 = (bf16[208,128]{1,0:T(8,128)(2,1)}, bf16[208,128]{1,0:T(8,128)(2,1)S(1)}, u32[]{:S(2)}, u32[]{:S(2)}) collective-permute-start(bf16[208,128]{1,0:T(8,128)(2,1)} %get-tuple-element.21), channel_id=1, source_target_pairs={{0,6},{1,7},{2,4},{3,5},{4,2},{5,3},{6,0},{7,1},{8,14},{9,15},{10,... | collective-permute-start | bytes 159752 | tf_op jit(solution)/shard_map/ppermute | solution.py:634
  13.4 2.9 %collective-permute-start.6 = (bf16[208,128]{1,0:T(8,128)(2,1)}, bf16[208,128]{1,0:T(8,128)(2,1)S(1)}, u32[]{:S(2)}, u32[]{:S(2)}) collective-permute-start(bf16[208,128]{1,0:T(8,128)(2,1)} %get-tuple-element.22), channel_id=1, source_target_pairs={{0,7},{1,6},{2,5},{3,4},{4,3},{5,2},{6,1},{7,0},{8,15},{9,14},{10,... | collective-permute-start | bytes 159752 | tf_op jit(solution)/shard_map/ppermute | solution.py:634
  16.4 4.3 %shard_map.113 = (bf16[2,576,256]{2,1,0:T(8,128)(2,1)}, bf16[256,384]{1,0:T(8,128)(2,1)}) custom-call(s32[7]{0:T(128)} %concatenate.3.meta_ref, bf16[256,768]{1,0:T(8,128)(2,1)} %table_ref.3, bf16[768,768]{1,0:T(8,128)(2,1)} %query_ref.3, bf16[768,768]{1,0:T(8,128)(2,1)} %key_ref.3, bf16[768,768]{1,0:T(8,128)(2,1)} %value_ref.3), custom_call_target="tpu_custom_call" | custom-call | flops 1000000000 | bytes 5000000 | tf_op jit(solution)/shard_map/pallas_call | solution.py:676
  21.5 1.1 %copy-done.6 = bf16[2,576,256]{2,1,0:T(8,128)(2,1)S(1)} copy-done((bf16[2,576,256]{2,1,0:T(8,128)(2,1)S(1)}, bf16[2,576,256]{2,1,0:T(8,128)(2,1)}, u32[]{:S(2)}) %copy-start.6) | copy-done | bytes 589848
  22.5 0.9 %shard_map.117 = bf16[8,128,384]{2,1,0:T(8,128)(2,1)} custom-call(bf16[128,768]{1,0:T(8,128)(2,1)S(1)} %bitcast.10, bf16[2,576,256]{2,1,0:T(8,128)(2,1)S(1)} %copy-done.6, bf16[208,128]{1,0:T(8,128)(2,1)S(1)} %collective-permute-done.rest_1_, bf16[208,128]{1,0:T(8,128)(2,1)S(1)} %collective-permute-done.1.rest_2_, ...), custom_call_target="tpu_custom_call" | custom-call | flops 100000000 | bytes 1000000 | tf_op jit(solution)/shard_map/pallas_call | solution.py:676
  23.5 4.4 %all-to-all-start.1 = ((bf16[8,128,384]{2,1,0:T(8,128)(2,1)}), bf16[8,128,384]{2,1,0:T(8,128)(2,1)S(1)}, u32[]{:S(2)}, u32[]{:S(2)}) async-start(bf16[8,128,384]{2,1,0:T(8,128)(2,1)} %shard_map.117), calls=%async_computation.1 | async-start | bytes 1572864 | tf_op jit(solution)/shard_map/all_to_all | solution.py:715
  28.0 10.9 %shard_map.115 = (bf16[4,576,128]{2,1,0:T(8,128)(2,1)}, bf16[2,576,128]{2,1,0:T(8,128)(2,1)S(1)}, bf16[192,1024]{1,0:T(8,128)(2,1)S(1)}) custom-call(s32[7]{0:T(128)S(1)} %copy-done.8, bf16[2,576,256]{2,1,0:T(8,128)(2,1)S(1)} %copy-done.7, f32[32,1024]{1,0:T(8,128)S(1)} %copy-done.13, f32[32,1024]{1,0:T(8,128)S(1)} %copy-done.12, ...), custom_call_target="tpu_custom_call" | custom-call | flops 8000000000 | bytes 8000000 | tf_op jit(solution)/shard_map/pallas_call | solution.py:676
  38.9 8.0 %all-to-all-done.1 = bf16[8,128,384]{2,1,0:T(8,128)(2,1)S(1)} async-done(((bf16[8,128,384]{2,1,0:T(8,128)(2,1)}), bf16[8,128,384]{2,1,0:T(8,128)(2,1)S(1)}, u32[]{:S(2)}, u32[]{:S(2)}) %all-to-all-start.1) | async-done | bytes 786464 | tf_op jit(solution)/shard_map/all_to_all | solution.py:715
  46.9 3.5 %all-to-all-start = ((bf16[4,576,128]{2,1,0:T(8,128)(2,1)}), bf16[4,576,128]{2,1,0:T(8,128)(2,1)S(1)}, u32[]{:S(2)}, u32[]{:S(2)}) async-start(bf16[4,576,128]{2,1,0:T(8,128)(2,1)} %get-tuple-element.23), calls=%async_computation | async-start | bytes 1179648 | tf_op jit(solution)/shard_map/all_to_all | solution.py:751
  51.4 1.5 %collective-permute-done.7 = bf16[864,128]{1,0:T(8,128)(2,1)S(1)} collective-permute-done((bf16[864,128]{1,0:T(8,128)(2,1)S(1)}, bf16[864,128]{1,0:T(8,128)(2,1)S(1)}, u32[]{:S(2)}, u32[]{:S(2)}) %collective-permute-start.7) | collective-permute-done | bytes 221216 | tf_op jit(solution)/shard_map/ppermute | solution.py:634
  53.6 1.5 %collective-permute-start.8 = (bf16[864,128]{1,0:T(8,128)(2,1)}, bf16[864,128]{1,0:T(8,128)(2,1)}, u32[]{:S(2)}, u32[]{:S(2)}) collective-permute-start(bf16[864,128]{1,0:T(8,128)(2,1)} %add.25.here_ref), channel_id=1, source_target_pairs={{0,16},{8,24},{16,0},{24,8},{1,17},{9,25},{17,1},{25,9},{2,18},{10... | collective-permute-start | bytes 663560 | tf_op jit(solution)/shard_map/ppermute | solution.py:634
  55.2 2.3 %all-to-all-done.rows_ref.after_ref = bf16[4,576,128]{2,1,0:T(8,128)(2,1)S(1)} async-done(((bf16[4,576,128]{2,1,0:T(8,128)(2,1)}), bf16[4,576,128]{2,1,0:T(8,128)(2,1)S(1)}, u32[]{:S(2)}, u32[]{:S(2)}) %all-to-all-start) | async-done | bytes 589856 | tf_op jit(solution)/shard_map/all_to_all | solution.py:751
  57.4 4.0 %collective-permute-done.8.there_ref = bf16[864,128]{1,0:T(8,128)(2,1)} collective-permute-done((bf16[864,128]{1,0:T(8,128)(2,1)}, bf16[864,128]{1,0:T(8,128)(2,1)}, u32[]{:S(2)}, u32[]{:S(2)}) %collective-permute-start.8) | collective-permute-done | bytes 221216 | tf_op jit(solution)/shard_map/ppermute | solution.py:634
  61.4 1.1 %shard_map.119 = (bf16[288,128]{1,0:T(8,128)(2,1)S(1)}, bf16[192,128]{1,0:T(8,128)(2,1)S(1)}, bf16[192,128]{1,0:T(8,128)(2,1)S(1)}, bf16[192,128]{1,0:T(8,128)(2,1)S(1)}, bf16[192,128]{1,0:T(8,128)(2,1)S(1)}) custom-call(s32[7]{0:T(128)S(1)} %copy-done.8, bf16[864,128]{1,0:T(8,128)(2,1)} %add.25.here_ref, bf16[864,128]{1,0:T(8,128)(2,1)} %collective-permute-done.8.there_ref, ...), custom_call_target="tpu_custom_call" | custom-call | flops 100000000 | bytes 1000000 | tf_op jit(solution)/shard_map/pallas_call | solution.py:676
  62.5 2.0 %collective-permute-start.9 = (bf16[192,128]{1,0:T(8,128)(2,1)S(1)}, bf16[192,128]{1,0:T(8,128)(2,1)S(1)}, u32[]{:S(2)}, u32[]{:S(2)}) collective-permute-start(bf16[192,128]{1,0:T(8,128)(2,1)S(1)} %get-tuple-element.30), channel_id=1, source_target_pairs={{0,1},{1,0},{2,3},{3,2},{4,5},{5,4},{6,7},{7,6},{8,9},{9,8},{10,11... | collective-permute-start | bytes 147464 | tf_op jit(solution)/shard_map/ppermute | solution.py:634
  65.9 4.7 %collective-permute-start.12 = (bf16[288,128]{1,0:T(8,128)(2,1)S(1)}, bf16[288,128]{1,0:T(8,128)(2,1)S(1)}, u32[]{:S(2)}, u32[]{:S(2)}) collective-permute-start(bf16[288,128]{1,0:T(8,128)(2,1)S(1)} %get-tuple-element.33.own_ref), channel_id=1, source_target_pairs={{0,6},{1,7},{8,14},{9,15},{16,22},{17,23},{24,30},{25,31}} | collective-permute-start | bytes 221192 | tf_op jit(solution)/shard_map/ppermute | solution.py:775
  70.7 2.0 %collective-permute-start.11 = (bf16[192,128]{1,0:T(8,128)(2,1)S(1)}, bf16[192,128]{1,0:T(8,128)(2,1)S(1)}, u32[]{:S(2)}, u32[]{:S(2)}) collective-permute-start(bf16[192,128]{1,0:T(8,128)(2,1)S(1)} %get-tuple-element.32), channel_id=1, source_target_pairs={{0,3},{1,2},{2,1},{3,0},{4,7},{5,6},{6,5},{7,4},{8,11},{9,10},{10,... | collective-permute-start | bytes 147464 | tf_op jit(solution)/shard_map/ppermute | solution.py:634
  72.7 1.3 %copy-done.2 = bf16[768,768]{1,0:T(8,128)(2,1)S(1)} copy-done((bf16[768,768]{1,0:T(8,128)(2,1)S(1)}, bf16[768,768]{1,0:T(8,128)(2,1)}, u32[]{:S(2)}) %copy-start.2) | copy-done | bytes 1179672
  74.0 1.9 %shard_map.116.after_ref = bf16[128,768]{1,0:T(8,128)(2,1)} custom-call(s32[1,128]{1,0:T(1,128)S(1)} %copy-done.9, bf16[256,768]{1,0:T(8,128)(2,1)S(1)} %copy-done.3, bf16[768,768]{1,0:T(8,128)(2,1)S(1)} %copy-done, bf16[768,768]{1,0:T(8,128)(2,1)S(1)} %copy-done.1, bf16[768,768]{1,0:T(8,128)(2,1)S(1)} %copy-done.2, ...), custom_call_target="tpu_custom_call" | custom-call | flops 1000000000 | bytes 5000000 | tf_op jit(solution)/shard_map/pallas_call | solution.py:676
  77.6 1.6 %collective-permute-done.15.other_ref = bf16[1152,128]{1,0:T(8,128)(2,1)S(1)} collective-permute-done((bf16[1152,128]{1,0:T(8,128)(2,1)S(1)}, bf16[1152,128]{1,0:T(8,128)(2,1)S(1)}, u32[]{:S(2)}, u32[]{:S(2)}) %collective-permute-start.15) | collective-permute-done | bytes 294944 | tf_op jit(solution)/shard_map/ppermute | solution.py:634
  79.1 2.1 %shard_map.121 = f32[384,768]{1,0:T(8,128)} custom-call(s32[7]{0:T(128)S(1)} %copy-done.8, bf16[256,384]{1,0:T(8,128)(2,1)S(1)} %copy-done.10, bf16[1152,128]{1,0:T(8,128)(2,1)S(1)} %shard_map.120.mine_ref, bf16[1152,128]{1,0:T(8,128)(2,1)S(1)} %collective-permute-done.15.other_ref), custom_call_target="tpu_custom_call" | custom-call | flops 1000000000 | bytes 5000000 | tf_op jit(solution)/shard_map/pallas_call | solution.py:676
  (54 shorter events, 6.7 us)
Async XLA Ops:
  0.6 12.0 %copy-start.14 = (s32[12]{0:T(128)S(1)}, s32[12]{0:T(128)}, u32[]{:S(2)}) copy-start(s32[12]{0:T(128)} %param.17) | copy-start | bytes 148
  3.2 10.2 %collective-permute-start.3 = (bf16[208,128]{1,0:T(8,128)(2,1)}, bf16[208,128]{1,0:T(8,128)(2,1)S(1)}, u32[]{:S(2)}, u32[]{:S(2)}) collective-permute-start(bf16[208,128]{1,0:T(8,128)(2,1)} %get-tuple-element.19.rest_0_), channel_id=1, source_target_pairs={{0,4},{1,5},{2,6},{3,7},{4,0},{5,1},{6,2},{7,3},{8,12},{9,13},{10,... | collective-permute-start | bytes 159752 | tf_op jit(solution)/shard_map/ppermute | solution.py:634
  7.3 9.0 %collective-permute-start.4 = (bf16[208,128]{1,0:T(8,128)(2,1)}, bf16[208,128]{1,0:T(8,128)(2,1)S(1)}, u32[]{:S(2)}, u32[]{:S(2)}) collective-permute-start(bf16[208,128]{1,0:T(8,128)(2,1)} %get-tuple-element.20), channel_id=1, source_target_pairs={{0,5},{1,4},{2,7},{3,6},{4,1},{5,0},{6,3},{7,2},{8,13},{9,12},{10,... | collective-permute-start | bytes 159752 | tf_op jit(solution)/shard_map/ppermute | solution.py:634
  8.5 12.2 %collective-permute-start = (bf16[208,128]{1,0:T(8,128)(2,1)}, bf16[208,128]{1,0:T(8,128)(2,1)S(1)}, u32[]{:S(2)}, u32[]{:S(2)}) collective-permute-start(bf16[208,128]{1,0:T(8,128)(2,1)} %get-tuple-element.20), channel_id=1, source_target_pairs={{0,1},{1,0},{2,3},{3,2},{4,5},{5,4},{6,7},{7,6},{8,9},{9,8},{10,11... | collective-permute-start | bytes 159752 | tf_op jit(solution)/shard_map/ppermute | solution.py:634
  8.8 11.9 %collective-permute-start.5 = (bf16[208,128]{1,0:T(8,128)(2,1)}, bf16[208,128]{1,0:T(8,128)(2,1)S(1)}, u32[]{:S(2)}, u32[]{:S(2)}) collective-permute-start(bf16[208,128]{1,0:T(8,128)(2,1)} %get-tuple-element.21), channel_id=1, source_target_pairs={{0,6},{1,7},{2,4},{3,5},{4,2},{5,3},{6,0},{7,1},{8,14},{9,15},{10,... | collective-permute-start | bytes 159752 | tf_op jit(solution)/shard_map/ppermute | solution.py:634
  12.7 8.0 %collective-permute-start.1 = (bf16[208,128]{1,0:T(8,128)(2,1)}, bf16[208,128]{1,0:T(8,128)(2,1)S(1)}, u32[]{:S(2)}, u32[]{:S(2)}) collective-permute-start(bf16[208,128]{1,0:T(8,128)(2,1)} %get-tuple-element.21), channel_id=1, source_target_pairs={{0,2},{1,3},{2,0},{3,1},{4,6},{5,7},{6,4},{7,5},{8,10},{9,11},{10,... | collective-permute-start | bytes 159752 | tf_op jit(solution)/shard_map/ppermute | solution.py:634
  13.4 8.1 %copy-start.5 = (bf16[1,128,768]{2,1,0:T(8,128)(2,1)S(1)}, bf16[1,128,768]{2,1,0:T(8,128)(2,1)}, u32[]{:S(2)}) copy-start(bf16[1,128,768]{2,1,0:T(8,128)(2,1)} %param.11) | copy-start | bytes 589828
  13.4 7.3 %collective-permute-start.6 = (bf16[208,128]{1,0:T(8,128)(2,1)}, bf16[208,128]{1,0:T(8,128)(2,1)S(1)}, u32[]{:S(2)}, u32[]{:S(2)}) collective-permute-start(bf16[208,128]{1,0:T(8,128)(2,1)} %get-tuple-element.22), channel_id=1, source_target_pairs={{0,7},{1,6},{2,5},{3,4},{4,3},{5,2},{6,1},{7,0},{8,15},{9,14},{10,... | collective-permute-start | bytes 159752 | tf_op jit(solution)/shard_map/ppermute | solution.py:634
  16.2 5.2 %collective-permute-start.2 = (bf16[208,128]{1,0:T(8,128)(2,1)}, bf16[208,128]{1,0:T(8,128)(2,1)S(1)}, u32[]{:S(2)}, u32[]{:S(2)}) collective-permute-start(bf16[208,128]{1,0:T(8,128)(2,1)} %get-tuple-element.22), channel_id=1, source_target_pairs={{0,3},{1,2},{2,1},{3,0},{4,7},{5,6},{6,5},{7,4},{8,11},{9,10},{10,... | collective-permute-start | bytes 159752 | tf_op jit(solution)/shard_map/ppermute | solution.py:634
  23.5 23.4 %all-to-all-start.1 = ((bf16[8,128,384]{2,1,0:T(8,128)(2,1)}), bf16[8,128,384]{2,1,0:T(8,128)(2,1)S(1)}, u32[]{:S(2)}, u32[]{:S(2)}) async-start(bf16[8,128,384]{2,1,0:T(8,128)(2,1)} %shard_map.117), calls=%async_computation.1 | async-start | bytes 1572864 | tf_op jit(solution)/shard_map/all_to_all | solution.py:715
  46.9 10.6 %all-to-all-start = ((bf16[4,576,128]{2,1,0:T(8,128)(2,1)}), bf16[4,576,128]{2,1,0:T(8,128)(2,1)S(1)}, u32[]{:S(2)}, u32[]{:S(2)}) async-start(bf16[4,576,128]{2,1,0:T(8,128)(2,1)} %get-tuple-element.23), calls=%async_computation | async-start | bytes 1179648 | tf_op jit(solution)/shard_map/all_to_all | solution.py:751
  50.4 22.3 %copy-start.1 = (bf16[768,768]{1,0:T(8,128)(2,1)S(1)}, bf16[768,768]{1,0:T(8,128)(2,1)}, u32[]{:S(2)}) copy-start(bf16[768,768]{1,0:T(8,128)(2,1)} %key_ref.3) | copy-start | bytes 3538948
  51.3 21.4 %copy-start = (bf16[768,768]{1,0:T(8,128)(2,1)S(1)}, bf16[768,768]{1,0:T(8,128)(2,1)}, u32[]{:S(2)}) copy-start(bf16[768,768]{1,0:T(8,128)(2,1)} %query_ref.3) | copy-start | bytes 3538948
  51.3 21.4 %copy-start.3 = (bf16[256,768]{1,0:T(8,128)(2,1)S(1)}, bf16[256,768]{1,0:T(8,128)(2,1)}, u32[]{:S(2)}) copy-start(bf16[256,768]{1,0:T(8,128)(2,1)} %table_ref.3) | copy-start | bytes 1179652
  51.3 21.4 %copy-start.9 = (s32[1,128]{1,0:T(1,128)S(1)}, s32[1,128]{1,0:T(1,128)}, u32[]{:S(2)}) copy-start(s32[1,128]{1,0:T(1,128)} %tokens_ref.3) | copy-start | bytes 1540
  51.3 1.5 %collective-permute-start.7 = (bf16[864,128]{1,0:T(8,128)(2,1)S(1)}, bf16[864,128]{1,0:T(8,128)(2,1)S(1)}, u32[]{:S(2)}, u32[]{:S(2)}) collective-permute-start(bf16[864,128]{1,0:T(8,128)(2,1)S(1)} %get-tuple-element.28), channel_id=1, source_target_pairs={{0,8},{8,0},{16,24},{24,16},{1,9},{9,1},{17,25},{25,17},{2,10},{10... | collective-permute-start | bytes 663560 | tf_op jit(solution)/shard_map/ppermute | solution.py:634
  53.6 7.8 %collective-permute-start.8 = (bf16[864,128]{1,0:T(8,128)(2,1)}, bf16[864,128]{1,0:T(8,128)(2,1)}, u32[]{:S(2)}, u32[]{:S(2)}) collective-permute-start(bf16[864,128]{1,0:T(8,128)(2,1)} %add.25.here_ref), channel_id=1, source_target_pairs={{0,16},{8,24},{16,0},{24,8},{1,17},{9,25},{17,1},{25,9},{2,18},{10... | collective-permute-start | bytes 663560 | tf_op jit(solution)/shard_map/ppermute | solution.py:634
  62.5 8.2 %collective-permute-start.9 = (bf16[192,128]{1,0:T(8,128)(2,1)S(1)}, bf16[192,128]{1,0:T(8,128)(2,1)S(1)}, u32[]{:S(2)}, u32[]{:S(2)}) collective-permute-start(bf16[192,128]{1,0:T(8,128)(2,1)S(1)} %get-tuple-element.30), channel_id=1, source_target_pairs={{0,1},{1,0},{2,3},{3,2},{4,5},{5,4},{6,7},{7,6},{8,9},{9,8},{10,11... | collective-permute-start | bytes 147464 | tf_op jit(solution)/shard_map/ppermute | solution.py:634
  64.6 11.4 %collective-permute-start.14 = (bf16[288,128]{1,0:T(8,128)(2,1)S(1)}, bf16[288,128]{1,0:T(8,128)(2,1)S(1)}, u32[]{:S(2)}, u32[]{:S(2)}) collective-permute-start(bf16[288,128]{1,0:T(8,128)(2,1)S(1)} %get-tuple-element.33.own_ref), channel_id=1, source_target_pairs={{4,6},{5,7},{12,14},{13,15},{20,22},{21,23},{28,30},{29,31}} | collective-permute-start | bytes 221192 | tf_op jit(solution)/shard_map/ppermute | solution.py:775
  65.2 10.7 %collective-permute-start.13 = (bf16[288,128]{1,0:T(8,128)(2,1)S(1)}, bf16[288,128]{1,0:T(8,128)(2,1)S(1)}, u32[]{:S(2)}, u32[]{:S(2)}) collective-permute-start(bf16[288,128]{1,0:T(8,128)(2,1)S(1)} %get-tuple-element.33.own_ref), channel_id=1, source_target_pairs={{2,6},{3,7},{10,14},{11,15},{18,22},{19,23},{26,30},{27,31}} | collective-permute-start | bytes 221192 | tf_op jit(solution)/shard_map/ppermute | solution.py:775
  65.9 10.1 %collective-permute-start.12 = (bf16[288,128]{1,0:T(8,128)(2,1)S(1)}, bf16[288,128]{1,0:T(8,128)(2,1)S(1)}, u32[]{:S(2)}, u32[]{:S(2)}) collective-permute-start(bf16[288,128]{1,0:T(8,128)(2,1)S(1)} %get-tuple-element.33.own_ref), channel_id=1, source_target_pairs={{0,6},{1,7},{8,14},{9,15},{16,22},{17,23},{24,30},{25,31}} | collective-permute-start | bytes 221192 | tf_op jit(solution)/shard_map/ppermute | solution.py:775
  70.6 5.3 %collective-permute-start.10 = (bf16[192,128]{1,0:T(8,128)(2,1)S(1)}, bf16[192,128]{1,0:T(8,128)(2,1)S(1)}, u32[]{:S(2)}, u32[]{:S(2)}) collective-permute-start(bf16[192,128]{1,0:T(8,128)(2,1)S(1)} %get-tuple-element.31), channel_id=1, source_target_pairs={{0,2},{1,3},{2,0},{3,1},{4,6},{5,7},{6,4},{7,5},{8,10},{9,11},{10,... | collective-permute-start | bytes 147464 | tf_op jit(solution)/shard_map/ppermute | solution.py:634
  70.7 5.2 %collective-permute-start.11 = (bf16[192,128]{1,0:T(8,128)(2,1)S(1)}, bf16[192,128]{1,0:T(8,128)(2,1)S(1)}, u32[]{:S(2)}, u32[]{:S(2)}) collective-permute-start(bf16[192,128]{1,0:T(8,128)(2,1)S(1)} %get-tuple-element.32), channel_id=1, source_target_pairs={{0,3},{1,2},{2,1},{3,0},{4,7},{5,6},{6,5},{7,4},{8,11},{9,10},{10,... | collective-permute-start | bytes 147464 | tf_op jit(solution)/shard_map/ppermute | solution.py:634
  77.5 1.6 %collective-permute-start.15 = (bf16[1152,128]{1,0:T(8,128)(2,1)S(1)}, bf16[1152,128]{1,0:T(8,128)(2,1)S(1)}, u32[]{:S(2)}, u32[]{:S(2)}) collective-permute-start(bf16[1152,128]{1,0:T(8,128)(2,1)S(1)} %shard_map.120.mine_ref), channel_id=1, source_target_pairs={{0,8},{8,0},{16,24},{24,16},{1,9},{9,1},{17,25},{25,17},{2,10},{10... | collective-permute-start | bytes 884744 | tf_op jit(solution)/shard_map/ppermute | solution.py:634
  (9 other events, 30.7 us)

commit v13 on v12

--- a/solution.py
+++ b/solution.py
@@ -318,7 +318,8 @@
     sine_ref,
     early_refs,
     rows_ref,
-    sums_ref,
+    keep_ref,
+    give_ref,
     attended_ref,
     value_key_ref,
     query_t_ref,
@@ -511,9 +512,11 @@
         place = pl.ds(
             pl.multiple_of(matrix * GROUP_COLS + head * HEAD_DIM, HEAD_DIM), HEAD_DIM
         )
-        for core in range(2):
-            lane = core * half_vocab
-            sums_ref[core, place, :] = sums[rows, lane : lane + half_vocab]
+        low = sums[rows, :half_vocab]
+        high = sums[rows, half_vocab:]
+        first = meta_ref[GROUP_HEADS + 2] == 0
+        keep_ref[place, :] = jnp.where(first, low, high)
+        give_ref[place, :] = jnp.where(first, high, low)
         for target in range(GROUPS):
             start = target * block
             near = grads[rows, start : start + block]
@@ -521,29 +524,26 @@
             rows_ref[target, place, :] = jnp.where(meta_ref[GROUP_HEADS + 1] < 2, near, far)
 
 
-def out_kernel(meta_ref, attended_ref, cotangent_ref, sums_ref, keep_ref, give_ref):
+def out_kernel(meta_ref, attended_ref, cotangent_ref, after_ref, keep_ref, give_ref):
+    del after_ref
     total = jnp.dot(attended_ref[...], cotangent_ref[...], preferred_element_type=jnp.float32)
     rows = total.shape[0] // 2
-    base = sums_ref.shape[1]
     lanes = keep_ref.shape[1]
     first = meta_ref[GROUP_HEADS + 2] == 0
-    keep_ref[:base, :] = jnp.where(first, sums_ref[0], sums_ref[1])
-    give_ref[:base, :] = jnp.where(first, sums_ref[1], sums_ref[0])
     for chunk in range(total.shape[1] // lanes):
         part = total[:, chunk * lanes : (chunk + 1) * lanes]
-        place = slice(base + chunk * rows, base + (chunk + 1) * rows)
+        place = slice(chunk * rows, (chunk + 1) * rows)
         keep_ref[place, :] = jnp.where(first, part[:rows], part[rows:]).astype(jnp.bfloat16)
         give_ref[place, :] = jnp.where(first, part[rows:], part[:rows]).astype(jnp.bfloat16)
 
 
-def combine_kernel(meta_ref, here_ref, there_ref, after_ref, out_ref, *piece_refs):
-    del after_ref
+def combine_kernel(meta_ref, here_ref, there_ref, rows_ref, *rest):
+    del rows_ref
     rows = GROUP_COLS
-    for turn, piece_ref in enumerate(piece_refs):
+    for turn, piece_ref in enumerate(rest[:GROUPS]):
         target = jnp.minimum(meta_ref[GROUP_HEADS + 1] ^ (turn // 2), 2)
         place = pl.ds(pl.multiple_of(target * rows, rows), rows)
         piece_ref[...] = here_ref[place, :] + there_ref[place, :]
-    out_ref[...] = here_ref[3 * rows :, :] + there_ref[3 * rows :, :]
 
 
 def gather_kernel(meta_ref, s0, s1, s2, s3, own_ref, o0, o1, o2, after_ref, mine_ref):
@@ -666,18 +666,24 @@
     cosine, sine_part = rope_table(length)
 
     def call(
-        body, operands, outs, scratch=(), steps=1, flops=10**8, moved=10**6, loose=0, grant=VMEM_BYTES
+        body, operands, outs, scratch=(), steps=1, flops=10**8, moved=10**6, loose=0, passed=False, grant=VMEM_BYTES
     ):
         spaces = [whole(operand.shape) for operand in operands]
         for index in range(loose):
             spaces[-1 - index] = pl.BlockSpec(memory_space=pl.ANY)
         if operands[0].ndim == 1:
             spaces[0] = pl.BlockSpec(memory_space=pltpu.SMEM)
+        results = [whole(shape) for shape, _ in outs]
+        aliases = {}
+        if passed:
+            results[-1] = pl.BlockSpec(memory_space=pl.ANY)
+            aliases = {len(operands) - 1: len(outs) - 1}
         return pl.pallas_call(
             body,
             grid=(steps,),
             in_specs=spaces,
-            out_specs=[whole(shape) for shape, _ in outs],
+            out_specs=results,
+            input_output_aliases=aliases,
             out_shape=[jax.ShapeDtypeStruct(shape, dtype) for shape, dtype in outs],
             scratch_shapes=list(scratch),
             compiler_params=pltpu.CompilerParams(
@@ -715,12 +721,12 @@
     late = lax.all_to_all(late, "seq", split_axis=0, concat_axis=0, tiled=True)
     heads_shape = (GROUP_HEADS, HEAD_DIM, length)
     rows_shape = (GROUP_HEADS, length, 2 * HEAD_DIM)
-    rows, sums, attended = call(
+    rows, keep, give, attended = call(
         attention_kernel,
         (meta, lookup, cosine, sine_part, *early),
         [
             ((GROUPS, 3 * GROUP_COLS, block), half),
-            ((2, 3 * GROUP_COLS, vocab // 2), half),
+            *[((3 * GROUP_COLS, vocab // 2), half)] * 2,
             ((GROUP_COLS, length), half),
         ],
         [
@@ -752,23 +758,26 @@
             chunks, "seq", split_axis=0, concat_axis=0, axis_index_groups=planes, tiled=True
         )
 
-    got_rows = over_plane(rows)
     lanes = vocab // 2
     out_rows = 3 * GROUP_COLS // 2
-    packed = 3 * GROUP_COLS + out_rows
+    here = keep + swapped(give, "dp", 1)
+    there = swapped(here, "dp", 2)
+    *pieces, rows = call(
+        combine_kernel,
+        (meta, here, there, rows),
+        [((GROUP_COLS, lanes), half)] * GROUPS + [(rows.shape, half)],
+        loose=1,
+        passed=True,
+    )
+    got_rows = over_plane(rows)
     keep, give = call(
         out_kernel,
-        (meta, attended, late.reshape(length, features // 2), sums),
-        [((packed, lanes), half)] * 2,
+        (meta, attended, late.reshape(length, features // 2), pieces[0]),
+        [((out_rows, lanes), half)] * 2,
+        loose=1,
     )
     here = keep + swapped(give, "dp", 1)
-    there = swapped(here, "dp", 2)
-    kept_out, *pieces = call(
-        combine_kernel,
-        (meta, here, there, got_rows),
-        [((out_rows, lanes), half)] + [((GROUP_COLS, lanes), half)] * GROUPS,
-        loose=1,
-    )
+    kept_out = here + swapped(here, "dp", 2)
     last = blocks - 2
     got = [pieces[0]] + [swapped(pieces[turn], "seq", turn) for turn in (1, 2, 3)]
     got_out = [

time: 81.7 us -> 86.3 us (1.056)
  waiting for transfers between devices: 18 us -> 8.93 us
  local copies, waits for them, and re-layouts: 4.01 us -> 11.5 us
  starting transfers between devices: 32.2 us -> 37.9 us
    all_to_all x1, waiting for transfers between devices: 7.95 us -> 0.01 us  [grouped_device(): late = lax.all_to_all(late, 'seq', split_axis=0, concat_axis=0, tiled=True)]
    unnamed x30 -> x56, local copies, waits for them, and re-layouts: 3.31 us -> 10.7 us
    ppermute x3, starting transfers between devices: 6.01 us -> 9.38 us  [grouped_device(): lax.ppermute(kept_out, 'seq', [(2 * z, last), (2 * z + 1, last + 1)])]
    all_to_all x1, waiting for transfers between devices: 2.27 us -> 0.01 us  [over_plane(): lax.all_to_all(chunks, 'seq', split_axis=0, concat_axis=0, axis_index_gro...]
    ppermute x13 -> x15, waiting for transfers between devices: 7.8 us -> 8.91 us  [swapped(): return lax.ppermute(block, axis, route)]
    ppermute x13 -> x15, starting transfers between devices: 18.2 us -> 19.3 us  [swapped(): return lax.ppermute(block, axis, route)]
  transfers between devices with their start and end apart: 18 -> 20, of which waited for: 6 -> 5; matrix products, arithmetic and copies ran while one was open for 2% -> 2% of each run, Pallas kernels for 22% -> 22%
where the time goes in v13:
time: 86.3 us; the launch traced here: 85.7 us
  starting transfers between devices  37.9 us (44%)
  Pallas kernels  25.7 us (30%)
  local copies, waits for them, and re-layouts  11.5 us (13%)
  waiting for transfers between devices  8.93 us (10%)
  between operations  0.92 us (1%)
    pallas_call x9, Pallas kernels, call(): pl.pallas_call(body, grid=(steps,), in_specs=spaces, out_specs=results, i...  25.7 us
    ppermute x15, starting transfers between devices, swapped(): return lax.ppermute(block, axis, route)  19.3 us
    unnamed x56, local copies, waits for them, and re-layouts  10.7 us
    ppermute x3, starting transfers between devices, grouped_device(): lax.ppermute(kept_out, 'seq', [(2 * z, last), (2 * z + 1, last + 1)])  9.38 us
    ppermute x15, waiting for transfers between devices, swapped(): return lax.ppermute(block, axis, route)  8.91 us
    all_to_all x1, starting transfers between devices, grouped_device(): late = lax.all_to_all(late, 'seq', split_axis=0, concat_axis=0, tiled=True)  4.86 us
    all_to_all x1, starting transfers between devices, over_plane(): lax.all_to_all(chunks, 'seq', split_axis=0, concat_axis=0, axis_index_gro...  4.31 us
  transfers between devices with their start and end apart: 20, of which 5 were waited for; matrix products, arithmetic and copies ran while one was open for 2% of the time, Pallas kernels for 22%

profile of v13, /device:TPU:0, one launch (start us, length us, event | category | flops | bytes accessed | tf_op | source)
XLA Modules:
  0.0 85.7 jit_solution(15924759443691361997)
XLA Ops:
  0.7 2.5 %shard_map.114 = (bf16[208,128]{1,0:T(8,128)(2,1)}, bf16[208,128]{1,0:T(8,128)(2,1)}, bf16[208,128]{1,0:T(8,128)(2,1)}, bf16[208,128]{1,0:T(8,128)(2,1)}) custom-call(s32[1]{0:T(128)} %bitcast.3.spot_ref, s32[1,128]{1,0:T(1,128)} %tokens_ref.3, bf16[128,768]{1,0:T(8,128)(2,1)} %bitcast.9, bf16[768,768]{1,0:T(8,128)(2,1)} %out_weights_ref.1), custom_call_target="tpu_custom_call" | custom-call | flops 100000000 | bytes 1000000 | tf_op jit(solution)/shard_map/pallas_call | solution.py:681
  3.2 2.9 %collective-permute-start = (bf16[208,128]{1,0:T(8,128)(2,1)}, bf16[208,128]{1,0:T(8,128)(2,1)S(1)}, u32[]{:S(2)}, u32[]{:S(2)}) collective-permute-start(bf16[208,128]{1,0:T(8,128)(2,1)} %get-tuple-element.21), channel_id=1, source_target_pairs={{0,1},{1,0},{2,3},{3,2},{4,5},{5,4},{6,7},{7,6},{8,9},{9,8},{10,11... | collective-permute-start | bytes 159752 | tf_op jit(solution)/shard_map/ppermute | solution.py:634
  6.2 1.6 %collective-permute-start.1 = (bf16[208,128]{1,0:T(8,128)(2,1)}, bf16[208,128]{1,0:T(8,128)(2,1)S(1)}, u32[]{:S(2)}, u32[]{:S(2)}) collective-permute-start(bf16[208,128]{1,0:T(8,128)(2,1)} %get-tuple-element.22), channel_id=1, source_target_pairs={{0,2},{1,3},{2,0},{3,1},{4,6},{5,7},{6,4},{7,5},{8,10},{9,11},{10,... | collective-permute-start | bytes 159752 | tf_op jit(solution)/shard_map/ppermute | solution.py:634
  7.7 2.6 %collective-permute-start.4 = (bf16[208,128]{1,0:T(8,128)(2,1)}, bf16[208,128]{1,0:T(8,128)(2,1)S(1)}, u32[]{:S(2)}, u32[]{:S(2)}) collective-permute-start(bf16[208,128]{1,0:T(8,128)(2,1)} %get-tuple-element.21), channel_id=1, source_target_pairs={{0,5},{1,4},{2,7},{3,6},{4,1},{5,0},{6,3},{7,2},{8,13},{9,12},{10,... | collective-permute-start | bytes 159752 | tf_op jit(solution)/shard_map/ppermute | solution.py:634
  10.3 1.8 %collective-permute-start.2 = (bf16[208,128]{1,0:T(8,128)(2,1)}, bf16[208,128]{1,0:T(8,128)(2,1)S(1)}, u32[]{:S(2)}, u32[]{:S(2)}) collective-permute-start(bf16[208,128]{1,0:T(8,128)(2,1)} %get-tuple-element.23), channel_id=1, source_target_pairs={{0,3},{1,2},{2,1},{3,0},{4,7},{5,6},{6,5},{7,4},{8,11},{9,10},{10,... | collective-permute-start | bytes 159752 | tf_op jit(solution)/shard_map/ppermute | solution.py:634
  12.9 2.9 %collective-permute-start.6 = (bf16[208,128]{1,0:T(8,128)(2,1)}, bf16[208,128]{1,0:T(8,128)(2,1)S(1)}, u32[]{:S(2)}, u32[]{:S(2)}) collective-permute-start(bf16[208,128]{1,0:T(8,128)(2,1)} %get-tuple-element.23), channel_id=1, source_target_pairs={{0,7},{1,6},{2,5},{3,4},{4,3},{5,2},{6,1},{7,0},{8,15},{9,14},{10,... | collective-permute-start | bytes 159752 | tf_op jit(solution)/shard_map/ppermute | solution.py:634
  16.5 4.3 %shard_map.113 = (bf16[2,576,256]{2,1,0:T(8,128)(2,1)}, bf16[256,384]{1,0:T(8,128)(2,1)}) custom-call(s32[7]{0:T(128)} %concatenate.3.meta_ref, bf16[256,768]{1,0:T(8,128)(2,1)} %table_ref.3, bf16[768,768]{1,0:T(8,128)(2,1)} %query_ref.3, bf16[768,768]{1,0:T(8,128)(2,1)} %key_ref.3, bf16[768,768]{1,0:T(8,128)(2,1)} %value_ref.3), custom_call_target="tpu_custom_call" | custom-call | flops 1000000000 | bytes 5000000 | tf_op jit(solution)/shard_map/pallas_call | solution.py:681
  23.1 4.9 %all-to-all-start.1 = ((bf16[8,128,384]{2,1,0:T(8,128)(2,1)}), bf16[8,128,384]{2,1,0:T(8,128)(2,1)S(1)}, u32[]{:S(2)}, u32[]{:S(2)}) async-start(bf16[8,128,384]{2,1,0:T(8,128)(2,1)} %shard_map.118), calls=%async_computation.1 | async-start | bytes 1572864 | tf_op jit(solution)/shard_map/all_to_all | solution.py:721
  28.0 10.3 %shard_map.115 = (bf16[4,576,128]{2,1,0:T(8,128)(2,1)S(1)}, bf16[576,128]{1,0:T(8,128)(2,1)S(1)}, bf16[576,128]{1,0:T(8,128)(2,1)S(1)}, bf16[192,1024]{1,0:T(8,128)(2,1)S(1)}) custom-call(s32[7]{0:T(128)S(1)} %copy-done.18, bf16[2,576,256]{2,1,0:T(8,128)(2,1)S(1)} %copy-done.10, f32[32,1024]{1,0:T(8,128)S(1)} %copy-done.25, f32[32,1024]{1,0:T(8,128)S(1)} %copy-done.26, ...), custom_call_target="tpu_custom_call" | custom-call | flops 8000000000 | bytes 8000000 | tf_op jit(solution)/shard_map/pallas_call | solution.py:681
  38.4 1.4 %collective-permute-done.7 = bf16[576,128]{1,0:T(8,128)(2,1)S(1)} collective-permute-done((bf16[576,128]{1,0:T(8,128)(2,1)S(1)}, bf16[576,128]{1,0:T(8,128)(2,1)S(1)}, u32[]{:S(2)}, u32[]{:S(2)}) %collective-permute-start.7) | collective-permute-done | bytes 147488 | tf_op jit(solution)/shard_map/ppermute | solution.py:634
  39.8 1.6 %collective-permute-start.8 = (bf16[576,128]{1,0:T(8,128)(2,1)S(1)}, bf16[576,128]{1,0:T(8,128)(2,1)S(1)}, u32[]{:S(2)}, u32[]{:S(2)}) collective-permute-start(bf16[576,128]{1,0:T(8,128)(2,1)S(1)} %add.31.here_ref), channel_id=1, source_target_pairs={{0,16},{8,24},{16,0},{24,8},{1,17},{9,25},{17,1},{25,9},{2,18},{10... | collective-permute-start | bytes 442376 | tf_op jit(solution)/shard_map/ppermute | solution.py:634
  41.4 4.4 %collective-permute-done.8.there_ref = bf16[576,128]{1,0:T(8,128)(2,1)S(1)} collective-permute-done((bf16[576,128]{1,0:T(8,128)(2,1)S(1)}, bf16[576,128]{1,0:T(8,128)(2,1)S(1)}, u32[]{:S(2)}, u32[]{:S(2)}) %collective-permute-start.8) | collective-permute-done | bytes 147488 | tf_op jit(solution)/shard_map/ppermute | solution.py:634
  50.5 4.3 %all-to-all-start = ((bf16[4,576,128]{2,1,0:T(8,128)(2,1)}), bf16[4,576,128]{2,1,0:T(8,128)(2,1)}, u32[]{:S(2)}, u32[]{:S(2)}) async-start(bf16[4,576,128]{2,1,0:T(8,128)(2,1)} %copy-done.5), calls=%async_computation | async-start | bytes 1179648 | tf_op jit(solution)/shard_map/all_to_all | solution.py:757
  54.8 1.1 %copy-done.4 = bf16[8,128,384]{2,1,0:T(8,128)(2,1)S(1)} copy-done((bf16[8,128,384]{2,1,0:T(8,128)(2,1)S(1)}, bf16[8,128,384]{2,1,0:T(8,128)(2,1)}, u32[]{:S(2)}) %copy-start.4) | copy-done | bytes 786456
  58.8 1.3 %collective-permute-done.12 = bf16[288,128]{1,0:T(8,128)(2,1)S(1)} collective-permute-done((bf16[288,128]{1,0:T(8,128)(2,1)S(1)}, bf16[288,128]{1,0:T(8,128)(2,1)S(1)}, u32[]{:S(2)}, u32[]{:S(2)}) %collective-permute-start.12) | collective-permute-done | bytes 73760 | tf_op jit(solution)/shard_map/ppermute | solution.py:634
  60.0 1.6 %collective-permute-start.13 = (bf16[288,128]{1,0:T(8,128)(2,1)S(1)}, bf16[288,128]{1,0:T(8,128)(2,1)S(1)}, u32[]{:S(2)}, u32[]{:S(2)}) collective-permute-start(bf16[288,128]{1,0:T(8,128)(2,1)S(1)} %add.32), channel_id=1, source_target_pairs={{0,16},{8,24},{16,0},{24,8},{1,17},{9,25},{17,1},{25,9},{2,18},{10... | collective-permute-start | bytes 221192 | tf_op jit(solution)/shard_map/ppermute | solution.py:634
  61.6 2.0 %collective-permute-start.10 = (bf16[192,128]{1,0:T(8,128)(2,1)}, bf16[192,128]{1,0:T(8,128)(2,1)S(1)}, u32[]{:S(2)}, u32[]{:S(2)}) collective-permute-start(bf16[192,128]{1,0:T(8,128)(2,1)} %copy-done.24), channel_id=1, source_target_pairs={{0,2},{1,3},{2,0},{3,1},{4,6},{5,7},{6,4},{7,5},{8,10},{9,11},{10,... | collective-permute-start | bytes 147464 | tf_op jit(solution)/shard_map/ppermute | solution.py:634
  63.6 1.5 %collective-permute-start.11 = (bf16[192,128]{1,0:T(8,128)(2,1)}, bf16[192,128]{1,0:T(8,128)(2,1)}, u32[]{:S(2)}, u32[]{:S(2)}) collective-permute-start(bf16[192,128]{1,0:T(8,128)(2,1)} %copy-done.23), channel_id=1, source_target_pairs={{0,3},{1,2},{2,1},{3,0},{4,7},{5,6},{6,5},{7,4},{8,11},{9,10},{10,... | collective-permute-start | bytes 147464 | tf_op jit(solution)/shard_map/ppermute | solution.py:634
  65.8 6.8 %collective-permute-start.14 = (bf16[288,128]{1,0:T(8,128)(2,1)}, bf16[288,128]{1,0:T(8,128)(2,1)}, u32[]{:S(2)}, u32[]{:S(2)}) collective-permute-start(bf16[288,128]{1,0:T(8,128)(2,1)} %add.33.own_ref), channel_id=1, source_target_pairs={{0,6},{1,7},{8,14},{9,15},{16,22},{17,23},{24,30},{25,31}} | collective-permute-start | bytes 221192 | tf_op jit(solution)/shard_map/ppermute | solution.py:784
  72.6 1.3 %collective-permute-start.15 = (bf16[288,128]{1,0:T(8,128)(2,1)}, bf16[288,128]{1,0:T(8,128)(2,1)}, u32[]{:S(2)}, u32[]{:S(2)}) collective-permute-start(bf16[288,128]{1,0:T(8,128)(2,1)} %add.33.own_ref), channel_id=1, source_target_pairs={{2,6},{3,7},{10,14},{11,15},{18,22},{19,23},{26,30},{27,31}} | collective-permute-start | bytes 221192 | tf_op jit(solution)/shard_map/ppermute | solution.py:784
  74.5 1.3 %collective-permute-start.16 = (bf16[288,128]{1,0:T(8,128)(2,1)}, bf16[288,128]{1,0:T(8,128)(2,1)}, u32[]{:S(2)}, u32[]{:S(2)}) collective-permute-start(bf16[288,128]{1,0:T(8,128)(2,1)} %add.33.own_ref), channel_id=1, source_target_pairs={{4,6},{5,7},{12,14},{13,15},{20,22},{21,23},{28,30},{29,31}} | collective-permute-start | bytes 221192 | tf_op jit(solution)/shard_map/ppermute | solution.py:784
  76.8 3.1 %shard_map.117.after_ref = bf16[128,768]{1,0:T(8,128)(2,1)} custom-call(s32[1,128]{1,0:T(1,128)S(1)} %copy-done.19, bf16[256,768]{1,0:T(8,128)(2,1)S(1)} %copy-done.6, bf16[768,768]{1,0:T(8,128)(2,1)S(1)} %copy-done, bf16[768,768]{1,0:T(8,128)(2,1)S(1)} %copy-done.1, bf16[768,768]{1,0:T(8,128)(2,1)S(1)} %copy-done.2, bf16[4,576,128]{2,1,0:T(8,128)(2,1)} %all-to-all-done.rows_ref), custom_call_target="tpu_custom_call" | custom-call | flops 1000000000 | bytes 5000000 | tf_op jit(solution)/shard_map/pallas_call | solution.py:681
  82.0 1.6 %collective-permute-done.17.other_ref = bf16[1152,128]{1,0:T(8,128)(2,1)S(1)} collective-permute-done((bf16[1152,128]{1,0:T(8,128)(2,1)S(1)}, bf16[1152,128]{1,0:T(8,128)(2,1)S(1)}, u32[]{:S(2)}, u32[]{:S(2)}) %collective-permute-start.17) | collective-permute-done | bytes 294944 | tf_op jit(solution)/shard_map/ppermute | solution.py:634
  83.6 2.1 %shard_map.121 = f32[384,768]{1,0:T(8,128)} custom-call(s32[7]{0:T(128)S(1)} %copy-done.18, bf16[256,384]{1,0:T(8,128)(2,1)S(1)} %copy-done.20, bf16[1152,128]{1,0:T(8,128)(2,1)S(1)} %shard_map.120.mine_ref, bf16[1152,128]{1,0:T(8,128)(2,1)S(1)} %collective-permute-done.17.other_ref), custom_call_target="tpu_custom_call" | custom-call | flops 1000000000 | bytes 5000000 | tf_op jit(solution)/shard_map/pallas_call | solution.py:681
  (86 shorter events, 15.8 us)
Async XLA Ops:
  3.2 9.7 %collective-permute-start = (bf16[208,128]{1,0:T(8,128)(2,1)}, bf16[208,128]{1,0:T(8,128)(2,1)S(1)}, u32[]{:S(2)}, u32[]{:S(2)}) collective-permute-start(bf16[208,128]{1,0:T(8,128)(2,1)} %get-tuple-element.21), channel_id=1, source_target_pairs={{0,1},{1,0},{2,3},{3,2},{4,5},{5,4},{6,7},{7,6},{8,9},{9,8},{10,11... | collective-permute-start | bytes 159752 | tf_op jit(solution)/shard_map/ppermute | solution.py:634
  6.2 9.6 %collective-permute-start.1 = (bf16[208,128]{1,0:T(8,128)(2,1)}, bf16[208,128]{1,0:T(8,128)(2,1)S(1)}, u32[]{:S(2)}, u32[]{:S(2)}) collective-permute-start(bf16[208,128]{1,0:T(8,128)(2,1)} %get-tuple-element.22), channel_id=1, source_target_pairs={{0,2},{1,3},{2,0},{3,1},{4,6},{5,7},{6,4},{7,5},{8,10},{9,11},{10,... | collective-permute-start | bytes 159752 | tf_op jit(solution)/shard_map/ppermute | solution.py:634
  7.7 13.3 %collective-permute-start.4 = (bf16[208,128]{1,0:T(8,128)(2,1)}, bf16[208,128]{1,0:T(8,128)(2,1)S(1)}, u32[]{:S(2)}, u32[]{:S(2)}) collective-permute-start(bf16[208,128]{1,0:T(8,128)(2,1)} %get-tuple-element.21), channel_id=1, source_target_pairs={{0,5},{1,4},{2,7},{3,6},{4,1},{5,0},{6,3},{7,2},{8,13},{9,12},{10,... | collective-permute-start | bytes 159752 | tf_op jit(solution)/shard_map/ppermute | solution.py:634
  10.3 10.8 %collective-permute-start.5 = (bf16[208,128]{1,0:T(8,128)(2,1)}, bf16[208,128]{1,0:T(8,128)(2,1)S(1)}, u32[]{:S(2)}, u32[]{:S(2)}) collective-permute-start(bf16[208,128]{1,0:T(8,128)(2,1)} %get-tuple-element.22), channel_id=1, source_target_pairs={{0,6},{1,7},{2,4},{3,5},{4,2},{5,3},{6,0},{7,1},{8,14},{9,15},{10,... | collective-permute-start | bytes 159752 | tf_op jit(solution)/shard_map/ppermute | solution.py:634
  10.3 10.4 %collective-permute-start.2 = (bf16[208,128]{1,0:T(8,128)(2,1)}, bf16[208,128]{1,0:T(8,128)(2,1)S(1)}, u32[]{:S(2)}, u32[]{:S(2)}) collective-permute-start(bf16[208,128]{1,0:T(8,128)(2,1)} %get-tuple-element.23), channel_id=1, source_target_pairs={{0,3},{1,2},{2,1},{3,0},{4,7},{5,6},{6,5},{7,4},{8,11},{9,10},{10,... | collective-permute-start | bytes 159752 | tf_op jit(solution)/shard_map/ppermute | solution.py:634
  12.9 8.2 %collective-permute-start.6 = (bf16[208,128]{1,0:T(8,128)(2,1)}, bf16[208,128]{1,0:T(8,128)(2,1)S(1)}, u32[]{:S(2)}, u32[]{:S(2)}) collective-permute-start(bf16[208,128]{1,0:T(8,128)(2,1)} %get-tuple-element.23), channel_id=1, source_target_pairs={{0,7},{1,6},{2,5},{3,4},{4,3},{5,2},{6,1},{7,0},{8,15},{9,14},{10,... | collective-permute-start | bytes 159752 | tf_op jit(solution)/shard_map/ppermute | solution.py:634
  15.8 5.3 %collective-permute-start.3 = (bf16[208,128]{1,0:T(8,128)(2,1)}, bf16[208,128]{1,0:T(8,128)(2,1)S(1)}, u32[]{:S(2)}, u32[]{:S(2)}) collective-permute-start(bf16[208,128]{1,0:T(8,128)(2,1)} %get-tuple-element.20.rest_0_), channel_id=1, source_target_pairs={{0,4},{1,5},{2,6},{3,7},{4,0},{5,1},{6,2},{7,3},{8,12},{9,13},{10,... | collective-permute-start | bytes 159752 | tf_op jit(solution)/shard_map/ppermute | solution.py:634
  23.1 26.5 %all-to-all-start.1 = ((bf16[8,128,384]{2,1,0:T(8,128)(2,1)}), bf16[8,128,384]{2,1,0:T(8,128)(2,1)S(1)}, u32[]{:S(2)}, u32[]{:S(2)}) async-start(bf16[8,128,384]{2,1,0:T(8,128)(2,1)} %shard_map.118), calls=%async_computation.1 | async-start | bytes 1572864 | tf_op jit(solution)/shard_map/all_to_all | solution.py:721
  38.3 1.4 %collective-permute-start.7 = (bf16[576,128]{1,0:T(8,128)(2,1)S(1)}, bf16[576,128]{1,0:T(8,128)(2,1)S(1)}, u32[]{:S(2)}, u32[]{:S(2)}) collective-permute-start(bf16[576,128]{1,0:T(8,128)(2,1)S(1)} %get-tuple-element.25), channel_id=1, source_target_pairs={{0,8},{8,0},{16,24},{24,16},{1,9},{9,1},{17,25},{25,17},{2,10},{10... | collective-permute-start | bytes 442376 | tf_op jit(solution)/shard_map/ppermute | solution.py:634
  39.8 6.0 %collective-permute-start.8 = (bf16[576,128]{1,0:T(8,128)(2,1)S(1)}, bf16[576,128]{1,0:T(8,128)(2,1)S(1)}, u32[]{:S(2)}, u32[]{:S(2)}) collective-permute-start(bf16[576,128]{1,0:T(8,128)(2,1)S(1)} %add.31.here_ref), channel_id=1, source_target_pairs={{0,16},{8,24},{16,0},{24,8},{1,17},{9,25},{17,1},{25,9},{2,18},{10... | collective-permute-start | bytes 442376 | tf_op jit(solution)/shard_map/ppermute | solution.py:634
  45.8 30.0 %copy-start.2 = (bf16[768,768]{1,0:T(8,128)(2,1)S(1)}, bf16[768,768]{1,0:T(8,128)(2,1)}, u32[]{:S(2)}) copy-start(bf16[768,768]{1,0:T(8,128)(2,1)} %value_ref.3) | copy-start | bytes 3538948
  50.5 25.3 %copy-start = (bf16[768,768]{1,0:T(8,128)(2,1)S(1)}, bf16[768,768]{1,0:T(8,128)(2,1)}, u32[]{:S(2)}) copy-start(bf16[768,768]{1,0:T(8,128)(2,1)} %query_ref.3) | copy-start | bytes 3538948
  50.5 25.3 %copy-start.1 = (bf16[768,768]{1,0:T(8,128)(2,1)S(1)}, bf16[768,768]{1,0:T(8,128)(2,1)}, u32[]{:S(2)}) copy-start(bf16[768,768]{1,0:T(8,128)(2,1)} %key_ref.3) | copy-start | bytes 3538948
  50.5 25.3 %all-to-all-start = ((bf16[4,576,128]{2,1,0:T(8,128)(2,1)}), bf16[4,576,128]{2,1,0:T(8,128)(2,1)}, u32[]{:S(2)}, u32[]{:S(2)}) async-start(bf16[4,576,128]{2,1,0:T(8,128)(2,1)} %copy-done.5), calls=%async_computation | async-start | bytes 1179648 | tf_op jit(solution)/shard_map/all_to_all | solution.py:757
  57.8 18.0 %copy-start.19 = (s32[1,128]{1,0:T(1,128)S(1)}, s32[1,128]{1,0:T(1,128)}, u32[]{:S(2)}) copy-start(s32[1,128]{1,0:T(1,128)} %tokens_ref.3) | copy-start | bytes 1540
  58.7 1.3 %collective-permute-start.12 = (bf16[288,128]{1,0:T(8,128)(2,1)S(1)}, bf16[288,128]{1,0:T(8,128)(2,1)S(1)}, u32[]{:S(2)}, u32[]{:S(2)}) collective-permute-start(bf16[288,128]{1,0:T(8,128)(2,1)S(1)} %get-tuple-element.35), channel_id=1, source_target_pairs={{0,8},{8,0},{16,24},{24,16},{1,9},{9,1},{17,25},{25,17},{2,10},{10... | collective-permute-start | bytes 221192 | tf_op jit(solution)/shard_map/ppermute | solution.py:634
  60.0 5.1 %collective-permute-start.13 = (bf16[288,128]{1,0:T(8,128)(2,1)S(1)}, bf16[288,128]{1,0:T(8,128)(2,1)S(1)}, u32[]{:S(2)}, u32[]{:S(2)}) collective-permute-start(bf16[288,128]{1,0:T(8,128)(2,1)S(1)} %add.32), channel_id=1, source_target_pairs={{0,16},{8,24},{16,0},{24,8},{1,17},{9,25},{17,1},{25,9},{2,18},{10... | collective-permute-start | bytes 221192 | tf_op jit(solution)/shard_map/ppermute | solution.py:634
  61.6 12.3 %collective-permute-start.10 = (bf16[192,128]{1,0:T(8,128)(2,1)}, bf16[192,128]{1,0:T(8,128)(2,1)S(1)}, u32[]{:S(2)}, u32[]{:S(2)}) collective-permute-start(bf16[192,128]{1,0:T(8,128)(2,1)} %copy-done.24), channel_id=1, source_target_pairs={{0,2},{1,3},{2,0},{3,1},{4,6},{5,7},{6,4},{7,5},{8,10},{9,11},{10,... | collective-permute-start | bytes 147464 | tf_op jit(solution)/shard_map/ppermute | solution.py:634
  63.6 16.2 %collective-permute-start.11 = (bf16[192,128]{1,0:T(8,128)(2,1)}, bf16[192,128]{1,0:T(8,128)(2,1)}, u32[]{:S(2)}, u32[]{:S(2)}) collective-permute-start(bf16[192,128]{1,0:T(8,128)(2,1)} %copy-done.23), channel_id=1, source_target_pairs={{0,3},{1,2},{2,1},{3,0},{4,7},{5,6},{6,5},{7,4},{8,11},{9,10},{10,... | collective-permute-start | bytes 147464 | tf_op jit(solution)/shard_map/ppermute | solution.py:634
  65.1 14.8 %collective-permute-start.9 = (bf16[192,128]{1,0:T(8,128)(2,1)}, bf16[192,128]{1,0:T(8,128)(2,1)}, u32[]{:S(2)}, u32[]{:S(2)}) collective-permute-start(bf16[192,128]{1,0:T(8,128)(2,1)} %copy-done.22), channel_id=1, source_target_pairs={{0,1},{1,0},{2,3},{3,2},{4,5},{5,4},{6,7},{7,6},{8,9},{9,8},{10,11... | collective-permute-start | bytes 147464 | tf_op jit(solution)/shard_map/ppermute | solution.py:634
  65.8 14.1 %collective-permute-start.14 = (bf16[288,128]{1,0:T(8,128)(2,1)}, bf16[288,128]{1,0:T(8,128)(2,1)}, u32[]{:S(2)}, u32[]{:S(2)}) collective-permute-start(bf16[288,128]{1,0:T(8,128)(2,1)} %add.33.own_ref), channel_id=1, source_target_pairs={{0,6},{1,7},{8,14},{9,15},{16,22},{17,23},{24,30},{25,31}} | collective-permute-start | bytes 221192 | tf_op jit(solution)/shard_map/ppermute | solution.py:784
  72.6 7.3 %collective-permute-start.15 = (bf16[288,128]{1,0:T(8,128)(2,1)}, bf16[288,128]{1,0:T(8,128)(2,1)}, u32[]{:S(2)}, u32[]{:S(2)}) collective-permute-start(bf16[288,128]{1,0:T(8,128)(2,1)} %add.33.own_ref), channel_id=1, source_target_pairs={{2,6},{3,7},{10,14},{11,15},{18,22},{19,23},{26,30},{27,31}} | collective-permute-start | bytes 221192 | tf_op jit(solution)/shard_map/ppermute | solution.py:784
  74.5 5.4 %collective-permute-start.16 = (bf16[288,128]{1,0:T(8,128)(2,1)}, bf16[288,128]{1,0:T(8,128)(2,1)}, u32[]{:S(2)}, u32[]{:S(2)}) collective-permute-start(bf16[288,128]{1,0:T(8,128)(2,1)} %add.33.own_ref), channel_id=1, source_target_pairs={{4,6},{5,7},{12,14},{13,15},{20,22},{21,23},{28,30},{29,31}} | collective-permute-start | bytes 221192 | tf_op jit(solution)/shard_map/ppermute | solution.py:784
  82.0 1.6 %collective-permute-start.17 = (bf16[1152,128]{1,0:T(8,128)(2,1)S(1)}, bf16[1152,128]{1,0:T(8,128)(2,1)S(1)}, u32[]{:S(2)}, u32[]{:S(2)}) collective-permute-start(bf16[1152,128]{1,0:T(8,128)(2,1)S(1)} %shard_map.120.mine_ref), channel_id=1, source_target_pairs={{0,8},{8,0},{16,24},{24,16},{1,9},{9,1},{17,25},{25,17},{2,10},{10... | collective-permute-start | bytes 884744 | tf_op jit(solution)/shard_map/ppermute | solution.py:634
  (24 other events, 72.4 us)

commit v14 on v12

--- a/solution.py
+++ b/solution.py
@@ -546,8 +546,7 @@
     out_ref[...] = here_ref[3 * rows :, :] + there_ref[3 * rows :, :]
 
 
-def gather_kernel(meta_ref, s0, s1, s2, s3, own_ref, o0, o1, o2, after_ref, mine_ref):
-    del after_ref
+def gather_kernel(meta_ref, s0, s1, s2, s3, own_ref, o0, o1, o2, mine_ref):
     rows = GROUP_COLS
     size = own_ref.shape[0]
 
@@ -763,17 +762,6 @@
     )
     here = keep + swapped(give, "dp", 1)
     there = swapped(here, "dp", 2)
-    kept_out, *pieces = call(
-        combine_kernel,
-        (meta, here, there, got_rows),
-        [((out_rows, lanes), half)] + [((GROUP_COLS, lanes), half)] * GROUPS,
-        loose=1,
-    )
-    last = blocks - 2
-    got = [pieces[0]] + [swapped(pieces[turn], "seq", turn) for turn in (1, 2, 3)]
-    got_out = [
-        lax.ppermute(kept_out, "seq", [(2 * z, last), (2 * z + 1, last + 1)]) for z in range(3)
-    ]
     (grad_input,) = call(
         input_kernel,
         (token_ids, table, w_query, w_key, w_value, got_rows),
@@ -781,11 +769,21 @@
         flops=10**9,
         moved=5 * 10**6,
     )
+    kept_out, *pieces = call(
+        combine_kernel,
+        (meta, here, there, grad_input),
+        [((out_rows, lanes), half)] + [((GROUP_COLS, lanes), half)] * GROUPS,
+        loose=1,
+    )
+    last = blocks - 2
+    got = [pieces[0]] + [swapped(pieces[turn], "seq", turn) for turn in (1, 2, 3)]
+    got_out = [
+        lax.ppermute(kept_out, "seq", [(2 * z, last), (2 * z + 1, last + 1)]) for z in range(3)
+    ]
     (mine,) = call(
         gather_kernel,
-        (meta, *got, kept_out, *got_out, grad_input),
+        (meta, *got, kept_out, *got_out),
         [((4 * out_rows, lanes), half)],
-        loose=1,
     )
     (weight_grads,) = call(
         weight_kernel,

time: 81.7 us -> 85.6 us (1.048)
  local copies, waits for them, and re-layouts: 4.01 us -> 12.7 us
  waiting for transfers between devices: 18 us -> 13.2 us
    unnamed x30 -> x44, local copies, waits for them, and re-layouts: 3.31 us -> 12 us
    all_to_all x1, waiting for transfers between devices: 7.95 us -> 3.38 us  [grouped_device(): late = lax.all_to_all(late, 'seq', split_axis=0, concat_axis=0, tiled=True)]
    all_to_all x1, waiting for transfers between devices: 2.27 us -> 0.01 us  [over_plane(): lax.all_to_all(chunks, 'seq', split_axis=0, concat_axis=0, axis_index_gro...]
    ppermute x13, waiting for transfers between devices: 7.8 us -> 9.76 us  [swapped(): return lax.ppermute(block, axis, route)]
    ppermute x3, starting transfers between devices: 6.01 us -> 4.39 us  [grouped_device(): lax.ppermute(kept_out, 'seq', [(2 * z, last), (2 * z + 1, last + 1)])]
  transfers between devices with their start and end apart: 18 -> 18, of which waited for: 6 -> 7; matrix products, arithmetic and copies ran while one was open for 2% -> 2% of each run, Pallas kernels for 22% -> 22%
where the time goes in v14:
time: 85.6 us; the launch traced here: 84.9 us
  starting transfers between devices  31.7 us (37%)
  Pallas kernels  25.7 us (30%)
  waiting for transfers between devices  13.2 us (15%)
  local copies, waits for them, and re-layouts  12.7 us (15%)
  between operations  0.88 us (1%)
    pallas_call x9, Pallas kernels, call(): pl.pallas_call(body, grid=(steps,), in_specs=spaces, out_specs=[whole(sha...  25.7 us
    ppermute x13, starting transfers between devices, swapped(): return lax.ppermute(block, axis, route)  18.3 us
    unnamed x44, local copies, waits for them, and re-layouts  12 us
    ppermute x13, waiting for transfers between devices, swapped(): return lax.ppermute(block, axis, route)  9.76 us
    all_to_all x1, starting transfers between devices, grouped_device(): late = lax.all_to_all(late, 'seq', split_axis=0, concat_axis=0, tiled=True)  4.85 us
    ppermute x3, starting transfers between devices, grouped_device(): lax.ppermute(kept_out, 'seq', [(2 * z, last), (2 * z + 1, last + 1)])  4.39 us
    all_to_all x1, starting transfers between devices, over_plane(): lax.all_to_all(chunks, 'seq', split_axis=0, concat_axis=0, axis_index_gro...  4.16 us
    all_to_all x1, waiting for transfers between devices, grouped_device(): late = lax.all_to_all(late, 'seq', split_axis=0, concat_axis=0, tiled=True)  3.38 us
  transfers between devices with their start and end apart: 18, of which 7 were waited for; matrix products, arithmetic and copies ran while one was open for 2% of the time, Pallas kernels for 22%

profile of v14, /device:TPU:0, one launch (start us, length us, event | category | flops | bytes accessed | tf_op | source)
XLA Modules:
  0.0 84.9 jit_solution(12954831451545083528)
XLA Ops:
  0.7 2.6 %shard_map.114 = (bf16[208,128]{1,0:T(8,128)(2,1)}, bf16[208,128]{1,0:T(8,128)(2,1)}, bf16[208,128]{1,0:T(8,128)(2,1)}, bf16[208,128]{1,0:T(8,128)(2,1)}) custom-call(s32[1]{0:T(128)} %bitcast.3.spot_ref, s32[1,128]{1,0:T(1,128)} %tokens_ref.3, bf16[128,768]{1,0:T(8,128)(2,1)} %bitcast.9, bf16[768,768]{1,0:T(8,128)(2,1)} %out_weights_ref.1), custom_call_target="tpu_custom_call" | custom-call | flops 100000000 | bytes 1000000 | tf_op jit(solution)/shard_map/pallas_call | solution.py:675
  3.2 2.9 %collective-permute-start = (bf16[208,128]{1,0:T(8,128)(2,1)}, bf16[208,128]{1,0:T(8,128)(2,1)S(1)}, u32[]{:S(2)}, u32[]{:S(2)}) collective-permute-start(bf16[208,128]{1,0:T(8,128)(2,1)} %get-tuple-element.20), channel_id=1, source_target_pairs={{0,1},{1,0},{2,3},{3,2},{4,5},{5,4},{6,7},{7,6},{8,9},{9,8},{10,11... | collective-permute-start | bytes 159752 | tf_op jit(solution)/shard_map/ppermute | solution.py:633
  6.2 1.6 %collective-permute-start.1 = (bf16[208,128]{1,0:T(8,128)(2,1)}, bf16[208,128]{1,0:T(8,128)(2,1)S(1)}, u32[]{:S(2)}, u32[]{:S(2)}) collective-permute-start(bf16[208,128]{1,0:T(8,128)(2,1)} %get-tuple-element.21), channel_id=1, source_target_pairs={{0,2},{1,3},{2,0},{3,1},{4,6},{5,7},{6,4},{7,5},{8,10},{9,11},{10,... | collective-permute-start | bytes 159752 | tf_op jit(solution)/shard_map/ppermute | solution.py:633
  7.7 2.6 %collective-permute-start.4 = (bf16[208,128]{1,0:T(8,128)(2,1)}, bf16[208,128]{1,0:T(8,128)(2,1)S(1)}, u32[]{:S(2)}, u32[]{:S(2)}) collective-permute-start(bf16[208,128]{1,0:T(8,128)(2,1)} %get-tuple-element.20), channel_id=1, source_target_pairs={{0,5},{1,4},{2,7},{3,6},{4,1},{5,0},{6,3},{7,2},{8,13},{9,12},{10,... | collective-permute-start | bytes 159752 | tf_op jit(solution)/shard_map/ppermute | solution.py:633
  10.3 1.8 %collective-permute-start.2 = (bf16[208,128]{1,0:T(8,128)(2,1)}, bf16[208,128]{1,0:T(8,128)(2,1)S(1)}, u32[]{:S(2)}, u32[]{:S(2)}) collective-permute-start(bf16[208,128]{1,0:T(8,128)(2,1)} %get-tuple-element.22), channel_id=1, source_target_pairs={{0,3},{1,2},{2,1},{3,0},{4,7},{5,6},{6,5},{7,4},{8,11},{9,10},{10,... | collective-permute-start | bytes 159752 | tf_op jit(solution)/shard_map/ppermute | solution.py:633
  12.9 2.9 %collective-permute-start.6 = (bf16[208,128]{1,0:T(8,128)(2,1)}, bf16[208,128]{1,0:T(8,128)(2,1)S(1)}, u32[]{:S(2)}, u32[]{:S(2)}) collective-permute-start(bf16[208,128]{1,0:T(8,128)(2,1)} %get-tuple-element.22), channel_id=1, source_target_pairs={{0,7},{1,6},{2,5},{3,4},{4,3},{5,2},{6,1},{7,0},{8,15},{9,14},{10,... | collective-permute-start | bytes 159752 | tf_op jit(solution)/shard_map/ppermute | solution.py:633
  16.5 4.3 %shard_map.113 = (bf16[2,576,256]{2,1,0:T(8,128)(2,1)}, bf16[256,384]{1,0:T(8,128)(2,1)}) custom-call(s32[7]{0:T(128)} %concatenate.3.meta_ref, bf16[256,768]{1,0:T(8,128)(2,1)} %table_ref.3, bf16[768,768]{1,0:T(8,128)(2,1)} %query_ref.3, bf16[768,768]{1,0:T(8,128)(2,1)} %key_ref.3, bf16[768,768]{1,0:T(8,128)(2,1)} %value_ref.3), custom_call_target="tpu_custom_call" | custom-call | flops 1000000000 | bytes 5000000 | tf_op jit(solution)/shard_map/pallas_call | solution.py:675
  23.1 4.8 %all-to-all-start.1 = ((bf16[8,128,384]{2,1,0:T(8,128)(2,1)}), bf16[8,128,384]{2,1,0:T(8,128)(2,1)S(1)}, u32[]{:S(2)}, u32[]{:S(2)}) async-start(bf16[8,128,384]{2,1,0:T(8,128)(2,1)} %shard_map.117), calls=%async_computation.1 | async-start | bytes 1572864 | tf_op jit(solution)/shard_map/all_to_all | solution.py:714
  30.6 10.2 %shard_map.115 = (bf16[4,576,128]{2,1,0:T(8,128)(2,1)S(1)}, bf16[2,576,128]{2,1,0:T(8,128)(2,1)S(1)}, bf16[192,1024]{1,0:T(8,128)(2,1)S(1)}) custom-call(s32[7]{0:T(128)S(1)} %copy-done.15, bf16[2,576,256]{2,1,0:T(8,128)(2,1)S(1)} %copy-done.10, f32[32,1024]{1,0:T(8,128)S(1)} %copy-done.19, f32[32,1024]{1,0:T(8,128)S(1)} %copy-done.20, ...), custom_call_target="tpu_custom_call" | custom-call | flops 8000000000 | bytes 8000000 | tf_op jit(solution)/shard_map/pallas_call | solution.py:675
  43.1 3.4 %all-to-all-done.1 = bf16[8,128,384]{2,1,0:T(8,128)(2,1)S(1)} async-done(((bf16[8,128,384]{2,1,0:T(8,128)(2,1)}), bf16[8,128,384]{2,1,0:T(8,128)(2,1)S(1)}, u32[]{:S(2)}, u32[]{:S(2)}) %all-to-all-start.1) | async-done | bytes 786464 | tf_op jit(solution)/shard_map/all_to_all | solution.py:714
  47.4 4.2 %all-to-all-start = ((bf16[4,576,128]{2,1,0:T(8,128)(2,1)}), bf16[4,576,128]{2,1,0:T(8,128)(2,1)}, u32[]{:S(2)}, u32[]{:S(2)}) async-start(bf16[4,576,128]{2,1,0:T(8,128)(2,1)} %copy-done.8), calls=%async_computation | async-start | bytes 1179648 | tf_op jit(solution)/shard_map/all_to_all | solution.py:750
  51.6 1.2 %copy-done.4 = bf16[8,128,384]{2,1,0:T(8,128)(2,1)S(1)} copy-done((bf16[8,128,384]{2,1,0:T(8,128)(2,1)S(1)}, bf16[8,128,384]{2,1,0:T(8,128)(2,1)}, u32[]{:S(2)}) %copy-start.4) | copy-done | bytes 786456
  55.8 1.5 %collective-permute-done.7 = bf16[864,128]{1,0:T(8,128)(2,1)S(1)} collective-permute-done((bf16[864,128]{1,0:T(8,128)(2,1)S(1)}, bf16[864,128]{1,0:T(8,128)(2,1)S(1)}, u32[]{:S(2)}, u32[]{:S(2)}) %collective-permute-start.7) | collective-permute-done | bytes 221216 | tf_op jit(solution)/shard_map/ppermute | solution.py:633
  58.0 1.5 %collective-permute-start.8 = (bf16[864,128]{1,0:T(8,128)(2,1)}, bf16[864,128]{1,0:T(8,128)(2,1)}, u32[]{:S(2)}, u32[]{:S(2)}) collective-permute-start(bf16[864,128]{1,0:T(8,128)(2,1)} %add.25.here_ref), channel_id=1, source_target_pairs={{0,16},{8,24},{16,0},{24,8},{1,17},{9,25},{17,1},{25,9},{2,18},{10... | collective-permute-start | bytes 663560 | tf_op jit(solution)/shard_map/ppermute | solution.py:633
  60.5 3.0 %shard_map.116.after_ref = bf16[128,768]{1,0:T(8,128)(2,1)} custom-call(s32[1,128]{1,0:T(1,128)S(1)} %copy-done.16, bf16[256,768]{1,0:T(8,128)(2,1)S(1)} %copy-done.5, bf16[768,768]{1,0:T(8,128)(2,1)S(1)} %copy-done, bf16[768,768]{1,0:T(8,128)(2,1)S(1)} %copy-done.1, bf16[768,768]{1,0:T(8,128)(2,1)S(1)} %copy-done.2, bf16[4,576,128]{2,1,0:T(8,128)(2,1)} %all-to-all-done.rows_ref), custom_call_target="tpu_custom_call" | custom-call | flops 1000000000 | bytes 5000000 | tf_op jit(solution)/shard_map/pallas_call | solution.py:675
  63.6 2.2 %collective-permute-done.8.there_ref = bf16[864,128]{1,0:T(8,128)(2,1)} collective-permute-done((bf16[864,128]{1,0:T(8,128)(2,1)}, bf16[864,128]{1,0:T(8,128)(2,1)}, u32[]{:S(2)}, u32[]{:S(2)}) %collective-permute-start.8) | collective-permute-done | bytes 221216 | tf_op jit(solution)/shard_map/ppermute | solution.py:633
  66.7 1.1 %shard_map.119 = (bf16[288,128]{1,0:T(8,128)(2,1)S(1)}, bf16[192,128]{1,0:T(8,128)(2,1)S(1)}, bf16[192,128]{1,0:T(8,128)(2,1)S(1)}, bf16[192,128]{1,0:T(8,128)(2,1)S(1)}, bf16[192,128]{1,0:T(8,128)(2,1)S(1)}) custom-call(s32[7]{0:T(128)S(1)} %copy-done.15, bf16[864,128]{1,0:T(8,128)(2,1)} %add.25.here_ref, ...), custom_call_target="tpu_custom_call" | custom-call | flops 100000000 | bytes 1000000 | tf_op jit(solution)/shard_map/pallas_call | solution.py:675
  67.9 2.0 %collective-permute-start.9 = (bf16[192,128]{1,0:T(8,128)(2,1)S(1)}, bf16[192,128]{1,0:T(8,128)(2,1)S(1)}, u32[]{:S(2)}, u32[]{:S(2)}) collective-permute-start(bf16[192,128]{1,0:T(8,128)(2,1)S(1)} %get-tuple-element.30), channel_id=1, source_target_pairs={{0,1},{1,0},{2,3},{3,2},{4,5},{5,4},{6,7},{7,6},{8,9},{9,8},{10,11... | collective-permute-start | bytes 147464 | tf_op jit(solution)/shard_map/ppermute | solution.py:633
  69.9 3.1 %collective-permute-start.12 = (bf16[288,128]{1,0:T(8,128)(2,1)S(1)}, bf16[288,128]{1,0:T(8,128)(2,1)S(1)}, u32[]{:S(2)}, u32[]{:S(2)}) collective-permute-start(bf16[288,128]{1,0:T(8,128)(2,1)S(1)} %get-tuple-element.33.own_ref), channel_id=1, source_target_pairs={{0,6},{1,7},{8,14},{9,15},{16,22},{17,23},{24,30},{25,31}} | collective-permute-start | bytes 221192 | tf_op jit(solution)/shard_map/ppermute | solution.py:781
  74.3 1.3 %collective-permute-start.10 = (bf16[192,128]{1,0:T(8,128)(2,1)S(1)}, bf16[192,128]{1,0:T(8,128)(2,1)S(1)}, u32[]{:S(2)}, u32[]{:S(2)}) collective-permute-start(bf16[192,128]{1,0:T(8,128)(2,1)S(1)} %get-tuple-element.31), channel_id=1, source_target_pairs={{0,2},{1,3},{2,0},{3,1},{4,6},{5,7},{6,4},{7,5},{8,10},{9,11},{10,... | collective-permute-start | bytes 147464 | tf_op jit(solution)/shard_map/ppermute | solution.py:633
  76.4 2.1 %collective-permute-done.10.s2 = bf16[192,128]{1,0:T(8,128)(2,1)S(1)} collective-permute-done((bf16[192,128]{1,0:T(8,128)(2,1)S(1)}, bf16[192,128]{1,0:T(8,128)(2,1)S(1)}, u32[]{:S(2)}, u32[]{:S(2)}) %collective-permute-start.10) | collective-permute-done | bytes 49184 | tf_op jit(solution)/shard_map/ppermute | solution.py:633
  78.5 2.1 %collective-permute-done.11.s3 = bf16[192,128]{1,0:T(8,128)(2,1)S(1)} collective-permute-done((bf16[192,128]{1,0:T(8,128)(2,1)S(1)}, bf16[192,128]{1,0:T(8,128)(2,1)S(1)}, u32[]{:S(2)}, u32[]{:S(2)}) %collective-permute-start.11) | collective-permute-done | bytes 49184 | tf_op jit(solution)/shard_map/ppermute | solution.py:633
  81.3 1.6 %collective-permute-done.15.other_ref = bf16[1152,128]{1,0:T(8,128)(2,1)S(1)} collective-permute-done((bf16[1152,128]{1,0:T(8,128)(2,1)S(1)}, bf16[1152,128]{1,0:T(8,128)(2,1)S(1)}, u32[]{:S(2)}, u32[]{:S(2)}) %collective-permute-start.15) | collective-permute-done | bytes 294944 | tf_op jit(solution)/shard_map/ppermute | solution.py:633
  82.8 2.1 %shard_map.121 = f32[384,768]{1,0:T(8,128)} custom-call(s32[7]{0:T(128)S(1)} %copy-done.15, bf16[256,384]{1,0:T(8,128)(2,1)S(1)} %copy-done.17, bf16[1152,128]{1,0:T(8,128)(2,1)S(1)} %shard_map.120.mine_ref, bf16[1152,128]{1,0:T(8,128)(2,1)S(1)} %collective-permute-done.15.other_ref), custom_call_target="tpu_custom_call" | custom-call | flops 1000000000 | bytes 5000000 | tf_op jit(solution)/shard_map/pallas_call | solution.py:675
  (68 shorter events, 18.0 us)
Async XLA Ops:
  0.6 11.5 %copy-start.21 = (s32[12]{0:T(128)S(1)}, s32[12]{0:T(128)}, u32[]{:S(2)}) copy-start(s32[12]{0:T(128)} %param.17) | copy-start | bytes 148
  3.2 9.6 %collective-permute-start = (bf16[208,128]{1,0:T(8,128)(2,1)}, bf16[208,128]{1,0:T(8,128)(2,1)S(1)}, u32[]{:S(2)}, u32[]{:S(2)}) collective-permute-start(bf16[208,128]{1,0:T(8,128)(2,1)} %get-tuple-element.20), channel_id=1, source_target_pairs={{0,1},{1,0},{2,3},{3,2},{4,5},{5,4},{6,7},{7,6},{8,9},{9,8},{10,11... | collective-permute-start | bytes 159752 | tf_op jit(solution)/shard_map/ppermute | solution.py:633
  6.2 9.6 %collective-permute-start.1 = (bf16[208,128]{1,0:T(8,128)(2,1)}, bf16[208,128]{1,0:T(8,128)(2,1)S(1)}, u32[]{:S(2)}, u32[]{:S(2)}) collective-permute-start(bf16[208,128]{1,0:T(8,128)(2,1)} %get-tuple-element.21), channel_id=1, source_target_pairs={{0,2},{1,3},{2,0},{3,1},{4,6},{5,7},{6,4},{7,5},{8,10},{9,11},{10,... | collective-permute-start | bytes 159752 | tf_op jit(solution)/shard_map/ppermute | solution.py:633
  7.7 13.3 %collective-permute-start.4 = (bf16[208,128]{1,0:T(8,128)(2,1)}, bf16[208,128]{1,0:T(8,128)(2,1)S(1)}, u32[]{:S(2)}, u32[]{:S(2)}) collective-permute-start(bf16[208,128]{1,0:T(8,128)(2,1)} %get-tuple-element.20), channel_id=1, source_target_pairs={{0,5},{1,4},{2,7},{3,6},{4,1},{5,0},{6,3},{7,2},{8,13},{9,12},{10,... | collective-permute-start | bytes 159752 | tf_op jit(solution)/shard_map/ppermute | solution.py:633
  10.3 10.8 %collective-permute-start.5 = (bf16[208,128]{1,0:T(8,128)(2,1)}, bf16[208,128]{1,0:T(8,128)(2,1)S(1)}, u32[]{:S(2)}, u32[]{:S(2)}) collective-permute-start(bf16[208,128]{1,0:T(8,128)(2,1)} %get-tuple-element.21), channel_id=1, source_target_pairs={{0,6},{1,7},{2,4},{3,5},{4,2},{5,3},{6,0},{7,1},{8,14},{9,15},{10,... | collective-permute-start | bytes 159752 | tf_op jit(solution)/shard_map/ppermute | solution.py:633
  10.3 10.4 %collective-permute-start.2 = (bf16[208,128]{1,0:T(8,128)(2,1)}, bf16[208,128]{1,0:T(8,128)(2,1)S(1)}, u32[]{:S(2)}, u32[]{:S(2)}) collective-permute-start(bf16[208,128]{1,0:T(8,128)(2,1)} %get-tuple-element.22), channel_id=1, source_target_pairs={{0,3},{1,2},{2,1},{3,0},{4,7},{5,6},{6,5},{7,4},{8,11},{9,10},{10,... | collective-permute-start | bytes 159752 | tf_op jit(solution)/shard_map/ppermute | solution.py:633
  12.9 8.2 %collective-permute-start.6 = (bf16[208,128]{1,0:T(8,128)(2,1)}, bf16[208,128]{1,0:T(8,128)(2,1)S(1)}, u32[]{:S(2)}, u32[]{:S(2)}) collective-permute-start(bf16[208,128]{1,0:T(8,128)(2,1)} %get-tuple-element.22), channel_id=1, source_target_pairs={{0,7},{1,6},{2,5},{3,4},{4,3},{5,2},{6,1},{7,0},{8,15},{9,14},{10,... | collective-permute-start | bytes 159752 | tf_op jit(solution)/shard_map/ppermute | solution.py:633
  15.8 5.3 %collective-permute-start.3 = (bf16[208,128]{1,0:T(8,128)(2,1)}, bf16[208,128]{1,0:T(8,128)(2,1)S(1)}, u32[]{:S(2)}, u32[]{:S(2)}) collective-permute-start(bf16[208,128]{1,0:T(8,128)(2,1)} %get-tuple-element.19.rest_0_), channel_id=1, source_target_pairs={{0,4},{1,5},{2,6},{3,7},{4,0},{5,1},{6,2},{7,3},{8,12},{9,13},{10,... | collective-permute-start | bytes 159752 | tf_op jit(solution)/shard_map/ppermute | solution.py:633
  23.1 23.4 %all-to-all-start.1 = ((bf16[8,128,384]{2,1,0:T(8,128)(2,1)}), bf16[8,128,384]{2,1,0:T(8,128)(2,1)S(1)}, u32[]{:S(2)}, u32[]{:S(2)}) async-start(bf16[8,128,384]{2,1,0:T(8,128)(2,1)} %shard_map.117), calls=%async_computation.1 | async-start | bytes 1572864 | tf_op jit(solution)/shard_map/all_to_all | solution.py:714
  30.6 28.9 %copy-start.2 = (bf16[768,768]{1,0:T(8,128)(2,1)S(1)}, bf16[768,768]{1,0:T(8,128)(2,1)}, u32[]{:S(2)}) copy-start(bf16[768,768]{1,0:T(8,128)(2,1)} %value_ref.3) | copy-start | bytes 3538948
  46.5 13.0 %copy-start.16 = (s32[1,128]{1,0:T(1,128)S(1)}, s32[1,128]{1,0:T(1,128)}, u32[]{:S(2)}) copy-start(s32[1,128]{1,0:T(1,128)} %tokens_ref.3) | copy-start | bytes 1540
  46.5 13.0 %copy-start.1 = (bf16[768,768]{1,0:T(8,128)(2,1)S(1)}, bf16[768,768]{1,0:T(8,128)(2,1)}, u32[]{:S(2)}) copy-start(bf16[768,768]{1,0:T(8,128)(2,1)} %key_ref.3) | copy-start | bytes 3538948
  47.4 12.1 %all-to-all-start = ((bf16[4,576,128]{2,1,0:T(8,128)(2,1)}), bf16[4,576,128]{2,1,0:T(8,128)(2,1)}, u32[]{:S(2)}, u32[]{:S(2)}) async-start(bf16[4,576,128]{2,1,0:T(8,128)(2,1)} %copy-done.8), calls=%async_computation | async-start | bytes 1179648 | tf_op jit(solution)/shard_map/all_to_all | solution.py:750
  51.6 8.0 %copy-start = (bf16[768,768]{1,0:T(8,128)(2,1)S(1)}, bf16[768,768]{1,0:T(8,128)(2,1)}, u32[]{:S(2)}) copy-start(bf16[768,768]{1,0:T(8,128)(2,1)} %query_ref.3) | copy-start | bytes 3538948
  55.7 1.5 %collective-permute-start.7 = (bf16[864,128]{1,0:T(8,128)(2,1)S(1)}, bf16[864,128]{1,0:T(8,128)(2,1)S(1)}, u32[]{:S(2)}, u32[]{:S(2)}) collective-permute-start(bf16[864,128]{1,0:T(8,128)(2,1)S(1)} %get-tuple-element.28), channel_id=1, source_target_pairs={{0,8},{8,0},{16,24},{24,16},{1,9},{9,1},{17,25},{25,17},{2,10},{10... | collective-permute-start | bytes 663560 | tf_op jit(solution)/shard_map/ppermute | solution.py:633
  58.0 7.8 %collective-permute-start.8 = (bf16[864,128]{1,0:T(8,128)(2,1)}, bf16[864,128]{1,0:T(8,128)(2,1)}, u32[]{:S(2)}, u32[]{:S(2)}) collective-permute-start(bf16[864,128]{1,0:T(8,128)(2,1)} %add.25.here_ref), channel_id=1, source_target_pairs={{0,16},{8,24},{16,0},{24,8},{1,17},{9,25},{17,1},{25,9},{2,18},{10... | collective-permute-start | bytes 663560 | tf_op jit(solution)/shard_map/ppermute | solution.py:633
  66.7 16.1 %copy-start.17 = (bf16[256,384]{1,0:T(8,128)(2,1)S(1)}, bf16[256,384]{1,0:T(8,128)(2,1)}, u32[]{:S(2)}) copy-start(bf16[256,384]{1,0:T(8,128)(2,1)} %get-tuple-element.24.normed_ref) | copy-start | bytes 589828
  67.9 7.7 %collective-permute-start.9 = (bf16[192,128]{1,0:T(8,128)(2,1)S(1)}, bf16[192,128]{1,0:T(8,128)(2,1)S(1)}, u32[]{:S(2)}, u32[]{:S(2)}) collective-permute-start(bf16[192,128]{1,0:T(8,128)(2,1)S(1)} %get-tuple-element.30), channel_id=1, source_target_pairs={{0,1},{1,0},{2,3},{3,2},{4,5},{5,4},{6,7},{7,6},{8,9},{9,8},{10,11... | collective-permute-start | bytes 147464 | tf_op jit(solution)/shard_map/ppermute | solution.py:633
  69.9 10.7 %collective-permute-start.12 = (bf16[288,128]{1,0:T(8,128)(2,1)S(1)}, bf16[288,128]{1,0:T(8,128)(2,1)S(1)}, u32[]{:S(2)}, u32[]{:S(2)}) collective-permute-start(bf16[288,128]{1,0:T(8,128)(2,1)S(1)} %get-tuple-element.33.own_ref), channel_id=1, source_target_pairs={{0,6},{1,7},{8,14},{9,15},{16,22},{17,23},{24,30},{25,31}} | collective-permute-start | bytes 221192 | tf_op jit(solution)/shard_map/ppermute | solution.py:781
  73.0 7.6 %collective-permute-start.13 = (bf16[288,128]{1,0:T(8,128)(2,1)S(1)}, bf16[288,128]{1,0:T(8,128)(2,1)S(1)}, u32[]{:S(2)}, u32[]{:S(2)}) collective-permute-start(bf16[288,128]{1,0:T(8,128)(2,1)S(1)} %get-tuple-element.33.own_ref), channel_id=1, source_target_pairs={{2,6},{3,7},{10,14},{11,15},{18,22},{19,23},{26,30},{27,31}} | collective-permute-start | bytes 221192 | tf_op jit(solution)/shard_map/ppermute | solution.py:781
  73.6 6.9 %collective-permute-start.14 = (bf16[288,128]{1,0:T(8,128)(2,1)S(1)}, bf16[288,128]{1,0:T(8,128)(2,1)S(1)}, u32[]{:S(2)}, u32[]{:S(2)}) collective-permute-start(bf16[288,128]{1,0:T(8,128)(2,1)S(1)} %get-tuple-element.33.own_ref), channel_id=1, source_target_pairs={{4,6},{5,7},{12,14},{13,15},{20,22},{21,23},{28,30},{29,31}} | collective-permute-start | bytes 221192 | tf_op jit(solution)/shard_map/ppermute | solution.py:781
  74.3 4.2 %collective-permute-start.10 = (bf16[192,128]{1,0:T(8,128)(2,1)S(1)}, bf16[192,128]{1,0:T(8,128)(2,1)S(1)}, u32[]{:S(2)}, u32[]{:S(2)}) collective-permute-start(bf16[192,128]{1,0:T(8,128)(2,1)S(1)} %get-tuple-element.31), channel_id=1, source_target_pairs={{0,2},{1,3},{2,0},{3,1},{4,6},{5,7},{6,4},{7,5},{8,10},{9,11},{10,... | collective-permute-start | bytes 147464 | tf_op jit(solution)/shard_map/ppermute | solution.py:633
  75.6 5.0 %collective-permute-start.11 = (bf16[192,128]{1,0:T(8,128)(2,1)S(1)}, bf16[192,128]{1,0:T(8,128)(2,1)S(1)}, u32[]{:S(2)}, u32[]{:S(2)}) collective-permute-start(bf16[192,128]{1,0:T(8,128)(2,1)S(1)} %get-tuple-element.32), channel_id=1, source_target_pairs={{0,3},{1,2},{2,1},{3,0},{4,7},{5,6},{6,5},{7,4},{8,11},{9,10},{10,... | collective-permute-start | bytes 147464 | tf_op jit(solution)/shard_map/ppermute | solution.py:633
  81.2 1.6 %collective-permute-start.15 = (bf16[1152,128]{1,0:T(8,128)(2,1)S(1)}, bf16[1152,128]{1,0:T(8,128)(2,1)S(1)}, u32[]{:S(2)}, u32[]{:S(2)}) collective-permute-start(bf16[1152,128]{1,0:T(8,128)(2,1)S(1)} %shard_map.120.mine_ref), channel_id=1, source_target_pairs={{0,8},{8,0},{16,24},{24,16},{1,9},{9,1},{17,25},{25,17},{2,10},{10... | collective-permute-start | bytes 884744 | tf_op jit(solution)/shard_map/ppermute | solution.py:633
  (16 other events, 27.0 us)

commit v15 on v12

--- a/solution.py
+++ b/solution.py
@@ -269,22 +269,25 @@
 
 def late_kernel(cotangent_ref, *rest):
     late_ref = rest[-1]
-    columns = late_ref.shape[2]
     for target in range(2 * GROUPS):
-        side = target // GROUPS
-        late_ref[target] = cotangent_ref[:, side * columns : (side + 1) * columns]
+        late_ref[target] = cotangent_ref[target // GROUPS]
 
 
 def prepare_kernel(
     meta_ref,
+    cotangent_ref,
     table_ref,
     query_ref,
     key_ref,
     value_ref,
+    halves_ref,
     lookup_ref,
     normed_ref,
     columns_ref,
 ):
+    columns = halves_ref.shape[2]
+    halves_ref[0] = cotangent_ref[:, :columns]
+    halves_ref[1] = cotangent_ref[:, columns:]
     normed = normed_table(table_ref)
     half = normed.shape[1] // 2
     normed_ref[...] = jnp.where(meta_ref[GROUP_HEADS] == 0, normed[:, :half], normed[:, half:])
@@ -697,10 +700,14 @@
     early = [sent[0]] + [None] * (blocks - 1)
     for turn in (4, 6, 5, 7, 2, 3, 1):
         early[turn] = swapped(sent[mirrored(turn)], "seq", turn)
-    lookup, normed = call(
+    halves, lookup, normed = call(
         prepare_kernel,
-        (meta, table, w_query, w_key, w_value),
-        [((2, 3 * GROUP_COLS, vocab), half), ((vocab, features // 2), half)],
+        (meta, grad_out, table, w_query, w_key, w_value),
+        [
+            ((2, block, features // 2), half),
+            ((2, 3 * GROUP_COLS, vocab), half),
+            ((vocab, features // 2), half),
+        ],
         [pltpu.VMEM((features, vocab), jnp.float32)],
         flops=10**9,
         moved=5 * 10**6,
@@ -708,7 +715,7 @@
     )
     (late,) = call(
         late_kernel,
-        (grad_out, lookup, *early[1:]),
+        (halves, lookup, *early[1:]),
         [((blocks, block, features // 2), half)],
         loose=blocks,
     )

time: 81.7 us -> 82.6 us (1.011)
  local copies, waits for them, and re-layouts: 4.01 us -> 4.93 us
    unnamed x30, local copies, waits for them, and re-layouts: 3.31 us -> 4.23 us
where the time goes in v15:
time: 82.6 us; the launch traced here: 82.1 us
  starting transfers between devices  32.2 us (39%)
  Pallas kernels  25.4 us (31%)
  waiting for transfers between devices  17.8 us (22%)
  local copies, waits for them, and re-layouts  4.93 us (6%)
  between operations  0.92 us (1%)
    pallas_call x9, Pallas kernels, call(): pl.pallas_call(body, grid=(steps,), in_specs=spaces, out_specs=[whole(sha...  25.4 us
    ppermute x13, starting transfers between devices, swapped(): return lax.ppermute(block, axis, route)  18.2 us
    all_to_all x1, waiting for transfers between devices, grouped_device(): late = lax.all_to_all(late, 'seq', split_axis=0, concat_axis=0, tiled=True)  7.85 us
    ppermute x13, waiting for transfers between devices, swapped(): return lax.ppermute(block, axis, route)  7.81 us
    ppermute x3, starting transfers between devices, grouped_device(): lax.ppermute(kept_out, 'seq', [(2 * z, last), (2 * z + 1, last + 1)])  6.01 us
    all_to_all x1, starting transfers between devices, grouped_device(): late = lax.all_to_all(late, 'seq', split_axis=0, concat_axis=0, tiled=True)  4.52 us
    unnamed x30, local copies, waits for them, and re-layouts  4.23 us
    all_to_all x1, starting transfers between devices, over_plane(): lax.all_to_all(chunks, 'seq', split_axis=0, concat_axis=0, axis_index_gro...  3.48 us
  transfers between devices with their start and end apart: 18, of which 6 were waited for; matrix products, arithmetic and copies ran while one was open for 2% of the time, Pallas kernels for 22%

profile of v15, /device:TPU:0, one launch (start us, length us, event | category | flops | bytes accessed | tf_op | source)
XLA Modules:
  0.0 82.1 jit_solution(17716039389452641437)
XLA Ops:
  0.7 2.5 %shard_map.114 = (bf16[208,128]{1,0:T(8,128)(2,1)}, bf16[208,128]{1,0:T(8,128)(2,1)}, bf16[208,128]{1,0:T(8,128)(2,1)}, bf16[208,128]{1,0:T(8,128)(2,1)}) custom-call(s32[1]{0:T(128)} %bitcast.3.spot_ref, s32[1,128]{1,0:T(1,128)} %tokens_ref.3, bf16[128,768]{1,0:T(8,128)(2,1)} %bitcast.9, bf16[768,768]{1,0:T(8,128)(2,1)} %out_weights_ref.1), custom_call_target="tpu_custom_call" | custom-call | flops 100000000 | bytes 1000000 | tf_op jit(solution)/shard_map/pallas_call | solution.py:679
  3.2 4.0 %collective-permute-start.3 = (bf16[208,128]{1,0:T(8,128)(2,1)}, bf16[208,128]{1,0:T(8,128)(2,1)S(1)}, u32[]{:S(2)}, u32[]{:S(2)}) collective-permute-start(bf16[208,128]{1,0:T(8,128)(2,1)} %get-tuple-element.20.rest_0_), channel_id=1, source_target_pairs={{0,4},{1,5},{2,6},{3,7},{4,0},{5,1},{6,2},{7,3},{8,12},{9,13},{10,... | collective-permute-start | bytes 159752 | tf_op jit(solution)/shard_map/ppermute | solution.py:637
  7.3 1.3 %collective-permute-start.4 = (bf16[208,128]{1,0:T(8,128)(2,1)}, bf16[208,128]{1,0:T(8,128)(2,1)S(1)}, u32[]{:S(2)}, u32[]{:S(2)}) collective-permute-start(bf16[208,128]{1,0:T(8,128)(2,1)} %get-tuple-element.21), channel_id=1, source_target_pairs={{0,5},{1,4},{2,7},{3,6},{4,1},{5,0},{6,3},{7,2},{8,13},{9,12},{10,... | collective-permute-start | bytes 159752 | tf_op jit(solution)/shard_map/ppermute | solution.py:637
  8.8 3.9 %collective-permute-start.5 = (bf16[208,128]{1,0:T(8,128)(2,1)}, bf16[208,128]{1,0:T(8,128)(2,1)S(1)}, u32[]{:S(2)}, u32[]{:S(2)}) collective-permute-start(bf16[208,128]{1,0:T(8,128)(2,1)} %get-tuple-element.22), channel_id=1, source_target_pairs={{0,6},{1,7},{2,4},{3,5},{4,2},{5,3},{6,0},{7,1},{8,14},{9,15},{10,... | collective-permute-start | bytes 159752 | tf_op jit(solution)/shard_map/ppermute | solution.py:637
  13.4 2.9 %collective-permute-start.6 = (bf16[208,128]{1,0:T(8,128)(2,1)}, bf16[208,128]{1,0:T(8,128)(2,1)S(1)}, u32[]{:S(2)}, u32[]{:S(2)}) collective-permute-start(bf16[208,128]{1,0:T(8,128)(2,1)} %get-tuple-element.23), channel_id=1, source_target_pairs={{0,7},{1,6},{2,5},{3,4},{4,3},{5,2},{6,1},{7,0},{8,15},{9,14},{10,... | collective-permute-start | bytes 159752 | tf_op jit(solution)/shard_map/ppermute | solution.py:637
  16.4 4.4 %shard_map.113 = (bf16[2,128,384]{2,1,0:T(8,128)(2,1)}, bf16[2,576,256]{2,1,0:T(8,128)(2,1)}, bf16[256,384]{1,0:T(8,128)(2,1)}) custom-call(s32[7]{0:T(128)} %concatenate.3.meta_ref, bf16[128,768]{1,0:T(8,128)(2,1)} %bitcast.10, bf16[256,768]{1,0:T(8,128)(2,1)} %table_ref.3, bf16[768,768]{1,0:T(8,128)(2,1)} %query_ref.3, bf16[768,768]{1,0:T(8,128)(2,1)} %key_ref.3, ...), custom_call_target="tpu_custom_call" | custom-call | flops 1000000000 | bytes 5000000 | tf_op jit(solution)/shard_map/pallas_call | solution.py:679
  21.5 1.1 %copy-done.5 = bf16[2,576,256]{2,1,0:T(8,128)(2,1)S(1)} copy-done((bf16[2,576,256]{2,1,0:T(8,128)(2,1)S(1)}, bf16[2,576,256]{2,1,0:T(8,128)(2,1)}, u32[]{:S(2)}) %copy-start.5) | copy-done | bytes 589848
  23.5 0.9 %shard_map.117 = bf16[8,128,384]{2,1,0:T(8,128)(2,1)} custom-call(bf16[2,128,384]{2,1,0:T(8,128)(2,1)S(1)} %copy-done.7, bf16[2,576,256]{2,1,0:T(8,128)(2,1)S(1)} %copy-done.5, bf16[208,128]{1,0:T(8,128)(2,1)S(1)} %collective-permute-done.rest_1_, bf16[208,128]{1,0:T(8,128)(2,1)S(1)} %collective-permute-done.1.rest_2_, ...), custom_call_target="tpu_custom_call" | custom-call | flops 100000000 | bytes 1000000 | tf_op jit(solution)/shard_map/pallas_call | solution.py:679
  24.4 4.5 %all-to-all-start.1 = ((bf16[8,128,384]{2,1,0:T(8,128)(2,1)}), bf16[8,128,384]{2,1,0:T(8,128)(2,1)S(1)}, u32[]{:S(2)}, u32[]{:S(2)}) async-start(bf16[8,128,384]{2,1,0:T(8,128)(2,1)} %shard_map.117), calls=%async_computation.1 | async-start | bytes 1572864 | tf_op jit(solution)/shard_map/all_to_all | solution.py:722
  29.0 10.9 %shard_map.115 = (bf16[4,576,128]{2,1,0:T(8,128)(2,1)}, bf16[2,576,128]{2,1,0:T(8,128)(2,1)S(1)}, bf16[192,1024]{1,0:T(8,128)(2,1)S(1)}) custom-call(s32[7]{0:T(128)S(1)} %copy-done.8, bf16[2,576,256]{2,1,0:T(8,128)(2,1)S(1)} %copy-done.6, f32[32,1024]{1,0:T(8,128)S(1)} %copy-done.13, f32[32,1024]{1,0:T(8,128)S(1)} %copy-done.12, ...), custom_call_target="tpu_custom_call" | custom-call | flops 8000000000 | bytes 8000000 | tf_op jit(solution)/shard_map/pallas_call | solution.py:679
  40.0 7.9 %all-to-all-done.1 = bf16[8,128,384]{2,1,0:T(8,128)(2,1)S(1)} async-done(((bf16[8,128,384]{2,1,0:T(8,128)(2,1)}), bf16[8,128,384]{2,1,0:T(8,128)(2,1)S(1)}, u32[]{:S(2)}, u32[]{:S(2)}) %all-to-all-start.1) | async-done | bytes 786464 | tf_op jit(solution)/shard_map/all_to_all | solution.py:722
  47.8 3.5 %all-to-all-start = ((bf16[4,576,128]{2,1,0:T(8,128)(2,1)}), bf16[4,576,128]{2,1,0:T(8,128)(2,1)S(1)}, u32[]{:S(2)}, u32[]{:S(2)}) async-start(bf16[4,576,128]{2,1,0:T(8,128)(2,1)} %get-tuple-element.24), calls=%async_computation | async-start | bytes 1179648 | tf_op jit(solution)/shard_map/all_to_all | solution.py:758
  52.4 1.5 %collective-permute-done.7 = bf16[864,128]{1,0:T(8,128)(2,1)S(1)} collective-permute-done((bf16[864,128]{1,0:T(8,128)(2,1)S(1)}, bf16[864,128]{1,0:T(8,128)(2,1)S(1)}, u32[]{:S(2)}, u32[]{:S(2)}) %collective-permute-start.7) | collective-permute-done | bytes 221216 | tf_op jit(solution)/shard_map/ppermute | solution.py:637
  54.6 1.5 %collective-permute-start.8 = (bf16[864,128]{1,0:T(8,128)(2,1)}, bf16[864,128]{1,0:T(8,128)(2,1)}, u32[]{:S(2)}, u32[]{:S(2)}) collective-permute-start(bf16[864,128]{1,0:T(8,128)(2,1)} %add.25.here_ref), channel_id=1, source_target_pairs={{0,16},{8,24},{16,0},{24,8},{1,17},{9,25},{17,1},{25,9},{2,18},{10... | collective-permute-start | bytes 663560 | tf_op jit(solution)/shard_map/ppermute | solution.py:637
  56.1 2.2 %all-to-all-done.rows_ref.after_ref = bf16[4,576,128]{2,1,0:T(8,128)(2,1)S(1)} async-done(((bf16[4,576,128]{2,1,0:T(8,128)(2,1)}), bf16[4,576,128]{2,1,0:T(8,128)(2,1)S(1)}, u32[]{:S(2)}, u32[]{:S(2)}) %all-to-all-start) | async-done | bytes 589856 | tf_op jit(solution)/shard_map/all_to_all | solution.py:758
  58.3 4.1 %collective-permute-done.8.there_ref = bf16[864,128]{1,0:T(8,128)(2,1)} collective-permute-done((bf16[864,128]{1,0:T(8,128)(2,1)}, bf16[864,128]{1,0:T(8,128)(2,1)}, u32[]{:S(2)}, u32[]{:S(2)}) %collective-permute-start.8) | collective-permute-done | bytes 221216 | tf_op jit(solution)/shard_map/ppermute | solution.py:637
  62.3 1.1 %shard_map.119 = (bf16[288,128]{1,0:T(8,128)(2,1)S(1)}, bf16[192,128]{1,0:T(8,128)(2,1)S(1)}, bf16[192,128]{1,0:T(8,128)(2,1)S(1)}, bf16[192,128]{1,0:T(8,128)(2,1)S(1)}, bf16[192,128]{1,0:T(8,128)(2,1)S(1)}) custom-call(s32[7]{0:T(128)S(1)} %copy-done.8, bf16[864,128]{1,0:T(8,128)(2,1)} %add.25.here_ref, bf16[864,128]{1,0:T(8,128)(2,1)} %collective-permute-done.8.there_ref, ...), custom_call_target="tpu_custom_call" | custom-call | flops 100000000 | bytes 1000000 | tf_op jit(solution)/shard_map/pallas_call | solution.py:679
  63.5 2.0 %collective-permute-start.9 = (bf16[192,128]{1,0:T(8,128)(2,1)S(1)}, bf16[192,128]{1,0:T(8,128)(2,1)S(1)}, u32[]{:S(2)}, u32[]{:S(2)}) collective-permute-start(bf16[192,128]{1,0:T(8,128)(2,1)S(1)} %get-tuple-element.32), channel_id=1, source_target_pairs={{0,1},{1,0},{2,3},{3,2},{4,5},{5,4},{6,7},{7,6},{8,9},{9,8},{10,11... | collective-permute-start | bytes 147464 | tf_op jit(solution)/shard_map/ppermute | solution.py:637
  66.8 4.7 %collective-permute-start.12 = (bf16[288,128]{1,0:T(8,128)(2,1)S(1)}, bf16[288,128]{1,0:T(8,128)(2,1)S(1)}, u32[]{:S(2)}, u32[]{:S(2)}) collective-permute-start(bf16[288,128]{1,0:T(8,128)(2,1)S(1)} %get-tuple-element.35.own_ref), channel_id=1, source_target_pairs={{0,6},{1,7},{8,14},{9,15},{16,22},{17,23},{24,30},{25,31}} | collective-permute-start | bytes 221192 | tf_op jit(solution)/shard_map/ppermute | solution.py:782
  71.6 2.0 %collective-permute-start.11 = (bf16[192,128]{1,0:T(8,128)(2,1)S(1)}, bf16[192,128]{1,0:T(8,128)(2,1)S(1)}, u32[]{:S(2)}, u32[]{:S(2)}) collective-permute-start(bf16[192,128]{1,0:T(8,128)(2,1)S(1)} %get-tuple-element.34), channel_id=1, source_target_pairs={{0,3},{1,2},{2,1},{3,0},{4,7},{5,6},{6,5},{7,4},{8,11},{9,10},{10,... | collective-permute-start | bytes 147464 | tf_op jit(solution)/shard_map/ppermute | solution.py:637
  73.7 1.3 %copy-done.2 = bf16[768,768]{1,0:T(8,128)(2,1)S(1)} copy-done((bf16[768,768]{1,0:T(8,128)(2,1)S(1)}, bf16[768,768]{1,0:T(8,128)(2,1)}, u32[]{:S(2)}) %copy-start.2) | copy-done | bytes 1179672
  74.9 1.9 %shard_map.116.after_ref = bf16[128,768]{1,0:T(8,128)(2,1)} custom-call(s32[1,128]{1,0:T(1,128)S(1)} %copy-done.9, bf16[256,768]{1,0:T(8,128)(2,1)S(1)} %copy-done.3, bf16[768,768]{1,0:T(8,128)(2,1)S(1)} %copy-done, bf16[768,768]{1,0:T(8,128)(2,1)S(1)} %copy-done.1, bf16[768,768]{1,0:T(8,128)(2,1)S(1)} %copy-done.2, ...), custom_call_target="tpu_custom_call" | custom-call | flops 1000000000 | bytes 5000000 | tf_op jit(solution)/shard_map/pallas_call | solution.py:679
  78.5 1.6 %collective-permute-done.15.other_ref = bf16[1152,128]{1,0:T(8,128)(2,1)S(1)} collective-permute-done((bf16[1152,128]{1,0:T(8,128)(2,1)S(1)}, bf16[1152,128]{1,0:T(8,128)(2,1)S(1)}, u32[]{:S(2)}, u32[]{:S(2)}) %collective-permute-start.15) | collective-permute-done | bytes 294944 | tf_op jit(solution)/shard_map/ppermute | solution.py:637
  80.1 2.1 %shard_map.121 = f32[384,768]{1,0:T(8,128)} custom-call(s32[7]{0:T(128)S(1)} %copy-done.8, bf16[256,384]{1,0:T(8,128)(2,1)S(1)} %copy-done.10, bf16[1152,128]{1,0:T(8,128)(2,1)S(1)} %shard_map.120.mine_ref, bf16[1152,128]{1,0:T(8,128)(2,1)S(1)} %collective-permute-done.15.other_ref), custom_call_target="tpu_custom_call" | custom-call | flops 1000000000 | bytes 5000000 | tf_op jit(solution)/shard_map/pallas_call | solution.py:679
  (54 shorter events, 7.5 us)
Async XLA Ops:
  0.6 12.0 %copy-start.14 = (s32[12]{0:T(128)S(1)}, s32[12]{0:T(128)}, u32[]{:S(2)}) copy-start(s32[12]{0:T(128)} %param.17) | copy-start | bytes 148
  3.2 10.1 %collective-permute-start.3 = (bf16[208,128]{1,0:T(8,128)(2,1)}, bf16[208,128]{1,0:T(8,128)(2,1)S(1)}, u32[]{:S(2)}, u32[]{:S(2)}) collective-permute-start(bf16[208,128]{1,0:T(8,128)(2,1)} %get-tuple-element.20.rest_0_), channel_id=1, source_target_pairs={{0,4},{1,5},{2,6},{3,7},{4,0},{5,1},{6,2},{7,3},{8,12},{9,13},{10,... | collective-permute-start | bytes 159752 | tf_op jit(solution)/shard_map/ppermute | solution.py:637
  7.3 9.0 %collective-permute-start.4 = (bf16[208,128]{1,0:T(8,128)(2,1)}, bf16[208,128]{1,0:T(8,128)(2,1)S(1)}, u32[]{:S(2)}, u32[]{:S(2)}) collective-permute-start(bf16[208,128]{1,0:T(8,128)(2,1)} %get-tuple-element.21), channel_id=1, source_target_pairs={{0,5},{1,4},{2,7},{3,6},{4,1},{5,0},{6,3},{7,2},{8,13},{9,12},{10,... | collective-permute-start | bytes 159752 | tf_op jit(solution)/shard_map/ppermute | solution.py:637
  8.5 12.3 %collective-permute-start = (bf16[208,128]{1,0:T(8,128)(2,1)}, bf16[208,128]{1,0:T(8,128)(2,1)S(1)}, u32[]{:S(2)}, u32[]{:S(2)}) collective-permute-start(bf16[208,128]{1,0:T(8,128)(2,1)} %get-tuple-element.21), channel_id=1, source_target_pairs={{0,1},{1,0},{2,3},{3,2},{4,5},{5,4},{6,7},{7,6},{8,9},{9,8},{10,11... | collective-permute-start | bytes 159752 | tf_op jit(solution)/shard_map/ppermute | solution.py:637
  8.8 12.0 %collective-permute-start.5 = (bf16[208,128]{1,0:T(8,128)(2,1)}, bf16[208,128]{1,0:T(8,128)(2,1)S(1)}, u32[]{:S(2)}, u32[]{:S(2)}) collective-permute-start(bf16[208,128]{1,0:T(8,128)(2,1)} %get-tuple-element.22), channel_id=1, source_target_pairs={{0,6},{1,7},{2,4},{3,5},{4,2},{5,3},{6,0},{7,1},{8,14},{9,15},{10,... | collective-permute-start | bytes 159752 | tf_op jit(solution)/shard_map/ppermute | solution.py:637
  12.7 8.1 %collective-permute-start.1 = (bf16[208,128]{1,0:T(8,128)(2,1)}, bf16[208,128]{1,0:T(8,128)(2,1)S(1)}, u32[]{:S(2)}, u32[]{:S(2)}) collective-permute-start(bf16[208,128]{1,0:T(8,128)(2,1)} %get-tuple-element.22), channel_id=1, source_target_pairs={{0,2},{1,3},{2,0},{3,1},{4,6},{5,7},{6,4},{7,5},{8,10},{9,11},{10,... | collective-permute-start | bytes 159752 | tf_op jit(solution)/shard_map/ppermute | solution.py:637
  13.4 7.4 %collective-permute-start.6 = (bf16[208,128]{1,0:T(8,128)(2,1)}, bf16[208,128]{1,0:T(8,128)(2,1)S(1)}, u32[]{:S(2)}, u32[]{:S(2)}) collective-permute-start(bf16[208,128]{1,0:T(8,128)(2,1)} %get-tuple-element.23), channel_id=1, source_target_pairs={{0,7},{1,6},{2,5},{3,4},{4,3},{5,2},{6,1},{7,0},{8,15},{9,14},{10,... | collective-permute-start | bytes 159752 | tf_op jit(solution)/shard_map/ppermute | solution.py:637
  16.2 5.2 %collective-permute-start.2 = (bf16[208,128]{1,0:T(8,128)(2,1)}, bf16[208,128]{1,0:T(8,128)(2,1)S(1)}, u32[]{:S(2)}, u32[]{:S(2)}) collective-permute-start(bf16[208,128]{1,0:T(8,128)(2,1)} %get-tuple-element.23), channel_id=1, source_target_pairs={{0,3},{1,2},{2,1},{3,0},{4,7},{5,6},{6,5},{7,4},{8,11},{9,10},{10,... | collective-permute-start | bytes 159752 | tf_op jit(solution)/shard_map/ppermute | solution.py:637
  24.4 23.4 %all-to-all-start.1 = ((bf16[8,128,384]{2,1,0:T(8,128)(2,1)}), bf16[8,128,384]{2,1,0:T(8,128)(2,1)S(1)}, u32[]{:S(2)}, u32[]{:S(2)}) async-start(bf16[8,128,384]{2,1,0:T(8,128)(2,1)} %shard_map.117), calls=%async_computation.1 | async-start | bytes 1572864 | tf_op jit(solution)/shard_map/all_to_all | solution.py:722
  47.8 10.4 %all-to-all-start = ((bf16[4,576,128]{2,1,0:T(8,128)(2,1)}), bf16[4,576,128]{2,1,0:T(8,128)(2,1)S(1)}, u32[]{:S(2)}, u32[]{:S(2)}) async-start(bf16[4,576,128]{2,1,0:T(8,128)(2,1)} %get-tuple-element.24), calls=%async_computation | async-start | bytes 1179648 | tf_op jit(solution)/shard_map/all_to_all | solution.py:758
  51.3 22.3 %copy-start.1 = (bf16[768,768]{1,0:T(8,128)(2,1)S(1)}, bf16[768,768]{1,0:T(8,128)(2,1)}, u32[]{:S(2)}) copy-start(bf16[768,768]{1,0:T(8,128)(2,1)} %key_ref.3) | copy-start | bytes 3538948
  52.2 21.4 %copy-start = (bf16[768,768]{1,0:T(8,128)(2,1)S(1)}, bf16[768,768]{1,0:T(8,128)(2,1)}, u32[]{:S(2)}) copy-start(bf16[768,768]{1,0:T(8,128)(2,1)} %query_ref.3) | copy-start | bytes 3538948
  52.2 21.4 %copy-start.3 = (bf16[256,768]{1,0:T(8,128)(2,1)S(1)}, bf16[256,768]{1,0:T(8,128)(2,1)}, u32[]{:S(2)}) copy-start(bf16[256,768]{1,0:T(8,128)(2,1)} %table_ref.3) | copy-start | bytes 1179652
  52.3 21.4 %copy-start.9 = (s32[1,128]{1,0:T(1,128)S(1)}, s32[1,128]{1,0:T(1,128)}, u32[]{:S(2)}) copy-start(s32[1,128]{1,0:T(1,128)} %tokens_ref.3) | copy-start | bytes 1540
  52.3 1.5 %collective-permute-start.7 = (bf16[864,128]{1,0:T(8,128)(2,1)S(1)}, bf16[864,128]{1,0:T(8,128)(2,1)S(1)}, u32[]{:S(2)}, u32[]{:S(2)}) collective-permute-start(bf16[864,128]{1,0:T(8,128)(2,1)S(1)} %get-tuple-element.30), channel_id=1, source_target_pairs={{0,8},{8,0},{16,24},{24,16},{1,9},{9,1},{17,25},{25,17},{2,10},{10... | collective-permute-start | bytes 663560 | tf_op jit(solution)/shard_map/ppermute | solution.py:637
  54.6 7.8 %collective-permute-start.8 = (bf16[864,128]{1,0:T(8,128)(2,1)}, bf16[864,128]{1,0:T(8,128)(2,1)}, u32[]{:S(2)}, u32[]{:S(2)}) collective-permute-start(bf16[864,128]{1,0:T(8,128)(2,1)} %add.25.here_ref), channel_id=1, source_target_pairs={{0,16},{8,24},{16,0},{24,8},{1,17},{9,25},{17,1},{25,9},{2,18},{10... | collective-permute-start | bytes 663560 | tf_op jit(solution)/shard_map/ppermute | solution.py:637
  63.5 8.2 %collective-permute-start.9 = (bf16[192,128]{1,0:T(8,128)(2,1)S(1)}, bf16[192,128]{1,0:T(8,128)(2,1)S(1)}, u32[]{:S(2)}, u32[]{:S(2)}) collective-permute-start(bf16[192,128]{1,0:T(8,128)(2,1)S(1)} %get-tuple-element.32), channel_id=1, source_target_pairs={{0,1},{1,0},{2,3},{3,2},{4,5},{5,4},{6,7},{7,6},{8,9},{9,8},{10,11... | collective-permute-start | bytes 147464 | tf_op jit(solution)/shard_map/ppermute | solution.py:637
  65.5 11.4 %collective-permute-start.14 = (bf16[288,128]{1,0:T(8,128)(2,1)S(1)}, bf16[288,128]{1,0:T(8,128)(2,1)S(1)}, u32[]{:S(2)}, u32[]{:S(2)}) collective-permute-start(bf16[288,128]{1,0:T(8,128)(2,1)S(1)} %get-tuple-element.35.own_ref), channel_id=1, source_target_pairs={{4,6},{5,7},{12,14},{13,15},{20,22},{21,23},{28,30},{29,31}} | collective-permute-start | bytes 221192 | tf_op jit(solution)/shard_map/ppermute | solution.py:782
  66.2 10.7 %collective-permute-start.13 = (bf16[288,128]{1,0:T(8,128)(2,1)S(1)}, bf16[288,128]{1,0:T(8,128)(2,1)S(1)}, u32[]{:S(2)}, u32[]{:S(2)}) collective-permute-start(bf16[288,128]{1,0:T(8,128)(2,1)S(1)} %get-tuple-element.35.own_ref), channel_id=1, source_target_pairs={{2,6},{3,7},{10,14},{11,15},{18,22},{19,23},{26,30},{27,31}} | collective-permute-start | bytes 221192 | tf_op jit(solution)/shard_map/ppermute | solution.py:782
  66.8 10.1 %collective-permute-start.12 = (bf16[288,128]{1,0:T(8,128)(2,1)S(1)}, bf16[288,128]{1,0:T(8,128)(2,1)S(1)}, u32[]{:S(2)}, u32[]{:S(2)}) collective-permute-start(bf16[288,128]{1,0:T(8,128)(2,1)S(1)} %get-tuple-element.35.own_ref), channel_id=1, source_target_pairs={{0,6},{1,7},{8,14},{9,15},{16,22},{17,23},{24,30},{25,31}} | collective-permute-start | bytes 221192 | tf_op jit(solution)/shard_map/ppermute | solution.py:782
  71.5 5.3 %collective-permute-start.10 = (bf16[192,128]{1,0:T(8,128)(2,1)S(1)}, bf16[192,128]{1,0:T(8,128)(2,1)S(1)}, u32[]{:S(2)}, u32[]{:S(2)}) collective-permute-start(bf16[192,128]{1,0:T(8,128)(2,1)S(1)} %get-tuple-element.33), channel_id=1, source_target_pairs={{0,2},{1,3},{2,0},{3,1},{4,6},{5,7},{6,4},{7,5},{8,10},{9,11},{10,... | collective-permute-start | bytes 147464 | tf_op jit(solution)/shard_map/ppermute | solution.py:637
  71.6 5.2 %collective-permute-start.11 = (bf16[192,128]{1,0:T(8,128)(2,1)S(1)}, bf16[192,128]{1,0:T(8,128)(2,1)S(1)}, u32[]{:S(2)}, u32[]{:S(2)}) collective-permute-start(bf16[192,128]{1,0:T(8,128)(2,1)S(1)} %get-tuple-element.34), channel_id=1, source_target_pairs={{0,3},{1,2},{2,1},{3,0},{4,7},{5,6},{6,5},{7,4},{8,11},{9,10},{10,... | collective-permute-start | bytes 147464 | tf_op jit(solution)/shard_map/ppermute | solution.py:637
  74.9 5.2 %copy-start.10 = (bf16[256,384]{1,0:T(8,128)(2,1)S(1)}, bf16[256,384]{1,0:T(8,128)(2,1)}, u32[]{:S(2)}) copy-start(bf16[256,384]{1,0:T(8,128)(2,1)} %get-tuple-element.25.normed_ref) | copy-start | bytes 589828
  78.4 1.6 %collective-permute-start.15 = (bf16[1152,128]{1,0:T(8,128)(2,1)S(1)}, bf16[1152,128]{1,0:T(8,128)(2,1)S(1)}, u32[]{:S(2)}, u32[]{:S(2)}) collective-permute-start(bf16[1152,128]{1,0:T(8,128)(2,1)S(1)} %shard_map.120.mine_ref), channel_id=1, source_target_pairs={{0,8},{8,0},{16,24},{24,16},{1,9},{9,1},{17,25},{25,17},{2,10},{10... | collective-permute-start | bytes 884744 | tf_op jit(solution)/shard_map/ppermute | solution.py:637
  (9 other events, 27.0 us)
